TPU v7x, 32 devices: a whole 2x2x4 slice. The times are simulated.
32 devices in a mesh: grp: 8 (over y, x, core), ep: 4 (over z).
Axes of the slice: x: 2, y: 2, z: 4, core: 2. Of those that a mesh axis runs over, the one named last changes fastest.
Arguments:
- residual_in: bfloat16 [4096, 2048], P(('grp', 'ep')), may hold values from -6 to 6
- attention_gain: bfloat16 [2048], replicated, may hold values from 0.5 to 1.5
- query_weight: bfloat16 [2048, 2048], P('grp', 'ep'), may hold values from -0.125 to 0.125
- query_bias: bfloat16 [2048], P('ep'), may hold values from -1.5 to 1.5
- key_weight: bfloat16 [2048, 2048], P('grp', 'ep'), may hold values from -0.125 to 0.125
- key_bias: bfloat16 [2048], P('ep'), may hold values from -1.5 to 1.5
- value_weight: bfloat16 [2048, 2048], P('grp', 'ep'), may hold values from -0.125 to 0.125
- value_bias: bfloat16 [2048], P('ep'), may hold values from -1.5 to 1.5
- output_weight: bfloat16 [2048, 2048], P('ep', 'grp'), may hold values from -1 to 1
- feedforward_gain: bfloat16 [2048], replicated, may hold values from 0.5 to 1.5
- router_weight: bfloat16 [2048, 8], replicated, may hold values from -0.0625 to 0.0625
- shared_logit_weight: bfloat16 [2048], replicated, may hold values from -0.125 to 0.125
- shared_gate_weight: bfloat16 [2048, 5632], P('grp', 'ep'), may hold values from -0.125 to 0.125
- shared_up_weight: bfloat16 [2048, 5632], P('grp', 'ep'), may hold values from -0.125 to 0.125
- shared_down_weight: bfloat16 [5632, 2048], P('ep', 'grp'), may hold values from -0.21875 to 0.21875
- expert_gate: bfloat16 [8, 2048, 1408], P('ep', 'grp'), may hold values from -0.125 to 0.125
- expert_up: bfloat16 [8, 2048, 1408], P('ep', 'grp'), may hold values from -0.125 to 0.125
- expert_down: bfloat16 [8, 1408, 2048], P('ep', 'grp'), may hold values from -0.875 to 0.875
- cotangent: bfloat16 [4096, 2048], P(('grp', 'ep')), may hold values from -6 to 6
- expert_index: int32 [4096, 4], P(('grp', 'ep')), may hold values from 0 to 7, all different within a row; in each aligned block of 128 rows (0 to 127, 128 to 255, ...) at most 96 rows name the same one
- token_live: int32 [4096], P(('grp', 'ep')), may hold values 0 or 1
- document_lengths: int32 [2, 4], replicated, may hold values from 1 to 1024, 2048 in all within a row
Outputs:
- layer_out: bfloat16 [4096, 2048], P(('grp', 'ep'))
- input_grad: float32 [4096, 2048], P(('grp', 'ep'))
- attention_gain_grad: float32 [2048], replicated
- query_weight_grad: float32 [2048, 2048], P('grp', 'ep')
- query_bias_grad: float32 [2048], P('ep')
- key_weight_grad: float32 [2048, 2048], P('grp', 'ep')
- key_bias_grad: float32 [2048], P('ep')
- value_weight_grad: float32 [2048, 2048], P('grp', 'ep')
- value_bias_grad: float32 [2048], P('ep')
- output_weight_grad: float32 [2048, 2048], P('ep', 'grp')
- feedforward_gain_grad: float32 [2048], replicated
- router_weight_grad: float32 [2048, 8], replicated
- shared_logit_grad: float32 [2048], replicated
- shared_gate_grad: float32 [2048, 5632], P('grp', 'ep')
- shared_up_grad: float32 [2048, 5632], P('grp', 'ep')
- shared_down_grad: float32 [5632, 2048], P('ep', 'grp')
- expert_gate_grad: float32 [8, 2048, 1408], P('ep', 'grp')
- expert_up_grad: float32 [8, 2048, 1408], P('ep', 'grp')
- expert_down_grad: float32 [8, 1408, 2048], P('ep', 'grp')
Inputs may be any that keep to these rules, and one draw needn't show every extreme that they name: `expert_index`: each row names 4 different experts; among the rows of one device no expert is named more than 96 times, a bound that some block reaches there. `document_lengths`: each row sums to 2048, and its largest entry is 1024.
All inputs are finite; a program needn't handle non-finite values. No bound on the sum of `token_live` on one device may be relied on, other than what follows from the above.
Results may differ from a plain program's by a relative error of at most 0.024.
Values may be sent and summed in bfloat16 or wider, within the bound.
A program may use at most 320 MiB of HBM per device.

v0:
```python
import jax
import jax.numpy as jnp
from jax import lax
from jax.sharding import PartitionSpec as P

HDIM = 128
SEQS = 2
DOCS = 4
WINDOW = 1024
CAP = 96


EPS = 1e-06
ROPE_BASE = 1000000.0
MASKED = -1e30


def passed_along(block, axis, distance):
    devices = range(lax.axis_size(axis))
    route = [(i - distance, i) for i in devices if i - distance in devices]
    return lax.ppermute(block, axis, route)


def matmul_plain(left, right):
    return jnp.dot(left, right, preferred_element_type=jnp.float32)


def matmul_last(left, right):
    return lax.dot_general(
        left, right, (((1,), (1,)), ((), ())), preferred_element_type=jnp.float32
    )


def matmul_first(left, right):
    return lax.dot_general(
        left, right, (((0,), (0,)), ((), ())), preferred_element_type=jnp.float32
    )


def norm_scale(values):
    return lax.rsqrt(jnp.mean(values * values, axis=-1, keepdims=True) + EPS)


def norm_backward(grad_normed, unit, scale, gain):
    grad_unit = grad_normed * gain
    inner = jnp.mean(grad_unit * unit, axis=-1, keepdims=True)
    return (scale * (grad_unit - unit * inner), jnp.sum(grad_normed * unit, axis=0))


def swish_slope(values):
    sigma = jax.nn.sigmoid(values)
    return sigma * (1.0 + values * (1.0 - sigma))


def doc_layout(document_lengths, seq_len, first, count):
    index = first + jnp.arange(count, dtype=jnp.int32)
    valid = index >= 0
    safe = jnp.maximum(index, 0)
    seq_of = safe // seq_len
    place = safe % seq_len
    seq_count = document_lengths.shape[0]
    picker = (seq_of[:, None] == jnp.arange(seq_count, dtype=jnp.int32)[None, :]).astype(jnp.int32)
    lengths = jnp.sum(picker[:, :, None] * document_lengths[None, :, :], axis=1)
    ends = jnp.cumsum(lengths, axis=1)
    doc = jnp.sum((ends <= place[:, None]).astype(jnp.int32), axis=1)
    earlier = jnp.arange(DOCS, dtype=jnp.int32)[None, :] < doc[:, None]
    before = jnp.sum(jnp.where(earlier, lengths, 0), axis=1)
    docid = jnp.where(valid, seq_of * DOCS + doc, -1)
    return (docid, place - before)


def rope_tables(position):
    half = HDIM // 2
    freq = ROPE_BASE ** (-(jnp.arange(half, dtype=jnp.float32) * 2.0 / HDIM))
    angle = position.astype(jnp.float32)[:, None] * freq[None, :]
    return (jnp.cos(angle)[:, None, :], jnp.sin(angle)[:, None, :])


def rotate(values, cosine, sine):
    half = values.shape[-1] // 2
    first = values[..., :half]
    second = values[..., half:]
    return jnp.concatenate(
        [first * cosine - second * sine, second * cosine + first * sine], axis=-1
    )


def unrotate(grads, cosine, sine):
    half = grads.shape[-1] // 2
    first = grads[..., :half]
    second = grads[..., half:]
    return jnp.concatenate(
        [first * cosine + second * sine, second * cosine - first * sine], axis=-1
    )


def masked_scores(query, keys_all, allowed):
    raw = jnp.einsum(
        "qhd,khd->hqk", query, keys_all, preferred_element_type=jnp.float32
    ) * HDIM ** (-0.5)
    return jnp.where(allowed[None, :, :], raw, MASKED)


def gather_rows(values):
    return lax.all_gather(values, "ep", axis=0, tiled=True)


def spread_rows(values):
    return lax.psum_scatter(values, "ep", scatter_dimension=0, tiled=True)


def swap_experts(values):
    return lax.all_to_all(values, "ep", split_axis=0, concat_axis=0, tiled=True)


def local(
    residual_in,
    attention_gain,
    query_weight,
    query_bias,
    key_weight,
    key_bias,
    value_weight,
    value_bias,
    output_weight,
    feedforward_gain,
    router_weight,
    shared_logit_weight,
    shared_gate_weight,
    shared_up_weight,
    shared_down_weight,
    expert_gate,
    expert_up,
    expert_down,
    cotangent,
    expert_index,
    token_live,
    document_lengths,
):
    ep_count = lax.axis_size("ep")
    grp_count = lax.axis_size("grp")
    rows_dev, width = residual_in.shape
    group_rows = rows_dev * ep_count
    seq_len = rows_dev * ep_count * grp_count // SEQS
    local_width = query_weight.shape[1]
    heads_local = local_width // HDIM
    experts_local = expert_gate.shape[0]
    expert_count = experts_local * ep_count
    capacity = CAP
    chosen_count = expert_index.shape[1]
    grp_index = lax.axis_index("grp")
    ep_index = lax.axis_index("ep")
    group_first = grp_index * group_rows
    back = -(-WINDOW // group_rows)
    (
        query_full,
        key_full,
        value_full,
        output_full,
        shared_gate_full,
        shared_up_full,
        shared_down_full,
        expert_gate_full,
        expert_up_full,
        expert_down_full,
    ) = (
        lax.all_gather(query_weight, "grp", axis=0, tiled=True),
        lax.all_gather(key_weight, "grp", axis=0, tiled=True),
        lax.all_gather(value_weight, "grp", axis=0, tiled=True),
        lax.all_gather(output_weight, "grp", axis=1, tiled=True),
        lax.all_gather(shared_gate_weight, "grp", axis=0, tiled=True),
        lax.all_gather(shared_up_weight, "grp", axis=0, tiled=True),
        lax.all_gather(shared_down_weight, "grp", axis=1, tiled=True),
        lax.all_gather(expert_gate, "grp", axis=1, tiled=True),
        lax.all_gather(expert_up, "grp", axis=1, tiled=True),
        lax.all_gather(expert_down, "grp", axis=1, tiled=True),
    )
    hidden_in = residual_in.astype(jnp.float32)
    scale_one = norm_scale(hidden_in)
    unit_one = hidden_in * scale_one
    gain_one = attention_gain.astype(jnp.float32)
    normed_one = (unit_one * gain_one).astype(jnp.bfloat16)
    rows_one = gather_rows(normed_one)
    query_lin = matmul_plain(rows_one, query_full) + query_bias.astype(jnp.float32)
    key_lin = matmul_plain(rows_one, key_full) + key_bias.astype(jnp.float32)
    value_lin = matmul_plain(rows_one, value_full) + value_bias.astype(jnp.float32)
    query_doc, query_position = doc_layout(document_lengths, seq_len, group_first, group_rows)
    cosine, sine = rope_tables(query_position)
    query = rotate(query_lin.reshape(group_rows, heads_local, HDIM), cosine, sine).astype(
        jnp.bfloat16
    )
    key = rotate(key_lin.reshape(group_rows, heads_local, HDIM), cosine, sine).astype(jnp.bfloat16)
    value = value_lin.astype(jnp.bfloat16).reshape(group_rows, heads_local, HDIM)
    moving = (key, value)
    earlier_pairs = []
    for step in range(back):
        moving = passed_along((moving[0], moving[1]), "grp", 1)
        earlier_pairs.insert(0, moving)
    keys_all = jnp.concatenate([pair[0] for pair in earlier_pairs] + [key], axis=0)
    values_all = jnp.concatenate([pair[1] for pair in earlier_pairs] + [value], axis=0)
    key_first = group_first - back * group_rows
    key_doc, key_position = doc_layout(
        document_lengths, seq_len, key_first, (back + 1) * group_rows
    )
    query_place = group_first + jnp.arange(group_rows, dtype=jnp.int32)
    key_place = key_first + jnp.arange((back + 1) * group_rows, dtype=jnp.int32)
    distance = query_place[:, None] - key_place[None, :]
    allowed = (distance >= 0) & (distance < WINDOW) & (query_doc[:, None] == key_doc[None, :])
    scores = masked_scores(query, keys_all, allowed)
    top = jnp.max(scores, axis=-1, keepdims=True)
    weights = jnp.exp(scores - top)
    total = jnp.sum(weights, axis=-1, keepdims=True)
    log_total = top + jnp.log(total)
    probs = weights / total
    attended = jnp.einsum(
        "hqk,khd->qhd", probs.astype(jnp.bfloat16), values_all, preferred_element_type=jnp.float32
    )
    attended = attended.astype(jnp.bfloat16).reshape(group_rows, local_width)
    mixed = hidden_in + spread_rows(matmul_plain(attended, output_full))
    scale_two = norm_scale(mixed)
    unit_two = mixed * scale_two
    gain_two = feedforward_gain.astype(jnp.float32)
    normed_two = (unit_two * gain_two).astype(jnp.bfloat16)
    router_probs = jax.nn.softmax(matmul_plain(normed_two, router_weight), axis=-1)
    chosen = (
        (expert_index[:, :, None] == jnp.arange(expert_count, dtype=jnp.int32)[None, None, :])
        & (token_live[:, None, None] > 0)
    ).astype(jnp.float32)
    gate = jnp.sum(chosen * router_probs[:, None, :], axis=-1)
    flat = chosen.reshape(rows_dev * chosen_count, expert_count)
    before = jnp.cumsum(flat, axis=0) - flat
    slot = jnp.sum(before * flat, axis=1)
    slot_hot = (slot[:, None] == jnp.arange(capacity, dtype=jnp.float32)[None, :]).astype(
        jnp.float32
    )
    route = (flat[:, :, None] * slot_hot[:, None, :]).reshape(
        rows_dev * chosen_count, expert_count * capacity
    )
    route_low = route.astype(jnp.bfloat16)
    token_map = jnp.sum(route.reshape(rows_dev, chosen_count, expert_count * capacity), axis=1)
    token_map = token_map.astype(jnp.bfloat16)
    buffer = jnp.einsum("tn,td->nd", token_map, normed_two, preferred_element_type=jnp.float32)
    buffer = buffer.astype(jnp.bfloat16).reshape(ep_count, experts_local, capacity, width)
    arrived = swap_experts(buffer)
    gate_pre = jnp.einsum(
        "sjcd,jdf->sjcf", arrived, expert_gate_full, preferred_element_type=jnp.float32
    )
    up_pre = jnp.einsum(
        "sjcd,jdf->sjcf", arrived, expert_up_full, preferred_element_type=jnp.float32
    )
    active = (jax.nn.silu(gate_pre) * up_pre).astype(jnp.bfloat16)
    result = jnp.einsum(
        "sjcf,jfd->sjcd", active, expert_down_full, preferred_element_type=jnp.float32
    )
    returned = swap_experts(result.astype(jnp.bfloat16))
    result_tok = jnp.einsum(
        "an,nd->ad",
        route_low,
        returned.reshape(expert_count * capacity, width),
        preferred_element_type=jnp.float32,
    ).reshape(rows_dev, chosen_count, width)
    routed = jnp.sum(gate[:, :, None] * result_tok, axis=1)
    rows_two = gather_rows(normed_two)
    shared_gate_pre = matmul_plain(rows_two, shared_gate_full)
    shared_up_pre = matmul_plain(rows_two, shared_up_full)
    shared_active = (jax.nn.silu(shared_gate_pre) * shared_up_pre).astype(jnp.bfloat16)
    shared_out = spread_rows(matmul_plain(shared_active, shared_down_full))
    logit_weight = shared_logit_weight.astype(jnp.float32)
    shared_scale = jax.nn.sigmoid(matmul_plain(normed_two, shared_logit_weight[:, None]))
    layer_out = (mixed + routed + shared_scale * shared_out).astype(jnp.bfloat16)
    grad_out = cotangent.astype(jnp.float32)
    grad_shared_out = (shared_scale * grad_out).astype(jnp.bfloat16)
    grad_shared_rows = gather_rows(grad_shared_out)
    grad_shared_active = matmul_last(grad_shared_rows, shared_down_full)
    grad_shared_gate_pre = (
        grad_shared_active * shared_up_pre * swish_slope(shared_gate_pre)
    ).astype(jnp.bfloat16)
    grad_shared_up_pre = (grad_shared_active * jax.nn.silu(shared_gate_pre)).astype(jnp.bfloat16)
    shared_down_grad = matmul_first(shared_active, grad_shared_rows)
    shared_gate_grad = matmul_first(rows_two, grad_shared_gate_pre)
    shared_up_grad = matmul_first(rows_two, grad_shared_up_pre)
    grad_normed_two = spread_rows(
        matmul_last(grad_shared_gate_pre, shared_gate_full)
        + matmul_last(grad_shared_up_pre, shared_up_full)
    )
    normed_float = normed_two.astype(jnp.float32)
    grad_logit = (
        jnp.sum(grad_out * shared_out, axis=-1, keepdims=True) * shared_scale * (1.0 - shared_scale)
    )
    shared_logit_grad = jnp.sum(normed_float * grad_logit, axis=0)
    grad_normed_two = grad_normed_two + grad_logit * logit_weight[None, :]
    grad_gate = jnp.sum(grad_out[:, None, :] * result_tok, axis=-1)
    grad_probs = jnp.sum(grad_gate[:, :, None] * chosen, axis=1)
    grad_logits = router_probs * (
        grad_probs - jnp.sum(router_probs * grad_probs, axis=-1, keepdims=True)
    )
    router_weight_grad = matmul_first(normed_float, grad_logits)
    grad_normed_two = grad_normed_two + matmul_last(grad_logits, router_weight.astype(jnp.float32))
    grad_result = (gate[:, :, None] * grad_out[:, None, :]).astype(jnp.bfloat16)
    grad_result = grad_result.reshape(rows_dev * chosen_count, width)
    grad_buffer = jnp.einsum(
        "an,ad->nd", route_low, grad_result, preferred_element_type=jnp.float32
    )
    grad_buffer = grad_buffer.astype(jnp.bfloat16).reshape(ep_count, experts_local, capacity, width)
    grad_arrived = swap_experts(grad_buffer)
    grad_active = jnp.einsum(
        "sjcd,jfd->sjcf", grad_arrived, expert_down_full, preferred_element_type=jnp.float32
    )
    grad_gate_pre = (grad_active * up_pre * swish_slope(gate_pre)).astype(jnp.bfloat16)
    grad_up_pre = (grad_active * jax.nn.silu(gate_pre)).astype(jnp.bfloat16)
    expert_gate_grad = jnp.einsum(
        "sjcd,sjcf->jdf", arrived, grad_gate_pre, preferred_element_type=jnp.float32
    )
    expert_up_grad = jnp.einsum(
        "sjcd,sjcf->jdf", arrived, grad_up_pre, preferred_element_type=jnp.float32
    )
    expert_down_grad = jnp.einsum(
        "sjcf,sjcd->jfd", active, grad_arrived, preferred_element_type=jnp.float32
    )
    grad_rows = jnp.einsum(
        "sjcf,jdf->sjcd", grad_gate_pre, expert_gate_full, preferred_element_type=jnp.float32
    ) + jnp.einsum(
        "sjcf,jdf->sjcd", grad_up_pre, expert_up_full, preferred_element_type=jnp.float32
    )
    grad_returned = swap_experts(grad_rows.astype(jnp.bfloat16))
    grad_tok = jnp.einsum(
        "an,nd->ad",
        route_low,
        grad_returned.reshape(expert_count * capacity, width),
        preferred_element_type=jnp.float32,
    ).reshape(rows_dev, chosen_count, width)
    grad_normed_two = grad_normed_two + jnp.sum(grad_tok, axis=1)
    grad_norm_part, feedforward_gain_grad = norm_backward(
        grad_normed_two, unit_two, scale_two, gain_two
    )
    grad_mixed = grad_out + grad_norm_part
    grad_branch = gather_rows(grad_mixed.astype(jnp.bfloat16))
    output_weight_grad = matmul_first(attended, grad_branch)
    grad_attended = matmul_last(grad_branch, output_full).astype(jnp.bfloat16)
    grad_attended = grad_attended.reshape(group_rows, heads_local, HDIM)
    scores_again = masked_scores(query, keys_all, allowed)
    probs_again = jnp.exp(scores_again - log_total)
    grad_probs_att = jnp.einsum(
        "qhd,khd->hqk", grad_attended, values_all, preferred_element_type=jnp.float32
    )
    inner = jnp.sum(probs_again * grad_probs_att, axis=-1, keepdims=True)
    grad_scores = (probs_again * (grad_probs_att - inner)).astype(jnp.bfloat16)
    grad_query = jnp.einsum(
        "hqk,khd->qhd", grad_scores, keys_all, preferred_element_type=jnp.float32
    ) * HDIM ** (-0.5)
    grad_keys_all = jnp.einsum(
        "hqk,qhd->khd", grad_scores, query, preferred_element_type=jnp.float32
    ) * HDIM ** (-0.5)
    grad_values_all = jnp.einsum(
        "hqk,qhd->khd",
        probs_again.astype(jnp.bfloat16),
        grad_attended,
        preferred_element_type=jnp.float32,
    )
    pieces = [
        (
            grad_keys_all[part * group_rows : (part + 1) * group_rows],
            grad_values_all[part * group_rows : (part + 1) * group_rows],
        )
        for part in range(back + 1)
    ]
    carried = pieces[0]
    for step in range(back):
        received = passed_along(carried, "grp", -1)
        carried = (pieces[step + 1][0] + received[0], pieces[step + 1][1] + received[1])
    grad_key_rot, grad_value = carried
    grad_query_lin = (
        unrotate(grad_query, cosine, sine).reshape(group_rows, local_width).astype(jnp.bfloat16)
    )
    grad_key_lin = (
        unrotate(grad_key_rot, cosine, sine).reshape(group_rows, local_width).astype(jnp.bfloat16)
    )
    grad_value_lin = grad_value.reshape(group_rows, local_width).astype(jnp.bfloat16)
    query_weight_grad = matmul_first(rows_one, grad_query_lin)
    key_weight_grad = matmul_first(rows_one, grad_key_lin)
    value_weight_grad = matmul_first(rows_one, grad_value_lin)
    bias_local = jnp.stack(
        [
            jnp.sum(grad_query_lin.astype(jnp.float32), axis=0),
            jnp.sum(grad_key_lin.astype(jnp.float32), axis=0),
            jnp.sum(grad_value_lin.astype(jnp.float32), axis=0),
        ],
        axis=0,
    )
    bias_full = lax.dynamic_update_slice(
        jnp.zeros((3, width), jnp.float32), bias_local, (jnp.int32(0), ep_index * local_width)
    )
    grad_normed_one = spread_rows(
        matmul_last(grad_query_lin, query_full)
        + matmul_last(grad_key_lin, key_full)
        + matmul_last(grad_value_lin, value_full)
    )
    grad_norm_one, attention_gain_grad = norm_backward(
        grad_normed_one, unit_one, scale_one, gain_one
    )
    input_grad = grad_mixed + grad_norm_one
    attention_gain_grad, feedforward_gain_grad, router_weight_grad, shared_logit_grad, bias_full = (
        lax.psum(
            (
                attention_gain_grad,
                feedforward_gain_grad,
                router_weight_grad,
                shared_logit_grad,
                bias_full,
            ),
            ("grp", "ep"),
        )
    )
    bias_mine = lax.dynamic_slice_in_dim(bias_full, ep_index * local_width, local_width, 1)
    (
        query_weight_grad,
        key_weight_grad,
        value_weight_grad,
        output_weight_grad,
        shared_gate_grad,
        shared_up_grad,
        shared_down_grad,
        expert_gate_grad,
        expert_up_grad,
        expert_down_grad,
    ) = (
        lax.psum_scatter(query_weight_grad, "grp", scatter_dimension=0, tiled=True),
        lax.psum_scatter(key_weight_grad, "grp", scatter_dimension=0, tiled=True),
        lax.psum_scatter(value_weight_grad, "grp", scatter_dimension=0, tiled=True),
        lax.psum_scatter(output_weight_grad, "grp", scatter_dimension=1, tiled=True),
        lax.psum_scatter(shared_gate_grad, "grp", scatter_dimension=0, tiled=True),
        lax.psum_scatter(shared_up_grad, "grp", scatter_dimension=0, tiled=True),
        lax.psum_scatter(shared_down_grad, "grp", scatter_dimension=1, tiled=True),
        lax.psum_scatter(expert_gate_grad, "grp", scatter_dimension=1, tiled=True),
        lax.psum_scatter(expert_up_grad, "grp", scatter_dimension=1, tiled=True),
        lax.psum_scatter(expert_down_grad, "grp", scatter_dimension=1, tiled=True),
    )
    return (
        layer_out,
        input_grad,
        attention_gain_grad,
        query_weight_grad,
        bias_mine[0],
        key_weight_grad,
        bias_mine[1],
        value_weight_grad,
        bias_mine[2],
        output_weight_grad,
        feedforward_gain_grad,
        router_weight_grad,
        shared_logit_grad,
        shared_gate_grad,
        shared_up_grad,
        shared_down_grad,
        expert_gate_grad,
        expert_up_grad,
        expert_down_grad,
    )


def solution(mesh):
    in_specs = (
        P(("grp", "ep"), None),
        P(),
        P("grp", "ep"),
        P("ep"),
        P("grp", "ep"),
        P("ep"),
        P("grp", "ep"),
        P("ep"),
        P("ep", "grp"),
        P(),
        P(),
        P(),
        P("grp", "ep"),
        P("grp", "ep"),
        P("ep", "grp"),
        P("ep", "grp", None),
        P("ep", "grp", None),
        P("ep", "grp", None),
        P(("grp", "ep"), None),
        P(("grp", "ep"), None),
        P(("grp", "ep")),
        P(),
    )
    out_specs = (
        P(("grp", "ep"), None),
        P(("grp", "ep"), None),
        P(),
        P("grp", "ep"),
        P("ep"),
        P("grp", "ep"),
        P("ep"),
        P("grp", "ep"),
        P("ep"),
        P("ep", "grp"),
        P(),
        P(),
        P(),
        P("grp", "ep"),
        P("grp", "ep"),
        P("ep", "grp"),
        P("ep", "grp", None),
        P("ep", "grp", None),
        P("ep", "grp", None),
    )
    return jax.shard_map(local, mesh=mesh, in_specs=in_specs, out_specs=out_specs, check_vma=False)
```

profile of v0, /device:TPU:0, one launch (start us, length us, event | category | flops | bytes accessed | tf_op | source)
XLA Modules:
  0.0 2339.8 jit_solution(5427845122557632036)
XLA Ops:
  16.3 43.8 %all-gather.15.cloned.1.call-done = bf16[512,2048]{1,0:T(8,128)(2,1)} async-done(((bf16[128,2048]{1,0:T(8,128)(2,1)}), bf16[512,2048]{1,0:T(8,128)(2,1)}) %all-gather.15.cloned.1.call-update) | async-done | bytes 2097168 | tf_op jit(solution)/shard_map/all_gather | solution.py:105
  60.1 28.5 %all-gather.21.cloned.1.call-done = bf16[2048,512]{1,0:T(8,128)(2,1)} async-done(((bf16[256,512]{1,0:T(8,128)(2,1)}), bf16[2048,512]{1,0:T(8,128)(2,1)}) %all-gather.21.cloned.1.call-update) | async-done | bytes 2097168 | tf_op jit(solution)/shard_map/all_gather | solution.py:168
  96.9 21.5 all-gather.19.cloned.1.call-done
  135.5 15.4 all-gather.17.cloned.1.call-done
  159.3 8.0 collective-permute-start.1
  190.4 80.5 %reduce-scatter.15.cloned.1.call-done = f32[128,2048]{1,0:T(8,128)} async-done(((f32[512,2048]{1,0:T(8,128)}), f32[128,2048]{1,0:T(8,128)}) %reduce-scatter.15.cloned.1.call-update) | async-done | bytes 1048592 | tf_op jit(solution)/shard_map/reduce_scatter | solution.py:109
  316.9 81.8 %all-gather.31.cloned.1.call-done = bf16[512,2048]{1,0:T(8,128)(2,1)} async-done(((bf16[128,2048]{1,0:T(8,128)(2,1)}), bf16[512,2048]{1,0:T(8,128)(2,1)}) %all-gather.31.cloned.1.call-update) | async-done | bytes 2097168 | tf_op jit(solution)/shard_map/all_gather | solution.py:105
  398.7 8.3 fusion.103
  406.9 39.7 %all-gather.35.cloned.1.call-done = bf16[2048,1408]{1,0:T(8,128)(2,1)} async-done(((bf16[256,1408]{1,0:T(8,128)(2,1)}), bf16[2048,1408]{1,0:T(8,128)(2,1)}) %all-gather.35.cloned.1.call-update) | async-done | bytes 5767184 | tf_op jit(solution)/shard_map/all_gather | solution.py:172
  446.6 8.3 fusion.104
  459.6 33.3 %all-gather.37.cloned.1.call-done = bf16[1408,2048]{1,0:T(8,128)(2,1)} async-done(((bf16[1408,256]{1,0:T(8,128)(2,1)}), bf16[1408,2048]{1,0:T(8,128)(2,1)}) %all-gather.37.cloned.1.call-update) | async-done | bytes 5767184 | tf_op jit(solution)/shard_map/all_gather | solution.py:173
  492.9 72.3 %all-gather.39.cloned.1.call-done = bf16[512,2048]{1,0:T(8,128)(2,1)} async-done(((bf16[128,2048]{1,0:T(8,128)(2,1)}), bf16[512,2048]{1,0:T(8,128)(2,1)}) %all-gather.39.cloned.1.call-update) | async-done | bytes 2097168 | tf_op jit(solution)/shard_map/all_gather | solution.py:105
  565.2 11.0 multiply_convert_fusion.2
  582.4 50.3 %all-gather.27.cloned.1.call-done = bf16[2,2048,1408]{2,1,0:T(8,128)(2,1)} async-done(((bf16[2,256,1408]{2,1,0:T(8,128)(2,1)}), bf16[2,2048,1408]{2,1,0:T(8,128)(2,1)}) %all-gather.27.cloned.1.call-update) | async-done | bytes 11534352 | tf_op jit(solution)/shard_map/all_gather | solution.py:175
  632.7 11.4 fusion.2
  644.0 58.4 %all-gather.25.cloned.1.call-done = bf16[2,2048,1408]{2,1,0:T(8,128)(2,1)} async-done(((bf16[2,256,1408]{2,1,0:T(8,128)(2,1)}), bf16[2,2048,1408]{2,1,0:T(8,128)(2,1)}) %all-gather.25.cloned.1.call-update) | async-done | bytes 11534352 | tf_op jit(solution)/shard_map/all_gather | solution.py:174
  702.5 11.4 fusion.6
  713.8 58.3 %all-gather.29.cloned.1.call-done = bf16[2,1408,2048]{2,1,0:T(8,128)(2,1)} async-done(((bf16[2,176,2048]{2,1,0:T(8,128)(2,1)}), bf16[2,1408,2048]{2,1,0:T(8,128)(2,1)}) %all-gather.29.cloned.1.call-update) | async-done | bytes 11534352 | tf_op jit(solution)/shard_map/all_gather | solution.py:176
  772.1 16.1 fusion.19
  788.2 8.6 fusion.38
  803.5 6.2 fusion.106
  809.7 7.8 convolution_add_fusion
  817.6 8.7 fusion
  826.4 12.2 fusion.41
  840.7 77.8 %all-to-all-done.1 = bf16[4,2,96,2048]{3,2,1,0:T(8,128)(2,1)} async-done(((bf16[4,2,96,2048]{3,2,1,0:T(8,128)(2,1)}), bf16[4,2,96,2048]{3,2,1,0:T(8,128)(2,1)}, u32[]{:S(2)}, u32[]{:S(2)}) %all-to-all-start.1) | async-done | bytes 3145760 | tf_op jit(solution)/shard_map/all_to_all | solution.py:113
  931.7 121.4 %all-to-all-done.3 = bf16[4,2,96,2048]{3,2,1,0:T(8,128)(2,1)} async-done(((bf16[4,2,96,2048]{3,2,1,0:T(8,128)(2,1)}), bf16[4,2,96,2048]{3,2,1,0:T(8,128)(2,1)}, u32[]{:S(2)}, u32[]{:S(2)}) %all-to-all-start.3) | async-done | bytes 3145760 | tf_op jit(solution)/shard_map/all_to_all | solution.py:113
  1061.3 44.6 %all-gather.41.cloned.1.call-done = bf16[512,2048]{1,0:T(8,128)(2,1)} async-done(((bf16[128,2048]{1,0:T(8,128)(2,1)}), bf16[512,2048]{1,0:T(8,128)(2,1)}) %all-gather.41.cloned.1.call-update) | async-done | bytes 2097168 | tf_op jit(solution)/shard_map/all_gather | solution.py:105
  1109.5 11.5 multiply_reduce_fusion
  1121.6 6.4 multiply_convert_fusion
  1143.8 7.1 collective-permute-done.5
  1171.3 7.7 fusion.113
  1180.6 7.5 fusion.114
  1189.7 7.3 fusion.115
  1219.2 13.3 convolution_bitcast_fusion.2
  1234.1 13.2 convolution_bitcast_fusion.1
  1249.0 13.1 convolution_bitcast_fusion
  1264.7 56.5 %all-reduce = (f32[2048]{0:T(1024)}, f32[3,2048]{1,0:T(4,128)S(1)}, f32[2048]{0:T(1024)}, f32[2048]{0:T(1024)}) all-reduce(f32[2048]{0:T(1024)S(1)} %get-tuple-element.23, f32[3,2048]{1,0:T(4,128)S(1)} %maximum_dynamic-update-slice_fusion, f32[2048]{0:T(1024)S(1)} %get-tuple-element.21, ...), channel_id=1, replica_groups=mesh['grp'=8,'ep'=4] {'grp','ep'}, use_global_device_ids=true, to_apply=%region_32.33 | all-reduce | flops 12288 | bytes 98304 | tf_op jit(solution)/shard_map/psum | solution.py:403
  1325.5 60.6 %all-reduce.3.cloned.1.call-done = f32[2048,8]{0,1:T(8,128)} async-done(((f32[2048,8]{0,1:T(8,128)}), f32[2048,8]{0,1:T(8,128)}) %all-reduce.3.cloned.1.call-update) | async-done | bytes 65552 | tf_op jit(solution)/shard_map/psum | solution.py:403
  1386.1 91.6 %reduce-scatter.31.cloned.1.call-done = f32[256,1408]{1,0:T(8,128)} async-done(((f32[2048,1408]{1,0:T(8,128)}), f32[256,1408]{1,0:T(8,128)}) %reduce-scatter.31.cloned.1.call-update) | async-done | bytes 1441808 | tf_op jit(solution)/shard_map/reduce_scatter | solution.py:431
  1477.6 90.9 %reduce-scatter.33.cloned.1.call-done = f32[256,1408]{1,0:T(8,128)} async-done(((f32[2048,1408]{1,0:T(8,128)}), f32[256,1408]{1,0:T(8,128)}) %reduce-scatter.33.cloned.1.call-update) | async-done | bytes 1441808 | tf_op jit(solution)/shard_map/reduce_scatter | solution.py:432
  1568.5 90.9 %reduce-scatter.35.cloned.1.call-done = f32[1408,256]{1,0:T(8,128)} async-done(((f32[1408,2048]{1,0:T(8,128)}), f32[1408,256]{1,0:T(8,128)}) %reduce-scatter.35.cloned.1.call-update) | async-done | bytes 1441808 | tf_op jit(solution)/shard_map/reduce_scatter | solution.py:433
  1659.4 55.3 %reduce-scatter.29.cloned.1.call-done = f32[512,256]{1,0:T(8,128)} async-done(((f32[512,2048]{1,0:T(8,128)}), f32[512,256]{1,0:T(8,128)}) %reduce-scatter.29.cloned.1.call-update) | async-done | bytes 524304 | tf_op jit(solution)/shard_map/reduce_scatter | solution.py:430
  1714.7 55.5 %reduce-scatter.23.cloned.1.call-done = f32[256,512]{1,0:T(8,128)} async-done(((f32[2048,512]{1,0:T(8,128)}), f32[256,512]{1,0:T(8,128)}) %reduce-scatter.23.cloned.1.call-update) | async-done | bytes 524304 | tf_op jit(solution)/shard_map/reduce_scatter | solution.py:427
  1770.2 55.3 %reduce-scatter.25.cloned.1.call-done = f32[256,512]{1,0:T(8,128)} async-done(((f32[2048,512]{1,0:T(8,128)}), f32[256,512]{1,0:T(8,128)}) %reduce-scatter.25.cloned.1.call-update) | async-done | bytes 524304 | tf_op jit(solution)/shard_map/reduce_scatter | solution.py:428
  1825.5 55.5 %reduce-scatter.27.cloned.1.call-done = f32[256,512]{1,0:T(8,128)} async-done(((f32[2048,512]{1,0:T(8,128)}), f32[256,512]{1,0:T(8,128)}) %reduce-scatter.27.cloned.1.call-update) | async-done | bytes 524304 | tf_op jit(solution)/shard_map/reduce_scatter | solution.py:429
  1881.0 150.0 %reduce-scatter.37.cloned.1.call-done = f32[2,256,1408]{2,1,0:T(8,128)} async-done(((f32[2,2048,1408]{2,1,0:T(8,128)}), f32[2,256,1408]{2,1,0:T(8,128)}) %reduce-scatter.37.cloned.1.call-update) | async-done | bytes 2883600 | tf_op jit(solution)/shard_map/reduce_scatter | solution.py:434
  2031.0 150.1 %reduce-scatter.39.cloned.1.call-done = f32[2,256,1408]{2,1,0:T(8,128)} async-done(((f32[2,2048,1408]{2,1,0:T(8,128)}), f32[2,256,1408]{2,1,0:T(8,128)}) %reduce-scatter.39.cloned.1.call-update) | async-done | bytes 2883600 | tf_op jit(solution)/shard_map/reduce_scatter | solution.py:435
  2181.2 150.1 %reduce-scatter.41.cloned.1.call-done = f32[2,176,2048]{2,1,0:T(8,128)} async-done(((f32[2,1408,2048]{2,1,0:T(8,128)}), f32[2,176,2048]{2,1,0:T(8,128)}) %reduce-scatter.41.cloned.1.call-update) | async-done | bytes 2883600 | tf_op jit(solution)/shard_map/reduce_scatter | solution.py:436
  (350 shorter events, 228.9 us)
Async XLA Ops:
  7.2 290.6 %copy-start = (bf16[2048,8]{0,1:T(8,128)(2,1)S(1)}, bf16[2048,8]{0,1:T(8,128)(2,1)}, u32[]{:S(2)}) copy-start(bf16[2048,8]{0,1:T(8,128)(2,1)} %param.32) | copy-start | bytes 98308
  7.2 52.8 %all-gather.15.cloned.1.call-start = ((), (), s32[]{:S(2)}) async-start(), calls=%async_computation.18 | async-start | bytes 2621440 | tf_op jit(solution)/shard_map/all_gather | solution.py:105
  11.3 77.3 %all-gather.21.cloned.1.call-start = ((), (), s32[]{:S(2)}) async-start(), calls=%async_computation.21 | async-start | bytes 2359296 | tf_op jit(solution)/shard_map/all_gather | solution.py:168
  12.0 106.4 %all-gather.19.cloned.1.call-start = ((), (), s32[]{:S(2)}) async-start(), calls=%async_computation.20 | async-start | bytes 2359296 | tf_op jit(solution)/shard_map/all_gather | solution.py:167
  12.8 138.1 %all-gather.17.cloned.1.call-start = ((), (), s32[]{:S(2)}) async-start(), calls=%async_computation.19 | async-start | bytes 2359296 | tf_op jit(solution)/shard_map/all_gather | solution.py:169
  13.4 171.4 %all-gather.23.cloned.1.call-start = ((), (), s32[]{:S(2)}) async-start(), calls=%async_computation.22 | async-start | bytes 2359296 | tf_op jit(solution)/shard_map/all_gather | solution.py:170
  13.9 257.0 %reduce-scatter.15.cloned.1.call-start = ((), (), s32[]{:S(2)}) async-start(), calls=%async_computation.23 | async-start | bytes 5242880 | tf_op jit(solution)/shard_map/reduce_scatter | solution.py:109
  16.3 110.8 %copy-start.20 = (f32[512,64]{1,0:T(8,128)}, f32[512,64]{1,0:T(8,128)S(1)}, u32[]{:S(2)}) copy-start(f32[512,64]{1,0:T(8,128)S(1)} %get-tuple-element.66) | copy-start | bytes 393220
  132.5 23.5 %collective-permute-start.2 = (bf16[512,4,128]{2,0,1:T(8,128)(2,1)}, bf16[512,4,128]{2,0,1:T(8,128)(2,1)}, u32[]{:S(2)}, u32[]{:S(2)}) collective-permute-start(bf16[512,4,128]{2,0,1:T(8,128)(2,1)} %pad_maximum_fusion.4), channel_id=1, source_target_pairs={{0,4},{4,8},{8,12},{12,16},{16,20},{20,24},{24,28},{1,5},{5,9},{9,... | collective-permute-start | bytes 1572872 | tf_op jit(solution)/shard_map/ppermute | solution.py:21
  153.9 5.4 collective-permute-start
  156.1 11.3 collective-permute-start.3
  159.3 14.5 collective-permute-start.1
  189.5 81.3 %copy-start.9 = (bf16[128,2048]{1,0:T(8,128)(2,1)S(1)}, bf16[128,2048]{1,0:T(8,128)(2,1)}, u32[]{:S(2)}) copy-start(bf16[128,2048]{1,0:T(8,128)(2,1)} %param.22) | copy-start | bytes 1572868
  189.6 127.3 %all-gather.33.cloned.1.call-start = ((), (), s32[]{:S(2)}) async-start(), calls=%async_computation.28 | async-start | bytes 6488064 | tf_op jit(solution)/shard_map/all_gather | solution.py:171
  190.3 84.4 %copy-start.47 = (bf16[2048]{0:T(1024)(128)(2,1)S(1)}, bf16[2048]{0:T(1024)(128)(2,1)}, u32[]{:S(2)}) copy-start(bf16[2048]{0:T(1024)(128)(2,1)} %param.33) | copy-start | bytes 12292
  190.3 208.3 %all-gather.31.cloned.1.call-start = ((), (), s32[]{:S(2)}) async-start(), calls=%async_computation.27 | async-start | bytes 2621440 | tf_op jit(solution)/shard_map/all_gather | solution.py:105
  190.4 85.7 %copy-start.7 = (bf16[128,2048]{1,0:T(8,128)(2,1)S(1)}, bf16[128,2048]{1,0:T(8,128)(2,1)}, u32[]{:S(2)}) copy-start(bf16[128,2048]{1,0:T(8,128)(2,1)} %param.40) | copy-start | bytes 1572868
  273.3 173.3 %all-gather.35.cloned.1.call-start = ((), (), s32[]{:S(2)}) async-start(), calls=%async_computation.29 | async-start | bytes 6488064 | tf_op jit(solution)/shard_map/all_gather | solution.py:172
  274.1 218.8 %all-gather.37.cloned.1.call-start = ((), (), s32[]{:S(2)}) async-start(), calls=%async_computation.30 | async-start | bytes 6488064 | tf_op jit(solution)/shard_map/all_gather | solution.py:173
  274.7 290.5 %all-gather.39.cloned.1.call-start = ((), (), s32[]{:S(2)}) async-start(), calls=%async_computation.32 | async-start | bytes 2621440 | tf_op jit(solution)/shard_map/all_gather | solution.py:105
  277.0 355.6 %all-gather.27.cloned.1.call-start = ((), (), s32[]{:S(2)}) async-start(), calls=%async_computation.25 | async-start | bytes 12976128 | tf_op jit(solution)/shard_map/all_gather | solution.py:175
  277.6 424.9 %all-gather.25.cloned.1.call-start = ((), (), s32[]{:S(2)}) async-start(), calls=%async_computation.24 | async-start | bytes 12976128 | tf_op jit(solution)/shard_map/all_gather | solution.py:174
  278.4 493.8 %all-gather.29.cloned.1.call-start = ((), (), s32[]{:S(2)}) async-start(), calls=%async_computation.26 | async-start | bytes 12976128 | tf_op jit(solution)/shard_map/all_gather | solution.py:176
  292.7 162.3 %all-to-all-start = ((bf16[4,2,96,2048]{3,2,1,0:T(8,128)(2,1)}), bf16[4,2,96,2048]{3,2,1,0:T(8,128)(2,1)}, u32[]{:S(2)}, u32[]{:S(2)}) async-start(bf16[4,2,96,2048]{3,2,1,0:T(8,128)(2,1)} %bitcast.195), calls=%async_computation.1 | async-start | bytes 6291456 | tf_op jit(solution)/shard_map/all_to_all | solution.py:113
  454.9 258.9 %all-to-all-start.2 = ((bf16[4,2,96,2048]{3,2,1,0:T(8,128)(2,1)}), bf16[4,2,96,2048]{3,2,1,0:T(8,128)(2,1)}, u32[]{:S(2)}, u32[]{:S(2)}) async-start(bf16[4,2,96,2048]{3,2,1,0:T(8,128)(2,1)} %bitcast.202), calls=%async_computation.5 | async-start | bytes 6291456 | tf_op jit(solution)/shard_map/all_to_all | solution.py:113
  459.6 465.4 %reduce-scatter.17.cloned.1.call-start = ((), (), s32[]{:S(2)}) async-start(), calls=%async_computation.31 | async-start | bytes 5242880 | tf_op jit(solution)/shard_map/reduce_scatter | solution.py:109
  798.7 119.7 %all-to-all-start.1 = ((bf16[4,2,96,2048]{3,2,1,0:T(8,128)(2,1)}), bf16[4,2,96,2048]{3,2,1,0:T(8,128)(2,1)}, u32[]{:S(2)}, u32[]{:S(2)}) async-start(bf16[4,2,96,2048]{3,2,1,0:T(8,128)(2,1)} %copy.120), calls=%async_computation.2 | async-start | bytes 6291456 | tf_op jit(solution)/shard_map/all_to_all | solution.py:113
  803.4 253.4 %reduce-scatter.19.cloned.1.call-start = ((), (), s32[]{:S(2)}) async-start(), calls=%async_computation.33 | async-start | bytes 5242880 | tf_op jit(solution)/shard_map/reduce_scatter | solution.py:109
  918.4 134.6 %all-to-all-start.3 = ((bf16[4,2,96,2048]{3,2,1,0:T(8,128)(2,1)}), bf16[4,2,96,2048]{3,2,1,0:T(8,128)(2,1)}, u32[]{:S(2)}, u32[]{:S(2)}) async-start(bf16[4,2,96,2048]{3,2,1,0:T(8,128)(2,1)} %copy.124), calls=%async_computation.6 | async-start | bytes 6291456 | tf_op jit(solution)/shard_map/all_to_all | solution.py:113
  923.1 182.8 %all-gather.41.cloned.1.call-start = ((), (), s32[]{:S(2)}) async-start(), calls=%async_computation.34 | async-start | bytes 2621440 | tf_op jit(solution)/shard_map/all_gather | solution.py:105
  1060.8 201.5 %reduce-scatter.21.cloned.1.call-start = ((), (), s32[]{:S(2)}) async-start(), calls=%async_computation.35 | async-start | bytes 5242880 | tf_op jit(solution)/shard_map/reduce_scatter | solution.py:109
  1130.7 6.1 collective-permute-start.4
  1135.2 6.0 collective-permute-start.6
  1136.9 14.0 collective-permute-start.5
  1142.4 21.1 collective-permute-start.7
  1169.4 216.7 %all-reduce.3.cloned.1.call-start = ((), (), s32[]{:S(2)}) async-start(), calls=%async_computation.40 | async-start | bytes 131072 | tf_op jit(solution)/shard_map/psum | solution.py:403
  1171.2 306.4 %reduce-scatter.31.cloned.1.call-start = ((), (), s32[]{:S(2)}) async-start(), calls=%async_computation.41 | async-start | bytes 12976128 | tf_op jit(solution)/shard_map/reduce_scatter | solution.py:431
  1179.0 389.5 %reduce-scatter.33.cloned.1.call-start = ((), (), s32[]{:S(2)}) async-start(), calls=%async_computation.42 | async-start | bytes 12976128 | tf_op jit(solution)/shard_map/reduce_scatter | solution.py:432
  1188.2 471.3 %reduce-scatter.35.cloned.1.call-start = ((), (), s32[]{:S(2)}) async-start(), calls=%async_computation.43 | async-start | bytes 12976128 | tf_op jit(solution)/shard_map/reduce_scatter | solution.py:433
  1197.1 517.6 %reduce-scatter.29.cloned.1.call-start = ((), (), s32[]{:S(2)}) async-start(), calls=%async_computation.39 | async-start | bytes 4718592 | tf_op jit(solution)/shard_map/reduce_scatter | solution.py:430
  1202.9 567.3 %reduce-scatter.23.cloned.1.call-start = ((), (), s32[]{:S(2)}) async-start(), calls=%async_computation.36 | async-start | bytes 4718592 | tf_op jit(solution)/shard_map/reduce_scatter | solution.py:427
  1208.8 616.7 %reduce-scatter.25.cloned.1.call-start = ((), (), s32[]{:S(2)}) async-start(), calls=%async_computation.37 | async-start | bytes 4718592 | tf_op jit(solution)/shard_map/reduce_scatter | solution.py:428
  1213.2 667.9 %reduce-scatter.27.cloned.1.call-start = ((), (), s32[]{:S(2)}) async-start(), calls=%async_computation.38 | async-start | bytes 4718592 | tf_op jit(solution)/shard_map/reduce_scatter | solution.py:429
  1217.6 813.4 %reduce-scatter.37.cloned.1.call-start = ((), (), s32[]{:S(2)}) async-start(), calls=%async_computation.44 | async-start | bytes 25952256 | tf_op jit(solution)/shard_map/reduce_scatter | solution.py:434
  1232.5 948.6 %reduce-scatter.39.cloned.1.call-start = ((), (), s32[]{:S(2)}) async-start(), calls=%async_computation.45 | async-start | bytes 25952256 | tf_op jit(solution)/shard_map/reduce_scatter | solution.py:435
  1247.4 1083.9 %reduce-scatter.41.cloned.1.call-start = ((), (), s32[]{:S(2)}) async-start(), calls=%async_computation.46 | async-start | bytes 25952256 | tf_op jit(solution)/shard_map/reduce_scatter | solution.py:436
  1262.1 59.8 %copy-start.8 = (bf16[128,2048]{1,0:T(8,128)(2,1)S(1)}, bf16[128,2048]{1,0:T(8,128)(2,1)}, u32[]{:S(2)}) copy-start(bf16[128,2048]{1,0:T(8,128)(2,1)} %param.40) | copy-start | bytes 1572868
  1321.8 1010.9 %copy-start.1 = (bf16[2048,8]{0,1:T(8,128)(2,1)S(1)}, bf16[2048,8]{0,1:T(8,128)(2,1)}, u32[]{:S(2)}) copy-start(bf16[2048,8]{0,1:T(8,128)(2,1)} %param.32) | copy-start | bytes 98308
  (63 other events, 640.4 us)
Sparse Core Ops, SparseCore 0:
  11.4 48.6 all-gather.14
  62.0 26.5 all-gather.20
  90.5 27.8 all-gather.18
  120.2 30.6 all-gather.16
  152.6 32.0 all-gather.22
  189.7 81.1 reduce-scatter.14
  272.9 43.8 all-gather.32
  319.1 79.5 all-gather.30
  400.7 45.8 all-gather.34
  448.5 44.3 all-gather.36
  495.1 69.9 all-gather.38
  567.1 65.5 all-gather.26
  634.7 67.6 all-gather.24
  704.4 67.6 all-gather.28
  774.4 118.1 reduce-scatter.16
  894.7 140.8 reduce-scatter.18
  1060.9 44.9 all-gather.40
  1169.5 92.3 reduce-scatter.20
  1268.0 118.0 all-reduce.2
  1390.0 87.5 reduce-scatter.30
  1481.7 86.7 reduce-scatter.32
  1572.6 86.7 reduce-scatter.34
  1663.4 51.3 reduce-scatter.28
  1718.9 51.3 reduce-scatter.22
  1774.2 51.3 reduce-scatter.24
  1829.7 51.3 reduce-scatter.26
  1885.1 145.9 reduce-scatter.36
  2035.2 145.8 reduce-scatter.38
  2185.4 145.8 reduce-scatter.40
where the time goes:
time: 2350 us; the launch traced here: 2340 us
  waiting for transfers between devices  1860 us (79%)
  matrix products  269 us (11%)
  blocking collectives  56.5 us (2%)
  local copies, waits for them, and re-layouts  51.7 us (2%)
  other arithmetic  43.7 us (2%)
  starting transfers between devices  42 us (2%)
    all_gather x4, waiting for transfers between devices, gather_rows(): return lax.all_gather(values, 'ep', axis=0, tiled=True)  242 us
    all_to_all x4, waiting for transfers between devices, swap_experts(): return lax.all_to_all(values, 'ep', split_axis=0, concat_axis=0, tiled=True)  199 us
    reduce_scatter x1, waiting for transfers between devices, local(): lax.psum_scatter(expert_down_grad, 'grp', scatter_dimension=1, tiled=True)  150 us
    reduce_scatter x1, waiting for transfers between devices, local(): lax.psum_scatter(expert_up_grad, 'grp', scatter_dimension=1, tiled=True)  150 us
    reduce_scatter x1, waiting for transfers between devices, local(): lax.psum_scatter(expert_gate_grad, 'grp', scatter_dimension=1, tiled=True)  150 us
    reduce_scatter x1, waiting for transfers between devices, local(): lax.psum_scatter(shared_gate_grad, 'grp', scatter_dimension=0, tiled=True)  91.6 us
    reduce_scatter x1, waiting for transfers between devices, local(): lax.psum_scatter(shared_up_grad, 'grp', scatter_dimension=0, tiled=True)  90.9 us
    reduce_scatter x1, waiting for transfers between devices, local(): lax.psum_scatter(shared_down_grad, 'grp', scatter_dimension=1, tiled=True)  90.9 us
  transfers between devices with their start and end apart: 41, of which 30 were waited for; matrix products, arithmetic and copies ran while one was open for 13% of the time, Pallas kernels for 0%

commit v1 on v0

v1 whole, which is shorter than its diff:
```python
import jax
import jax.numpy as jnp
from jax import lax
from jax.sharding import PartitionSpec as P

HDIM = 128
SEQS = 2
DOCS = 4
WINDOW = 1024
EPS = 1e-06
ROPE_BASE = 1000000.0
MASKED = -1e30
F32 = jnp.float32
BF16 = jnp.bfloat16


def dot(left, right):
    return jnp.dot(left, right, preferred_element_type=F32)


def dot_last(left, right):
    return lax.dot_general(left, right, (((1,), (1,)), ((), ())), preferred_element_type=F32)


def dot_first(left, right):
    return lax.dot_general(left, right, (((0,), (0,)), ((), ())), preferred_element_type=F32)


def across(block, mask):
    count = lax.axis_size("grp")
    return lax.ppermute(block, "grp", [(i, i ^ mask) for i in range(count)])


def quad_bits():
    return [1 << b for b in range((lax.axis_size("grp") // 2).bit_length() - 1)]


def flip_columns(values, quad):
    quads = lax.axis_size("grp") // 2
    axis = values.ndim - 1
    block = values.shape[axis] // quads
    return jnp.concatenate(
        [
            lax.dynamic_slice_in_dim(values, (quad ^ key) * block, block, axis)
            for key in range(quads)
        ],
        axis=axis,
    )


def gather_quads(pieces, order):
    pieces = dict(pieces)
    for bit in order:
        for key, piece in list(pieces.items()):
            pieces[key | bit] = across(piece, 2 * bit)
    return pieces


def reduce_quads(pieces, order):
    pieces = {key: piece.astype(BF16) for key, piece in pieces.items()}
    for bit in order:
        for key in [key for key in pieces if key & bit]:
            arrived = across(pieces.pop(key), 2 * bit)
            kept = pieces[key ^ bit]
            pieces[key ^ bit] = (kept.astype(F32) + arrived.astype(F32)).astype(BF16)
    return pieces


def together(*values):
    return lax.optimization_barrier(values)


def sum_everywhere(values, masks_grp, masks_ep):
    for mask in masks_grp:
        values = values + across(values, mask)
    count = lax.axis_size("ep")
    for mask in masks_ep:
        values = values + lax.ppermute(values, "ep", [(i, i ^ mask) for i in range(count)])
    return values


def in_order(pieces, axis):
    return jnp.concatenate([pieces[key] for key in sorted(pieces)], axis=axis)


def place_quads(pieces, quad, axis):
    size = pieces[0].shape[axis]
    shape = list(pieces[0].shape)
    shape[axis] = size * len(pieces)
    whole = jnp.zeros(shape, pieces[0].dtype)
    for key in sorted(pieces):
        whole = lax.dynamic_update_slice_in_dim(whole, pieces[key], (quad ^ key) * size, axis)
    return whole


def take_quads(whole, quad, quads, axis):
    size = whole.shape[axis] // quads
    return {
        key: lax.dynamic_slice_in_dim(whole, (quad ^ key) * size, size, axis)
        for key in range(quads)
    }


def merge_core(kept, arrived, core, axis):
    first = jnp.where(core == 0, kept, arrived)
    second = jnp.where(core == 0, arrived, kept)
    return jnp.concatenate([first, second], axis=axis)


def split_core(values, core, axis):
    half = values.shape[axis] // 2
    first = lax.slice_in_dim(values, 0, half, axis=axis)
    second = lax.slice_in_dim(values, half, 2 * half, axis=axis)
    return jnp.where(core == 0, first, second), jnp.where(core == 0, second, first)


def gather_rows(values):
    own = lax.all_gather(values, "ep", axis=0, tiled=True)
    return jnp.concatenate([own, across(own, 1)], axis=0)


def spread_rows(values):
    half = values.shape[0] // 2
    arrived = across(values[half:], 1)
    mine = (values[:half].astype(F32) + arrived.astype(F32)).astype(BF16)
    return lax.psum_scatter(mine, "ep", scatter_dimension=0, tiled=True).astype(F32)


def norm_scale(values):
    return lax.rsqrt(jnp.mean(values * values, axis=-1, keepdims=True) + EPS)


def norm_backward(grad_normed, unit, scale, gain):
    grad_unit = grad_normed * gain
    inner = jnp.mean(grad_unit * unit, axis=-1, keepdims=True)
    return scale * (grad_unit - unit * inner), jnp.sum(grad_normed * unit, axis=0)


def swish_slope(values):
    sigma = jax.nn.sigmoid(values)
    return sigma * (1.0 + values * (1.0 - sigma))


def doc_layout(document_lengths, seq_len, index):
    valid = index >= 0
    safe = jnp.maximum(index, 0)
    seq_of = safe // seq_len
    place = safe % seq_len
    seq_count = document_lengths.shape[0]
    picker = (seq_of[:, None] == jnp.arange(seq_count, dtype=jnp.int32)[None, :]).astype(jnp.int32)
    lengths = jnp.sum(picker[:, :, None] * document_lengths[None, :, :], axis=1)
    ends = jnp.cumsum(lengths, axis=1)
    doc = jnp.sum((ends <= place[:, None]).astype(jnp.int32), axis=1)
    earlier = jnp.arange(DOCS, dtype=jnp.int32)[None, :] < doc[:, None]
    before = jnp.sum(jnp.where(earlier, lengths, 0), axis=1)
    return jnp.where(valid, seq_of * DOCS + doc, -1), place - before


def rope_tables(position):
    half = HDIM // 2
    freq = ROPE_BASE ** (-(jnp.arange(half, dtype=F32) * 2.0 / HDIM))
    angle = position.astype(F32)[:, None] * freq[None, :]
    return jnp.cos(angle)[:, None, :], jnp.sin(angle)[:, None, :]


def rotate(values, cosine, sine):
    half = values.shape[-1] // 2
    first, second = values[..., :half], values[..., half:]
    return jnp.concatenate(
        [first * cosine - second * sine, second * cosine + first * sine], axis=-1
    )


def unrotate(grads, cosine, sine):
    return rotate(grads, cosine, -sine)


def masked_scores(query, keys_all, allowed):
    raw = jnp.einsum("qhd,khd->hqk", query, keys_all, preferred_element_type=F32) * HDIM ** (-0.5)
    return jnp.where(allowed[None, :, :], raw, MASKED)


def two_parts(values):
    high = values.astype(BF16)
    return high, (values - high.astype(F32)).astype(BF16)


def local(
    residual_in,
    attention_gain,
    query_weight,
    query_bias,
    key_weight,
    key_bias,
    value_weight,
    value_bias,
    output_weight,
    feedforward_gain,
    router_weight,
    shared_logit_weight,
    shared_gate_weight,
    shared_up_weight,
    shared_down_weight,
    expert_gate,
    expert_up,
    expert_down,
    cotangent,
    expert_index,
    token_live,
    document_lengths,
):
    ep_count = lax.axis_size("ep")
    grp_count = lax.axis_size("grp")
    quads = grp_count // 2
    rows_dev, width = residual_in.shape
    group_rows = rows_dev * ep_count
    pair_rows = 2 * group_rows
    seq_len = group_rows * grp_count // SEQS
    expert_count = expert_gate.shape[0] * ep_count
    ffe = expert_gate.shape[2]
    ffs_half = shared_gate_weight.shape[1] // 2
    grp = lax.axis_index("grp")
    ep = lax.axis_index("ep")
    core = grp % 2
    quad = grp // 2
    back = -(-WINDOW // pair_rows)
    heads = query_weight.shape[1] // HDIM // 2
    head_width = heads * HDIM
    up_order = quad_bits()
    down_order = up_order[::-1]

    hidden_in = residual_in.astype(F32)
    grad_out = cotangent.astype(F32)
    gain_one = attention_gain.astype(F32)
    gain_two = feedforward_gain.astype(F32)
    router_all = jnp.concatenate([router_weight, shared_logit_weight[:, None]], axis=1)
    router_flipped = flip_columns(router_all.T, quad).T

    scale_one = norm_scale(hidden_in)
    unit_one = hidden_in * scale_one
    normed_one = (unit_one * gain_one).astype(BF16)
    rows_one = gather_rows(flip_columns(normed_one, quad))

    cut = len(up_order) // 2
    up_one, up_two = up_order[:cut], up_order[cut:]
    down_one, down_two = down_order[: len(down_order) - cut], down_order[len(down_order) - cut :]
    qk_keep, qk_other = zip(
        *[split_core(weight, core, 1) for weight in (query_weight, key_weight, value_weight)]
    )
    qkv_keep, qkv_other = jnp.concatenate(qk_keep, 1), jnp.concatenate(qk_other, 1)
    qkv_block = merge_core(qkv_keep, across(qkv_other, 1), core, 0)
    qkv_cut = qkv_block.shape[1] // 2
    qkv_a = gather_quads({0: qkv_block[:, :qkv_cut]}, up_order)
    qkv_b = gather_quads({0: qkv_block[:, qkv_cut:]}, down_order)
    qkv_full = jnp.concatenate([in_order(qkv_a, 0), in_order(qkv_b, 0)], axis=1)

    o_keep, o_other = split_core(output_weight, core, 0)
    o_block = merge_core(o_keep, across(o_other, 1), core, 1)
    sg_keep, sg_other = split_core(shared_gate_weight, core, 1)
    su_keep, su_other = split_core(shared_up_weight, core, 1)
    gu_keep = jnp.concatenate([sg_keep, su_keep], axis=1)
    gu_other = jnp.concatenate([sg_other, su_other], axis=1)
    gu_block = merge_core(gu_keep, across(gu_other, 1), core, 0)
    sd_keep, sd_other = split_core(shared_down_weight, core, 0)
    sd_block = merge_core(sd_keep, across(sd_other, 1), core, 1)

    def expert_block(weight):
        keep, other = split_core(weight, core, 0)
        return merge_core(keep[0], across(other[0], 1), core, 0)

    eg_block, eu_block, ed_block = [
        expert_block(weight) for weight in (expert_gate, expert_up, expert_down)
    ]
    ed_cut = width // 2
    eda_block, edb_block = ed_block[:, :ed_cut], ed_block[:, ed_cut:]

    o_some = gather_quads({0: o_block}, down_one)
    gu_some = gather_quads({0: gu_block}, up_one)
    sd_some = gather_quads({0: sd_block}, down_one)
    (
        rows_one, qkv_full, o_some, gu_some, sd_some, eg_block, eu_block, eda_block, edb_block,
        cot_low,
    ) = together(
        rows_one, qkv_full, o_some, gu_some, sd_some, eg_block, eu_block, eda_block, edb_block,
        cotangent,
    )

    experts = jnp.arange(expert_count, dtype=jnp.int32)
    chosen = (
        (expert_index[:, :, None] == experts[None, None, :]) & (token_live[:, None, None] > 0)
    ).any(axis=1)
    chosen = chosen.astype(BF16)
    cot_rows = gather_rows(
        jnp.concatenate([cot_low, jnp.pad(chosen, ((0, 0), (0, 128 - expert_count)))], axis=1)
    )
    chosen = chosen.astype(F32)

    o_pieces = gather_quads(o_some, down_two)
    gu_pieces = gather_quads(gu_some, up_two)
    sd_pieces = gather_quads(sd_some, down_two)
    bias = jnp.concatenate(
        [split_core(b, core, 0)[0] for b in (query_bias, key_bias, value_bias)]
    ).astype(F32)
    lin = dot(rows_one, qkv_full) + bias[None, :]

    def pair_places(steps):
        count = jnp.arange(group_rows, dtype=jnp.int32)
        first = (grp - 2 * steps) * group_rows
        other = ((grp ^ 1) - 2 * steps) * group_rows
        return jnp.concatenate([first + count, other + count])

    query_place = pair_places(0)
    key_place = jnp.concatenate([pair_places(step) for step in range(back, -1, -1)])
    query_doc, query_position = doc_layout(document_lengths, seq_len, query_place)
    key_doc, _ = doc_layout(document_lengths, seq_len, key_place)
    cosine, sine = rope_tables(query_position)
    query, key, value = [
        lin[:, part * head_width : (part + 1) * head_width].reshape(pair_rows, heads, HDIM)
        for part in range(3)
    ]
    query = rotate(query, cosine, sine).astype(BF16)
    key = rotate(key, cosine, sine).astype(BF16)
    value = value.astype(BF16)

    seq_groups = grp_count // SEQS

    def shifted(block, steps):
        route = [
            (i, i + 2 * steps)
            for i in range(grp_count)
            if 0 <= i + 2 * steps < grp_count and i // seq_groups == (i + 2 * steps) // seq_groups
        ]
        return lax.ppermute(block, "grp", route)

    key_value = jnp.concatenate([key, value], axis=1)
    key_value_all = jnp.concatenate(
        [shifted(key_value, step) for step in range(back, 0, -1)] + [key_value], axis=0
    )
    keys_all, values_all = key_value_all[:, :heads], key_value_all[:, heads:]
    distance = query_place[:, None] - key_place[None, :]
    allowed = (distance >= 0) & (distance < WINDOW) & (query_doc[:, None] == key_doc[None, :])
    scores = masked_scores(query, keys_all, allowed)
    top = jnp.max(scores, axis=-1, keepdims=True)
    weights = jnp.exp(scores - top)
    total = jnp.sum(weights, axis=-1, keepdims=True)
    log_total = top + jnp.log(total)
    probs = weights / total
    attended = jnp.einsum(
        "hqk,khd->qhd", probs.astype(BF16), values_all, preferred_element_type=F32
    )
    attended = attended.astype(BF16).reshape(pair_rows, head_width)
    (
        attended, o_pieces, gu_pieces, sd_pieces, eg_block, eu_block, eda_block, edb_block, cot_rows,
    ) = together(
        attended, o_pieces, gu_pieces, sd_pieces, eg_block, eu_block, eda_block, edb_block, cot_rows,
    )
    o_full = place_quads(o_pieces, quad, 1)
    gu_full = in_order(gu_pieces, 0)
    sd_full = place_quads(sd_pieces, quad, 1)
    cot_rows, chosen_rows = cot_rows[:, :width], cot_rows[:, width : width + expert_count]
    chosen_rows = chosen_rows.astype(F32)
    eg_some = gather_quads({0: eg_block}, up_one)
    eu_some = gather_quads({0: eu_block}, down_one)
    eda_some = gather_quads({0: eda_block}, up_one)
    edb_some = gather_quads({0: edb_block}, down_one)
    mixed = hidden_in + spread_rows(dot(attended, o_full).astype(BF16))
    mixed, eg_some, eu_some, eda_some, edb_some = together(
        mixed, eg_some, eu_some, eda_some, edb_some
    )
    eg_pieces = gather_quads(eg_some, up_two)
    eu_pieces = gather_quads(eu_some, down_two)

    scale_two = norm_scale(mixed)
    unit_two = mixed * scale_two
    normed_two = (unit_two * gain_two).astype(BF16)
    rows_two = gather_rows(flip_columns(normed_two, quad))
    rows_two, eg_pieces, eu_pieces, eda_some, edb_some = together(
        rows_two, eg_pieces, eu_pieces, eda_some, edb_some
    )
    eg_full = in_order(eg_pieces, 0)
    eu_full = in_order(eu_pieces, 0)
    ed_full = jnp.concatenate(
        [
            place_quads(gather_quads(eda_some, up_two), quad, 0),
            place_quads(gather_quads(edb_some, down_two), quad, 0),
        ],
        axis=1,
    )

    def router(rows, weight):
        logits = dot(rows, weight)
        return jax.nn.softmax(logits[:, :expert_count], axis=-1), jax.nn.sigmoid(
            logits[:, expert_count:]
        )

    probs_rows, shared_scale_rows = router(rows_two, router_flipped)
    router_probs, shared_scale = router(normed_two, router_all)
    mine = (experts == ep * 2 + core).astype(F32)[None, :]
    gate = jnp.sum(probs_rows * chosen_rows * mine, axis=1, keepdims=True)

    gu_pre = dot(rows_two, gu_full)
    sg_pre, su_pre = gu_pre[:, :ffs_half], gu_pre[:, ffs_half:]
    shared_active = (jax.nn.silu(sg_pre) * su_pre).astype(BF16)
    shared_part = dot(shared_active, sd_full)
    cot_float = cot_rows.astype(F32)
    grad_shared_out = (shared_scale_rows * cot_float).astype(BF16)
    shared_dot = jnp.sum(cot_float * shared_part, axis=1, keepdims=True)
    grad_shared_active = dot_last(grad_shared_out, sd_full)
    grad_gu = jnp.concatenate(
        [
            (grad_shared_active * su_pre * swish_slope(sg_pre)).astype(BF16),
            (grad_shared_active * jax.nn.silu(sg_pre)).astype(BF16),
        ],
        axis=1,
    )
    grad_rows_shared = dot_last(grad_gu, gu_full)

    gate_pre = dot(rows_two, eg_full)
    up_pre = dot(rows_two, eu_full)
    active = (jax.nn.silu(gate_pre) * up_pre).astype(BF16)
    result = dot(active, ed_full).astype(BF16).astype(F32)
    grad_gate = jnp.sum(cot_float * result, axis=1, keepdims=True)
    forward_part = gate * result + shared_scale_rows * shared_part
    grad_result = (gate * cot_float).astype(BF16)
    grad_active = dot_last(grad_result, ed_full)
    grad_gate_pre = (grad_active * up_pre * swish_slope(gate_pre)).astype(BF16)
    grad_up_pre = (grad_active * jax.nn.silu(gate_pre)).astype(BF16)
    grad_rows = (dot_last(grad_gate_pre, eg_full) + dot_last(grad_up_pre, eu_full)).astype(BF16)
    grad_part = (grad_rows.astype(F32) + grad_rows_shared).astype(BF16)
    extra = jnp.concatenate(
        [part * mine.astype(BF16) for value in (grad_gate, shared_dot) for part in two_parts(value)],
        axis=1,
    )
    extra = jnp.pad(extra, ((0, 0), (0, 128 - extra.shape[1])))
    block = width // quads

    def row_grads(rows, grads):
        return {k: dot_first(rows[:, k * block : (k + 1) * block], grads) for k in range(quads)}

    def column_grads(acts, grads):
        return {k: dot_first(acts, part) for k, part in take_quads(grads, quad, quads, 1).items()}

    sd_grad = reduce_quads(column_grads(shared_active, grad_shared_out), down_one)
    gu_grad = reduce_quads(row_grads(rows_two, grad_gu), up_one)
    ed_grad = take_quads(dot_first(active, grad_result).astype(BF16), quad, quads, 0)
    eda_grad = reduce_quads({k: v[:, :ed_cut] for k, v in ed_grad.items()}, up_one)
    edb_grad = reduce_quads({k: v[:, ed_cut:] for k, v in ed_grad.items()}, down_one)
    spread = spread_rows(jnp.concatenate([grad_part, extra], axis=1))
    eg_grad = row_grads(rows_two, grad_gate_pre)
    eu_grad = row_grads(rows_two, grad_up_pre)
    spread, sd_grad, gu_grad, eda_grad, edb_grad, eg_grad, eu_grad, forward_part = together(
        spread, sd_grad, gu_grad, eda_grad, edb_grad,
        {k: v.astype(BF16) for k, v in eg_grad.items()},
        {k: v.astype(BF16) for k, v in eu_grad.items()},
        forward_part.astype(BF16),
    )
    grad_normed_two = flip_columns(spread[:, :width], quad)
    side = spread[:, width : width + 4 * expert_count].reshape(rows_dev, 4, expert_count)
    grad_gate_own = side[:, 0] + side[:, 1]
    shared_dot_own = jnp.sum(side[:, 2] + side[:, 3], axis=1, keepdims=True)

    grad_logit = shared_dot_own * shared_scale * (1.0 - shared_scale)
    grad_probs = grad_gate_own * chosen
    grad_logits = router_probs * (
        grad_probs - jnp.sum(router_probs * grad_probs, axis=-1, keepdims=True)
    )
    grad_router = jnp.concatenate([grad_logits, grad_logit], axis=1)
    router_grad = dot_first(normed_two.astype(F32), grad_router)
    grad_normed_two = grad_normed_two + dot_last(grad_router, router_all.astype(F32))
    grad_norm_part, ff_gain_grad = norm_backward(grad_normed_two, unit_two, scale_two, gain_two)
    grad_mixed = grad_out + grad_norm_part
    grad_branch = gather_rows(grad_mixed.astype(BF16))
    eg_grad = reduce_quads(eg_grad, up_one)
    eu_grad = reduce_quads(eu_grad, down_one)
    ep_masks = [1 << b for b in range(ep_count.bit_length() - 1)]
    grp_masks = [1 << b for b in range(grp_count.bit_length() - 1)]
    grad_branch, eg_grad, eu_grad, sd_grad, gu_grad, eda_grad, edb_grad, forward_part = together(
        grad_branch, eg_grad, eu_grad, sd_grad, gu_grad, eda_grad, edb_grad, forward_part
    )
    layer_sum = spread_rows(forward_part)
    layer_out = (mixed + layer_sum).astype(BF16)
    sd_grad = reduce_quads(sd_grad, down_two)[0]
    gu_grad = reduce_quads(gu_grad, up_two)[0]
    ed_grad = jnp.concatenate(
        [reduce_quads(eda_grad, up_two)[0], reduce_quads(edb_grad, down_two)[0]], axis=1
    )
    early = sum_everywhere(
        jnp.concatenate([ff_gain_grad[None], router_grad.T], axis=0), grp_masks, ep_masks
    )
    ff_gain_grad, router_grad = early[0], early[1:]
    o_grad = {k: v.astype(BF16) for k, v in column_grads(attended, grad_branch).items()}

    grad_attended = dot_last(grad_branch, o_full).astype(BF16).reshape(pair_rows, heads, HDIM)
    scores_again = masked_scores(query, keys_all, allowed)
    probs_again = jnp.exp(scores_again - log_total)
    grad_probs_att = jnp.einsum(
        "qhd,khd->hqk", grad_attended, values_all, preferred_element_type=F32
    )
    inner = jnp.sum(probs_again * grad_probs_att, axis=-1, keepdims=True)
    grad_scores = (probs_again * (grad_probs_att - inner)).astype(BF16)
    grad_query = jnp.einsum(
        "hqk,khd->qhd", grad_scores, keys_all, preferred_element_type=F32
    ) * HDIM ** (-0.5)
    grad_keys_all = jnp.einsum(
        "hqk,qhd->khd", grad_scores, query, preferred_element_type=F32
    ) * HDIM ** (-0.5)
    grad_values_all = jnp.einsum(
        "hqk,qhd->khd", probs_again.astype(BF16), grad_attended, preferred_element_type=F32
    )
    grad_kv_all = jnp.concatenate([grad_keys_all, grad_values_all], axis=1)
    (
        grad_kv_all, layer_out, sd_grad, gu_grad, ed_grad, ff_gain_grad, router_grad, eg_grad,
        eu_grad, o_grad,
    ) = together(
        grad_kv_all, layer_out, sd_grad, gu_grad, ed_grad, ff_gain_grad, router_grad, eg_grad,
        eu_grad, o_grad,
    )
    grad_kv = grad_kv_all[back * pair_rows :]
    for step in range(1, back + 1):
        first = (back - step) * pair_rows
        sent = grad_kv_all[first : first + pair_rows].astype(BF16)
        grad_kv = grad_kv + shifted(sent, -step).astype(F32)
    grad_lin = jnp.concatenate(
        [
            unrotate(grad_query, cosine, sine),
            unrotate(grad_kv[:, :heads], cosine, sine),
            grad_kv[:, heads:],
        ],
        axis=1,
    )
    grad_lin = grad_lin.astype(BF16).reshape(pair_rows, 3 * head_width)
    partial = dot_last(grad_lin, qkv_full)
    gain_rows = flip_columns(gain_one, quad)
    att_gain_part = jnp.sum(partial * rows_one.astype(F32), axis=0) / gain_rows
    bias_part = jnp.sum(grad_lin.astype(F32), axis=0)
    late = jnp.concatenate([flip_columns(att_gain_part, quad), bias_part])
    late = sum_everywhere(late, grp_masks[1:], [])
    att_gain_grad = sum_everywhere(late[:width], grp_masks[:1], ep_masks)
    bias_mine = merge_core(
        late[width:].reshape(3, head_width),
        across(late[width:], 1).reshape(3, head_width),
        core,
        1,
    )
    grad_normed_one = flip_columns(spread_rows(partial.astype(BF16)), quad)
    grad_norm_one, _ = norm_backward(grad_normed_one, unit_one, scale_one, gain_one)
    input_grad = grad_mixed + grad_norm_one

    def back_to_cores(summed, cut_axis, join_axis):
        keep, other = split_core(summed, core, cut_axis)
        return merge_core(keep, across(other, 1), core, join_axis).astype(F32)

    def back_to_experts(summed):
        keep, other = split_core(summed, core, 0)
        arrived = across(other, 1)
        return jnp.stack(
            [jnp.where(core == 0, keep, arrived), jnp.where(core == 0, arrived, keep)]
        ).astype(F32)

    eg_grad = reduce_quads(eg_grad, up_two)[0]
    eu_grad = reduce_quads(eu_grad, down_two)[0]
    o_grad = reduce_quads(o_grad, down_order)[0]
    qkv_a_grad = reduce_quads(row_grads(rows_one, grad_lin[:, :qkv_cut]), up_order)[0]
    qkv_b_grad = reduce_quads(row_grads(rows_one, grad_lin[:, qkv_cut:]), down_order)[0]
    qkv_grad = jnp.concatenate([qkv_a_grad, qkv_b_grad], axis=1)
    q_grad, k_grad, v_grad = [
        back_to_cores(qkv_grad[:, part * head_width : (part + 1) * head_width], 0, 1)
        for part in range(3)
    ]
    return (
        layer_out,
        input_grad,
        att_gain_grad,
        q_grad,
        bias_mine[0],
        k_grad,
        bias_mine[1],
        v_grad,
        bias_mine[2],
        back_to_cores(o_grad, 1, 0),
        ff_gain_grad,
        router_grad[:expert_count].T,
        router_grad[expert_count],
        back_to_cores(gu_grad[:, :ffs_half], 0, 1),
        back_to_cores(gu_grad[:, ffs_half:], 0, 1),
        back_to_cores(sd_grad, 1, 0),
        back_to_experts(eg_grad),
        back_to_experts(eu_grad),
        back_to_experts(ed_grad),
    )


def solution(mesh):
    tokens = P(("grp", "ep"), None)
    rows, columns, experts = P("grp", "ep"), P("ep", "grp"), P("ep", "grp", None)
    in_specs = (
        tokens, P(), rows, P("ep"), rows, P("ep"), rows, P("ep"), columns, P(), P(), P(),
        rows, rows, columns, experts, experts, experts, tokens, tokens, P(("grp", "ep")), P(),
    )
    out_specs = (
        tokens, tokens, P(), rows, P("ep"), rows, P("ep"), rows, P("ep"), columns, P(), P(), P(),
        rows, rows, columns, experts, experts, experts,
    )
    return jax.shard_map(local, mesh=mesh, in_specs=in_specs, out_specs=out_specs, check_vma=False)
```

time: 2350 us -> 1060 us (0.45)
  waiting for transfers between devices: 1860 us -> 455 us
  other arithmetic: 43.7 us -> 158 us
  blocking collectives: 56.5 us -> 0 us
  starting transfers between devices: 42 us -> 84.8 us
  local copies, waits for them, and re-layouts: 51.7 us -> 75.3 us
    reduce_scatter x14 -> x4, waiting for transfers between devices: 1030 us -> 53.2 us  [spread_rows(): lax.psum_scatter(mine, 'ep', scatter_dimension=0, tiled=True).astype(F32)]
    all_gather x14 -> x4, waiting for transfers between devices: 558 us -> 50.1 us  [gather_rows(): own = lax.all_gather(values, 'ep', axis=0, tiled=True)]
    ppermute x8 -> x92, waiting for transfers between devices: 11 us -> 351 us  [the longest x86 318 us: across(): return lax.ppermute(block, 'grp', [(i, i ^ mask) for i in range(count)])]
    all_to_all x4 -> x0, waiting for transfers between devices: 199 us -> none  [swap_experts(): return lax.all_to_all(values, 'ep', split_axis=0, concat_axis=0, tiled=True)]
    psum x1 -> x0, waiting for transfers between devices: 60.6 us -> none  [local(): lax.psum((attention_gain_grad, feedforward_gain_grad, router_weight_grad,...]
    psum x1 -> x0, blocking collectives: 56.5 us -> none  [local(): lax.psum((attention_gain_grad, feedforward_gain_grad, router_weight_grad,...]
    ppermute x8 -> x92, starting transfers between devices: 20.9 us -> 75.4 us  [the longest x86 67.9 us: across(): return lax.ppermute(block, 'grp', [(i, i ^ mask) for i in range(count)])]
    convert_element_type x18 -> x43, other arithmetic: 13.8 us -> 64.1 us  [the longest x13 20.4 us: reduce_quads(): pieces[key ^ bit] = (kept.astype(F32) + arrived.astype(F32)).astype(BF16)]
  transfers between devices with their start and end apart: 41 -> 100, of which waited for: 30 -> 41; matrix products, arithmetic and copies ran while one was open for 13% -> 35% of each run, Pallas kernels for 0% -> 0%
where the time goes in v1:
time: 1060 us; the launch traced here: 1040 us
  waiting for transfers between devices  455 us (43%)
  matrix products  254 us (24%)
  other arithmetic  158 us (15%)
  starting transfers between devices  84.8 us (8%)
  local copies, waits for them, and re-layouts  75.3 us (7%)
  between operations  17.3 us (2%)
    ppermute x86, waiting for transfers between devices, across(): return lax.ppermute(block, 'grp', [(i, i ^ mask) for i in range(count)])  318 us
    dot_general x30, matrix products, dot_first(): lax.dot_general(left, right, (((0,), (0,)), ((), ())), preferred_element_...  81.8 us
    dot_general x8, matrix products, dot_last(): lax.dot_general(left, right, (((1,), (1,)), ((), ())), preferred_element_...  69.2 us
    ppermute x86, starting transfers between devices, across(): return lax.ppermute(block, 'grp', [(i, i ^ mask) for i in range(count)])  67.9 us
    dot_general x9, matrix products, dot(): return jnp.dot(left, right, preferred_element_type=F32)  54.3 us
    reduce_scatter x4, waiting for transfers between devices, spread_rows(): lax.psum_scatter(mine, 'ep', scatter_dimension=0, tiled=True).astype(F32)  53.2 us
    all_gather x4, waiting for transfers between devices, gather_rows(): own = lax.all_gather(values, 'ep', axis=0, tiled=True)  50.1 us
    unnamed x330, local copies, waits for them, and re-layouts  32.9 us
  transfers between devices with their start and end apart: 100, of which 41 were waited for; matrix products, arithmetic and copies ran while one was open for 35% of the time, Pallas kernels for 0%

profile of v1, /device:TPU:0, one launch (start us, length us, event | category | flops | bytes accessed | tf_op | source)
XLA Modules:
  0.0 1044.7 jit_solution(438405106490018085)
XLA Ops:
  55.4 4.9 all-gather.5.cloned.1.call-done
  71.4 5.5 collective-permute-done.3
  78.3 29.0 %collective-permute-done.7 = bf16[512,384]{1,0:T(8,128)(2,1)S(1)} collective-permute-done((bf16[512,384]{1,0:T(8,128)(2,1)}, bf16[512,384]{1,0:T(8,128)(2,1)S(1)}, u32[]{:S(2)}, u32[]{:S(2)}) %collective-permute-start.7) | collective-permute-done | bytes 393248 | tf_op jit(solution)/shard_map/ppermute | solution.py:31
  107.7 11.7 %maximum_maximum_fusion = bf16[2048,768]{1,0:T(8,128)(2,1)S(1)} fusion(bf16[512,384]{1,0:T(8,128)(2,1)S(1)} %collective-permute-done.7, bf16[512,384]{1,0:T(8,128)(2,1)} %collective-permute-done.6, bf16[512,384]{1,0:T(8,128)(2,1)} %collective-permute-done.5, bf16[512,384]{1,0:T(8,128)(2,1)S(1)} %copy-done.68, ...), kind=kLoop, calls=%fused_computation.51 | loop fusion | flops 25165824 | bytes 6291456 | tf_op jit(solution)/shard_map/concatenate | solution.py:255
  120.0 5.1 collective-permute-done.13
  159.7 16.2 %collective-permute-done.17 = bf16[1024,4,128]{2,0,1:T(8,128)(2,1)S(1)} collective-permute-done((bf16[1024,4,128]{2,0,1:T(8,128)(2,1)S(1)}, bf16[1024,4,128]{2,0,1:T(8,128)(2,1)S(1)}, u32[]{:S(2)}, u32[]{:S(2)}) %collective-permute-start.17) | collective-permute-done | bytes 1048608 | tf_op jit(solution)/shard_map/ppermute | solution.py:333
  178.9 7.9 fusion.156
  186.8 8.2 fusion
  195.1 8.2 fusion.37
  207.0 8.5 collective-permute-done.19
  227.6 8.9 all-gather.9.cloned.1.call-start
  240.6 31.3 %reduce-scatter.13.cloned.1.call-done = bf16[128,2048]{1,0:T(8,128)(2,1)} async-done(((bf16[512,2048]{1,0:T(8,128)(2,1)}), bf16[128,2048]{1,0:T(8,128)(2,1)}) %reduce-scatter.13.cloned.1.call-update) | async-done | bytes 524304 | tf_op jit(solution)/shard_map/reduce_scatter | solution.py:126
  273.2 12.8 %collective-permute-done.28 = bf16[352,1024]{1,0:T(8,128)(2,1)} collective-permute-done((bf16[352,1024]{1,0:T(8,128)(2,1)}, bf16[352,1024]{1,0:T(8,128)(2,1)}, u32[]{:S(2)}, u32[]{:S(2)}) %collective-permute-start.28) | collective-permute-done | bytes 720928 | tf_op jit(solution)/shard_map/ppermute | solution.py:31
  288.6 45.2 %all-gather.9.cloned.1.call-done = bf16[512,2048]{1,0:T(8,128)(2,1)} async-done(((bf16[128,2048]{1,0:T(8,128)(2,1)}), bf16[512,2048]{1,0:T(8,128)(2,1)}) %all-gather.9.cloned.1.call-update) | async-done | bytes 2097168 | tf_op jit(solution)/shard_map/all_gather | solution.py:118
  353.1 21.0 %collective-permute-done.31 = bf16[512,1408]{1,0:T(8,128)(2,1)S(1)} collective-permute-done((bf16[512,1408]{1,0:T(8,128)(2,1)S(1)}, bf16[512,1408]{1,0:T(8,128)(2,1)S(1)}, u32[]{:S(2)}, u32[]{:S(2)}) %collective-permute-start.31) | collective-permute-done | bytes 1441824 | tf_op jit(solution)/shard_map/ppermute | solution.py:31
  374.1 30.5 %collective-permute-done.32 = bf16[512,1408]{1,0:T(8,128)(2,1)S(1)} collective-permute-done((bf16[512,1408]{1,0:T(8,128)(2,1)}, bf16[512,1408]{1,0:T(8,128)(2,1)S(1)}, u32[]{:S(2)}, u32[]{:S(2)}) %collective-permute-start.32) | collective-permute-done | bytes 1441824 | tf_op jit(solution)/shard_map/ppermute | solution.py:31
  406.1 10.7 %fusion.161 = f32[1024,1408]{0,1:T(8,128)} fusion(bf16[1024,2048]{1,0:T(8,128)(2,1)S(1)} %pad_maximum_fusion.3, bf16[2048,1408]{1,0:T(8,128)(2,1)} %copy-done.83), kind=kOutput, calls=%fused_computation.504 | convolution fusion | flops 5905580032 | bytes 15728640 | tf_op jit(solution)/shard_map/dot_general | solution.py:18
  419.3 7.7 multiply_convert_fusion.6
  427.0 5.9 fusion.162
  442.8 8.5 fusion.158
  453.4 8.8 fusion.157
  488.2 8.7 collective-permute-done.38
  500.2 15.2 %multiply_convert_fusion.2 = (bf16[1024,1408]{1,0:T(8,128)(2,1)}, bf16[1024,1408]{1,0:T(8,128)(2,1)}, bf16[1024,1408]{1,0:T(8,128)(2,1)}) fusion(f32[1024,1408]{1,0:T(8,128)} %fusion.158, f32[1024,1408]{1,0:T(8,128)} %fusion.157, bf16[1408,1024]{1,0:T(8,128)(2,1)} %constant_dynamic-update-slice_fusion.21, ...), kind=kOutput, calls=%fused_computation.34 | convolution fusion | flops 5945032704 | bytes 30150656 | tf_op jit(solution)/shard_map/dot_general | solution.py:22
  515.4 14.2 %fusion.9 = (f32[1024]{0:T(1024)S(1)}, f32[1024]{0:T(1024)S(1)}, bf16[1024,2048]{0,1:T(8,128)(2,1)}) fusion(bf16[1024,2176]{0,1:T(8,128)(2,1)S(1)} %bitcast.131, f32[1024,2048]{0,1:T(8,128)} %fusion.162, f32[1024]{0:T(1024)S(1)} %bitcast.161, f32[1024]{0:T(1024)S(1)} %multiply_reduce_fusion.6, bf16[1024,1408]{1,0:T(8,128)(2,1)} %get-tuple-element.254, ...), kind=kOutput, calls=%fused_computation.22 | convolution fusion | flops 5940180992 | bytes 25444352 | tf_op jit(solution)/shard_map/dot_general | solution.py:18
  529.8 11.9 %fusion.159 = f32[1024,2048]{1,0:T(8,128)} fusion(bf16[1024,1408]{1,0:T(8,128)(2,1)} %get-tuple-element.253, bf16[2048,1408]{1,0:T(8,128)(2,1)} %copy-done.84), kind=kOutput, calls=%fused_computation.502 | convolution fusion | flops 5905580032 | bytes 17039360 | tf_op jit(solution)/shard_map/dot_general | solution.py:22
  541.7 10.8 %fusion.160 = f32[1024,2048]{1,0:T(8,128)} fusion(bf16[1024,1408]{1,0:T(8,128)(2,1)S(1)} %copy-done.134, bf16[2048,1408]{1,0:T(8,128)(2,1)} %copy-done.85), kind=kOutput, calls=%fused_computation.503 | convolution fusion | flops 5905580032 | bytes 17039360 | tf_op jit(solution)/shard_map/dot_general | solution.py:22
  552.5 13.8 %add_convert_fusion = bf16[1024,2048]{1,0:T(8,128)(2,1)} fusion(f32[1024,2048]{1,0:T(8,128)} %fusion.159, f32[1024,2048]{1,0:T(8,128)} %fusion.160, bf16[2048,1408]{1,0:T(8,128)(2,1)} %copy-done.83, bf16[1024,704]{0,1:T(8,128)(2,1)} %copy-done.142, bf16[1024,704]{0,1:T(8,128)(2,1)S(1)} %copy-done.140), kind=kOutput, calls=%fused_computation.25 | convolution fusion | flops 5921832960 | bytes 29622272 | tf_op jit(solution)/shard_map/dot_general | solution.py:22
  570.5 6.6 convolution_convert_fusion
  591.3 5.3 convolution_convert_fusion.8
  596.6 4.9 convolution_convert_fusion.7
  622.2 7.4 collective-permute-done.45
  629.6 13.1 %collective-permute-done.44 = bf16[352,1024]{1,0:T(8,128)(2,1)S(1)} collective-permute-done((bf16[352,1024]{1,0:T(8,128)(2,1)S(1)}, bf16[352,1024]{1,0:T(8,128)(2,1)S(1)}, u32[]{:S(2)}, u32[]{:S(2)}) %collective-permute-start.44) | collective-permute-done | bytes 720928 | tf_op jit(solution)/shard_map/ppermute | solution.py:31
  661.9 61.4 %collective-permute-done.59 = f32[10,2048]{1,0:T(8,128)S(1)} collective-permute-done((f32[10,2048]{1,0:T(8,128)S(1)}, f32[10,2048]{1,0:T(8,128)S(1)}, u32[]{:S(2)}, u32[]{:S(2)}) %collective-permute-start.59) | collective-permute-done | bytes 81952 | tf_op jit(solution)/shard_map/ppermute | solution.py:31
  731.1 5.0 collective-permute-done.61
  737.6 5.3 collective-permute-done.62
  750.9 9.9 collective-permute-done.51
  763.8 23.9 %collective-permute-done.52 = bf16[512,1408]{1,0:T(8,128)(2,1)} collective-permute-done((bf16[512,1408]{1,0:T(8,128)(2,1)}, bf16[512,1408]{1,0:T(8,128)(2,1)}, u32[]{:S(2)}, u32[]{:S(2)}) %collective-permute-start.52) | collective-permute-done | bytes 1441824 | tf_op jit(solution)/shard_map/ppermute | solution.py:31
  798.1 10.4 multiply_reduce_fusion
  811.0 10.4 multiply_convert_fusion
  821.4 7.1 fusion.27
  841.6 6.9 fusion.36
  848.5 8.4 fusion.28
  862.6 23.0 %collective-permute-done.56 = bf16[352,1024]{1,0:T(8,128)(2,1)S(1)} collective-permute-done((bf16[352,1024]{1,0:T(8,128)(2,1)}, bf16[352,1024]{1,0:T(8,128)(2,1)S(1)}, u32[]{:S(2)}, u32[]{:S(2)}) %collective-permute-start.56) | collective-permute-done | bytes 720928 | tf_op jit(solution)/shard_map/ppermute | solution.py:31
  899.4 6.2 collective-permute-done.81
  911.6 16.9 %collective-permute-done.82 = bf16[256,512]{1,0:T(8,128)(2,1)S(1)} collective-permute-done((bf16[256,512]{1,0:T(8,128)(2,1)S(1)}, bf16[256,512]{1,0:T(8,128)(2,1)S(1)}, u32[]{:S(2)}, u32[]{:S(2)}) %collective-permute-start.82) | collective-permute-done | bytes 262176 | tf_op jit(solution)/shard_map/ppermute | solution.py:31
  940.7 7.2 multiply_reduce_fusion.1
  991.4 6.6 collective-permute-done.77
  1012.3 21.8 %reduce-scatter.19.cloned.1.call-done = bf16[128,2048]{1,0:T(8,128)(2,1)} async-done(((bf16[512,2048]{1,0:T(8,128)(2,1)}), bf16[128,2048]{1,0:T(8,128)(2,1)}) %reduce-scatter.19.cloned.1.call-update) | async-done | bytes 524304 | tf_op jit(solution)/shard_map/reduce_scatter | solution.py:126
  (765 shorter events, 388.8 us)
Async XLA Ops:
  7.2 53.1 %all-gather.5.cloned.1.call-start = ((), (), s32[]{:S(2)}) async-start(), calls=%async_computation.4 | async-start | bytes 2621440 | tf_op jit(solution)/shard_map/all_gather | solution.py:118
  11.5 183.5 %all-gather.7.cloned.1.call-start = ((), (), s32[]{:S(2)}) async-start(), calls=%async_computation.5 | async-start | bytes 2785280 | tf_op jit(solution)/shard_map/all_gather | solution.py:118
  13.5 30.2 %collective-permute-start.1 = (bf16[256,768]{1,0:T(8,128)(2,1)}, bf16[256,768]{1,0:T(8,128)(2,1)}, u32[]{:S(2)}, u32[]{:S(2)}) collective-permute-start(bf16[256,768]{1,0:T(8,128)(2,1)} %pad_maximum_fusion.23), channel_id=1, source_target_pairs={{0,4},{4,0},{8,12},{12,8},{16,20},{20,16},{24,28},{28,24},{1,5},{5... | collective-permute-start | bytes 1179656 | tf_op jit(solution)/shard_map/ppermute | solution.py:31
  17.0 35.1 %collective-permute-start.10 = (bf16[256,1408]{1,0:T(8,128)(2,1)}, bf16[256,1408]{1,0:T(8,128)(2,1)}, u32[]{:S(2)}, u32[]{:S(2)}) collective-permute-start(bf16[256,1408]{1,0:T(8,128)(2,1)} %pad_maximum_fusion.16), channel_id=1, source_target_pairs={{0,4},{4,0},{8,12},{12,8},{16,20},{20,16},{24,28},{28,24},{1,5},{5... | collective-permute-start | bytes 2162696 | tf_op jit(solution)/shard_map/ppermute | solution.py:31
  19.3 29.0 %collective-permute-start.14 = (bf16[256,1408]{1,0:T(8,128)(2,1)}, bf16[256,1408]{1,0:T(8,128)(2,1)}, u32[]{:S(2)}, u32[]{:S(2)}) collective-permute-start(bf16[256,1408]{1,0:T(8,128)(2,1)} %select_bitcast_fusion.8), channel_id=1, source_target_pairs={{0,4},{4,0},{8,12},{12,8},{16,20},{20,16},{24,28},{28,24},{1,5},{5... | collective-permute-start | bytes 2162696 | tf_op jit(solution)/shard_map/ppermute | solution.py:31
  60.3 59.1 %collective-permute-start = (bf16[512,2048]{1,0:T(8,128)(2,1)}, bf16[512,2048]{1,0:T(8,128)(2,1)S(1)}, u32[]{:S(2)}, u32[]{:S(2)}) collective-permute-start(bf16[512,2048]{1,0:T(8,128)(2,1)} %all-gather.5.cloned.1.call-done), channel_id=1, source_target_pairs={{0,4},{4,0},{8,12},{12,8},{16,20},{20,16},{24,28},{28,24},{1,5},{5... | collective-permute-start | bytes 6291464 | tf_op jit(solution)/shard_map/ppermute | solution.py:31
  61.9 63.2 %collective-permute-start.11 = (bf16[512,1408]{1,0:T(8,128)(2,1)S(1)}, bf16[512,1408]{1,0:T(8,128)(2,1)}, u32[]{:S(2)}, u32[]{:S(2)}) collective-permute-start(bf16[512,1408]{1,0:T(8,128)(2,1)S(1)} %copy-done.23), channel_id=1, source_target_pairs={{0,8},{4,12},{8,0},{12,4},{16,24},{20,28},{24,16},{28,20},{1,9},{5... | collective-permute-start | bytes 4325384 | tf_op jit(solution)/shard_map/ppermute | solution.py:31
  66.1 41.2 %collective-permute-start.7 = (bf16[512,384]{1,0:T(8,128)(2,1)}, bf16[512,384]{1,0:T(8,128)(2,1)S(1)}, u32[]{:S(2)}, u32[]{:S(2)}) collective-permute-start(bf16[512,384]{1,0:T(8,128)(2,1)} %collective-permute-done.6), channel_id=1, source_target_pairs={{0,8},{4,12},{8,0},{12,4},{16,24},{20,28},{24,16},{28,20},{1,9},{5... | collective-permute-start | bytes 1179656 | tf_op jit(solution)/shard_map/ppermute | solution.py:31
  68.8 38.9 %collective-permute-start.4 = (bf16[512,384]{1,0:T(8,128)(2,1)}, bf16[512,384]{1,0:T(8,128)(2,1)S(1)}, u32[]{:S(2)}, u32[]{:S(2)}) collective-permute-start(bf16[512,384]{1,0:T(8,128)(2,1)} %collective-permute-done.2), channel_id=1, source_target_pairs={{0,16},{4,20},{8,24},{12,28},{16,0},{20,4},{24,8},{28,12},{1,17},{... | collective-permute-start | bytes 1179656 | tf_op jit(solution)/shard_map/ppermute | solution.py:31
  76.9 43.1 %collective-permute-start.9 = (bf16[256,512]{1,0:T(8,128)(2,1)S(1)}, bf16[256,512]{1,0:T(8,128)(2,1)S(1)}, u32[]{:S(2)}, u32[]{:S(2)}) collective-permute-start(bf16[256,512]{1,0:T(8,128)(2,1)S(1)} %copy-done.74), channel_id=1, source_target_pairs={{0,16},{4,20},{8,24},{12,28},{16,0},{20,4},{24,8},{28,12},{1,17},{... | collective-permute-start | bytes 786440 | tf_op jit(solution)/shard_map/ppermute | solution.py:31
  145.6 126.4 %reduce-scatter.13.cloned.1.call-start = ((), (), s32[]{:S(2)}) async-start(), calls=%async_computation.8 | async-start | bytes 2621440 | tf_op jit(solution)/shard_map/reduce_scatter | solution.py:126
  155.6 39.4 %collective-permute-start.18 = (bf16[256,512]{1,0:T(8,128)(2,1)S(1)}, bf16[256,512]{1,0:T(8,128)(2,1)}, u32[]{:S(2)}, u32[]{:S(2)}) collective-permute-start(bf16[256,512]{1,0:T(8,128)(2,1)S(1)} %copy-done.75), channel_id=1, source_target_pairs={{0,8},{4,12},{8,0},{12,4},{16,24},{20,28},{24,16},{28,20},{1,9},{5... | collective-permute-start | bytes 786440 | tf_op jit(solution)/shard_map/ppermute | solution.py:31
  155.7 59.9 %collective-permute-start.20 = (bf16[512,1408]{1,0:T(8,128)(2,1)S(1)}, bf16[512,1408]{1,0:T(8,128)(2,1)}, u32[]{:S(2)}, u32[]{:S(2)}) collective-permute-start(bf16[512,1408]{1,0:T(8,128)(2,1)S(1)} %copy-done.24), channel_id=1, source_target_pairs={{0,16},{4,20},{8,24},{12,28},{16,0},{20,4},{24,8},{28,12},{1,17},{... | collective-permute-start | bytes 4325384 | tf_op jit(solution)/shard_map/ppermute | solution.py:31
  156.3 62.2 %collective-permute-start.21 = (bf16[512,1408]{1,0:T(8,128)(2,1)}, bf16[512,1408]{1,0:T(8,128)(2,1)}, u32[]{:S(2)}, u32[]{:S(2)}) collective-permute-start(bf16[512,1408]{1,0:T(8,128)(2,1)} %collective-permute-done.11), channel_id=1, source_target_pairs={{0,16},{4,20},{8,24},{12,28},{16,0},{20,4},{24,8},{28,12},{1,17},{... | collective-permute-start | bytes 4325384 | tf_op jit(solution)/shard_map/ppermute | solution.py:31
  157.8 57.8 %collective-permute-start.22 = (bf16[704,512]{1,0:T(8,128)(2,1)}, bf16[704,512]{1,0:T(8,128)(2,1)}, u32[]{:S(2)}, u32[]{:S(2)}) collective-permute-start(bf16[704,512]{1,0:T(8,128)(2,1)} %pad_maximum_fusion.17), channel_id=1, source_target_pairs={{0,8},{4,12},{8,0},{12,4},{16,24},{20,28},{24,16},{28,20},{1,9},{5... | collective-permute-start | bytes 2162696 | tf_op jit(solution)/shard_map/ppermute | solution.py:31
  176.0 39.6 %collective-permute-start.23 = (bf16[704,512]{1,0:T(8,128)(2,1)}, bf16[704,512]{1,0:T(8,128)(2,1)}, u32[]{:S(2)}, u32[]{:S(2)}) collective-permute-start(bf16[704,512]{1,0:T(8,128)(2,1)} %collective-permute-done.13), channel_id=1, source_target_pairs={{0,8},{4,12},{8,0},{12,4},{16,24},{20,28},{24,16},{28,20},{1,9},{5... | collective-permute-start | bytes 2162696 | tf_op jit(solution)/shard_map/ppermute | solution.py:31
  227.6 106.3 %all-gather.9.cloned.1.call-start = ((), (), s32[]{:S(2)}) async-start(), calls=%async_computation.6 | async-start | bytes 2621440 | tf_op jit(solution)/shard_map/all_gather | solution.py:118
  236.5 50.6 %collective-permute-start.26 = (bf16[512,1408]{1,0:T(8,128)(2,1)}, bf16[512,1408]{1,0:T(8,128)(2,1)}, u32[]{:S(2)}, u32[]{:S(2)}) collective-permute-start(bf16[512,1408]{1,0:T(8,128)(2,1)} %get-tuple-element.160), channel_id=1, source_target_pairs={{0,8},{4,12},{8,0},{12,4},{16,24},{20,28},{24,16},{28,20},{1,9},{5... | collective-permute-start | bytes 4325384 | tf_op jit(solution)/shard_map/ppermute | solution.py:31
  238.2 48.9 %collective-permute-start.27 = (bf16[512,1408]{1,0:T(8,128)(2,1)S(1)}, bf16[512,1408]{1,0:T(8,128)(2,1)}, u32[]{:S(2)}, u32[]{:S(2)}) collective-permute-start(bf16[512,1408]{1,0:T(8,128)(2,1)S(1)} %get-tuple-element.156), channel_id=1, source_target_pairs={{0,16},{4,20},{8,24},{12,28},{16,0},{20,4},{24,8},{28,12},{1,17},{... | collective-permute-start | bytes 4325384 | tf_op jit(solution)/shard_map/ppermute | solution.py:31
  238.7 47.2 %collective-permute-start.28 = (bf16[352,1024]{1,0:T(8,128)(2,1)}, bf16[352,1024]{1,0:T(8,128)(2,1)}, u32[]{:S(2)}, u32[]{:S(2)}) collective-permute-start(bf16[352,1024]{1,0:T(8,128)(2,1)} %get-tuple-element.152), channel_id=1, source_target_pairs={{0,8},{4,12},{8,0},{12,4},{16,24},{20,28},{24,16},{28,20},{1,9},{5... | collective-permute-start | bytes 2162696 | tf_op jit(solution)/shard_map/ppermute | solution.py:31
  239.1 48.0 %collective-permute-start.29 = (bf16[352,1024]{1,0:T(8,128)(2,1)}, bf16[352,1024]{1,0:T(8,128)(2,1)}, u32[]{:S(2)}, u32[]{:S(2)}) collective-permute-start(bf16[352,1024]{1,0:T(8,128)(2,1)} %get-tuple-element.154), channel_id=1, source_target_pairs={{0,16},{4,20},{8,24},{12,28},{16,0},{20,4},{24,8},{28,12},{1,17},{... | collective-permute-start | bytes 2162696 | tf_op jit(solution)/shard_map/ppermute | solution.py:31
  288.5 366.0 %reduce-scatter.15.cloned.1.call-start = ((), (), s32[]{:S(2)}) async-start(), calls=%async_computation.9 | async-start | bytes 2785280 | tf_op jit(solution)/shard_map/reduce_scatter | solution.py:126
  339.7 34.4 %collective-permute-start.31 = (bf16[512,1408]{1,0:T(8,128)(2,1)S(1)}, bf16[512,1408]{1,0:T(8,128)(2,1)S(1)}, u32[]{:S(2)}, u32[]{:S(2)}) collective-permute-start(bf16[512,1408]{1,0:T(8,128)(2,1)S(1)} %copy-done.25), channel_id=1, source_target_pairs={{0,16},{4,20},{8,24},{12,28},{16,0},{20,4},{24,8},{28,12},{1,17},{... | collective-permute-start | bytes 4325384 | tf_op jit(solution)/shard_map/ppermute | solution.py:31
  341.2 63.4 %collective-permute-start.32 = (bf16[512,1408]{1,0:T(8,128)(2,1)}, bf16[512,1408]{1,0:T(8,128)(2,1)S(1)}, u32[]{:S(2)}, u32[]{:S(2)}) collective-permute-start(bf16[512,1408]{1,0:T(8,128)(2,1)} %collective-permute-done.26), channel_id=1, source_target_pairs={{0,16},{4,20},{8,24},{12,28},{16,0},{20,4},{24,8},{28,12},{1,17},{... | collective-permute-start | bytes 4325384 | tf_op jit(solution)/shard_map/ppermute | solution.py:31
  341.7 62.9 %collective-permute-start.33 = (bf16[512,1408]{1,0:T(8,128)(2,1)S(1)}, bf16[512,1408]{1,0:T(8,128)(2,1)S(1)}, u32[]{:S(2)}, u32[]{:S(2)}) collective-permute-start(bf16[512,1408]{1,0:T(8,128)(2,1)S(1)} %get-tuple-element.156), channel_id=1, source_target_pairs={{0,8},{4,12},{8,0},{12,4},{16,24},{20,28},{24,16},{28,20},{1,9},{5... | collective-permute-start | bytes 4325384 | tf_op jit(solution)/shard_map/ppermute | solution.py:31
  343.2 62.9 %collective-permute-start.34 = (bf16[512,1408]{1,0:T(8,128)(2,1)}, bf16[512,1408]{1,0:T(8,128)(2,1)S(1)}, u32[]{:S(2)}, u32[]{:S(2)}) collective-permute-start(bf16[512,1408]{1,0:T(8,128)(2,1)} %collective-permute-done.27), channel_id=1, source_target_pairs={{0,8},{4,12},{8,0},{12,4},{16,24},{20,28},{24,16},{28,20},{1,9},{5... | collective-permute-start | bytes 4325384 | tf_op jit(solution)/shard_map/ppermute | solution.py:31
  463.8 33.0 %collective-permute-start.38 = (bf16[352,1024]{1,0:T(8,128)(2,1)}, bf16[352,1024]{1,0:T(8,128)(2,1)S(1)}, u32[]{:S(2)}, u32[]{:S(2)}) collective-permute-start(bf16[352,1024]{1,0:T(8,128)(2,1)} %collective-permute-done.29), channel_id=1, source_target_pairs={{0,8},{4,12},{8,0},{12,4},{16,24},{20,28},{24,16},{28,20},{1,9},{5... | collective-permute-start | bytes 2162696 | tf_op jit(solution)/shard_map/ppermute | solution.py:31
  472.1 138.4 %collective-permute-start.40 = (bf16[704,512]{1,0:T(8,128)(2,1)}, bf16[704,512]{1,0:T(8,128)(2,1)}, u32[]{:S(2)}, u32[]{:S(2)}) collective-permute-start(bf16[704,512]{1,0:T(8,128)(2,1)} %convolution_convert_fusion.17), channel_id=1, source_target_pairs={{0,16},{4,20},{8,24},{12,28},{16,0},{20,4},{24,8},{28,12},{1,17},{... | collective-permute-start | bytes 2162696 | tf_op jit(solution)/shard_map/ppermute | solution.py:31
  481.4 133.3 %collective-permute-start.41 = (bf16[704,512]{1,0:T(8,128)(2,1)}, bf16[704,512]{1,0:T(8,128)(2,1)}, u32[]{:S(2)}, u32[]{:S(2)}) collective-permute-start(bf16[704,512]{1,0:T(8,128)(2,1)} %convolution_convert_fusion.15), channel_id=1, source_target_pairs={{0,16},{4,20},{8,24},{12,28},{16,0},{20,4},{24,8},{28,12},{1,17},{... | collective-permute-start | bytes 2162696 | tf_op jit(solution)/shard_map/ppermute | solution.py:31
  485.8 159.5 %collective-permute-start.42 = (bf16[512,1408]{1,0:T(8,128)(2,1)}, bf16[512,1408]{1,0:T(8,128)(2,1)}, u32[]{:S(2)}, u32[]{:S(2)}) collective-permute-start(bf16[512,1408]{1,0:T(8,128)(2,1)} %convolution_convert_fusion.13), channel_id=1, source_target_pairs={{0,8},{4,12},{8,0},{12,4},{16,24},{20,28},{24,16},{28,20},{1,9},{5... | collective-permute-start | bytes 4325384 | tf_op jit(solution)/shard_map/ppermute | solution.py:31
  496.9 153.2 %collective-permute-start.43 = (bf16[512,1408]{1,0:T(8,128)(2,1)}, bf16[512,1408]{1,0:T(8,128)(2,1)}, u32[]{:S(2)}, u32[]{:S(2)}) collective-permute-start(bf16[512,1408]{1,0:T(8,128)(2,1)} %convolution_convert_fusion.11), channel_id=1, source_target_pairs={{0,8},{4,12},{8,0},{12,4},{16,24},{20,28},{24,16},{28,20},{1,9},{5... | collective-permute-start | bytes 4325384 | tf_op jit(solution)/shard_map/ppermute | solution.py:31
  587.6 28.0 %collective-permute-start.47 = (bf16[352,1024]{1,0:T(8,128)(2,1)}, bf16[352,1024]{1,0:T(8,128)(2,1)S(1)}, u32[]{:S(2)}, u32[]{:S(2)}) collective-permute-start(bf16[352,1024]{1,0:T(8,128)(2,1)} %get-tuple-element.263), channel_id=1, source_target_pairs={{0,16},{4,20},{8,24},{12,28},{16,0},{20,4},{24,8},{28,12},{1,17},{... | collective-permute-start | bytes 2162696 | tf_op jit(solution)/shard_map/ppermute | solution.py:31
  591.1 153.1 %all-gather.11.cloned.1.call-start = ((), (), s32[]{:S(2)}) async-start(), calls=%async_computation.7 | async-start | bytes 2621440 | tf_op jit(solution)/shard_map/all_gather | solution.py:118
  614.7 28.0 %collective-permute-start.44 = (bf16[352,1024]{1,0:T(8,128)(2,1)S(1)}, bf16[352,1024]{1,0:T(8,128)(2,1)S(1)}, u32[]{:S(2)}, u32[]{:S(2)}) collective-permute-start(bf16[352,1024]{1,0:T(8,128)(2,1)S(1)} %get-tuple-element.265), channel_id=1, source_target_pairs={{0,8},{4,12},{8,0},{12,4},{16,24},{20,28},{24,16},{28,20},{1,9},{5... | collective-permute-start | bytes 2162696 | tf_op jit(solution)/shard_map/ppermute | solution.py:31
  658.0 230.1 %reduce-scatter.17.cloned.1.call-start = ((), (), s32[]{:S(2)}) async-start(), calls=%async_computation.10 | async-start | bytes 2621440 | tf_op jit(solution)/shard_map/reduce_scatter | solution.py:126
  658.1 86.0 %collective-permute-start.49 = (bf16[512,1408]{1,0:T(8,128)(2,1)}, bf16[512,1408]{1,0:T(8,128)(2,1)}, u32[]{:S(2)}, u32[]{:S(2)}) collective-permute-start(bf16[512,1408]{1,0:T(8,128)(2,1)} %convolution_convert_fusion.9), channel_id=1, source_target_pairs={{0,8},{4,12},{8,0},{12,4},{16,24},{20,28},{24,16},{28,20},{1,9},{5... | collective-permute-start | bytes 4325384 | tf_op jit(solution)/shard_map/ppermute | solution.py:31
  659.6 87.9 %collective-permute-start.50 = (bf16[512,1408]{1,0:T(8,128)(2,1)}, bf16[512,1408]{1,0:T(8,128)(2,1)}, u32[]{:S(2)}, u32[]{:S(2)}) collective-permute-start(bf16[512,1408]{1,0:T(8,128)(2,1)} %convolution_convert_fusion.7), channel_id=1, source_target_pairs={{0,8},{4,12},{8,0},{12,4},{16,24},{20,28},{24,16},{28,20},{1,9},{5... | collective-permute-start | bytes 4325384 | tf_op jit(solution)/shard_map/ppermute | solution.py:31
  661.0 62.3 %collective-permute-start.59 = (f32[10,2048]{1,0:T(8,128)S(1)}, f32[10,2048]{1,0:T(8,128)S(1)}, u32[]{:S(2)}, u32[]{:S(2)}) collective-permute-start(f32[10,2048]{1,0:T(8,128)S(1)} %fusion.215), channel_id=1, source_target_pairs={{0,8},{4,12},{8,0},{12,4},{16,24},{20,28},{24,16},{28,20},{1,9},{5... | collective-permute-start | bytes 245768 | tf_op jit(solution)/shard_map/ppermute | solution.py:31
  724.6 36.3 %collective-permute-start.51 = (bf16[512,1408]{1,0:T(8,128)(2,1)}, bf16[512,1408]{1,0:T(8,128)(2,1)}, u32[]{:S(2)}, u32[]{:S(2)}) collective-permute-start(bf16[512,1408]{1,0:T(8,128)(2,1)} %convolution_convert_fusion.4), channel_id=1, source_target_pairs={{0,16},{4,20},{8,24},{12,28},{16,0},{20,4},{24,8},{28,12},{1,17},{... | collective-permute-start | bytes 4325384 | tf_op jit(solution)/shard_map/ppermute | solution.py:31
  736.8 50.9 %collective-permute-start.52 = (bf16[512,1408]{1,0:T(8,128)(2,1)}, bf16[512,1408]{1,0:T(8,128)(2,1)}, u32[]{:S(2)}, u32[]{:S(2)}) collective-permute-start(bf16[512,1408]{1,0:T(8,128)(2,1)} %convolution_convert_fusion.3), channel_id=1, source_target_pairs={{0,16},{4,20},{8,24},{12,28},{16,0},{20,4},{24,8},{28,12},{1,17},{... | collective-permute-start | bytes 4325384 | tf_op jit(solution)/shard_map/ppermute | solution.py:31
  744.1 46.5 %collective-permute-start.48 = (bf16[512,2048]{1,0:T(8,128)(2,1)}, bf16[512,2048]{1,0:T(8,128)(2,1)S(1)}, u32[]{:S(2)}, u32[]{:S(2)}) collective-permute-start(bf16[512,2048]{1,0:T(8,128)(2,1)} %all-gather.11.cloned.1.call-done), channel_id=1, source_target_pairs={{0,4},{4,0},{8,12},{12,8},{16,20},{20,16},{24,28},{28,24},{1,5},{5... | collective-permute-start | bytes 6291464 | tf_op jit(solution)/shard_map/ppermute | solution.py:31
  795.8 32.8 %collective-permute-start.53 = (bf16[512,2048]{0,1:T(8,128)(2,1)}, bf16[512,2048]{0,1:T(8,128)(2,1)}, u32[]{:S(2)}, u32[]{:S(2)}) collective-permute-start(bf16[512,2048]{0,1:T(8,128)(2,1)} %slice.456), channel_id=1, source_target_pairs={{0,4},{4,0},{8,12},{12,8},{16,20},{20,16},{24,28},{28,24},{1,5},{5... | collective-permute-start | bytes 6291464 | tf_op jit(solution)/shard_map/ppermute | solution.py:31
  836.2 197.8 %reduce-scatter.19.cloned.1.call-start = ((), (), s32[]{:S(2)}) async-start(), calls=%async_computation.11 | async-start | bytes 2621440 | tf_op jit(solution)/shard_map/reduce_scatter | solution.py:126
  838.1 49.2 %collective-permute-start.55 = (bf16[512,1408]{1,0:T(8,128)(2,1)}, bf16[512,1408]{1,0:T(8,128)(2,1)S(1)}, u32[]{:S(2)}, u32[]{:S(2)}) collective-permute-start(bf16[512,1408]{1,0:T(8,128)(2,1)} %fusion.25), channel_id=1, source_target_pairs={{0,16},{4,20},{8,24},{12,28},{16,0},{20,4},{24,8},{28,12},{1,17},{... | collective-permute-start | bytes 4325384 | tf_op jit(solution)/shard_map/ppermute | solution.py:31
  841.0 44.6 %collective-permute-start.56 = (bf16[352,1024]{1,0:T(8,128)(2,1)}, bf16[352,1024]{1,0:T(8,128)(2,1)S(1)}, u32[]{:S(2)}, u32[]{:S(2)}) collective-permute-start(bf16[352,1024]{1,0:T(8,128)(2,1)} %get-tuple-element.197), channel_id=1, source_target_pairs={{0,16},{4,20},{8,24},{12,28},{16,0},{20,4},{24,8},{28,12},{1,17},{... | collective-permute-start | bytes 2162696 | tf_op jit(solution)/shard_map/ppermute | solution.py:31
  894.9 40.2 %collective-permute-start.63 = (bf16[1024,4,128]{2,0,1:T(8,128)(2,1)S(1)}, bf16[1024,4,128]{2,0,1:T(8,128)(2,1)S(1)}, u32[]{:S(2)}, u32[]{:S(2)}) collective-permute-start(bf16[1024,4,128]{2,0,1:T(8,128)(2,1)S(1)} %slice.912), channel_id=1, source_target_pairs={{8,0},{12,4},{24,16},{28,20},{9,1},{13,5},{25,17},{29,21},{10,2},{... | collective-permute-start | bytes 3145736 | tf_op jit(solution)/shard_map/ppermute | solution.py:333
  905.6 76.9 %collective-permute-start.87 = (bf16[512,1408]{1,0:T(8,128)(2,1)}, bf16[512,1408]{1,0:T(8,128)(2,1)}, u32[]{:S(2)}, u32[]{:S(2)}) collective-permute-start(bf16[512,1408]{1,0:T(8,128)(2,1)} %add_convert_fusion.11), channel_id=1, source_target_pairs={{0,16},{4,20},{8,24},{12,28},{16,0},{20,4},{24,8},{28,12},{1,17},{... | collective-permute-start | bytes 4325384 | tf_op jit(solution)/shard_map/ppermute | solution.py:31
  911.5 74.9 %collective-permute-start.89 = (bf16[512,1408]{1,0:T(8,128)(2,1)}, bf16[512,1408]{1,0:T(8,128)(2,1)}, u32[]{:S(2)}, u32[]{:S(2)}) collective-permute-start(bf16[512,1408]{1,0:T(8,128)(2,1)} %add_convert_fusion.9), channel_id=1, source_target_pairs={{0,8},{4,12},{8,0},{12,4},{16,24},{20,28},{24,16},{28,20},{1,9},{5... | collective-permute-start | bytes 4325384 | tf_op jit(solution)/shard_map/ppermute | solution.py:31
  (207 other events, 2986.5 us)
Sparse Core Ops, SparseCore 0:
  11.6 48.6 all-gather.4
  145.7 48.6 all-gather.6
  227.7 44.2 reduce-scatter.12
  288.6 45.2 all-gather.8
  591.2 43.4 reduce-scatter.14
  658.2 43.5 all-gather.10
  836.4 41.8 reduce-scatter.16
  991.5 42.4 reduce-scatter.18

commit v2 on v1

v2 whole, which is shorter than its diff:
```python
import functools

import jax
import jax.numpy as jnp
from jax import lax
from jax.experimental import pallas as pl
from jax.experimental.pallas import tpu as pltpu
from jax.sharding import PartitionSpec as P

HDIM = 128
SEQS = 2
DOCS = 4
WINDOW = 1024
EPS = 1e-06
ROPE_BASE = 1000000.0
MASKED = -1e30
F32 = jnp.float32
BF16 = jnp.bfloat16
TILE = 256
LANES = 128
MIB = 1 << 20


def dot(left, right):
    return jnp.dot(left, right, preferred_element_type=F32)


def dot_last(left, right):
    return lax.dot_general(left, right, (((1,), (1,)), ((), ())), preferred_element_type=F32)


def dot_first(left, right):
    return lax.dot_general(left, right, (((0,), (0,)), ((), ())), preferred_element_type=F32)


def across(block, mask):
    count = lax.axis_size("grp")
    return lax.ppermute(block, "grp", [(i, i ^ mask) for i in range(count)])


def quad_bits():
    return [1 << b for b in range((lax.axis_size("grp") // 2).bit_length() - 1)]


def flip_columns(values, quad):
    quads = lax.axis_size("grp") // 2
    axis = values.ndim - 1
    block = values.shape[axis] // quads
    return jnp.concatenate(
        [
            lax.dynamic_slice_in_dim(values, (quad ^ key) * block, block, axis)
            for key in range(quads)
        ],
        axis=axis,
    )


def gather_quads(pieces, order):
    pieces = dict(pieces)
    for bit in order:
        for key, piece in list(pieces.items()):
            pieces[key | bit] = across(piece, 2 * bit)
    return pieces


def send_quads(pieces, bit, keys):
    return {key: across(pieces[key], 2 * bit) for key in keys}


def add_quads(pieces, arrived, bit):
    return {
        key: (piece.astype(F32) + arrived[key | bit].astype(F32)).astype(BF16)
        for key, piece in pieces.items()
        if not key & bit
    }


def reduce_quads(pieces, order):
    for bit in order:
        arrived = send_quads(pieces, bit, [key for key in pieces if key & bit])
        pieces = add_quads(pieces, arrived, bit)
    return pieces


def together(*values):
    return lax.optimization_barrier(values)


def sum_everywhere(values, masks_grp, masks_ep):
    for mask in masks_grp:
        values = values + across(values, mask)
    count = lax.axis_size("ep")
    for mask in masks_ep:
        values = values + lax.ppermute(values, "ep", [(i, i ^ mask) for i in range(count)])
    return values


def gather_rest(pieces, order):
    found = {}
    for key, piece in pieces.items():
        if key:
            found.update({key | k: v for k, v in gather_quads({0: piece}, order).items()})
    return found


def listed(pieces):
    return [pieces[key] for key in sorted(pieces)]


def place_quads(pieces, quad, axis):
    size = pieces[0].shape[axis]
    shape = list(pieces[0].shape)
    shape[axis] = size * len(pieces)
    whole = jnp.zeros(shape, pieces[0].dtype)
    for key in sorted(pieces):
        whole = lax.dynamic_update_slice_in_dim(whole, pieces[key], (quad ^ key) * size, axis)
    return whole


def take_quads(whole, quad, quads, axis):
    size = whole.shape[axis] // quads
    return {
        key: lax.dynamic_slice_in_dim(whole, (quad ^ key) * size, size, axis)
        for key in range(quads)
    }


def merge_core(kept, arrived, core, axis):
    first = jnp.where(core == 0, kept, arrived)
    second = jnp.where(core == 0, arrived, kept)
    return jnp.concatenate([first, second], axis=axis)


def split_core(values, core, axis):
    half = values.shape[axis] // 2
    first = lax.slice_in_dim(values, 0, half, axis=axis)
    second = lax.slice_in_dim(values, half, 2 * half, axis=axis)
    return jnp.where(core == 0, first, second), jnp.where(core == 0, second, first)


def norm_scale(values):
    return lax.rsqrt(jnp.mean(values * values, axis=-1, keepdims=True) + EPS)


def norm_backward(grad_normed, unit, scale, gain):
    grad_unit = grad_normed * gain
    inner = jnp.mean(grad_unit * unit, axis=-1, keepdims=True)
    return scale * (grad_unit - unit * inner), jnp.sum(grad_normed * unit, axis=0)


def doc_layout(document_lengths, seq_len, index):
    valid = index >= 0
    safe = jnp.maximum(index, 0)
    seq_of = safe // seq_len
    place = safe % seq_len
    seq_count = document_lengths.shape[0]
    picker = (seq_of[:, None] == jnp.arange(seq_count, dtype=jnp.int32)[None, :]).astype(jnp.int32)
    lengths = jnp.sum(picker[:, :, None] * document_lengths[None, :, :], axis=1)
    ends = jnp.cumsum(lengths, axis=1)
    doc = jnp.sum((ends <= place[:, None]).astype(jnp.int32), axis=1)
    earlier = jnp.arange(DOCS, dtype=jnp.int32)[None, :] < doc[:, None]
    before = jnp.sum(jnp.where(earlier, lengths, 0), axis=1)
    return jnp.where(valid, seq_of * DOCS + doc, -1), place - before


def rope_tables(position):
    half = HDIM // 2
    freq = ROPE_BASE ** (-(jnp.arange(half, dtype=F32) * 2.0 / HDIM))
    angle = position.astype(F32)[:, None] * freq[None, :]
    cosine, sine = jnp.cos(angle), jnp.sin(angle)
    return jnp.concatenate([cosine, cosine], axis=1), jnp.concatenate([-sine, sine], axis=1)


def turn(values, cosine, sine):
    return values * cosine + pltpu.roll(values, HDIM // 2, 1) * sine


def call(kernel, grid, ins, outs, shapes, limit, flops, scratch=(), name=None):
    moved = 0
    for shape in shapes:
        moved += shape.size * shape.dtype.itemsize

    def run(*args):
        total = moved + sum(a.size * a.dtype.itemsize for a in args)
        return pl.pallas_call(
            kernel,
            grid=grid,
            in_specs=ins,
            out_specs=outs,
            out_shape=shapes,
            scratch_shapes=scratch,
            compiler_params=pltpu.CompilerParams(vmem_limit_bytes=limit * MIB),
            cost_estimate=pl.CostEstimate(
                flops=flops, bytes_accessed=total, transcendentals=0
            ),
            name=name,
        )(*args)

    return run


def whole(shape):
    return pl.BlockSpec(shape, lambda *_: (0,) * len(shape), pipeline_mode=pl.Buffered(1))


def rows_spec(columns, tile=TILE):
    return pl.BlockSpec((tile, columns), lambda i: (i, 0))


def shaped(rows, columns, dtype):
    return jax.ShapeDtypeStruct((rows, columns), dtype)


def sum_pieces(x, refs):
    block = x.shape[1] // len(refs)
    total = dot(x[:, :block], refs[0][...])
    for key in range(1, len(refs)):
        total = total + dot(x[:, key * block : (key + 1) * block], refs[key][...])
    return total


def project_kernel(heads, quads, x_ref, bias_ref, cos_ref, sin_ref, *rest):
    wa_refs, wb_refs, (q_ref, kv_ref) = rest[:quads], rest[quads : 2 * quads], rest[2 * quads :]
    x = x_ref[...]
    lin = jnp.concatenate([sum_pieces(x, wa_refs), sum_pieces(x, wb_refs)], axis=1) + bias_ref[...]
    cosine, sine = cos_ref[...], sin_ref[...]
    for head in range(3 * heads):
        part = lin[:, head * HDIM : (head + 1) * HDIM]
        if head < 2 * heads:
            part = turn(part, cosine, sine)
        if head < heads:
            q_ref[:, head * HDIM : (head + 1) * HDIM] = part.astype(BF16)
        else:
            kv_ref[:, (head - heads) * HDIM : (head - heads + 1) * HDIM] = part.astype(BF16)


def project(x, wa, wb, bias, cosine, sine, heads):
    rows, width = x.shape
    quads, (block, cut) = len(wa), wa[0].shape
    return call(
        functools.partial(project_kernel, heads, quads),
        (rows // TILE,),
        [rows_spec(width), whole((1, 2 * cut))]
        + [rows_spec(HDIM)] * 2
        + [whole((block, cut))] * (2 * quads),
        [rows_spec(heads * HDIM), rows_spec(2 * heads * HDIM)],
        [shaped(rows, heads * HDIM, BF16), shaped(rows, 2 * heads * HDIM, BF16)],
        32,
        4 * rows * width * cut,
        name="project",
    )(x, bias, cosine, sine, *wa, *wb)


def window_keys(before_refs, own_ref, place, pair_rows, step):
    parts = []
    start = step * TILE
    reach = -WINDOW + start
    for back, ref in enumerate(before_refs):
        first = -(len(before_refs) - back) * pair_rows
        low = max(reach - first, 0)
        if low < pair_rows:
            parts.append(ref[low:, place])
    parts.append(own_ref[max(reach, 0) : start + TILE, place])
    return jnp.concatenate(parts, axis=0) if len(parts) > 1 else parts[0]


def probabilities(query, keys, key_place, low, high, peak):
    scores = dot_last(query, keys) * HDIM ** (-0.5)
    scores = jnp.where((key_place >= low) & (key_place <= high), scores, MASKED)
    if peak is None:
        top = jnp.max(scores, axis=1, keepdims=True)
        weights = jnp.exp(scores - top)
        total = jnp.sum(weights, axis=1, keepdims=True)
        return weights / total, top + jnp.log(total)
    return jnp.exp(scores - peak), peak


def attend_kernel(back, pair_rows, heads, q_ref, *rest):
    before, (own_ref, place_ref, low_ref, high_ref, out_ref, log_ref) = rest[:back], rest[back:]
    for head in range(heads):
        cols = slice(head * HDIM, (head + 1) * HDIM)
        value_cols = slice((heads + head) * HDIM, (heads + head + 1) * HDIM)
        for step in range(pair_rows // TILE):
            rows = slice(step * TILE, (step + 1) * TILE)
            first = back * pair_rows - WINDOW + step * TILE
            places = place_ref[:, max(first, 0) : back * pair_rows + (step + 1) * TILE]
            keys = window_keys(before, own_ref, cols, pair_rows, step)
            values = window_keys(before, own_ref, value_cols, pair_rows, step)
            probs, logs = probabilities(
                q_ref[rows, cols], keys, places, low_ref[rows, :], high_ref[rows, :], None
            )
            out_ref[rows, cols] = dot(probs.astype(BF16), values).astype(BF16)
            log_ref[rows, cols] = jnp.broadcast_to(logs, (TILE, HDIM))


def attend(query, before, own, places, low, high):
    rows, columns = query.shape
    heads = columns // HDIM
    back = len(before)
    return call(
        functools.partial(attend_kernel, back, rows, heads),
        (),
        [pl.BlockSpec(memory_space=pltpu.VMEM)] * (5 + back),
        [pl.BlockSpec(memory_space=pltpu.VMEM)] * 2,
        [shaped(rows, columns, BF16), shaped(rows, columns, F32)],
        40,
        4 * rows * columns * (WINDOW + TILE),
        name="attend",
    )(query, *before, own, places, low, high)


def attend_back_kernel(back, pair_rows, heads, q_ref, grad_ref, log_ref, *rest):
    before = rest[:back]
    own_ref, place_ref, low_ref, high_ref, cos_ref, sin_ref = rest[back : back + 6]
    dq_ref, own_out = rest[back + 6 : back + 8]
    before_out = rest[back + 8 : 2 * back + 8]
    total_ref = rest[-1]
    total_ref[...] = jnp.zeros_like(total_ref)
    for head in range(heads):
        cols = slice(head * HDIM, (head + 1) * HDIM)
        value_cols = slice((heads + head) * HDIM, (heads + head + 1) * HDIM)
        for step in range(pair_rows // TILE):
            rows = slice(step * TILE, (step + 1) * TILE)
            first = max(back * pair_rows - WINDOW + step * TILE, 0)
            last = back * pair_rows + (step + 1) * TILE
            keys = window_keys(before, own_ref, cols, pair_rows, step)
            values = window_keys(before, own_ref, value_cols, pair_rows, step)
            query, grad = q_ref[rows, cols], grad_ref[rows, cols]
            peak = jnp.concatenate([log_ref[rows, cols]] * ((last - first) // HDIM), axis=1)
            probs, _ = probabilities(
                query, keys, place_ref[:, first:last], low_ref[rows, :], high_ref[rows, :], peak
            )
            grad_probs = dot_last(grad, values)
            inner = jnp.sum(probs * grad_probs, axis=1, keepdims=True)
            grad_scores = (probs * (grad_probs - inner)).astype(BF16)
            grad_query = dot(grad_scores, keys) * HDIM ** (-0.5)
            dq_ref[rows, cols] = turn(grad_query, cos_ref[rows, :], -sin_ref[rows, :]).astype(BF16)
            total_ref[first:last, cols] += dot_first(grad_scores, query) * HDIM ** (-0.5)
            total_ref[first:last, value_cols] += dot_first(probs.astype(BF16), grad)
    own_out[...] = total_ref[back * pair_rows :, :]
    for step in range(back):
        before_out[step][...] = total_ref[step * pair_rows : (step + 1) * pair_rows, :].astype(BF16)


def attend_back(query, grad, logs, before, own, places, low, high, cosine, sine):
    rows, columns = query.shape
    back = len(before)
    return call(
        functools.partial(attend_back_kernel, back, rows, columns // HDIM),
        (),
        [pl.BlockSpec(memory_space=pltpu.VMEM)] * (9 + back),
        [pl.BlockSpec(memory_space=pltpu.VMEM)] * (2 + back),
        [shaped(rows, columns, BF16), shaped(rows, 2 * columns, F32)]
        + [shaped(rows, 2 * columns, BF16)] * back,
        48,
        10 * rows * columns * (WINDOW + TILE),
        scratch=[pltpu.VMEM(((back + 1) * rows, 2 * columns), F32)],
        name="attend_back",
    )(query, grad, logs, *before, own, places, low, high, cosine, sine)


def collect_kernel(heads, back, quads, dq_ref, own_ref, cos_ref, sin_ref, x_ref, *rest):
    arrived, wa_refs, wb_refs = rest[:back], rest[back : back + quads], rest[back + quads : back + 2 * quads]
    out_ref, part_ref, gain_ref, bias_ref = rest[back + 2 * quads :]
    columns = heads * HDIM
    total = own_ref[...]
    for ref in arrived:
        total = total + ref[...].astype(F32)
    cosine, sine = cos_ref[...], -sin_ref[...]
    heads_out = [dq_ref[...]]
    for head in range(2 * heads):
        part = total[:, head * HDIM : (head + 1) * HDIM]
        if head < heads:
            part = turn(part, cosine, sine)
        heads_out.append(part.astype(BF16))
    grads = jnp.concatenate(heads_out, axis=1)
    out_ref[...] = grads

    @pl.when(pl.program_id(0) == 0)
    def _():
        gain_ref[...] = jnp.zeros_like(gain_ref)
        bias_ref[...] = jnp.zeros_like(bias_ref)

    bias_ref[...] += jnp.sum(grads.astype(F32), axis=0, keepdims=True)
    cut = 3 * columns // 2
    block = x_ref.shape[1] // quads
    for key in range(quads):
        cols = slice(key * block, (key + 1) * block)
        part = dot_last(grads[:, :cut], wa_refs[key][...]) + dot_last(grads[:, cut:], wb_refs[key][...])
        part_ref[:, cols] = part.astype(BF16)
        gain_ref[:, cols] += jnp.sum(part * x_ref[:, cols].astype(F32), axis=0, keepdims=True)


def collect(grad_query, own, cosine, sine, x, arrived, wa, wb):
    rows, columns = grad_query.shape
    width = x.shape[1]
    quads, (block, cut) = len(wa), wa[0].shape
    fixed = lambda i: (0, 0)
    return call(
        functools.partial(collect_kernel, columns // HDIM, len(arrived), quads),
        (rows // TILE,),
        [rows_spec(columns), rows_spec(2 * columns)]
        + [rows_spec(HDIM)] * 2
        + [rows_spec(width)]
        + [rows_spec(2 * columns)] * len(arrived)
        + [whole((block, cut))] * (2 * quads),
        [
            rows_spec(3 * columns),
            rows_spec(width),
            pl.BlockSpec((1, width), fixed),
            pl.BlockSpec((1, 3 * columns), fixed),
        ],
        [
            shaped(rows, 3 * columns, BF16),
            shaped(rows, width, BF16),
            shaped(1, width, F32),
            shaped(1, 3 * columns, F32),
        ],
        32,
        4 * rows * width * cut,
        name="collect",
    )(grad_query, own, cosine, sine, x, *arrived, *wa, *wb)


def expert_kernel(routed, quads, x_ref, wd_ref, cot_ref, scale_ref, *rest):
    if routed:
        wg_refs, wu_refs, rest = rest[:quads], rest[quads : 2 * quads], rest[2 * quads :]
        part_in, grad_in, dot_in, lane_ref = rest[:4]
        rest = rest[4:]
    else:
        wgu_refs, rest = rest[:quads], rest[quads:]
    x = x_ref[...]
    hidden, width = wd_ref.shape
    if routed:
        gate_pre = sum_pieces(x, wg_refs)
        up_pre = sum_pieces(x, wu_refs)
    else:
        pre = sum_pieces(x, wgu_refs)
        gate_pre, up_pre = pre[:, :hidden], pre[:, hidden:]
    sigma = jax.nn.sigmoid(gate_pre)
    swish = gate_pre * sigma
    active = (swish * up_pre).astype(BF16)
    rest[0][...] = active
    cot = cot_ref[...].astype(F32)
    scale = scale_ref[...]
    grad_result = (scale * cot).astype(BF16)
    rest[1][...] = grad_result
    grad_active = dot_last(grad_result, wd_ref[...])
    grad_up = grad_active * swish
    grad_gate = grad_active * up_pre * (sigma * (1.0 + gate_pre * (1.0 - sigma)))
    result = dot(active, wd_ref[...])
    if routed:
        result = result.astype(BF16).astype(F32)
    inner = jnp.sum(cot * result, axis=1, keepdims=True)
    part = scale * result
    block = width // quads
    if not routed:
        part_ref, grad_ref, inner_ref, both_ref = rest[2:]
        both = jnp.concatenate([grad_gate, grad_up], axis=1).astype(BF16)
        both_ref[...] = both
        part_ref[...] = part.astype(BF16)
        for key in range(quads):
            grad = dot_last(both, wgu_refs[key][...])
            grad_ref[:, key * block : (key + 1) * block] = grad.astype(BF16)
        inner_ref[...] = inner
        return
    part_ref, grad_ref, gate_ref, up_ref = rest[2:]
    grad_gate, grad_up = grad_gate.astype(BF16), grad_up.astype(BF16)
    gate_ref[...] = grad_gate
    up_ref[...] = grad_up
    part_ref[...] = (part + part_in[...].astype(F32)).astype(BF16)
    for key in range(quads):
        cols = slice(key * block, (key + 1) * block)
        grad = dot_last(grad_gate, wg_refs[key][...]) + dot_last(grad_up, wu_refs[key][...])
        grad = grad.astype(BF16).astype(F32) + grad_in[:, cols].astype(F32)
        grad_ref[:, cols] = grad.astype(BF16)
    lane = lane_ref[...]
    extra = jnp.zeros((x.shape[0], LANES), F32)
    for slot, value in enumerate((inner, dot_in[...])):
        high = value.astype(BF16).astype(F32)
        extra = extra + jnp.where(lane == 2 * slot, high, 0.0)
        extra = extra + jnp.where(lane == 2 * slot + 1, value - high, 0.0)
    grad_ref[:, width:] = extra.astype(BF16)


def expert(x, pieces, wd, cot, scale, routed=()):
    rows, width = x.shape
    hidden = wd.shape[0]
    quads = len(pieces) // 2 if routed else len(pieces)
    ins = [rows_spec(width), whole((hidden, width)), rows_spec(width), rows_spec(1)]
    ins += [whole(piece.shape) for piece in pieces]
    outs = [rows_spec(hidden), rows_spec(width), rows_spec(width)]
    shapes = [shaped(rows, hidden, BF16), shaped(rows, width, BF16), shaped(rows, width, BF16)]
    if routed:
        ins += [rows_spec(width), rows_spec(width), rows_spec(1), whole((1, LANES))]
        outs += [rows_spec(width + LANES), rows_spec(hidden), rows_spec(hidden)]
        shapes += [shaped(rows, width + LANES, BF16)] + [shaped(rows, hidden, BF16)] * 2
    else:
        outs += [rows_spec(width), rows_spec(1), rows_spec(2 * hidden)]
        shapes += [shaped(rows, width, BF16), shaped(rows, 1, F32), shaped(rows, 2 * hidden, BF16)]
    return call(
        functools.partial(expert_kernel, bool(routed), quads),
        (rows // TILE,),
        ins,
        outs,
        shapes,
        60,
        12 * rows * width * hidden,
        name="expert" if routed else "shared",
    )(x, wd, cot, scale, *pieces, *routed)


def local(
    residual_in,
    attention_gain,
    query_weight,
    query_bias,
    key_weight,
    key_bias,
    value_weight,
    value_bias,
    output_weight,
    feedforward_gain,
    router_weight,
    shared_logit_weight,
    shared_gate_weight,
    shared_up_weight,
    shared_down_weight,
    expert_gate,
    expert_up,
    expert_down,
    cotangent,
    expert_index,
    token_live,
    document_lengths,
):
    ep_count = lax.axis_size("ep")
    grp_count = lax.axis_size("grp")
    quads = grp_count // 2
    rows_dev, width = residual_in.shape
    group_rows = rows_dev * ep_count
    pair_rows = 2 * group_rows
    seq_len = group_rows * grp_count // SEQS
    expert_count = expert_gate.shape[0] * ep_count
    ffe = expert_gate.shape[2]
    ffs_half = shared_gate_weight.shape[1] // 2
    grp = lax.axis_index("grp")
    ep = lax.axis_index("ep")
    core = grp % 2
    quad = grp // 2
    back = -(-WINDOW // pair_rows)
    heads = query_weight.shape[1] // HDIM // 2
    head_width = heads * HDIM
    up_order = quad_bits()
    down_order = up_order[::-1]

    block = width // quads
    cut = len(up_order) // 2
    up_one, up_two = up_order[:cut], up_order[cut:]
    down_one, down_two = down_order[: len(down_order) - cut], down_order[len(down_order) - cut :]
    ep_masks = [1 << b for b in range(ep_count.bit_length() - 1)]
    quad_masks = [2 * bit for bit in up_order]
    seq_groups = grp_count // SEQS
    experts = jnp.arange(expert_count, dtype=jnp.int32)
    ed_cut = width // 2

    def shifted(values, steps):
        route = [
            (i, i + 2 * steps)
            for i in range(grp_count)
            if 0 <= i + 2 * steps < grp_count and i // seq_groups == (i + 2 * steps) // seq_groups
        ]
        return lax.ppermute(values, "grp", route)

    def gathered(values):
        return lax.all_gather(values, "ep", axis=0, tiled=True)

    def scattered(values):
        return lax.psum_scatter(values, "ep", scatter_dimension=0, tiled=True).astype(F32)

    def core_sum(values):
        keep, other = split_core(values, core, 0)
        return (keep.astype(F32) + across(other, 1).astype(F32)).astype(BF16)

    def row_grads(rows, grads):
        return {
            k: dot_first(rows[:, k * block : (k + 1) * block], grads).astype(BF16)
            for k in range(quads)
        }

    def column_grads(acts, grads):
        return {
            k: dot_first(acts, part).astype(BF16)
            for k, part in take_quads(grads, quad, quads, 1).items()
        }

    hidden_in = residual_in.astype(F32)
    grad_out = cotangent.astype(F32)
    gain_one = attention_gain.astype(F32)
    gain_two = feedforward_gain.astype(F32)
    router_all = jnp.concatenate([router_weight, shared_logit_weight[:, None]], axis=1)
    router_flipped = flip_columns(router_all.T, quad).T
    scale_one = norm_scale(hidden_in)
    unit_one = hidden_in * scale_one
    normed_one = (unit_one * gain_one).astype(BF16)
    group_one = gathered(flip_columns(normed_one, quad))

    qk_keep, qk_other = zip(
        *[split_core(weight, core, 1) for weight in (query_weight, key_weight, value_weight)]
    )
    qkv_keep, qkv_other = jnp.concatenate(qk_keep, 1), jnp.concatenate(qk_other, 1)
    qkv_block = merge_core(qkv_keep, across(qkv_other, 1), core, 0)
    qkv_cut = qkv_block.shape[1] // 2
    qkv_a = {0: qkv_block[:, :qkv_cut]}
    qkv_b = {0: qkv_block[:, qkv_cut:]}
    (
        qkv_a, qkv_b, output_weight, shared_gate_weight, shared_up_weight, shared_down_weight,
        expert_gate, expert_up, expert_down,
    ) = together(
        qkv_a, qkv_b, output_weight, shared_gate_weight, shared_up_weight, shared_down_weight,
        expert_gate, expert_up, expert_down,
    )
    qkv_a_one, qkv_a_two = gather_quads(qkv_a, up_one), gather_quads(qkv_a, up_two)
    qkv_b_one, qkv_b_two = gather_quads(qkv_b, down_one), gather_quads(qkv_b, down_two)

    o_keep, o_other = split_core(output_weight, core, 0)
    o_block = merge_core(o_keep, across(o_other, 1), core, 1)
    sg_keep, sg_other = split_core(shared_gate_weight, core, 1)
    su_keep, su_other = split_core(shared_up_weight, core, 1)
    gu_keep = jnp.concatenate([sg_keep, su_keep], axis=1)
    gu_other = jnp.concatenate([sg_other, su_other], axis=1)
    gu_block = merge_core(gu_keep, across(gu_other, 1), core, 0)
    sd_keep, sd_other = split_core(shared_down_weight, core, 0)
    sd_block = merge_core(sd_keep, across(sd_other, 1), core, 1)

    def expert_block(weight):
        keep, other = split_core(weight, core, 0)
        return merge_core(keep[0], across(other[0], 1), core, 0)

    eg_block, eu_block, ed_block = [
        expert_block(weight) for weight in (expert_gate, expert_up, expert_down)
    ]
    eda_block, edb_block = ed_block[:, :ed_cut], ed_block[:, ed_cut:]

    (
        qkv_a_one, qkv_a_two, qkv_b_one, qkv_b_two, o_block, gu_block, sd_block, eg_block, eu_block,
        eda_block, edb_block,
    ) = together(
        qkv_a_one, qkv_a_two, qkv_b_one, qkv_b_two, o_block, gu_block, sd_block, eg_block, eu_block,
        eda_block, edb_block,
    )
    qkv_a_rest = gather_rest(qkv_a_one, up_two)
    qkv_b_rest = gather_rest(qkv_b_one, down_two)
    o_one, o_two = gather_quads({0: o_block}, down_one), gather_quads({0: o_block}, down_two)
    sd_one, sd_two = gather_quads({0: sd_block}, down_one), gather_quads({0: sd_block}, down_two)
    (
        group_one, qkv_a, qkv_b, o_one, o_two, sd_one, sd_two, gu_block, eg_block, eu_block,
        eda_block, edb_block, cotangent,
    ) = together(
        group_one, qkv_a_one | qkv_a_two | qkv_a_rest, qkv_b_one | qkv_b_two | qkv_b_rest, o_one,
        o_two, sd_one, sd_two, gu_block, eg_block, eu_block, eda_block, edb_block, cotangent,
    )

    rows_one = merge_core(group_one, across(group_one, 1), core, 0)
    gu_two = gather_quads({0: gu_block}, up_two)
    o_rest = gather_rest(o_one, down_two)
    chosen = (
        (expert_index[:, :, None] == experts[None, None, :]) & (token_live[:, None, None] > 0)
    ).any(axis=1)
    chosen = chosen.astype(BF16)
    cot_group = gathered(
        jnp.concatenate([cotangent, jnp.pad(chosen, ((0, 0), (0, LANES - expert_count)))], axis=1)
    )
    chosen = chosen.astype(F32)
    qkv_a, qkv_b = listed(qkv_a), listed(qkv_b)
    bias = jnp.concatenate(
        [split_core(b, core, 0)[0] for b in (query_bias, key_bias, value_bias)]
    ).astype(F32)
    key_place = (quad - back) * pair_rows + jnp.arange((back + 1) * pair_rows, dtype=jnp.int32)
    query_place = key_place[back * pair_rows :]
    _, position = doc_layout(document_lengths, seq_len, query_place)
    low = jnp.maximum(query_place - position, query_place - WINDOW + 1)[:, None]
    high, key_place = query_place[:, None], key_place[None, :]
    cosine, sine = rope_tables(position)
    query, key_value = project(rows_one, qkv_a, qkv_b, bias[None, :], cosine, sine, heads)

    before = [shifted(key_value, step) for step in range(back, 0, -1)]
    query, before, gu_two, o_rest, sd_one, edb_block = together(
        query, before, gu_two, o_rest, sd_one, edb_block
    )
    sd_rest = gather_rest(sd_one, down_two)
    edb_one = gather_quads({0: edb_block}, down_one)
    attended, log_total = attend(query, before, key_value, key_place, low, high)
    o_full = place_quads(o_one | o_two | o_rest, quad, 1)
    branch = dot(attended, o_full).astype(BF16)
    branch, cot_group, sd_rest, edb_one = together(branch, cot_group, sd_rest, edb_one)
    branch = core_sum(branch)
    branch, gu_block, eu_block, eda_block, cot_group = together(
        branch, gu_block, eu_block, eda_block, cot_group
    )
    branch_sum = scattered(branch)
    cot_other = across(cot_group, 1)
    gu_one = gather_quads({0: gu_block}, up_one)
    eda_one, eda_two = gather_quads({0: eda_block}, up_one), gather_quads({0: eda_block}, up_two)
    eu_one = gather_quads({0: eu_block}, down_one)
    branch_sum, cot_other, gu_one, eda_one, eda_two, eu_one, eg_block, edb_block = together(
        branch_sum, cot_other, gu_one, eda_one, eda_two, eu_one, eg_block, edb_block
    )

    eg_one = gather_quads({0: eg_block}, up_one)
    edb_two, edb_rest = gather_quads({0: edb_block}, down_two), gather_rest(edb_one, down_two)
    gu_rest, eda_rest = gather_rest(gu_one, up_two), gather_rest(eda_one, up_two)
    mixed = hidden_in + branch_sum
    scale_two = norm_scale(mixed)
    unit_two = mixed * scale_two
    normed_two = (unit_two * gain_two).astype(BF16)
    group_two = gathered(flip_columns(normed_two, quad))
    cot_rows = merge_core(cot_group, cot_other, core, 0)
    sd_full = place_quads(sd_one | sd_two | sd_rest, quad, 1)
    group_two, eg_one, edb_two, edb_rest, gu_rest, eda_rest = together(
        group_two, eg_one, edb_two, edb_rest, gu_rest, eda_rest
    )
    rows_two = merge_core(group_two, across(group_two, 1), core, 0)
    (
        rows_two, cot_rows, sd_full, eg_one, edb_two, edb_rest, gu_rest, eda_rest, eu_one, eu_block,
        eg_block,
    ) = together(
        rows_two, cot_rows, sd_full, eg_one, edb_two, edb_rest, gu_rest, eda_rest, eu_one, eu_block,
        eg_block,
    )
    eu_two, eg_two = gather_quads({0: eu_block}, down_two), gather_quads({0: eg_block}, up_two)
    gu_pieces = listed(gu_one | gu_two | gu_rest)
    ed_full = jnp.concatenate(
        [
            place_quads(eda_one | eda_two | eda_rest, quad, 0),
            place_quads(edb_one | edb_two | edb_rest, quad, 0),
        ],
        axis=1,
    )

    def router(rows, weight):
        logits = dot(rows, weight)
        return jax.nn.softmax(logits[:, :expert_count], axis=-1), jax.nn.sigmoid(
            logits[:, expert_count:]
        )

    chosen_rows = cot_rows[:, width : width + expert_count].astype(F32)
    probs_rows, shared_scale_rows = router(rows_two, router_flipped)
    router_probs, shared_scale = router(normed_two, router_all)
    mine = (experts == ep * 2 + core).astype(F32)[None, :]
    gate = jnp.sum(probs_rows * chosen_rows * mine, axis=1, keepdims=True)

    shared_active, grad_shared_out, part, grad_part, shared_dot, grad_gu = expert(
        rows_two, gu_pieces, sd_full, cot_rows, shared_scale_rows
    )
    grad_gu, grad_part, eu_two, eg_two, eu_one, eg_one = together(
        grad_gu, grad_part, eu_two, eg_two, eu_one, eg_one
    )
    eu_rest, eg_rest = gather_rest(eu_one, down_two), gather_rest(eg_one, up_two)
    gu_grad = row_grads(rows_two, grad_gu)
    sd_grad = column_grads(shared_active, grad_shared_out)
    grad_part, eg_pieces, eu_pieces, ed_full, gu_grad, sd_grad = together(
        grad_part, eg_one | eg_two | eg_rest, eu_one | eu_two | eu_rest, ed_full, gu_grad, sd_grad
    )
    up_keys = [key for key in gu_grad if key & up_one[0]]
    down_keys = [key for key in gu_grad if key & down_one[0]]
    gu_sent = send_quads(gu_grad, up_one[0], up_keys)
    sd_sent = send_quads(sd_grad, down_one[0], down_keys)

    lanes = jnp.arange(LANES, dtype=jnp.int32)
    lanes = jnp.where(lanes % expert_count == ep * 2 + core, lanes // expert_count, -1)[None, :]
    active, grad_result, forward_part, packed, grad_gate_pre, grad_up_pre = expert(
        rows_two,
        listed(eg_pieces) + listed(eu_pieces),
        ed_full,
        cot_rows,
        gate,
        (part, grad_part, shared_dot, lanes),
    )
    packed, gu_grad, gu_sent, sd_grad, sd_sent = together(packed, gu_grad, gu_sent, sd_grad, sd_sent)
    packed = core_sum(packed)
    gu_grad = reduce_quads(add_quads(gu_grad, gu_sent, up_one[0]), up_one[1:])
    sd_grad = reduce_quads(add_quads(sd_grad, sd_sent, down_one[0]), down_one[1:])
    packed, gu_grad, sd_grad, active, grad_gate_pre, grad_up_pre = together(
        packed, gu_grad, sd_grad, active, grad_gate_pre, grad_up_pre
    )
    spread = scattered(packed)
    ed_grad = take_quads(dot_first(active, grad_result).astype(BF16), quad, quads, 0)
    eda_grad = {k: v[:, :ed_cut] for k, v in ed_grad.items()}
    edb_grad = {k: v[:, ed_cut:] for k, v in ed_grad.items()}
    gu_grad = reduce_quads(gu_grad, up_two)[0]
    sd_grad = reduce_quads(sd_grad, down_two)[0]
    eda_sent = send_quads(eda_grad, up_one[0], up_keys)
    edb_sent = send_quads(edb_grad, down_one[0], down_keys)
    eg_grad = row_grads(rows_two, grad_gate_pre)
    eu_grad = row_grads(rows_two, grad_up_pre)
    spread, gu_grad, sd_grad, eg_grad, eu_grad = together(spread, gu_grad, sd_grad, eg_grad, eu_grad)

    grad_normed_two = flip_columns(spread[:, :width], quad)
    side = spread[:, width : width + 4 * expert_count].reshape(rows_dev, 4, expert_count)
    grad_gate_own = side[:, 0] + side[:, 1]
    shared_dot_own = jnp.sum(side[:, 2] + side[:, 3], axis=1, keepdims=True)
    grad_logit = shared_dot_own * shared_scale * (1.0 - shared_scale)
    grad_probs = grad_gate_own * chosen
    grad_logits = router_probs * (
        grad_probs - jnp.sum(router_probs * grad_probs, axis=-1, keepdims=True)
    )
    grad_router = jnp.concatenate([grad_logits, grad_logit], axis=1)
    router_grad = dot_first(normed_two.astype(F32), grad_router)
    grad_normed_two = grad_normed_two + dot_last(grad_router, router_all.astype(F32))
    grad_norm_part, ff_gain_grad = norm_backward(grad_normed_two, unit_two, scale_two, gain_two)
    grad_mixed = grad_out + grad_norm_part
    branch_low, eda_grad, eda_sent, edb_grad, edb_sent, eg_grad, eu_grad, forward_part = together(
        grad_mixed.astype(BF16), eda_grad, eda_sent, edb_grad, edb_sent, eg_grad, eu_grad,
        forward_part,
    )
    group_branch = gathered(branch_low)
    half = len(up_keys) // 2
    eg_sent = send_quads(eg_grad, up_one[0], up_keys[:half])
    eu_sent = send_quads(eu_grad, down_one[0], down_keys[:half])
    eda_grad = reduce_quads(add_quads(eda_grad, eda_sent, up_one[0]), up_one[1:])
    edb_grad = reduce_quads(add_quads(edb_grad, edb_sent, down_one[0]), down_one[1:])
    forward_sum = core_sum(forward_part)
    group_branch, forward_sum, eg_grad, eg_sent, eu_grad, eu_sent, eda_grad, edb_grad = together(
        group_branch, forward_sum, eg_grad, eg_sent, eu_grad, eu_sent, eda_grad, edb_grad
    )
    grad_branch = merge_core(group_branch, across(group_branch, 1), core, 0)
    eg_sent |= send_quads(eg_grad, up_one[0], up_keys[half:])
    eu_sent |= send_quads(eu_grad, down_one[0], down_keys[half:])

    layer_sum = scattered(forward_sum)
    grad_attended = dot_last(grad_branch, o_full).astype(BF16)
    grad_query, grad_own, *grad_before = attend_back(
        query, grad_attended, log_total, before, key_value, key_place, low, high, cosine, sine
    )
    grad_query, grad_before, eg_grad, eg_sent, eu_grad, eu_sent, eda_grad, edb_grad = together(
        grad_query, grad_before, eg_grad, eg_sent, eu_grad, eu_sent, eda_grad, edb_grad
    )
    arrived = [shifted(sent, step - back) for step, sent in enumerate(grad_before)]
    eg_grad = reduce_quads(add_quads(eg_grad, eg_sent, up_one[0]), up_one[1:])
    eu_grad = reduce_quads(add_quads(eu_grad, eu_sent, down_one[0]), down_one[1:])
    eg_grad = reduce_quads(eg_grad, up_two)[0]
    o_grad = column_grads(attended, grad_branch)
    arrived, o_grad, layer_sum, eg_grad, eu_grad, eda_grad, edb_grad = together(
        arrived, o_grad, layer_sum, eg_grad, eu_grad, eda_grad, edb_grad
    )
    layer_out = (mixed + layer_sum).astype(BF16)
    eda_grad = reduce_quads(eda_grad, up_two)[0]
    edb_grad = reduce_quads(edb_grad, down_two)[0]
    grad_lin, partial, att_gain_part, bias_part = collect(
        grad_query, grad_own, cosine, sine, rows_one, arrived, qkv_a, qkv_b
    )
    grad_lin_a, grad_lin_b = grad_lin[:, :qkv_cut], grad_lin[:, qkv_cut:]
    partial_sum = core_sum(partial)

    att_gain_part = flip_columns(att_gain_part[0], quad) / gain_one
    late = jnp.concatenate(
        [bias_part[0], att_gain_part, ff_gain_grad, router_grad.T.reshape(-1)]
    )
    qkv_a_grad = row_grads(rows_one, grad_lin_a)
    qkv_b_grad = row_grads(rows_one, grad_lin_b)
    partial_sum, qkv_a_grad, qkv_b_grad, late, eda_grad, edb_grad, eu_grad = together(
        partial_sum, qkv_a_grad, qkv_b_grad, late, eda_grad, edb_grad, eu_grad
    )
    grad_normed_one = scattered(partial_sum)
    eu_grad = reduce_quads(eu_grad, down_two)[0]
    o_grad = reduce_quads(o_grad, down_order)[0]
    qkv_a_grad = reduce_quads(qkv_a_grad, up_order)[0]
    qkv_b_grad = reduce_quads(qkv_b_grad, down_order)[0]
    qkv_grad = jnp.concatenate([qkv_a_grad, qkv_b_grad], axis=1)
    late = sum_everywhere(late, quad_masks, [])
    bias_part = late[: 3 * head_width]
    bias_mine = merge_core(
        bias_part.reshape(3, head_width), across(bias_part, 1).reshape(3, head_width), core, 1
    )
    late = sum_everywhere(late[3 * head_width :], [1], ep_masks)
    att_gain_grad, ff_gain_grad = late[:width], late[width : 2 * width]
    router_grad = late[2 * width :].reshape(expert_count + 1, width)
    grad_norm_one, _ = norm_backward(
        flip_columns(grad_normed_one, quad), unit_one, scale_one, gain_one
    )
    input_grad = grad_mixed + grad_norm_one

    def back_to_cores(summed, cut_axis, join_axis):
        keep, other = split_core(summed, core, cut_axis)
        return merge_core(keep, across(other, 1), core, join_axis).astype(F32)

    def back_to_experts(summed):
        keep, other = split_core(summed, core, 0)
        arrived = across(other, 1)
        return jnp.stack(
            [jnp.where(core == 0, keep, arrived), jnp.where(core == 0, arrived, keep)]
        ).astype(F32)

    ed_grad = jnp.concatenate([eda_grad, edb_grad], axis=1)
    q_grad, k_grad, v_grad = [
        back_to_cores(qkv_grad[:, part * head_width : (part + 1) * head_width], 0, 1)
        for part in range(3)
    ]
    return (
        layer_out,
        input_grad,
        att_gain_grad,
        q_grad,
        bias_mine[0],
        k_grad,
        bias_mine[1],
        v_grad,
        bias_mine[2],
        back_to_cores(o_grad, 1, 0),
        ff_gain_grad,
        router_grad[:expert_count].T,
        router_grad[expert_count],
        back_to_cores(gu_grad[:, :ffs_half], 0, 1),
        back_to_cores(gu_grad[:, ffs_half:], 0, 1),
        back_to_cores(sd_grad, 1, 0),
        back_to_experts(eg_grad),
        back_to_experts(eu_grad),
        back_to_experts(ed_grad),
    )


def solution(mesh):
    tokens = P(("grp", "ep"), None)
    rows, columns, experts = P("grp", "ep"), P("ep", "grp"), P("ep", "grp", None)
    in_specs = (
        tokens, P(), rows, P("ep"), rows, P("ep"), rows, P("ep"), columns, P(), P(), P(),
        rows, rows, columns, experts, experts, experts, tokens, tokens, P(("grp", "ep")), P(),
    )
    out_specs = (
        tokens, tokens, P(), rows, P("ep"), rows, P("ep"), rows, P("ep"), columns, P(), P(), P(),
        rows, rows, columns, experts, experts, experts,
    )
    return jax.shard_map(local, mesh=mesh, in_specs=in_specs, out_specs=out_specs, check_vma=False)
```

time: 1060 us -> 841 us (0.79)
  matrix products: 254 us -> 83.5 us
  Pallas kernels: 0 us -> 113 us
  waiting for transfers between devices: 455 us -> 345 us
  other arithmetic: 158 us -> 139 us
  local copies, waits for them, and re-layouts: 75.3 us -> 60.1 us
    pallas_call x0 -> x6, Pallas kernels: none -> 113 us  [run(): pl.pallas_call(kernel, grid=grid, in_specs=ins, out_specs=outs, out_shape...]
    dot_general x8 -> x2, matrix products: 69.2 us -> 3.68 us  [dot_last(): lax.dot_general(left, right, (((1,), (1,)), ((), ())), preferred_element_...]
    dot_general x9 -> x3, matrix products: 54.3 us -> 4.66 us  [dot(): return jnp.dot(left, right, preferred_element_type=F32)]
    dot_general x6 -> x0, matrix products: 49 us -> none  [the longest x1 10.4 us: local(): jnp.einsum('qhd,khd->hqk', grad_attended, values_all, preferred_element_t...]
    all_gather x4, waiting for transfers between devices: 50.1 us -> 9.1 us  [gathered(): return lax.all_gather(values, 'ep', axis=0, tiled=True)]
    ppermute x86 -> x83, waiting for transfers between devices: 318 us -> 288 us  [across(): return lax.ppermute(block, 'grp', [(i, i ^ mask) for i in range(count)])]
    ppermute x2, waiting for transfers between devices: 16.2 us -> 0.01 us  [shifted(): return lax.ppermute(values, 'grp', route)]
    concatenate x14 -> x5, other arithmetic: 26.3 us -> 10.2 us  [the longest x1 5.14 us: local(): jnp.concatenate([place_quads(eda_one | eda_two | eda_rest, quad, 0), plac...]
  transfers between devices with their start and end apart: 100 -> 95, of which waited for: 41 -> 36; matrix products, arithmetic and copies ran while one was open for 35% -> 25% of each run, Pallas kernels for 0% -> 13%
where the time goes in v2:
time: 841 us; the launch traced here: 831 us
  waiting for transfers between devices  345 us (41%)
  other arithmetic  139 us (17%)
  Pallas kernels  113 us (13%)
  matrix products  83.5 us (10%)
  starting transfers between devices  74.2 us (9%)
  local copies, waits for them, and re-layouts  60.1 us (7%)
  between operations  16.5 us (2%)
    ppermute x83, waiting for transfers between devices, across(): return lax.ppermute(block, 'grp', [(i, i ^ mask) for i in range(count)])  288 us
    pallas_call x6, Pallas kernels, run(): pl.pallas_call(kernel, grid=grid, in_specs=ins, out_specs=outs, out_shape...  113 us
    dot_general x30, matrix products, dot_first(): lax.dot_general(left, right, (((0,), (0,)), ((), ())), preferred_element_...  75.2 us
    ppermute x83, starting transfers between devices, across(): return lax.ppermute(block, 'grp', [(i, i ^ mask) for i in range(count)])  67.9 us
    convert_element_type x23, other arithmetic, add_quads(): (piece.astype(F32) + arrived[key | bit].astype(F32)).astype(BF16)  44.5 us
    reduce_scatter x4, waiting for transfers between devices, scattered(): lax.psum_scatter(values, 'ep', scatter_dimension=0, tiled=True).astype(F32)  40 us
    unnamed x285, local copies, waits for them, and re-layouts  27.4 us
    dynamic_update_slice x16, local copies, waits for them, and re-layouts, place_quads(): lax.dynamic_update_slice_in_dim(whole, pieces[key], (quad ^ key) * size,...  19.7 us
  transfers between devices with their start and end apart: 95, of which 36 were waited for; matrix products, arithmetic and copies ran while one was open for 25% of the time, Pallas kernels for 13%

profile of v2, /device:TPU:0, one launch (start us, length us, event | category | flops | bytes accessed | tf_op | source)
XLA Modules:
  0.0 831.4 jit_solution(15774231536784977413)
XLA Ops:
  31.1 5.8 collective-permute-done.3.rest_6_.rest_7_
  43.7 19.3 %collective-permute-done.13 = bf16[256,512]{1,0:T(8,128)(2,1)} collective-permute-done((bf16[256,512]{1,0:T(8,128)(2,1)S(1)}, bf16[256,512]{1,0:T(8,128)(2,1)}, u32[]{:S(2)}, u32[]{:S(2)}) %collective-permute-start.13) | collective-permute-done | bytes 262176 | tf_op jit(solution)/shard_map/ppermute | solution.py:38
  63.8 7.1 collective-permute-done.14
  72.0 3.2 fusion.55
  84.4 6.0 project.1
  96.8 25.7 %collective-permute-done.20 = bf16[256,512]{1,0:T(8,128)(2,1)} collective-permute-done((bf16[256,512]{1,0:T(8,128)(2,1)}, bf16[256,512]{1,0:T(8,128)(2,1)}, u32[]{:S(2)}, u32[]{:S(2)}) %collective-permute-start.20) | collective-permute-done | bytes 262176 | tf_op jit(solution)/shard_map/ppermute | solution.py:38
  128.6 8.4 %attend.1 = (bf16[1024,256]{1,0:T(8,128)(2,1)S(1)}, f32[1024,256]{1,0:T(8,128)S(1)}) custom-call(bf16[1024,256]{1,0:T(8,128)(2,1)S(1)} %copy-done.35, bf16[1024,512]{1,0:T(8,128)(2,1)S(1)} %collective-permute-done.18.rest_0_, bf16[1024,512]{1,0:T(8,128)(2,1)} %get-tuple-element.296.rest_1_, s32[1,2048]{1,0:T(1,128)S(1)} %iota_add_fusion.rest_2_, ...), custom_call_target="tpu_custom_call" | custom-call | flops 1342177280 | bytes 4210688 | tf_op jit(solution)/shard_map/attend/pallas_call | solution.py:185
  138.8 3.2 convolution_convert_fusion.1
  145.0 4.1 collective-permute-done.23
  156.1 40.0 %reduce-scatter.5.cloned.1.call-done = bf16[128,2048]{1,0:T(8,128)(2,1)} async-done(((bf16[512,2048]{1,0:T(8,128)(2,1)}), bf16[128,2048]{1,0:T(8,128)(2,1)}) %reduce-scatter.5.cloned.1.call-update) | async-done | bytes 524304 | tf_op jit(solution)/shard_map/reduce_scatter | solution.py:579
  197.2 4.4 collective-permute-done.26
  210.2 44.3 %collective-permute-done.31 = bf16[352,1024]{1,0:T(8,128)(2,1)} collective-permute-done((bf16[352,1024]{1,0:T(8,128)(2,1)}, bf16[352,1024]{1,0:T(8,128)(2,1)}, u32[]{:S(2)}, u32[]{:S(2)}) %collective-permute-start.31) | collective-permute-done | bytes 720928 | tf_op jit(solution)/shard_map/ppermute | solution.py:38
  254.5 13.7 %collective-permute-done.30 = bf16[352,1024]{1,0:T(8,128)(2,1)} collective-permute-done((bf16[352,1024]{1,0:T(8,128)(2,1)S(1)}, bf16[352,1024]{1,0:T(8,128)(2,1)}, u32[]{:S(2)}, u32[]{:S(2)}) %collective-permute-start.30) | collective-permute-done | bytes 720928 | tf_op jit(solution)/shard_map/ppermute | solution.py:38
  290.0 27.2 %shared.1 = (bf16[1024,704]{1,0:T(8,128)(2,1)}, bf16[1024,2048]{1,0:T(8,128)(2,1)}, bf16[1024,2048]{1,0:T(8,128)(2,1)}, bf16[1024,2048]{1,0:T(8,128)(2,1)}, f32[...) custom-call(bf16[1024,2048]{1,0:T(8,128)(2,1)} %copy-done.65, bf16[704,2048]{1,0:T(8,128)(2,1)} %copy-done.70, ...), custom_call_target="tpu_custom_call" | custom-call | flops 17716740096 | bytes 34217984 | tf_op jit(solution)/shard_map/shared/pallas_call | solution.py:185
  317.2 3.5 convolution_convert_fusion.14
  335.8 5.1 pad_maximum_fusion.2.wd_ref
  342.3 3.0 convolution_convert_fusion.10
  345.3 3.0 convolution_convert_fusion.11
  348.3 3.0 convolution_convert_fusion.12
  351.3 3.0 convolution_convert_fusion.13
  354.2 20.5 %collective-permute-done.37.rest_3_ = bf16[512,1408]{1,0:T(8,128)(2,1)} collective-permute-done((bf16[512,1408]{1,0:T(8,128)(2,1)}, bf16[512,1408]{1,0:T(8,128)(2,1)}, u32[]{:S(2)}, u32[]{:S(2)}) %collective-permute-start.37) | collective-permute-done | bytes 1441824 | tf_op jit(solution)/shard_map/ppermute | solution.py:38
  379.1 51.7 %expert.1 = (bf16[1024,1408]{1,0:T(8,128)(2,1)}, bf16[1024,2048]{1,0:T(8,128)(2,1)}, bf16[1024,2048]{1,0:T(8,128)(2,1)}, bf16[1024,2176]{1,0:T(8,128)(2,1)}, bf1...) custom-call(bf16[1024,2048]{1,0:T(8,128)(2,1)} %copy-done.65, bf16[1408,2048]{1,0:T(8,128)(2,1)} %pad_maximum_fusion.2.wd_ref, ...), custom_call_target="tpu_custom_call" | custom-call | flops 35433480192 | bytes 55845376 | tf_op jit(solution)/shard_map/expert/pallas_call | solution.py:185
  430.8 7.7 collective-permute-done.40
  453.8 8.9 %convolution_convert_fusion = bf16[1408,2048]{1,0:T(8,128)(2,1)S(1)} fusion(bf16[1024,1408]{1,0:T(8,128)(2,1)} %get-tuple-element.415, bf16[1024,2048]{1,0:T(8,128)(2,1)} %get-tuple-element.416), kind=kOutput, calls=%fused_computation | convolution fusion | flops 5908463616 | bytes 12845056 | tf_op jit(solution)/shard_map/dot_general | solution.py:33
  470.2 5.2 convolution_convert_fusion.2
  475.4 5.1 convolution_convert_fusion.3
  480.6 3.0 convolution_convert_fusion.4
  483.6 3.0 convolution_convert_fusion.5
  489.5 3.0 convolution_convert_fusion.7
  492.5 3.0 convolution_convert_fusion.8
  495.4 3.0 convolution_convert_fusion.9
  498.5 16.4 %collective-permute-done.45 = bf16[704,512]{1,0:T(8,128)(2,1)} collective-permute-done((bf16[704,512]{1,0:T(8,128)(2,1)S(1)}, bf16[704,512]{1,0:T(8,128)(2,1)}, u32[]{:S(2)}, u32[]{:S(2)}) %collective-permute-start.45) | collective-permute-done | bytes 720928 | tf_op jit(solution)/shard_map/ppermute | solution.py:38
  550.8 19.1 %collective-permute-done.51 = bf16[512,1408]{1,0:T(8,128)(2,1)} collective-permute-done((bf16[512,1408]{1,0:T(8,128)(2,1)}, bf16[512,1408]{1,0:T(8,128)(2,1)}, u32[]{:S(2)}, u32[]{:S(2)}) %collective-permute-start.51) | collective-permute-done | bytes 1441824 | tf_op jit(solution)/shard_map/ppermute | solution.py:38
  570.4 9.1 %all-gather.11.cloned.1.call-done = bf16[512,2048]{1,0:T(8,128)(2,1)} async-done(((bf16[128,2048]{1,0:T(8,128)(2,1)}), bf16[512,2048]{1,0:T(8,128)(2,1)}) %all-gather.11.cloned.1.call-update) | async-done | bytes 2097168 | tf_op jit(solution)/shard_map/all_gather | solution.py:576
  597.1 14.0 %attend_back.1 = (bf16[1024,256]{1,0:T(8,128)(2,1)S(1)}, f32[1024,512]{1,0:T(8,128)}, bf16[1024,512]{1,0:T(8,128)(2,1)}) custom-call(bf16[1024,256]{1,0:T(8,128)(2,1)S(1)} %copy-done.36, bf16[1024,256]{1,0:T(8,128)(2,1)S(1)} %fusion.4.grad_ref, f32[1024,256]{1,0:T(8,128)S(1)} %copy-done.33, bf16[1024,512]{1,0:T(8,128)(2,1)} %copy-done.31, ...), custom_call_target="tpu_custom_call" | custom-call | flops 3355443200 | bytes 8929280 | tf_op jit(solution)/shard_map/attend_back/pallas_call | solution.py:185
  611.1 11.2 %collective-permute-done.54 = bf16[512,1408]{1,0:T(8,128)(2,1)} collective-permute-done((bf16[512,1408]{1,0:T(8,128)(2,1)}, bf16[512,1408]{1,0:T(8,128)(2,1)}, u32[]{:S(2)}, u32[]{:S(2)}) %collective-permute-start.54) | collective-permute-done | bytes 1441824 | tf_op jit(solution)/shard_map/ppermute | solution.py:38
  638.6 19.3 %collective-permute-done.57 = bf16[512,1408]{1,0:T(8,128)(2,1)S(1)} collective-permute-done((bf16[512,1408]{1,0:T(8,128)(2,1)S(1)}, bf16[512,1408]{1,0:T(8,128)(2,1)S(1)}, u32[]{:S(2)}, u32[]{:S(2)}) %collective-permute-start.57) | collective-permute-done | bytes 1441824 | tf_op jit(solution)/shard_map/ppermute | solution.py:38
  657.9 3.0 add_convert_fusion.7
  676.0 6.1 collect.1
  699.3 15.4 %collective-permute-done.77 = bf16[256,512]{1,0:T(8,128)(2,1)} collective-permute-done((bf16[256,512]{1,0:T(8,128)(2,1)}, bf16[256,512]{1,0:T(8,128)(2,1)}, u32[]{:S(2)}, u32[]{:S(2)}) %collective-permute-start.77) | collective-permute-done | bytes 262176 | tf_op jit(solution)/shard_map/ppermute | solution.py:38
  718.7 3.5 collective-permute-done.78
  732.0 4.2 add_convert_fusion.1
  737.6 3.7 collective-permute-done.61
  742.9 3.1 collective-permute-done.62
  753.1 4.6 collective-permute-done.64
  758.7 31.9 %collective-permute-done.67 = bf16[512,384]{1,0:T(8,128)(2,1)} collective-permute-done((bf16[512,384]{1,0:T(8,128)(2,1)}, bf16[512,384]{1,0:T(8,128)(2,1)}, u32[]{:S(2)}, u32[]{:S(2)}) %collective-permute-start.67) | collective-permute-done | bytes 393248 | tf_op jit(solution)/shard_map/ppermute | solution.py:38
  796.2 3.6 collective-permute-done.65
  806.0 3.4 collective-permute-done.73
  (676 shorter events, 296.3 us)
Async XLA Ops:
  7.2 63.8 %all-gather.5.cloned.1.call-start = ((), (), s32[]{:S(2)}) async-start(), calls=%async_computation.4 | async-start | bytes 2621440 | tf_op jit(solution)/shard_map/all_gather | solution.py:576
  13.2 128.7 %all-gather.7.cloned.1.call-start = ((), (), s32[]{:S(2)}) async-start(), calls=%async_computation.5 | async-start | bytes 2785280 | tf_op jit(solution)/shard_map/all_gather | solution.py:576
  38.0 33.0 %collective-permute-start.15 = (bf16[704,512]{1,0:T(8,128)(2,1)}, bf16[704,512]{1,0:T(8,128)(2,1)}, u32[]{:S(2)}, u32[]{:S(2)}) collective-permute-start(bf16[704,512]{1,0:T(8,128)(2,1)} %pad_maximum_fusion.14), channel_id=1, source_target_pairs={{0,16},{4,20},{8,24},{12,28},{16,0},{20,4},{24,8},{28,12},{1,17},{... | collective-permute-start | bytes 2162696 | tf_op jit(solution)/shard_map/ppermute | solution.py:38
  77.1 119.0 %reduce-scatter.5.cloned.1.call-start = ((), (), s32[]{:S(2)}) async-start(), calls=%async_computation.6 | async-start | bytes 2621440 | tf_op jit(solution)/shard_map/reduce_scatter | solution.py:579
  80.3 42.2 %collective-permute-start.19 = (bf16[512,1408]{1,0:T(8,128)(2,1)}, bf16[512,1408]{1,0:T(8,128)(2,1)}, u32[]{:S(2)}, u32[]{:S(2)}) collective-permute-start(bf16[512,1408]{1,0:T(8,128)(2,1)} %pad_maximum_fusion.6.rest_0_), channel_id=1, source_target_pairs={{0,16},{4,20},{8,24},{12,28},{16,0},{20,4},{24,8},{28,12},{1,17},{... | collective-permute-start | bytes 4325384 | tf_op jit(solution)/shard_map/ppermute | solution.py:38
  151.8 116.4 %all-gather.9.cloned.1.call-start = ((), (), s32[]{:S(2)}) async-start(), calls=%async_computation.7 | async-start | bytes 2621440 | tf_op jit(solution)/shard_map/all_gather | solution.py:576
  151.8 50.2 %collective-permute-start.24 = (bf16[512,2176]{1,0:T(8,128)(2,1)}, bf16[512,2176]{1,0:T(8,128)(2,1)}, u32[]{:S(2)}, u32[]{:S(2)}) collective-permute-start(bf16[512,2176]{1,0:T(8,128)(2,1)} %all-gather.7.cloned.1.call-done), channel_id=1, source_target_pairs={{0,4},{4,0},{8,12},{12,8},{16,20},{20,16},{24,28},{28,24},{1,5},{5... | collective-permute-start | bytes 6684680 | tf_op jit(solution)/shard_map/ppermute | solution.py:38
  152.0 50.0 %collective-permute-start.25 = (bf16[512,1408]{1,0:T(8,128)(2,1)}, bf16[512,1408]{1,0:T(8,128)(2,1)}, u32[]{:S(2)}, u32[]{:S(2)}) collective-permute-start(bf16[512,1408]{1,0:T(8,128)(2,1)} %pad_maximum_fusion.6.rest_0_), channel_id=1, source_target_pairs={{0,8},{4,12},{8,0},{12,4},{16,24},{20,28},{24,16},{28,20},{1,9},{5... | collective-permute-start | bytes 4325384 | tf_op jit(solution)/shard_map/ppermute | solution.py:38
  152.7 49.3 %collective-permute-start.28 = (bf16[512,1408]{1,0:T(8,128)(2,1)}, bf16[512,1408]{1,0:T(8,128)(2,1)}, u32[]{:S(2)}, u32[]{:S(2)}) collective-permute-start(bf16[512,1408]{1,0:T(8,128)(2,1)} %get-tuple-element.379.rest_4_), channel_id=1, source_target_pairs={{0,16},{4,20},{8,24},{12,28},{16,0},{20,4},{24,8},{28,12},{1,17},{... | collective-permute-start | bytes 4325384 | tf_op jit(solution)/shard_map/ppermute | solution.py:38
  153.9 47.7 %collective-permute-start.26 = (bf16[352,1024]{1,0:T(8,128)(2,1)S(1)}, bf16[352,1024]{1,0:T(8,128)(2,1)}, u32[]{:S(2)}, u32[]{:S(2)}) collective-permute-start(bf16[352,1024]{1,0:T(8,128)(2,1)S(1)} %copy-done.79), channel_id=1, source_target_pairs={{0,8},{4,12},{8,0},{12,4},{16,24},{20,28},{24,16},{28,20},{1,9},{5... | collective-permute-start | bytes 2162696 | tf_op jit(solution)/shard_map/ppermute | solution.py:38
  155.5 46.6 %collective-permute-start.27 = (bf16[352,1024]{1,0:T(8,128)(2,1)S(1)}, bf16[352,1024]{1,0:T(8,128)(2,1)}, u32[]{:S(2)}, u32[]{:S(2)}) collective-permute-start(bf16[352,1024]{1,0:T(8,128)(2,1)S(1)} %copy-done.79), channel_id=1, source_target_pairs={{0,16},{4,20},{8,24},{12,28},{16,0},{20,4},{24,8},{28,12},{1,17},{... | collective-permute-start | bytes 2162696 | tf_op jit(solution)/shard_map/ppermute | solution.py:38
  203.7 317.0 %reduce-scatter.7.cloned.1.call-start = ((), (), s32[]{:S(2)}) async-start(), calls=%async_computation.8 | async-start | bytes 2785280 | tf_op jit(solution)/shard_map/reduce_scatter | solution.py:579
  204.1 64.0 %collective-permute-start.29 = (bf16[512,1408]{1,0:T(8,128)(2,1)}, bf16[512,1408]{1,0:T(8,128)(2,1)}, u32[]{:S(2)}, u32[]{:S(2)}) collective-permute-start(bf16[512,1408]{1,0:T(8,128)(2,1)} %get-tuple-element.375.rest_0_), channel_id=1, source_target_pairs={{0,8},{4,12},{8,0},{12,4},{16,24},{20,28},{24,16},{28,20},{1,9},{5... | collective-permute-start | bytes 4325384 | tf_op jit(solution)/shard_map/ppermute | solution.py:38
  205.5 62.6 %collective-permute-start.32 = (bf16[512,1408]{1,0:T(8,128)(2,1)}, bf16[512,1408]{1,0:T(8,128)(2,1)}, u32[]{:S(2)}, u32[]{:S(2)}) collective-permute-start(bf16[512,1408]{1,0:T(8,128)(2,1)} %collective-permute-done.25.rest_1_), channel_id=1, source_target_pairs={{0,16},{4,20},{8,24},{12,28},{16,0},{20,4},{24,8},{28,12},{1,17},{... | collective-permute-start | bytes 4325384 | tf_op jit(solution)/shard_map/ppermute | solution.py:38
  206.9 47.6 %collective-permute-start.31 = (bf16[352,1024]{1,0:T(8,128)(2,1)}, bf16[352,1024]{1,0:T(8,128)(2,1)}, u32[]{:S(2)}, u32[]{:S(2)}) collective-permute-start(bf16[352,1024]{1,0:T(8,128)(2,1)} %collective-permute-done.22), channel_id=1, source_target_pairs={{0,8},{4,12},{8,0},{12,4},{16,24},{20,28},{24,16},{28,20},{1,9},{5... | collective-permute-start | bytes 2162696 | tf_op jit(solution)/shard_map/ppermute | solution.py:38
  207.4 60.7 %collective-permute-start.30 = (bf16[352,1024]{1,0:T(8,128)(2,1)S(1)}, bf16[352,1024]{1,0:T(8,128)(2,1)}, u32[]{:S(2)}, u32[]{:S(2)}) collective-permute-start(bf16[352,1024]{1,0:T(8,128)(2,1)S(1)} %copy-done.78), channel_id=1, source_target_pairs={{0,8},{4,12},{8,0},{12,4},{16,24},{20,28},{24,16},{28,20},{1,9},{5... | collective-permute-start | bytes 2162696 | tf_op jit(solution)/shard_map/ppermute | solution.py:38
  209.0 59.2 %collective-permute-start.33 = (bf16[352,1024]{1,0:T(8,128)(2,1)}, bf16[352,1024]{1,0:T(8,128)(2,1)}, u32[]{:S(2)}, u32[]{:S(2)}) collective-permute-start(bf16[352,1024]{1,0:T(8,128)(2,1)} %collective-permute-done.26), channel_id=1, source_target_pairs={{0,16},{4,20},{8,24},{12,28},{16,0},{20,4},{24,8},{28,12},{1,17},{... | collective-permute-start | bytes 2162696 | tf_op jit(solution)/shard_map/ppermute | solution.py:38
  287.3 53.6 %collective-permute-start.35 = (bf16[512,1408]{1,0:T(8,128)(2,1)}, bf16[512,1408]{1,0:T(8,128)(2,1)}, u32[]{:S(2)}, u32[]{:S(2)}) collective-permute-start(bf16[512,1408]{1,0:T(8,128)(2,1)} %get-tuple-element.379.rest_4_), channel_id=1, source_target_pairs={{0,8},{4,12},{8,0},{12,4},{16,24},{20,28},{24,16},{28,20},{1,9},{5... | collective-permute-start | bytes 4325384 | tf_op jit(solution)/shard_map/ppermute | solution.py:38
  288.6 52.3 %collective-permute-start.36 = (bf16[512,1408]{1,0:T(8,128)(2,1)}, bf16[512,1408]{1,0:T(8,128)(2,1)}, u32[]{:S(2)}, u32[]{:S(2)}) collective-permute-start(bf16[512,1408]{1,0:T(8,128)(2,1)} %get-tuple-element.375.rest_0_), channel_id=1, source_target_pairs={{0,16},{4,20},{8,24},{12,28},{16,0},{20,4},{24,8},{28,12},{1,17},{... | collective-permute-start | bytes 4325384 | tf_op jit(solution)/shard_map/ppermute | solution.py:38
  340.9 33.7 %collective-permute-start.37 = (bf16[512,1408]{1,0:T(8,128)(2,1)}, bf16[512,1408]{1,0:T(8,128)(2,1)}, u32[]{:S(2)}, u32[]{:S(2)}) collective-permute-start(bf16[512,1408]{1,0:T(8,128)(2,1)} %collective-permute-done.29.rest_1_), channel_id=1, source_target_pairs={{0,16},{4,20},{8,24},{12,28},{16,0},{20,4},{24,8},{28,12},{1,17},{... | collective-permute-start | bytes 4325384 | tf_op jit(solution)/shard_map/ppermute | solution.py:38
  341.6 33.5 %collective-permute-start.38 = (bf16[512,1408]{1,0:T(8,128)(2,1)}, bf16[512,1408]{1,0:T(8,128)(2,1)}, u32[]{:S(2)}, u32[]{:S(2)}) collective-permute-start(bf16[512,1408]{1,0:T(8,128)(2,1)} %collective-permute-done.28.rest_6_), channel_id=1, source_target_pairs={{0,8},{4,12},{8,0},{12,4},{16,24},{20,28},{24,16},{28,20},{1,9},{5... | collective-permute-start | bytes 4325384 | tf_op jit(solution)/shard_map/ppermute | solution.py:38
  375.0 55.8 %collective-permute-start.39 = (bf16[512,1408]{1,0:T(8,128)(2,1)}, bf16[512,1408]{1,0:T(8,128)(2,1)}, u32[]{:S(2)}, u32[]{:S(2)}) collective-permute-start(bf16[512,1408]{1,0:T(8,128)(2,1)} %convolution_convert_fusion.12), channel_id=1, source_target_pairs={{0,8},{4,12},{8,0},{12,4},{16,24},{20,28},{24,16},{28,20},{1,9},{5... | collective-permute-start | bytes 4325384 | tf_op jit(solution)/shard_map/ppermute | solution.py:38
  375.8 62.7 %collective-permute-start.40 = (bf16[512,1408]{1,0:T(8,128)(2,1)}, bf16[512,1408]{1,0:T(8,128)(2,1)}, u32[]{:S(2)}, u32[]{:S(2)}) collective-permute-start(bf16[512,1408]{1,0:T(8,128)(2,1)} %convolution_convert_fusion.10), channel_id=1, source_target_pairs={{0,8},{4,12},{8,0},{12,4},{16,24},{20,28},{24,16},{28,20},{1,9},{5... | collective-permute-start | bytes 4325384 | tf_op jit(solution)/shard_map/ppermute | solution.py:38
  377.1 53.7 %collective-permute-start.41 = (bf16[704,512]{1,0:T(8,128)(2,1)}, bf16[704,512]{1,0:T(8,128)(2,1)}, u32[]{:S(2)}, u32[]{:S(2)}) collective-permute-start(bf16[704,512]{1,0:T(8,128)(2,1)} %convolution_convert_fusion.15), channel_id=1, source_target_pairs={{0,16},{4,20},{8,24},{12,28},{16,0},{20,4},{24,8},{28,12},{1,17},{... | collective-permute-start | bytes 2162696 | tf_op jit(solution)/shard_map/ppermute | solution.py:38
  378.5 52.3 %collective-permute-start.42 = (bf16[704,512]{1,0:T(8,128)(2,1)}, bf16[704,512]{1,0:T(8,128)(2,1)}, u32[]{:S(2)}, u32[]{:S(2)}) collective-permute-start(bf16[704,512]{1,0:T(8,128)(2,1)} %convolution_convert_fusion.14), channel_id=1, source_target_pairs={{0,16},{4,20},{8,24},{12,28},{16,0},{20,4},{24,8},{28,12},{1,17},{... | collective-permute-start | bytes 2162696 | tf_op jit(solution)/shard_map/ppermute | solution.py:38
  465.2 67.5 %collective-permute-start.46 = (bf16[352,1024]{1,0:T(8,128)(2,1)}, bf16[352,1024]{1,0:T(8,128)(2,1)}, u32[]{:S(2)}, u32[]{:S(2)}) collective-permute-start(bf16[352,1024]{1,0:T(8,128)(2,1)} %get-tuple-element.519), channel_id=1, source_target_pairs={{0,8},{4,12},{8,0},{12,4},{16,24},{20,28},{24,16},{28,20},{1,9},{5... | collective-permute-start | bytes 2162696 | tf_op jit(solution)/shard_map/ppermute | solution.py:38
  465.9 66.8 %collective-permute-start.47 = (bf16[352,1024]{1,0:T(8,128)(2,1)}, bf16[352,1024]{1,0:T(8,128)(2,1)}, u32[]{:S(2)}, u32[]{:S(2)}) collective-permute-start(bf16[352,1024]{1,0:T(8,128)(2,1)} %get-tuple-element.517), channel_id=1, source_target_pairs={{0,8},{4,12},{8,0},{12,4},{16,24},{20,28},{24,16},{28,20},{1,9},{5... | collective-permute-start | bytes 2162696 | tf_op jit(solution)/shard_map/ppermute | solution.py:38
  467.2 65.5 %collective-permute-start.48 = (bf16[352,1024]{1,0:T(8,128)(2,1)}, bf16[352,1024]{1,0:T(8,128)(2,1)}, u32[]{:S(2)}, u32[]{:S(2)}) collective-permute-start(bf16[352,1024]{1,0:T(8,128)(2,1)} %get-tuple-element.521), channel_id=1, source_target_pairs={{0,16},{4,20},{8,24},{12,28},{16,0},{20,4},{24,8},{28,12},{1,17},{... | collective-permute-start | bytes 2162696 | tf_op jit(solution)/shard_map/ppermute | solution.py:38
  468.6 46.3 %collective-permute-start.45 = (bf16[704,512]{1,0:T(8,128)(2,1)S(1)}, bf16[704,512]{1,0:T(8,128)(2,1)}, u32[]{:S(2)}, u32[]{:S(2)}) collective-permute-start(bf16[704,512]{1,0:T(8,128)(2,1)S(1)} %copy-done.102), channel_id=1, source_target_pairs={{0,8},{4,12},{8,0},{12,4},{16,24},{20,28},{24,16},{28,20},{1,9},{5... | collective-permute-start | bytes 2162696 | tf_op jit(solution)/shard_map/ppermute | solution.py:38
  469.2 49.3 %collective-permute-start.44 = (bf16[512,1408]{1,0:T(8,128)(2,1)}, bf16[512,1408]{1,0:T(8,128)(2,1)}, u32[]{:S(2)}, u32[]{:S(2)}) collective-permute-start(bf16[512,1408]{1,0:T(8,128)(2,1)} %add_convert_fusion.11), channel_id=1, source_target_pairs={{0,16},{4,20},{8,24},{12,28},{16,0},{20,4},{24,8},{28,12},{1,17},{... | collective-permute-start | bytes 4325384 | tf_op jit(solution)/shard_map/ppermute | solution.py:38
  470.0 109.5 %all-gather.11.cloned.1.call-start = ((), (), s32[]{:S(2)}) async-start(), calls=%async_computation.9 | async-start | bytes 2621440 | tf_op jit(solution)/shard_map/all_gather | solution.py:576
  533.0 127.9 %reduce-scatter.9.cloned.1.call-start = ((), (), s32[]{:S(2)}) async-start(), calls=%async_computation.10 | async-start | bytes 2621440 | tf_op jit(solution)/shard_map/reduce_scatter | solution.py:579
  535.6 34.3 %collective-permute-start.51 = (bf16[512,1408]{1,0:T(8,128)(2,1)}, bf16[512,1408]{1,0:T(8,128)(2,1)}, u32[]{:S(2)}, u32[]{:S(2)}) collective-permute-start(bf16[512,1408]{1,0:T(8,128)(2,1)} %convolution_convert_fusion.8), channel_id=1, source_target_pairs={{0,8},{4,12},{8,0},{12,4},{16,24},{20,28},{24,16},{28,20},{1,9},{5... | collective-permute-start | bytes 4325384 | tf_op jit(solution)/shard_map/ppermute | solution.py:38
  536.4 34.0 %collective-permute-start.52 = (bf16[512,1408]{1,0:T(8,128)(2,1)}, bf16[512,1408]{1,0:T(8,128)(2,1)}, u32[]{:S(2)}, u32[]{:S(2)}) collective-permute-start(bf16[512,1408]{1,0:T(8,128)(2,1)} %convolution_convert_fusion.3), channel_id=1, source_target_pairs={{0,16},{4,20},{8,24},{12,28},{16,0},{20,4},{24,8},{28,12},{1,17},{... | collective-permute-start | bytes 4325384 | tf_op jit(solution)/shard_map/ppermute | solution.py:38
  538.8 43.9 %collective-permute-start.81 = (bf16[256,704]{1,0:T(8,128)(2,1)}, bf16[256,704]{1,0:T(8,128)(2,1)}, u32[]{:S(2)}, u32[]{:S(2)}) collective-permute-start(bf16[256,704]{1,0:T(8,128)(2,1)} %broadcast_select_fusion.25), channel_id=1, source_target_pairs={{0,4},{4,0},{8,12},{12,8},{16,20},{20,16},{24,28},{28,24},{1,5},{5... | collective-permute-start | bytes 1081352 | tf_op jit(solution)/shard_map/ppermute | solution.py:38
  588.3 34.0 %collective-permute-start.54 = (bf16[512,1408]{1,0:T(8,128)(2,1)}, bf16[512,1408]{1,0:T(8,128)(2,1)}, u32[]{:S(2)}, u32[]{:S(2)}) collective-permute-start(bf16[512,1408]{1,0:T(8,128)(2,1)} %convolution_convert_fusion.6), channel_id=1, source_target_pairs={{0,8},{4,12},{8,0},{12,4},{16,24},{20,28},{24,16},{28,20},{1,9},{5... | collective-permute-start | bytes 4325384 | tf_op jit(solution)/shard_map/ppermute | solution.py:38
  589.9 33.7 %collective-permute-start.55 = (bf16[512,1408]{1,0:T(8,128)(2,1)}, bf16[512,1408]{1,0:T(8,128)(2,1)}, u32[]{:S(2)}, u32[]{:S(2)}) collective-permute-start(bf16[512,1408]{1,0:T(8,128)(2,1)} %convolution_convert_fusion.2), channel_id=1, source_target_pairs={{0,16},{4,20},{8,24},{12,28},{16,0},{20,4},{24,8},{28,12},{1,17},{... | collective-permute-start | bytes 4325384 | tf_op jit(solution)/shard_map/ppermute | solution.py:38
  592.6 226.9 %reduce-scatter.11.cloned.1.call-start = ((), (), s32[]{:S(2)}) async-start(), calls=%async_computation.11 | async-start | bytes 2621440 | tf_op jit(solution)/shard_map/reduce_scatter | solution.py:579
  625.4 32.5 %collective-permute-start.57 = (bf16[512,1408]{1,0:T(8,128)(2,1)S(1)}, bf16[512,1408]{1,0:T(8,128)(2,1)S(1)}, u32[]{:S(2)}, u32[]{:S(2)}) collective-permute-start(bf16[512,1408]{1,0:T(8,128)(2,1)S(1)} %add_convert_fusion.8), channel_id=1, source_target_pairs={{0,16},{4,20},{8,24},{12,28},{16,0},{20,4},{24,8},{28,12},{1,17},{... | collective-permute-start | bytes 4325384 | tf_op jit(solution)/shard_map/ppermute | solution.py:38
  630.9 32.1 %collective-permute-start.56 = (bf16[1024,512]{1,0:T(8,128)(2,1)}, bf16[1024,512]{1,0:T(8,128)(2,1)S(1)}, u32[]{:S(2)}, u32[]{:S(2)}) collective-permute-start(bf16[1024,512]{1,0:T(8,128)(2,1)} %get-tuple-element.460), channel_id=1, source_target_pairs={{8,0},{12,4},{24,16},{28,20},{9,1},{13,5},{25,17},{29,21},{10,2},{... | collective-permute-start | bytes 3145736 | tf_op jit(solution)/shard_map/ppermute | solution.py:573
  689.5 36.2 %collective-permute-start.60 = (bf16[352,1024]{1,0:T(8,128)(2,1)S(1)}, bf16[352,1024]{1,0:T(8,128)(2,1)}, u32[]{:S(2)}, u32[]{:S(2)}) collective-permute-start(bf16[352,1024]{1,0:T(8,128)(2,1)S(1)} %copy-done.100), channel_id=1, source_target_pairs={{0,8},{4,12},{8,0},{12,4},{16,24},{20,28},{24,16},{28,20},{1,9},{5... | collective-permute-start | bytes 2162696 | tf_op jit(solution)/shard_map/ppermute | solution.py:38
  690.1 37.1 %collective-permute-start.59 = (bf16[352,1024]{1,0:T(8,128)(2,1)}, bf16[352,1024]{1,0:T(8,128)(2,1)}, u32[]{:S(2)}, u32[]{:S(2)}) collective-permute-start(bf16[352,1024]{1,0:T(8,128)(2,1)} %add_convert_fusion.17), channel_id=1, source_target_pairs={{0,16},{4,20},{8,24},{12,28},{16,0},{20,4},{24,8},{28,12},{1,17},{... | collective-permute-start | bytes 2162696 | tf_op jit(solution)/shard_map/ppermute | solution.py:38
  693.1 37.5 %collective-permute-start.58 = (bf16[512,2048]{1,0:T(8,128)(2,1)}, bf16[512,2048]{1,0:T(8,128)(2,1)}, u32[]{:S(2)}, u32[]{:S(2)}) collective-permute-start(bf16[512,2048]{1,0:T(8,128)(2,1)} %broadcast_select_fusion.3), channel_id=1, source_target_pairs={{0,4},{4,0},{8,12},{12,8},{16,20},{20,16},{24,28},{28,24},{1,5},{5... | collective-permute-start | bytes 6291464 | tf_op jit(solution)/shard_map/ppermute | solution.py:38
  747.0 54.6 %collective-permute-start.86 = (bf16[176,2048]{1,0:T(8,128)(2,1)}, bf16[176,2048]{1,0:T(8,128)(2,1)}, u32[]{:S(2)}, u32[]{:S(2)}) collective-permute-start(bf16[176,2048]{1,0:T(8,128)(2,1)} %broadcast_select_fusion.13), channel_id=1, source_target_pairs={{0,4},{4,0},{8,12},{12,8},{16,20},{20,16},{24,28},{28,24},{1,5},{5... | collective-permute-start | bytes 2162696 | tf_op jit(solution)/shard_map/ppermute | solution.py:38
  747.5 66.0 %collective-permute-start.84 = (bf16[512,1408]{1,0:T(8,128)(2,1)}, bf16[512,1408]{1,0:T(8,128)(2,1)}, u32[]{:S(2)}, u32[]{:S(2)}) collective-permute-start(bf16[512,1408]{1,0:T(8,128)(2,1)} %add_convert_fusion.5), channel_id=1, source_target_pairs={{0,8},{4,12},{8,0},{12,4},{16,24},{20,28},{24,16},{28,20},{1,9},{5... | collective-permute-start | bytes 4325384 | tf_op jit(solution)/shard_map/ppermute | solution.py:38
  748.9 41.8 %collective-permute-start.67 = (bf16[512,384]{1,0:T(8,128)(2,1)}, bf16[512,384]{1,0:T(8,128)(2,1)}, u32[]{:S(2)}, u32[]{:S(2)}) collective-permute-start(bf16[512,384]{1,0:T(8,128)(2,1)} %convolution_convert_fusion.22), channel_id=1, source_target_pairs={{0,8},{4,12},{8,0},{12,4},{16,24},{20,28},{24,16},{28,20},{1,9},{5... | collective-permute-start | bytes 1179656 | tf_op jit(solution)/shard_map/ppermute | solution.py:38
  749.5 44.4 %collective-permute-start.72 = (bf16[512,384]{1,0:T(8,128)(2,1)}, bf16[512,384]{1,0:T(8,128)(2,1)}, u32[]{:S(2)}, u32[]{:S(2)}) collective-permute-start(bf16[512,384]{1,0:T(8,128)(2,1)} %convolution_convert_fusion.18), channel_id=1, source_target_pairs={{0,16},{4,20},{8,24},{12,28},{16,0},{20,4},{24,8},{28,12},{1,17},{... | collective-permute-start | bytes 1179656 | tf_op jit(solution)/shard_map/ppermute | solution.py:38
  757.7 53.0 %collective-permute-start.66 = (bf16[512,384]{1,0:T(8,128)(2,1)}, bf16[512,384]{1,0:T(8,128)(2,1)S(1)}, u32[]{:S(2)}, u32[]{:S(2)}) collective-permute-start(bf16[512,384]{1,0:T(8,128)(2,1)} %convolution_convert_fusion.24), channel_id=1, source_target_pairs={{0,8},{4,12},{8,0},{12,4},{16,24},{20,28},{24,16},{28,20},{1,9},{5... | collective-permute-start | bytes 1179656 | tf_op jit(solution)/shard_map/ppermute | solution.py:38
  (188 other events, 2607.0 us)
Sparse Core Ops, SparseCore 0:
  13.4 48.3 all-gather.4
  77.2 47.8 all-gather.6
  151.9 44.1 reduce-scatter.4
  203.8 47.0 all-gather.8
  470.1 47.0 reduce-scatter.6
  533.1 46.2 all-gather.10
  592.8 40.7 reduce-scatter.8
  751.1 41.6 reduce-scatter.10

commit v3 on v2

--- a/solution.py
+++ b/solution.py
@@ -107,13 +107,16 @@
     return [pieces[key] for key in sorted(pieces)]
 
 
-def place_quads(pieces, quad, axis):
-    size = pieces[0].shape[axis]
-    shape = list(pieces[0].shape)
-    shape[axis] = size * len(pieces)
-    whole = jnp.zeros(shape, pieces[0].dtype)
+def place_quads(pieces, quad, axis, whole=None, other=0):
+    size = pieces[0].shape[axis] if whole is None else whole.shape[axis] // (lax.axis_size("grp") // 2)
+    if whole is None:
+        shape = list(pieces[0].shape)
+        shape[axis] = size * len(pieces)
+        whole = jnp.zeros(shape, pieces[0].dtype)
     for key in sorted(pieces):
-        whole = lax.dynamic_update_slice_in_dim(whole, pieces[key], (quad ^ key) * size, axis)
+        start = [other, other]
+        start[axis] = (quad ^ key) * size
+        whole = lax.dynamic_update_slice(whole, pieces[key], start)
     return whole
 
 
@@ -416,7 +419,7 @@
             shaped(1, width, F32),
             shaped(1, 3 * columns, F32),
         ],
-        32,
+        60,
         4 * rows * width * cut,
         name="collect",
     )(grad_query, own, cosine, sine, x, *arrived, *wa, *wb)
@@ -582,10 +585,9 @@
         keep, other = split_core(values, core, 0)
         return (keep.astype(F32) + across(other, 1).astype(F32)).astype(BF16)
 
-    def row_grads(rows, grads):
+    def row_grads(rows, grads, keys=range(quads)):
         return {
-            k: dot_first(rows[:, k * block : (k + 1) * block], grads).astype(BF16)
-            for k in range(quads)
+            k: dot_first(rows[:, k * block : (k + 1) * block], grads).astype(BF16) for k in keys
         }
 
     def column_grads(acts, grads):
@@ -653,47 +655,46 @@
     qkv_b_rest = gather_rest(qkv_b_one, down_two)
     o_one, o_two = gather_quads({0: o_block}, down_one), gather_quads({0: o_block}, down_two)
     sd_one, sd_two = gather_quads({0: sd_block}, down_one), gather_quads({0: sd_block}, down_two)
-    (
-        group_one, qkv_a, qkv_b, o_one, o_two, sd_one, sd_two, gu_block, eg_block, eu_block,
-        eda_block, edb_block, cotangent,
-    ) = together(
-        group_one, qkv_a_one | qkv_a_two | qkv_a_rest, qkv_b_one | qkv_b_two | qkv_b_rest, o_one,
-        o_two, sd_one, sd_two, gu_block, eg_block, eu_block, eda_block, edb_block, cotangent,
-    )
-
-    rows_one = merge_core(group_one, across(group_one, 1), core, 0)
-    gu_two = gather_quads({0: gu_block}, up_two)
-    o_rest = gather_rest(o_one, down_two)
     chosen = (
         (expert_index[:, :, None] == experts[None, None, :]) & (token_live[:, None, None] > 0)
     ).any(axis=1)
-    chosen = chosen.astype(BF16)
-    cot_group = gathered(
-        jnp.concatenate([cotangent, jnp.pad(chosen, ((0, 0), (0, LANES - expert_count)))], axis=1)
+    cot_packed = jnp.concatenate(
+        [cotangent, jnp.pad(chosen.astype(BF16), ((0, 0), (0, LANES - expert_count)))], axis=1
     )
     chosen = chosen.astype(F32)
-    qkv_a, qkv_b = listed(qkv_a), listed(qkv_b)
     bias = jnp.concatenate(
         [split_core(b, core, 0)[0] for b in (query_bias, key_bias, value_bias)]
-    ).astype(F32)
+    ).astype(F32)[None, :]
     key_place = (quad - back) * pair_rows + jnp.arange((back + 1) * pair_rows, dtype=jnp.int32)
     query_place = key_place[back * pair_rows :]
     _, position = doc_layout(document_lengths, seq_len, query_place)
     low = jnp.maximum(query_place - position, query_place - WINDOW + 1)[:, None]
     high, key_place = query_place[:, None], key_place[None, :]
     cosine, sine = rope_tables(position)
-    query, key_value = project(rows_one, qkv_a, qkv_b, bias[None, :], cosine, sine, heads)
-
+    (
+        group_one, qkv_a, qkv_b, o_one, o_two, sd_one, sd_two, gu_block, eg_block, eu_block,
+        eda_block, edb_block, cot_packed, bias, cosine, sine, low, high,
+    ) = together(
+        group_one, qkv_a_one | qkv_a_two | qkv_a_rest, qkv_b_one | qkv_b_two | qkv_b_rest, o_one,
+        o_two, sd_one, sd_two, gu_block, eg_block, eu_block, eda_block, edb_block, cot_packed, bias,
+        cosine, sine, low, high,
+    )
+
+    rows_one = merge_core(group_one, across(group_one, 1), core, 0)
+    gu_two = gather_quads({0: gu_block}, up_two)
+    o_rest, sd_rest = gather_rest(o_one, down_two), gather_rest(sd_one, down_two)
+    cot_group = gathered(cot_packed)
+    qkv_a, qkv_b = listed(qkv_a), listed(qkv_b)
+    query, key_value = project(rows_one, qkv_a, qkv_b, bias, cosine, sine, heads)
+
+    query, key_value, o_rest, sd_rest = together(query, key_value, o_rest, sd_rest)
     before = [shifted(key_value, step) for step in range(back, 0, -1)]
-    query, before, gu_two, o_rest, sd_one, edb_block = together(
-        query, before, gu_two, o_rest, sd_one, edb_block
-    )
-    sd_rest = gather_rest(sd_one, down_two)
-    edb_one = gather_quads({0: edb_block}, down_one)
+    o_full = place_quads(o_one | o_two | o_rest, quad, 1)
+    query, before, gu_two, edb_block, o_full = together(query, before, gu_two, edb_block, o_full)
+    edb_one, edb_two = gather_quads({0: edb_block}, down_one), gather_quads({0: edb_block}, down_two)
     attended, log_total = attend(query, before, key_value, key_place, low, high)
-    o_full = place_quads(o_one | o_two | o_rest, quad, 1)
     branch = dot(attended, o_full).astype(BF16)
-    branch, cot_group, sd_rest, edb_one = together(branch, cot_group, sd_rest, edb_one)
+    branch, cot_group, edb_one, edb_two = together(branch, cot_group, edb_one, edb_two)
     branch = core_sum(branch)
     branch, gu_block, eu_block, eda_block, cot_group = together(
         branch, gu_block, eu_block, eda_block, cot_group
@@ -703,12 +704,18 @@
     gu_one = gather_quads({0: gu_block}, up_one)
     eda_one, eda_two = gather_quads({0: eda_block}, up_one), gather_quads({0: eda_block}, up_two)
     eu_one = gather_quads({0: eu_block}, down_one)
-    branch_sum, cot_other, gu_one, eda_one, eda_two, eu_one, eg_block, edb_block = together(
-        branch_sum, cot_other, gu_one, eda_one, eda_two, eu_one, eg_block, edb_block
+    sd_full = place_quads(sd_one | sd_two | sd_rest, quad, 1)
+    ed_full = jnp.zeros((eda_block.shape[0] * quads, width), BF16)
+    ed_full = place_quads(edb_one | edb_two, quad, 0, ed_full, ed_cut)
+    branch_sum, cot_other, gu_one, eda_one, eda_two, eu_one, eg_block, edb_one, sd_full, ed_full = (
+        together(
+            branch_sum, cot_other, gu_one, eda_one, eda_two, eu_one, eg_block, edb_one, sd_full,
+            ed_full,
+        )
     )
 
     eg_one = gather_quads({0: eg_block}, up_one)
-    edb_two, edb_rest = gather_quads({0: edb_block}, down_two), gather_rest(edb_one, down_two)
+    edb_rest = gather_rest(edb_one, down_two)
     gu_rest, eda_rest = gather_rest(gu_one, up_two), gather_rest(eda_one, up_two)
     mixed = hidden_in + branch_sum
     scale_two = norm_scale(mixed)
@@ -716,27 +723,18 @@
     normed_two = (unit_two * gain_two).astype(BF16)
     group_two = gathered(flip_columns(normed_two, quad))
     cot_rows = merge_core(cot_group, cot_other, core, 0)
-    sd_full = place_quads(sd_one | sd_two | sd_rest, quad, 1)
-    group_two, eg_one, edb_two, edb_rest, gu_rest, eda_rest = together(
-        group_two, eg_one, edb_two, edb_rest, gu_rest, eda_rest
-    )
+    ed_full = place_quads(eda_one | eda_two, quad, 0, ed_full)
+    (
+        group_two, eg_one, edb_rest, gu_rest, eda_rest, eu_block, eg_block, eu_one, cot_rows,
+        ed_full,
+    ) = together(
+        group_two, eg_one, edb_rest, gu_rest, eda_rest, eu_block, eg_block, eu_one, cot_rows,
+        ed_full,
+    )
+    eu_two, eg_two = gather_quads({0: eu_block}, down_two), gather_quads({0: eg_block}, up_two)
+    eu_rest, eg_rest = gather_rest(eu_one, down_two), gather_rest(eg_one, up_two)
     rows_two = merge_core(group_two, across(group_two, 1), core, 0)
-    (
-        rows_two, cot_rows, sd_full, eg_one, edb_two, edb_rest, gu_rest, eda_rest, eu_one, eu_block,
-        eg_block,
-    ) = together(
-        rows_two, cot_rows, sd_full, eg_one, edb_two, edb_rest, gu_rest, eda_rest, eu_one, eu_block,
-        eg_block,
-    )
-    eu_two, eg_two = gather_quads({0: eu_block}, down_two), gather_quads({0: eg_block}, up_two)
     gu_pieces = listed(gu_one | gu_two | gu_rest)
-    ed_full = jnp.concatenate(
-        [
-            place_quads(eda_one | eda_two | eda_rest, quad, 0),
-            place_quads(edb_one | edb_two | edb_rest, quad, 0),
-        ],
-        axis=1,
-    )
 
     def router(rows, weight):
         logits = dot(rows, weight)
@@ -753,18 +751,23 @@
     shared_active, grad_shared_out, part, grad_part, shared_dot, grad_gu = expert(
         rows_two, gu_pieces, sd_full, cot_rows, shared_scale_rows
     )
-    grad_gu, grad_part, eu_two, eg_two, eu_one, eg_one = together(
-        grad_gu, grad_part, eu_two, eg_two, eu_one, eg_one
-    )
-    eu_rest, eg_rest = gather_rest(eu_one, down_two), gather_rest(eg_one, up_two)
-    gu_grad = row_grads(rows_two, grad_gu)
+    grad_part, part, eu_two, eg_two, eu_rest, eg_rest, eda_rest, edb_rest, ed_full = together(
+        grad_part, part, eu_two, eg_two, eu_rest, eg_rest, eda_rest, edb_rest, ed_full
+    )
+    ed_full = place_quads(eda_rest, quad, 0, ed_full)
+    ed_full = place_quads(edb_rest, quad, 0, ed_full, ed_cut)
+    gu_cut = 2 * ffs_half * 3 // 4 // LANES * LANES
+    gua_grad = row_grads(rows_two, grad_gu[:, :gu_cut])
+    gub_grad = row_grads(rows_two, grad_gu[:, gu_cut:])
     sd_grad = column_grads(shared_active, grad_shared_out)
-    grad_part, eg_pieces, eu_pieces, ed_full, gu_grad, sd_grad = together(
-        grad_part, eg_one | eg_two | eg_rest, eu_one | eu_two | eu_rest, ed_full, gu_grad, sd_grad
-    )
-    up_keys = [key for key in gu_grad if key & up_one[0]]
-    down_keys = [key for key in gu_grad if key & down_one[0]]
-    gu_sent = send_quads(gu_grad, up_one[0], up_keys)
+    grad_part, eg_pieces, eu_pieces, ed_full, gua_grad, gub_grad, sd_grad = together(
+        grad_part, eg_one | eg_two | eg_rest, eu_one | eu_two | eu_rest, ed_full, gua_grad,
+        gub_grad, sd_grad,
+    )
+    up_keys = [key for key in gua_grad if key & up_one[0]]
+    down_keys = [key for key in gua_grad if key & down_one[0]]
+    gua_sent = send_quads(gua_grad, up_one[0], up_keys)
+    gub_sent = send_quads(gub_grad, down_one[0], down_keys)
     sd_sent = send_quads(sd_grad, down_one[0], down_keys)
 
     lanes = jnp.arange(LANES, dtype=jnp.int32)
@@ -777,24 +780,32 @@
         gate,
         (part, grad_part, shared_dot, lanes),
     )
-    packed, gu_grad, gu_sent, sd_grad, sd_sent = together(packed, gu_grad, gu_sent, sd_grad, sd_sent)
+    packed, forward_part, gua_sent, gub_sent, sd_sent, gua_grad, gub_grad, sd_grad = together(
+        packed, forward_part, gua_sent, gub_sent, sd_sent, gua_grad, gub_grad, sd_grad
+    )
     packed = core_sum(packed)
-    gu_grad = reduce_quads(add_quads(gu_grad, gu_sent, up_one[0]), up_one[1:])
+    (
+        packed, gua_grad, gub_grad, sd_grad, active, grad_result, grad_gate_pre, grad_up_pre,
+    ) = together(
+        packed, gua_grad, gub_grad, sd_grad, active, grad_result, grad_gate_pre, grad_up_pre,
+    )
+    spread = scattered(packed)
+    gua_grad = reduce_quads(add_quads(gua_grad, gua_sent, up_one[0]), up_one[1:])
+    gub_grad = reduce_quads(add_quads(gub_grad, gub_sent, down_one[0]), down_one[1:])
     sd_grad = reduce_quads(add_quads(sd_grad, sd_sent, down_one[0]), down_one[1:])
-    packed, gu_grad, sd_grad, active, grad_gate_pre, grad_up_pre = together(
-        packed, gu_grad, sd_grad, active, grad_gate_pre, grad_up_pre
-    )
-    spread = scattered(packed)
     ed_grad = take_quads(dot_first(active, grad_result).astype(BF16), quad, quads, 0)
     eda_grad = {k: v[:, :ed_cut] for k, v in ed_grad.items()}
     edb_grad = {k: v[:, ed_cut:] for k, v in ed_grad.items()}
-    gu_grad = reduce_quads(gu_grad, up_two)[0]
+    gua_grad = reduce_quads(gua_grad, up_two)[0]
+    gub_grad = reduce_quads(gub_grad, down_two)[0]
     sd_grad = reduce_quads(sd_grad, down_two)[0]
     eda_sent = send_quads(eda_grad, up_one[0], up_keys)
     edb_sent = send_quads(edb_grad, down_one[0], down_keys)
-    eg_grad = row_grads(rows_two, grad_gate_pre)
-    eu_grad = row_grads(rows_two, grad_up_pre)
-    spread, gu_grad, sd_grad, eg_grad, eu_grad = together(spread, gu_grad, sd_grad, eg_grad, eu_grad)
+    half = len(up_keys) // 2
+    keys = range(quads)
+    eg_grad = row_grads(rows_two, grad_gate_pre, up_keys)
+    eu_grad = row_grads(rows_two, grad_up_pre, down_keys[:half])
+    spread, eg_grad, eu_grad = together(spread, eg_grad, eu_grad)
 
     grad_normed_two = flip_columns(spread[:, :width], quad)
     side = spread[:, width : width + 4 * expert_count].reshape(rows_dev, 4, expert_count)
@@ -810,77 +821,34 @@
     grad_normed_two = grad_normed_two + dot_last(grad_router, router_all.astype(F32))
     grad_norm_part, ff_gain_grad = norm_backward(grad_normed_two, unit_two, scale_two, gain_two)
     grad_mixed = grad_out + grad_norm_part
-    branch_low, eda_grad, eda_sent, edb_grad, edb_sent, eg_grad, eu_grad, forward_part = together(
-        grad_mixed.astype(BF16), eda_grad, eda_sent, edb_grad, edb_sent, eg_grad, eu_grad,
-        forward_part,
+    (
+        branch_low, eda_grad, eda_sent, edb_grad, edb_sent, gua_grad, gub_grad, sd_grad,
+        grad_gate_pre, grad_up_pre, eg_grad, eu_grad, forward_part,
+    ) = together(
+        grad_mixed.astype(BF16), eda_grad, eda_sent, edb_grad, edb_sent, gua_grad, gub_grad, sd_grad,
+        grad_gate_pre, grad_up_pre, eg_grad, eu_grad, forward_part,
     )
     group_branch = gathered(branch_low)
-    half = len(up_keys) // 2
     eg_sent = send_quads(eg_grad, up_one[0], up_keys[:half])
     eu_sent = send_quads(eu_grad, down_one[0], down_keys[:half])
     eda_grad = reduce_quads(add_quads(eda_grad, eda_sent, up_one[0]), up_one[1:])
     edb_grad = reduce_quads(add_quads(edb_grad, edb_sent, down_one[0]), down_one[1:])
-    forward_sum = core_sum(forward_part)
-    group_branch, forward_sum, eg_grad, eg_sent, eu_grad, eu_sent, eda_grad, edb_grad = together(
-        group_branch, forward_sum, eg_grad, eg_sent, eu_grad, eu_sent, eda_grad, edb_grad
+    eda_grad = reduce_quads(eda_grad, up_two)[0]
+    edb_grad = reduce_quads(edb_grad, down_two)[0]
+    eg_grad |= row_grads(rows_two, grad_gate_pre, [k for k in keys if k not in eg_grad])
+    eu_grad |= row_grads(rows_two, grad_up_pre, [k for k in keys if k not in eu_grad])
+    group_branch, forward_part, eg_grad, eg_sent, eu_grad, eu_sent, eda_grad, edb_grad = together(
+        group_branch, forward_part, eg_grad, eg_sent, eu_grad, eu_sent, eda_grad, edb_grad
     )
     grad_branch = merge_core(group_branch, across(group_branch, 1), core, 0)
     eg_sent |= send_quads(eg_grad, up_one[0], up_keys[half:])
     eu_sent |= send_quads(eu_grad, down_one[0], down_keys[half:])
 
-    layer_sum = scattered(forward_sum)
+    layer_sum = scattered(core_sum(forward_part))
     grad_attended = dot_last(grad_branch, o_full).astype(BF16)
     grad_query, grad_own, *grad_before = attend_back(
         query, grad_attended, log_total, before, key_value, key_place, low, high, cosine, sine
     )
-    grad_query, grad_before, eg_grad, eg_sent, eu_grad, eu_sent, eda_grad, edb_grad = together(
-        grad_query, grad_before, eg_grad, eg_sent, eu_grad, eu_sent, eda_grad, edb_grad
-    )
-    arrived = [shifted(sent, step - back) for step, sent in enumerate(grad_before)]
-    eg_grad = reduce_quads(add_quads(eg_grad, eg_sent, up_one[0]), up_one[1:])
-    eu_grad = reduce_quads(add_quads(eu_grad, eu_sent, down_one[0]), down_one[1:])
-    eg_grad = reduce_quads(eg_grad, up_two)[0]
-    o_grad = column_grads(attended, grad_branch)
-    arrived, o_grad, layer_sum, eg_grad, eu_grad, eda_grad, edb_grad = together(
-        arrived, o_grad, layer_sum, eg_grad, eu_grad, eda_grad, edb_grad
-    )
-    layer_out = (mixed + layer_sum).astype(BF16)
-    eda_grad = reduce_quads(eda_grad, up_two)[0]
-    edb_grad = reduce_quads(edb_grad, down_two)[0]
-    grad_lin, partial, att_gain_part, bias_part = collect(
-        grad_query, grad_own, cosine, sine, rows_one, arrived, qkv_a, qkv_b
-    )
-    grad_lin_a, grad_lin_b = grad_lin[:, :qkv_cut], grad_lin[:, qkv_cut:]
-    partial_sum = core_sum(partial)
-
-    att_gain_part = flip_columns(att_gain_part[0], quad) / gain_one
-    late = jnp.concatenate(
-        [bias_part[0], att_gain_part, ff_gain_grad, router_grad.T.reshape(-1)]
-    )
-    qkv_a_grad = row_grads(rows_one, grad_lin_a)
-    qkv_b_grad = row_grads(rows_one, grad_lin_b)
-    partial_sum, qkv_a_grad, qkv_b_grad, late, eda_grad, edb_grad, eu_grad = together(
-        partial_sum, qkv_a_grad, qkv_b_grad, late, eda_grad, edb_grad, eu_grad
-    )
-    grad_normed_one = scattered(partial_sum)
-    eu_grad = reduce_quads(eu_grad, down_two)[0]
-    o_grad = reduce_quads(o_grad, down_order)[0]
-    qkv_a_grad = reduce_quads(qkv_a_grad, up_order)[0]
-    qkv_b_grad = reduce_quads(qkv_b_grad, down_order)[0]
-    qkv_grad = jnp.concatenate([qkv_a_grad, qkv_b_grad], axis=1)
-    late = sum_everywhere(late, quad_masks, [])
-    bias_part = late[: 3 * head_width]
-    bias_mine = merge_core(
-        bias_part.reshape(3, head_width), across(bias_part, 1).reshape(3, head_width), core, 1
-    )
-    late = sum_everywhere(late[3 * head_width :], [1], ep_masks)
-    att_gain_grad, ff_gain_grad = late[:width], late[width : 2 * width]
-    router_grad = late[2 * width :].reshape(expert_count + 1, width)
-    grad_norm_one, _ = norm_backward(
-        flip_columns(grad_normed_one, quad), unit_one, scale_one, gain_one
-    )
-    input_grad = grad_mixed + grad_norm_one
-
     def back_to_cores(summed, cut_axis, join_axis):
         keep, other = split_core(summed, core, cut_axis)
         return merge_core(keep, across(other, 1), core, join_axis).astype(F32)
@@ -892,7 +860,77 @@
             [jnp.where(core == 0, keep, arrived), jnp.where(core == 0, arrived, keep)]
         ).astype(F32)
 
-    ed_grad = jnp.concatenate([eda_grad, edb_grad], axis=1)
+    (
+        grad_query, grad_before, grad_branch, eg_grad, eu_grad, gua_grad, gub_grad, sd_grad,
+        eda_grad, edb_grad,
+    ) = together(
+        grad_query, grad_before, grad_branch, eg_grad, eu_grad, gua_grad, gub_grad, sd_grad,
+        eda_grad, edb_grad,
+    )
+    arrived = [shifted(sent, step - back) for step, sent in enumerate(grad_before)]
+    eg_grad = reduce_quads(add_quads(eg_grad, eg_sent, up_one[0]), up_one[1:])
+    eu_grad = reduce_quads(add_quads(eu_grad, eu_sent, down_one[0]), down_one[1:])
+    eg_rest = send_quads(eg_grad, up_two[0], [key for key in eg_grad if key & up_two[0]])
+    gu_grad = jnp.concatenate([gua_grad, gub_grad], axis=1)
+    sg_grad = back_to_cores(gu_grad[:, :ffs_half], 0, 1)
+    su_grad = back_to_cores(gu_grad[:, ffs_half:], 0, 1)
+    sd_grad = back_to_cores(sd_grad, 1, 0)
+    o_grad = column_grads(attended, grad_branch)
+    o_sent = send_quads(o_grad, down_order[0], down_keys)
+    arrived, eg_grad, eu_grad, o_grad, sg_grad, su_grad, sd_grad, eda_grad, edb_grad = together(
+        arrived, eg_grad, eu_grad, o_grad, sg_grad, su_grad, sd_grad, eda_grad, edb_grad
+    )
+    eu_keys = [key for key in eu_grad if key & down_two[0]]
+    eu_cut = eu_block.shape[0] // 2
+    eu_rest = send_quads({key: eu_grad[key][:eu_cut] for key in eu_keys}, down_two[0], eu_keys)
+    grad_lin, partial, att_gain_part, bias_part = collect(
+        grad_query, grad_own, cosine, sine, rows_one, arrived, qkv_a, qkv_b
+    )
+    partial, eg_rest, eu_rest, eu_grad, o_grad, o_sent = together(
+        partial, eg_rest, eu_rest, eu_grad, o_grad, o_sent
+    )
+    partial_sum = core_sum(partial)
+
+    (
+        partial_sum, grad_lin, att_gain_part, bias_part, eg_grad, eg_rest, eu_grad, o_grad, o_sent,
+    ) = together(
+        partial_sum, grad_lin, att_gain_part, bias_part, eg_grad, eg_rest, eu_grad, o_grad, o_sent,
+    )
+    grad_normed_one = scattered(partial_sum)
+    eu_last = send_quads({key: eu_grad[key][eu_cut:] for key in eu_keys}, down_two[0], eu_keys)
+    grad_lin_a, grad_lin_b = grad_lin[:, :qkv_cut], grad_lin[:, qkv_cut:]
+    qkv_a_grad = reduce_quads(row_grads(rows_one, grad_lin_a), up_order)[0]
+    qkv_b_grad = reduce_quads(row_grads(rows_one, grad_lin_b), down_order)[0]
+    o_grad = add_quads(o_grad, o_sent, down_order[0])
+    o_grad = reduce_quads(o_grad, down_order[1:])[0]
+    att_gain_part = flip_columns(att_gain_part[0], quad) / gain_one
+    late = jnp.concatenate([bias_part[0], att_gain_part, ff_gain_grad, router_grad.T.reshape(-1)])
+    late = sum_everywhere(late, quad_masks, [])
+    bias_part = late[: 3 * head_width]
+    late = sum_everywhere(late[3 * head_width :], [1], ep_masks)
+    (
+        grad_normed_one, o_grad, qkv_a_grad, qkv_b_grad, bias_part, late, eu_last, eg_grad, eg_rest,
+        eda_grad, edb_grad, layer_sum,
+    ) = together(
+        grad_normed_one, o_grad, qkv_a_grad, qkv_b_grad, bias_part, late, eu_last, eg_grad, eg_rest,
+        eda_grad, edb_grad, layer_sum,
+    )
+    eg_grad = reduce_quads(add_quads(eg_grad, eg_rest, up_two[0]), up_two[1:])[0]
+    eg_grad = back_to_experts(eg_grad)
+    ed_grad = back_to_experts(jnp.concatenate([eda_grad, edb_grad], axis=1))
+    layer_out = (mixed + layer_sum).astype(BF16)
+    bias_mine = merge_core(
+        bias_part.reshape(3, head_width), across(bias_part, 1).reshape(3, head_width), core, 1
+    )
+    eu_rest = {key: jnp.concatenate([eu_rest[key], eu_last[key]], axis=0) for key in eu_rest}
+    eu_grad = reduce_quads(add_quads(eu_grad, eu_rest, down_two[0]), down_two[1:])[0]
+    qkv_grad = jnp.concatenate([qkv_a_grad, qkv_b_grad], axis=1)
+    att_gain_grad, ff_gain_grad = late[:width], late[width : 2 * width]
+    router_grad = late[2 * width :].reshape(expert_count + 1, width)
+    grad_norm_one, _ = norm_backward(
+        flip_columns(grad_normed_one, quad), unit_one, scale_one, gain_one
+    )
+    input_grad = grad_mixed + grad_norm_one
     q_grad, k_grad, v_grad = [
         back_to_cores(qkv_grad[:, part * head_width : (part + 1) * head_width], 0, 1)
         for part in range(3)
@@ -911,12 +949,12 @@
         ff_gain_grad,
         router_grad[:expert_count].T,
         router_grad[expert_count],
-        back_to_cores(gu_grad[:, :ffs_half], 0, 1),
-        back_to_cores(gu_grad[:, ffs_half:], 0, 1),
-        back_to_cores(sd_grad, 1, 0),
-        back_to_experts(eg_grad),
+        sg_grad,
+        su_grad,
+        sd_grad,
+        eg_grad,
         back_to_experts(eu_grad),
-        back_to_experts(ed_grad),
+        ed_grad,
     )
 
 

time: 841 us -> 749 us (0.89)
  waiting for transfers between devices: 345 us -> 228 us
    ppermute x83 -> x87, waiting for transfers between devices: 288 us -> 154 us  [across(): return lax.ppermute(block, 'grp', [(i, i ^ mask) for i in range(count)])]
    ppermute x2, waiting for transfers between devices: 0.01 us -> 28.6 us  [shifted(): return lax.ppermute(values, 'grp', route)]
    all_gather x4, waiting for transfers between devices: 9.1 us -> 0.04 us  [gathered(): return lax.all_gather(values, 'ep', axis=0, tiled=True)]
    dynamic_update_slice x16 -> x18, local copies, waits for them, and re-layouts: 19.7 us -> 28.2 us  [place_quads(): whole = lax.dynamic_update_slice(whole, pieces[key], start)]
    convert_element_type x23 -> x18, other arithmetic: 44.5 us -> 36.8 us  [add_quads(): (piece.astype(F32) + arrived[key | bit].astype(F32)).astype(BF16)]
    select_n x13 -> x16, other arithmetic: 14.2 us -> 20.2 us  [split_core(): jnp.where(core == 0, second, first)]
    dot_general x30 -> x34, matrix products: 75.2 us -> 80.5 us  [dot_first(): lax.dot_general(left, right, (((0,), (0,)), ((), ())), preferred_element_...]
    unnamed x285 -> x325, local copies, waits for them, and re-layouts: 27.4 us -> 22.2 us
  transfers between devices with their start and end apart: 95 -> 99, of which waited for: 36 -> 32; matrix products, arithmetic and copies ran while one was open for 25% -> 33% of each run, Pallas kernels for 13% -> 16%
where the time goes in v3:
time: 749 us; the launch traced here: 740 us
  waiting for transfers between devices  228 us (30%)
  other arithmetic  146 us (19%)
  Pallas kernels  117 us (16%)
  matrix products  89.8 us (12%)
  starting transfers between devices  76.8 us (10%)
  local copies, waits for them, and re-layouts  65 us (9%)
  between operations  16.6 us (2%)
    ppermute x87, waiting for transfers between devices, across(): return lax.ppermute(block, 'grp', [(i, i ^ mask) for i in range(count)])  154 us
    pallas_call x6, Pallas kernels, run(): pl.pallas_call(kernel, grid=grid, in_specs=ins, out_specs=outs, out_shape...  117 us
    dot_general x34, matrix products, dot_first(): lax.dot_general(left, right, (((0,), (0,)), ((), ())), preferred_element_...  80.5 us
    ppermute x87, starting transfers between devices, across(): return lax.ppermute(block, 'grp', [(i, i ^ mask) for i in range(count)])  69.4 us
    convert_element_type x18, other arithmetic, add_quads(): (piece.astype(F32) + arrived[key | bit].astype(F32)).astype(BF16)  36.8 us
    reduce_scatter x4, waiting for transfers between devices, scattered(): lax.psum_scatter(values, 'ep', scatter_dimension=0, tiled=True).astype(F32)  34.2 us
    ppermute x2, waiting for transfers between devices, shifted(): return lax.ppermute(values, 'grp', route)  28.6 us
    dynamic_update_slice x18, local copies, waits for them, and re-layouts, place_quads(): whole = lax.dynamic_update_slice(whole, pieces[key], start)  28.2 us
  transfers between devices with their start and end apart: 99, of which 32 were waited for; matrix products, arithmetic and copies ran while one was open for 33% of the time, Pallas kernels for 16%

profile of v3, /device:TPU:0, one launch (start us, length us, event | category | flops | bytes accessed | tf_op | source)
XLA Modules:
  0.0 740.2 jit_solution(9495035740827199722)
XLA Ops:
  12.7 3.1 fusion.65
  33.5 5.6 collective-permute-done.3.rest_6_.rest_7_
  46.0 19.0 %collective-permute-done.13 = bf16[256,512]{1,0:T(8,128)(2,1)} collective-permute-done((bf16[256,512]{1,0:T(8,128)(2,1)}, bf16[256,512]{1,0:T(8,128)(2,1)}, u32[]{:S(2)}, u32[]{:S(2)}) %collective-permute-start.13) | collective-permute-done | bytes 262176 | tf_op jit(solution)/shard_map/ppermute | solution.py:38
  66.8 6.2 collective-permute-done.14
  82.4 7.0 project.1
  89.3 8.3 %collective-permute-done.18 = bf16[256,512]{1,0:T(8,128)(2,1)S(1)} collective-permute-done((bf16[256,512]{1,0:T(8,128)(2,1)}, bf16[256,512]{1,0:T(8,128)(2,1)S(1)}, u32[]{:S(2)}, u32[]{:S(2)}) %collective-permute-start.18) | collective-permute-done | bytes 262176 | tf_op jit(solution)/shard_map/ppermute | solution.py:38
  103.5 5.5 collective-permute-done.21.rest_2_
  109.0 13.5 %collective-permute-done.20.rest_0_ = bf16[1024,512]{1,0:T(8,128)(2,1)S(1)} collective-permute-done((bf16[1024,512]{1,0:T(8,128)(2,1)S(1)}, bf16[1024,512]{1,0:T(8,128)(2,1)S(1)}, u32[]{:S(2)}, u32[]{:S(2)}) %collective-permute-start.20) | collective-permute-done | bytes 1048608 | tf_op jit(solution)/shard_map/ppermute | solution.py:576
  128.4 6.7 attend.1
  137.0 3.2 convolution_convert_fusion.1
  143.9 4.1 collective-permute-done.24
  164.0 3.2 broadcast_in_dim.26
  173.3 22.3 %reduce-scatter.5.cloned.1.call-done = bf16[128,2048]{1,0:T(8,128)(2,1)} async-done(((bf16[512,2048]{1,0:T(8,128)(2,1)}), bf16[128,2048]{1,0:T(8,128)(2,1)}) %reduce-scatter.5.cloned.1.call-update) | async-done | bytes 524304 | tf_op jit(solution)/shard_map/reduce_scatter | solution.py:582
  196.8 3.7 collective-permute-done.27
  211.6 3.0 broadcast_select_fusion.2
  219.9 34.2 %collective-permute-done.31 = bf16[352,1024]{1,0:T(8,128)(2,1)} collective-permute-done((bf16[352,1024]{1,0:T(8,128)(2,1)}, bf16[352,1024]{1,0:T(8,128)(2,1)}, u32[]{:S(2)}, u32[]{:S(2)}) %collective-permute-start.31) | collective-permute-done | bytes 720928 | tf_op jit(solution)/shard_map/ppermute | solution.py:38
  262.5 3.0 pad_maximum_fusion.1.x_ref
  268.1 27.3 %shared.1 = (bf16[1024,704]{1,0:T(8,128)(2,1)}, bf16[1024,2048]{1,0:T(8,128)(2,1)}, bf16[1024,2048]{1,0:T(8,128)(2,1)}, bf16[1024,2048]{1,0:T(8,128)(2,1)}, f32[...) custom-call(bf16[1024,2048]{1,0:T(8,128)(2,1)} %pad_maximum_fusion.1.x_ref, ...), custom_call_target="tpu_custom_call" | custom-call | flops 17716740096 | bytes 34217984 | tf_op jit(solution)/shard_map/shared/pallas_call | solution.py:188
  295.3 3.7 convolution_convert_fusion.14
  299.0 3.4 convolution_convert_fusion.15
  339.4 3.8 collective-permute-done.41
  344.6 51.5 %expert.1 = (bf16[1024,1408]{1,0:T(8,128)(2,1)}, bf16[1024,2048]{1,0:T(8,128)(2,1)}, bf16[1024,2048]{1,0:T(8,128)(2,1)}, bf16[1024,2176]{1,0:T(8,128)(2,1)}, bf1...) custom-call(bf16[1024,2048]{1,0:T(8,128)(2,1)} %pad_maximum_fusion.1.x_ref, ...), custom_call_target="tpu_custom_call" | custom-call | flops 35433480192 | bytes 55845376 | tf_op jit(solution)/shard_map/expert/pallas_call | solution.py:188
  396.2 4.0 broadcast_select_fusion
  404.8 5.1 add_convert_fusion
  419.2 5.2 convolution_convert_fusion.8
  424.4 3.0 convolution_convert_fusion.9
  427.3 8.3 %convolution_convert_fusion = bf16[1408,2048]{1,0:T(8,128)(2,1)S(1)} fusion(bf16[1024,1408]{1,0:T(8,128)(2,1)} %get-tuple-element.445, bf16[1024,2048]{1,0:T(8,128)(2,1)S(1)} %copy-done.159), kind=kOutput, calls=%fused_computation | convolution fusion | flops 5908463616 | bytes 12845056 | tf_op jit(solution)/shard_map/dot_general | solution.py:33
  435.6 3.0 fusion.119
  450.1 3.1 add_convert_fusion.10
  453.3 11.8 %reduce-scatter.7.cloned.1.call-done = bf16[128,2176]{1,0:T(8,128)(2,1)} async-done(((bf16[512,2176]{1,0:T(8,128)(2,1)}), bf16[128,2176]{1,0:T(8,128)(2,1)}) %reduce-scatter.7.cloned.1.call-update) | async-done | bytes 557072 | tf_op jit(solution)/shard_map/reduce_scatter | solution.py:582
  484.0 4.9 convolution_convert_fusion.2
  491.9 3.0 convolution_convert_fusion.4
  494.9 3.0 convolution_convert_fusion.5
  505.6 21.5 %collective-permute-done.53 = bf16[512,1408]{1,0:T(8,128)(2,1)} collective-permute-done((bf16[512,1408]{1,0:T(8,128)(2,1)S(1)}, bf16[512,1408]{1,0:T(8,128)(2,1)}, u32[]{:S(2)}, u32[]{:S(2)}) %collective-permute-start.53) | collective-permute-done | bytes 1441824 | tf_op jit(solution)/shard_map/ppermute | solution.py:38
  536.6 14.1 %attend_back.1 = (bf16[1024,256]{1,0:T(8,128)(2,1)S(1)}, f32[1024,512]{1,0:T(8,128)}, bf16[1024,512]{1,0:T(8,128)(2,1)S(1)}) custom-call(bf16[1024,256]{1,0:T(8,128)(2,1)S(1)} %copy-done.19, bf16[1024,256]{1,0:T(8,128)(2,1)S(1)} %convolution_convert_fusion.18.grad_ref, f32[1024,256]{1,0:T(8,128)S(1)} %copy-done.16, bf16[1024,512]{1,0:T(8,128)(2,1)} %copy-done.14, ...), custom_call_target="tpu_custom_call" | custom-call | flops 3355443200 | bytes 8929280 | tf_op jit(solution)/shard_map/attend_back/pallas_call | solution.py:188
  555.9 4.2 add_convert_fusion.1
  564.3 3.5 add_convert_fusion.7
  569.2 3.0 add_convert_fusion.9
  584.6 15.1 %collective-permute-done.58.rest_0_ = bf16[1024,512]{1,0:T(8,128)(2,1)S(1)} collective-permute-done((bf16[1024,512]{1,0:T(8,128)(2,1)S(1)}, bf16[1024,512]{1,0:T(8,128)(2,1)S(1)}, u32[]{:S(2)}, u32[]{:S(2)}) %collective-permute-start.58) | collective-permute-done | bytes 1048608 | tf_op jit(solution)/shard_map/ppermute | solution.py:576
  602.7 10.7 %collect.1 = (bf16[1024,768]{1,0:T(8,128)(2,1)}, bf16[1024,2048]{1,0:T(8,128)(2,1)}, f32[1,2048]{1,0:T(1,128)}, f32[1,768]{1,0:T(1,128)}) custom-call(bf16[1024,256]{1,0:T(8,128)(2,1)} %copy-done.7, f32[1024,512]{1,0:T(8,128)} %get-tuple-element.494.own_ref, f32[1024,128]{1,0:T(8,128)} %copy-done.2, f32[1024,128]{1,0:T(8,128)} %copy-done.1, ...), custom_call_target="tpu_custom_call" | custom-call | flops 3221225472 | bytes 17837056 | tf_op jit(solution)/shard_map/collect/pallas_call | solution.py:188
  613.3 3.4 collective-permute-done.67
  616.7 5.1 collective-permute-done.66
  626.2 4.0 collective-permute-done.68
  630.2 5.6 add_convert_fusion.2
  652.6 8.6 %collective-permute-done.79 = f32[22528]{0:T(1024)S(1)} collective-permute-done((f32[22528]{0:T(1024)S(1)}, f32[22528]{0:T(1024)S(1)}, u32[]{:S(2)}, u32[]{:S(2)}) %collective-permute-start.79) | collective-permute-done | bytes 90144 | tf_op jit(solution)/shard_map/ppermute | solution.py:94
  662.4 6.0 collective-permute-done.74
  685.7 3.2 fusion.15
  695.1 4.4 collective-permute-done.81
  (732 shorter events, 315.7 us)
Async XLA Ops:
  7.2 65.9 %all-gather.5.cloned.1.call-start = ((), (), s32[]{:S(2)}) async-start(), calls=%async_computation.4 | async-start | bytes 2621440 | tf_op jit(solution)/shard_map/all_gather | solution.py:579
  12.3 127.9 %all-gather.7.cloned.1.call-start = ((), (), s32[]{:S(2)}) async-start(), calls=%async_computation.5 | async-start | bytes 2785280 | tf_op jit(solution)/shard_map/all_gather | solution.py:579
  40.0 33.0 %collective-permute-start.15 = (bf16[704,512]{1,0:T(8,128)(2,1)}, bf16[704,512]{1,0:T(8,128)(2,1)}, u32[]{:S(2)}, u32[]{:S(2)}) collective-permute-start(bf16[704,512]{1,0:T(8,128)(2,1)} %pad_maximum_fusion.10), channel_id=1, source_target_pairs={{0,16},{4,20},{8,24},{12,28},{16,0},{20,4},{24,8},{28,12},{1,17},{... | collective-permute-start | bytes 2162696 | tf_op jit(solution)/shard_map/ppermute | solution.py:38
  41.6 31.5 %collective-permute-start.16 = (bf16[704,512]{1,0:T(8,128)(2,1)}, bf16[704,512]{1,0:T(8,128)(2,1)}, u32[]{:S(2)}, u32[]{:S(2)}) collective-permute-start(bf16[704,512]{1,0:T(8,128)(2,1)} %pad_maximum_fusion.10), channel_id=1, source_target_pairs={{0,8},{4,12},{8,0},{12,4},{16,24},{20,28},{24,16},{28,20},{1,9},{5... | collective-permute-start | bytes 2162696 | tf_op jit(solution)/shard_map/ppermute | solution.py:38
  43.3 29.7 %collective-permute-start.11 = (bf16[512,384]{1,0:T(8,128)(2,1)S(1)}, bf16[512,384]{1,0:T(8,128)(2,1)}, u32[]{:S(2)}, u32[]{:S(2)}) collective-permute-start(bf16[512,384]{1,0:T(8,128)(2,1)S(1)} %collective-permute-done.1.rest_1_.rest_2_), channel_id=1, source_target_pairs={{0,16},{4,20},{8,24},{12,28},{16,0},{20,4},{24,8},{28,12},{1,17},{... | collective-permute-start | bytes 1179656 | tf_op jit(solution)/shard_map/ppermute | solution.py:38
  44.5 28.5 %collective-permute-start.12 = (bf16[512,384]{1,0:T(8,128)(2,1)S(1)}, bf16[512,384]{1,0:T(8,128)(2,1)}, u32[]{:S(2)}, u32[]{:S(2)}) collective-permute-start(bf16[512,384]{1,0:T(8,128)(2,1)S(1)} %collective-permute-done.3.rest_6_.rest_7_), channel_id=1, source_target_pairs={{0,8},{4,12},{8,0},{12,4},{16,24},{20,28},{24,16},{28,20},{1,9},{5... | collective-permute-start | bytes 1179656 | tf_op jit(solution)/shard_map/ppermute | solution.py:38
  73.2 122.4 %reduce-scatter.5.cloned.1.call-start = ((), (), s32[]{:S(2)}) async-start(), calls=%async_computation.6 | async-start | bytes 2621440 | tf_op jit(solution)/shard_map/reduce_scatter | solution.py:582
  73.2 24.4 %collective-permute-start.19 = (bf16[704,512]{1,0:T(8,128)(2,1)}, bf16[704,512]{1,0:T(8,128)(2,1)S(1)}, u32[]{:S(2)}, u32[]{:S(2)}) collective-permute-start(bf16[704,512]{1,0:T(8,128)(2,1)} %collective-permute-done.15), channel_id=1, source_target_pairs={{0,8},{4,12},{8,0},{12,4},{16,24},{20,28},{24,16},{28,20},{1,9},{5... | collective-permute-start | bytes 2162696 | tf_op jit(solution)/shard_map/ppermute | solution.py:38
  75.3 33.6 %collective-permute-start.21 = (bf16[512,1408]{1,0:T(8,128)(2,1)}, bf16[512,1408]{1,0:T(8,128)(2,1)S(1)}, u32[]{:S(2)}, u32[]{:S(2)}) collective-permute-start(bf16[512,1408]{1,0:T(8,128)(2,1)} %pad_maximum_fusion.4.rest_0_), channel_id=1, source_target_pairs={{0,16},{4,20},{8,24},{12,28},{16,0},{20,4},{24,8},{28,12},{1,17},{... | collective-permute-start | bytes 4325384 | tf_op jit(solution)/shard_map/ppermute | solution.py:38
  97.7 24.8 %collective-permute-start.20 = (bf16[1024,512]{1,0:T(8,128)(2,1)S(1)}, bf16[1024,512]{1,0:T(8,128)(2,1)S(1)}, u32[]{:S(2)}, u32[]{:S(2)}) collective-permute-start(bf16[1024,512]{1,0:T(8,128)(2,1)S(1)} %get-tuple-element.327.rest_1_), channel_id=1, source_target_pairs={{0,8},{4,12},{16,24},{20,28},{1,9},{5,13},{17,25},{21,29},{2,10},{... | collective-permute-start | bytes 3145736 | tf_op jit(solution)/shard_map/ppermute | solution.py:576
  150.7 104.5 %all-gather.9.cloned.1.call-start = ((), (), s32[]{:S(2)}) async-start(), calls=%async_computation.7 | async-start | bytes 2621440 | tf_op jit(solution)/shard_map/all_gather | solution.py:579
  150.7 50.9 %collective-permute-start.25 = (bf16[512,2176]{1,0:T(8,128)(2,1)}, bf16[512,2176]{1,0:T(8,128)(2,1)}, u32[]{:S(2)}, u32[]{:S(2)}) collective-permute-start(bf16[512,2176]{1,0:T(8,128)(2,1)} %all-gather.7.cloned.1.call-done), channel_id=1, source_target_pairs={{0,4},{4,0},{8,12},{12,8},{16,20},{20,16},{24,28},{28,24},{1,5},{5... | collective-permute-start | bytes 6684680 | tf_op jit(solution)/shard_map/ppermute | solution.py:38
  150.9 50.7 %collective-permute-start.26 = (bf16[512,1408]{1,0:T(8,128)(2,1)}, bf16[512,1408]{1,0:T(8,128)(2,1)}, u32[]{:S(2)}, u32[]{:S(2)}) collective-permute-start(bf16[512,1408]{1,0:T(8,128)(2,1)} %pad_maximum_fusion.4.rest_0_), channel_id=1, source_target_pairs={{0,8},{4,12},{8,0},{12,4},{16,24},{20,28},{24,16},{28,20},{1,9},{5... | collective-permute-start | bytes 4325384 | tf_op jit(solution)/shard_map/ppermute | solution.py:38
  152.3 49.3 %collective-permute-start.29 = (bf16[512,1408]{1,0:T(8,128)(2,1)}, bf16[512,1408]{1,0:T(8,128)(2,1)}, u32[]{:S(2)}, u32[]{:S(2)}) collective-permute-start(bf16[512,1408]{1,0:T(8,128)(2,1)} %get-tuple-element.409.rest_4_), channel_id=1, source_target_pairs={{0,16},{4,20},{8,24},{12,28},{16,0},{20,4},{24,8},{28,12},{1,17},{... | collective-permute-start | bytes 4325384 | tf_op jit(solution)/shard_map/ppermute | solution.py:38
  157.6 42.8 %collective-permute-start.27 = (bf16[352,1024]{1,0:T(8,128)(2,1)S(1)}, bf16[352,1024]{1,0:T(8,128)(2,1)S(1)}, u32[]{:S(2)}, u32[]{:S(2)}) collective-permute-start(bf16[352,1024]{1,0:T(8,128)(2,1)S(1)} %copy-done.70), channel_id=1, source_target_pairs={{0,8},{4,12},{8,0},{12,4},{16,24},{20,28},{24,16},{28,20},{1,9},{5... | collective-permute-start | bytes 2162696 | tf_op jit(solution)/shard_map/ppermute | solution.py:38
  158.3 43.3 %collective-permute-start.28 = (bf16[352,1024]{1,0:T(8,128)(2,1)S(1)}, bf16[352,1024]{1,0:T(8,128)(2,1)}, u32[]{:S(2)}, u32[]{:S(2)}) collective-permute-start(bf16[352,1024]{1,0:T(8,128)(2,1)S(1)} %copy-done.70), channel_id=1, source_target_pairs={{0,16},{4,20},{8,24},{12,28},{16,0},{20,4},{24,8},{28,12},{1,17},{... | collective-permute-start | bytes 2162696 | tf_op jit(solution)/shard_map/ppermute | solution.py:38
  205.0 260.1 %reduce-scatter.7.cloned.1.call-start = ((), (), s32[]{:S(2)}) async-start(), calls=%async_computation.8 | async-start | bytes 2785280 | tf_op jit(solution)/shard_map/reduce_scatter | solution.py:582
  205.4 49.7 %collective-permute-start.30 = (bf16[512,1408]{1,0:T(8,128)(2,1)}, bf16[512,1408]{1,0:T(8,128)(2,1)}, u32[]{:S(2)}, u32[]{:S(2)}) collective-permute-start(bf16[512,1408]{1,0:T(8,128)(2,1)} %get-tuple-element.405.rest_0_), channel_id=1, source_target_pairs={{0,8},{4,12},{8,0},{12,4},{16,24},{20,28},{24,16},{28,20},{1,9},{5... | collective-permute-start | bytes 4325384 | tf_op jit(solution)/shard_map/ppermute | solution.py:38
  206.5 48.6 %collective-permute-start.32 = (bf16[512,1408]{1,0:T(8,128)(2,1)}, bf16[512,1408]{1,0:T(8,128)(2,1)}, u32[]{:S(2)}, u32[]{:S(2)}) collective-permute-start(bf16[512,1408]{1,0:T(8,128)(2,1)} %collective-permute-done.26.rest_1_), channel_id=1, source_target_pairs={{0,16},{4,20},{8,24},{12,28},{16,0},{20,4},{24,8},{28,12},{1,17},{... | collective-permute-start | bytes 4325384 | tf_op jit(solution)/shard_map/ppermute | solution.py:38
  207.8 46.3 %collective-permute-start.31 = (bf16[352,1024]{1,0:T(8,128)(2,1)}, bf16[352,1024]{1,0:T(8,128)(2,1)}, u32[]{:S(2)}, u32[]{:S(2)}) collective-permute-start(bf16[352,1024]{1,0:T(8,128)(2,1)} %collective-permute-done.22), channel_id=1, source_target_pairs={{0,8},{4,12},{8,0},{12,4},{16,24},{20,28},{24,16},{28,20},{1,9},{5... | collective-permute-start | bytes 2162696 | tf_op jit(solution)/shard_map/ppermute | solution.py:38
  208.9 46.3 %collective-permute-start.33 = (bf16[352,1024]{1,0:T(8,128)(2,1)}, bf16[352,1024]{1,0:T(8,128)(2,1)}, u32[]{:S(2)}, u32[]{:S(2)}) collective-permute-start(bf16[352,1024]{1,0:T(8,128)(2,1)} %copy-done.71), channel_id=1, source_target_pairs={{0,16},{4,20},{8,24},{12,28},{16,0},{20,4},{24,8},{28,12},{1,17},{... | collective-permute-start | bytes 2162696 | tf_op jit(solution)/shard_map/ppermute | solution.py:38
  255.9 67.9 %collective-permute-start.35 = (bf16[512,1408]{1,0:T(8,128)(2,1)}, bf16[512,1408]{1,0:T(8,128)(2,1)}, u32[]{:S(2)}, u32[]{:S(2)}) collective-permute-start(bf16[512,1408]{1,0:T(8,128)(2,1)} %get-tuple-element.409.rest_4_), channel_id=1, source_target_pairs={{0,8},{4,12},{8,0},{12,4},{16,24},{20,28},{24,16},{28,20},{1,9},{5... | collective-permute-start | bytes 4325384 | tf_op jit(solution)/shard_map/ppermute | solution.py:38
  256.6 67.2 %collective-permute-start.36 = (bf16[512,1408]{1,0:T(8,128)(2,1)}, bf16[512,1408]{1,0:T(8,128)(2,1)}, u32[]{:S(2)}, u32[]{:S(2)}) collective-permute-start(bf16[512,1408]{1,0:T(8,128)(2,1)} %get-tuple-element.405.rest_0_), channel_id=1, source_target_pairs={{0,16},{4,20},{8,24},{12,28},{16,0},{20,4},{24,8},{28,12},{1,17},{... | collective-permute-start | bytes 4325384 | tf_op jit(solution)/shard_map/ppermute | solution.py:38
  258.0 65.8 %collective-permute-start.37 = (bf16[512,1408]{1,0:T(8,128)(2,1)}, bf16[512,1408]{1,0:T(8,128)(2,1)}, u32[]{:S(2)}, u32[]{:S(2)}) collective-permute-start(bf16[512,1408]{1,0:T(8,128)(2,1)} %collective-permute-done.29.rest_6_), channel_id=1, source_target_pairs={{0,8},{4,12},{8,0},{12,4},{16,24},{20,28},{24,16},{28,20},{1,9},{5... | collective-permute-start | bytes 4325384 | tf_op jit(solution)/shard_map/ppermute | solution.py:38
  259.3 64.5 %collective-permute-start.38 = (bf16[512,1408]{1,0:T(8,128)(2,1)}, bf16[512,1408]{1,0:T(8,128)(2,1)}, u32[]{:S(2)}, u32[]{:S(2)}) collective-permute-start(bf16[512,1408]{1,0:T(8,128)(2,1)} %collective-permute-done.30.rest_1_), channel_id=1, source_target_pairs={{0,16},{4,20},{8,24},{12,28},{16,0},{20,4},{24,8},{28,12},{1,17},{... | collective-permute-start | bytes 4325384 | tf_op jit(solution)/shard_map/ppermute | solution.py:38
  335.3 60.8 %collective-permute-start.39 = (bf16[512,1024]{1,0:T(8,128)(2,1)}, bf16[512,1024]{1,0:T(8,128)(2,1)}, u32[]{:S(2)}, u32[]{:S(2)}) collective-permute-start(bf16[512,1024]{1,0:T(8,128)(2,1)} %convolution_convert_fusion.12), channel_id=1, source_target_pairs={{0,8},{4,12},{8,0},{12,4},{16,24},{20,28},{24,16},{28,20},{1,9},{5... | collective-permute-start | bytes 3145736 | tf_op jit(solution)/shard_map/ppermute | solution.py:38
  336.0 60.2 %collective-permute-start.40 = (bf16[512,1024]{1,0:T(8,128)(2,1)}, bf16[512,1024]{1,0:T(8,128)(2,1)}, u32[]{:S(2)}, u32[]{:S(2)}) collective-permute-start(bf16[512,1024]{1,0:T(8,128)(2,1)} %convolution_convert_fusion.10), channel_id=1, source_target_pairs={{0,8},{4,12},{8,0},{12,4},{16,24},{20,28},{24,16},{28,20},{1,9},{5... | collective-permute-start | bytes 3145736 | tf_op jit(solution)/shard_map/ppermute | solution.py:38
  337.3 58.8 %collective-permute-start.43 = (bf16[704,512]{1,0:T(8,128)(2,1)}, bf16[704,512]{1,0:T(8,128)(2,1)}, u32[]{:S(2)}, u32[]{:S(2)}) collective-permute-start(bf16[704,512]{1,0:T(8,128)(2,1)} %convolution_convert_fusion.15), channel_id=1, source_target_pairs={{0,16},{4,20},{8,24},{12,28},{16,0},{20,4},{24,8},{28,12},{1,17},{... | collective-permute-start | bytes 2162696 | tf_op jit(solution)/shard_map/ppermute | solution.py:38
  338.0 58.1 %collective-permute-start.44 = (bf16[704,512]{1,0:T(8,128)(2,1)}, bf16[704,512]{1,0:T(8,128)(2,1)}, u32[]{:S(2)}, u32[]{:S(2)}) collective-permute-start(bf16[704,512]{1,0:T(8,128)(2,1)} %convolution_convert_fusion.14), channel_id=1, source_target_pairs={{0,16},{4,20},{8,24},{12,28},{16,0},{20,4},{24,8},{28,12},{1,17},{... | collective-permute-start | bytes 2162696 | tf_op jit(solution)/shard_map/ppermute | solution.py:38
  343.2 52.9 %collective-permute-start.42 = (bf16[512,384]{1,0:T(8,128)(2,1)}, bf16[512,384]{1,0:T(8,128)(2,1)S(1)}, u32[]{:S(2)}, u32[]{:S(2)}) collective-permute-start(bf16[512,384]{1,0:T(8,128)(2,1)} %convolution_convert_fusion.27), channel_id=1, source_target_pairs={{0,16},{4,20},{8,24},{12,28},{16,0},{20,4},{24,8},{28,12},{1,17},{... | collective-permute-start | bytes 1179656 | tf_op jit(solution)/shard_map/ppermute | solution.py:38
  412.5 34.4 %collective-permute-start.52 = (bf16[704,512]{1,0:T(8,128)(2,1)}, bf16[704,512]{1,0:T(8,128)(2,1)}, u32[]{:S(2)}, u32[]{:S(2)}) collective-permute-start(bf16[704,512]{1,0:T(8,128)(2,1)} %add_convert_fusion.20), channel_id=1, source_target_pairs={{0,8},{4,12},{8,0},{12,4},{16,24},{20,28},{24,16},{28,20},{1,9},{5... | collective-permute-start | bytes 2162696 | tf_op jit(solution)/shard_map/ppermute | solution.py:38
  414.0 29.6 %collective-permute-start.51 = (bf16[512,384]{1,0:T(8,128)(2,1)}, bf16[512,384]{1,0:T(8,128)(2,1)}, u32[]{:S(2)}, u32[]{:S(2)}) collective-permute-start(bf16[512,384]{1,0:T(8,128)(2,1)} %add_convert_fusion.24), channel_id=1, source_target_pairs={{0,8},{4,12},{8,0},{12,4},{16,24},{20,28},{24,16},{28,20},{1,9},{5... | collective-permute-start | bytes 1179656 | tf_op jit(solution)/shard_map/ppermute | solution.py:38
  418.0 32.1 %collective-permute-start.50 = (bf16[512,1024]{1,0:T(8,128)(2,1)}, bf16[512,1024]{1,0:T(8,128)(2,1)}, u32[]{:S(2)}, u32[]{:S(2)}) collective-permute-start(bf16[512,1024]{1,0:T(8,128)(2,1)} %add_convert_fusion.11), channel_id=1, source_target_pairs={{0,16},{4,20},{8,24},{12,28},{16,0},{20,4},{24,8},{28,12},{1,17},{... | collective-permute-start | bytes 3145736 | tf_op jit(solution)/shard_map/ppermute | solution.py:38
  418.7 111.1 %all-gather.11.cloned.1.call-start = ((), (), s32[]{:S(2)}) async-start(), calls=%async_computation.9 | async-start | bytes 2621440 | tf_op jit(solution)/shard_map/all_gather | solution.py:579
  438.6 37.7 %collective-permute-start.46 = (bf16[352,1024]{1,0:T(8,128)(2,1)}, bf16[352,1024]{1,0:T(8,128)(2,1)}, u32[]{:S(2)}, u32[]{:S(2)}) collective-permute-start(bf16[352,1024]{1,0:T(8,128)(2,1)} %get-tuple-element.564), channel_id=1, source_target_pairs={{0,8},{4,12},{8,0},{12,4},{16,24},{20,28},{24,16},{28,20},{1,9},{5... | collective-permute-start | bytes 2162696 | tf_op jit(solution)/shard_map/ppermute | solution.py:38
  439.2 37.1 %collective-permute-start.47 = (bf16[352,1024]{1,0:T(8,128)(2,1)}, bf16[352,1024]{1,0:T(8,128)(2,1)}, u32[]{:S(2)}, u32[]{:S(2)}) collective-permute-start(bf16[352,1024]{1,0:T(8,128)(2,1)} %get-tuple-element.562), channel_id=1, source_target_pairs={{0,8},{4,12},{8,0},{12,4},{16,24},{20,28},{24,16},{28,20},{1,9},{5... | collective-permute-start | bytes 2162696 | tf_op jit(solution)/shard_map/ppermute | solution.py:38
  443.6 32.8 %collective-permute-start.48 = (bf16[352,1024]{1,0:T(8,128)(2,1)}, bf16[352,1024]{1,0:T(8,128)(2,1)}, u32[]{:S(2)}, u32[]{:S(2)}) collective-permute-start(bf16[352,1024]{1,0:T(8,128)(2,1)} %get-tuple-element.566), channel_id=1, source_target_pairs={{0,16},{4,20},{8,24},{12,28},{16,0},{20,4},{24,8},{28,12},{1,17},{... | collective-permute-start | bytes 2162696 | tf_op jit(solution)/shard_map/ppermute | solution.py:38
  447.0 29.4 %collective-permute-start.49 = (bf16[352,1024]{1,0:T(8,128)(2,1)}, bf16[352,1024]{1,0:T(8,128)(2,1)}, u32[]{:S(2)}, u32[]{:S(2)}) collective-permute-start(bf16[352,1024]{1,0:T(8,128)(2,1)} %get-tuple-element.561), channel_id=1, source_target_pairs={{0,16},{4,20},{8,24},{12,28},{16,0},{20,4},{24,8},{28,12},{1,17},{... | collective-permute-start | bytes 2162696 | tf_op jit(solution)/shard_map/ppermute | solution.py:38
  476.4 206.2 %reduce-scatter.11.cloned.1.call-start = ((), (), s32[]{:S(2)}) async-start(), calls=%async_computation.11 | async-start | bytes 2621440 | tf_op jit(solution)/shard_map/reduce_scatter | solution.py:582
  482.9 44.3 %collective-permute-start.53 = (bf16[512,1408]{1,0:T(8,128)(2,1)S(1)}, bf16[512,1408]{1,0:T(8,128)(2,1)}, u32[]{:S(2)}, u32[]{:S(2)}) collective-permute-start(bf16[512,1408]{1,0:T(8,128)(2,1)S(1)} %copy-done.147), channel_id=1, source_target_pairs={{0,8},{4,12},{8,0},{12,4},{16,24},{20,28},{24,16},{28,20},{1,9},{5... | collective-permute-start | bytes 4325384 | tf_op jit(solution)/shard_map/ppermute | solution.py:38
  483.4 46.4 %collective-permute-start.54 = (bf16[512,1408]{1,0:T(8,128)(2,1)S(1)}, bf16[512,1408]{1,0:T(8,128)(2,1)}, u32[]{:S(2)}, u32[]{:S(2)}) collective-permute-start(bf16[512,1408]{1,0:T(8,128)(2,1)S(1)} %copy-done.148), channel_id=1, source_target_pairs={{0,16},{4,20},{8,24},{12,28},{16,0},{20,4},{24,8},{28,12},{1,17},{... | collective-permute-start | bytes 4325384 | tf_op jit(solution)/shard_map/ppermute | solution.py:38
  532.9 43.6 %collective-permute-start.60 = (bf16[512,1408]{1,0:T(8,128)(2,1)}, bf16[512,1408]{1,0:T(8,128)(2,1)}, u32[]{:S(2)}, u32[]{:S(2)}) collective-permute-start(bf16[512,1408]{1,0:T(8,128)(2,1)} %convolution_convert_fusion.2), channel_id=1, source_target_pairs={{0,16},{4,20},{8,24},{12,28},{16,0},{20,4},{24,8},{28,12},{1,17},{... | collective-permute-start | bytes 4325384 | tf_op jit(solution)/shard_map/ppermute | solution.py:38
  534.3 37.8 %collective-permute-start.59 = (bf16[512,1408]{1,0:T(8,128)(2,1)}, bf16[512,1408]{1,0:T(8,128)(2,1)}, u32[]{:S(2)}, u32[]{:S(2)}) collective-permute-start(bf16[512,1408]{1,0:T(8,128)(2,1)} %convolution_convert_fusion.8), channel_id=1, source_target_pairs={{0,8},{4,12},{8,0},{12,4},{16,24},{20,28},{24,16},{28,20},{1,9},{5... | collective-permute-start | bytes 4325384 | tf_op jit(solution)/shard_map/ppermute | solution.py:38
  560.0 133.7 %reduce-scatter.9.cloned.1.call-start = ((), (), s32[]{:S(2)}) async-start(), calls=%async_computation.10 | async-start | bytes 2621440 | tf_op jit(solution)/shard_map/reduce_scatter | solution.py:582
  572.1 27.5 %collective-permute-start.58 = (bf16[1024,512]{1,0:T(8,128)(2,1)S(1)}, bf16[1024,512]{1,0:T(8,128)(2,1)S(1)}, u32[]{:S(2)}, u32[]{:S(2)}) collective-permute-start(bf16[1024,512]{1,0:T(8,128)(2,1)S(1)} %get-tuple-element.495), channel_id=1, source_target_pairs={{8,0},{12,4},{24,16},{28,20},{9,1},{13,5},{25,17},{29,21},{10,2},{... | collective-permute-start | bytes 3145736 | tf_op jit(solution)/shard_map/ppermute | solution.py:576
  576.5 45.3 %collective-permute-start.64 = (bf16[512,1408]{1,0:T(8,128)(2,1)}, bf16[512,1408]{1,0:T(8,128)(2,1)}, u32[]{:S(2)}, u32[]{:S(2)}) collective-permute-start(bf16[512,1408]{1,0:T(8,128)(2,1)} %add_convert_fusion.8), channel_id=1, source_target_pairs={{0,16},{4,20},{8,24},{12,28},{16,0},{20,4},{24,8},{28,12},{1,17},{... | collective-permute-start | bytes 4325384 | tf_op jit(solution)/shard_map/ppermute | solution.py:38
  648.2 37.5 %collective-permute-start.73 = (bf16[512,384]{1,0:T(8,128)(2,1)}, bf16[512,384]{1,0:T(8,128)(2,1)}, u32[]{:S(2)}, u32[]{:S(2)}) collective-permute-start(bf16[512,384]{1,0:T(8,128)(2,1)} %convolution_convert_fusion.21), channel_id=1, source_target_pairs={{0,16},{4,20},{8,24},{12,28},{16,0},{20,4},{24,8},{28,12},{1,17},{... | collective-permute-start | bytes 1179656 | tf_op jit(solution)/shard_map/ppermute | solution.py:38
  650.3 38.6 %collective-permute-start.70 = (bf16[512,384]{1,0:T(8,128)(2,1)}, bf16[512,384]{1,0:T(8,128)(2,1)S(1)}, u32[]{:S(2)}, u32[]{:S(2)}) collective-permute-start(bf16[512,384]{1,0:T(8,128)(2,1)} %convolution_convert_fusion.25), channel_id=1, source_target_pairs={{0,8},{4,12},{8,0},{12,4},{16,24},{20,28},{24,16},{28,20},{1,9},{5... | collective-permute-start | bytes 1179656 | tf_op jit(solution)/shard_map/ppermute | solution.py:38
  (212 other events, 3075.3 us)
Sparse Core Ops, SparseCore 0:
  12.4 48.3 all-gather.4
  73.3 47.8 all-gather.6
  150.8 44.7 reduce-scatter.4
  205.1 46.5 all-gather.8
  418.8 46.2 reduce-scatter.6
  476.5 45.9 all-gather.10
  560.1 42.5 reduce-scatter.10
  636.0 47.2 reduce-scatter.8

commit v4 on v3

--- a/solution.py
+++ b/solution.py
@@ -63,23 +63,23 @@
     return pieces
 
 
-def send_quads(pieces, bit, keys):
-    return {key: across(pieces[key], 2 * bit) for key in keys}
-
-
-def add_quads(pieces, arrived, bit):
-    return {
-        key: (piece.astype(F32) + arrived[key | bit].astype(F32)).astype(BF16)
-        for key, piece in pieces.items()
-        if not key & bit
-    }
-
-
-def reduce_quads(pieces, order):
-    for bit in order:
-        arrived = send_quads(pieces, bit, [key for key in pieces if key & bit])
-        pieces = add_quads(pieces, arrived, bit)
-    return pieces
+def add_low(left, right):
+    return (left.astype(F32) + right.astype(F32)).astype(BF16)
+
+
+def first_sum(parts, arrived):
+    half = parts[0].shape[0]
+    if len(arrived) == 1:
+        arrived = (arrived[0][:half], arrived[0][half:])
+    return add_low(parts[0], arrived[0]), add_low(parts[1], arrived[1])
+
+
+def rest_parts(kept, arrived, order):
+    for bit in order[2:]:
+        stack = add_rows(kept, arrived)
+        half = stack.shape[0] // 2
+        kept, arrived = stack[:half], across(stack[half:], 2 * bit)
+    return kept, arrived
 
 
 def together(*values):
@@ -178,20 +178,25 @@
     return values * cosine + pltpu.roll(values, HDIM // 2, 1) * sine
 
 
-def call(kernel, grid, ins, outs, shapes, limit, flops, scratch=(), name=None):
+def call(kernel, grid, ins, outs, shapes, limit, flops, scratch=(), name=None, scalars=0):
     moved = 0
     for shape in shapes:
         moved += shape.size * shape.dtype.itemsize
 
     def run(*args):
         total = moved + sum(a.size * a.dtype.itemsize for a in args)
+        if flops == 0:
+            total = 0
         return pl.pallas_call(
             kernel,
-            grid=grid,
-            in_specs=ins,
-            out_specs=outs,
+            grid_spec=pltpu.PrefetchScalarGridSpec(
+                num_scalar_prefetch=scalars,
+                grid=grid,
+                in_specs=ins,
+                out_specs=outs,
+                scratch_shapes=scratch,
+            ),
             out_shape=shapes,
-            scratch_shapes=scratch,
             compiler_params=pltpu.CompilerParams(vmem_limit_bytes=limit * MIB),
             cost_estimate=pl.CostEstimate(
                 flops=flops, bytes_accessed=total, transcendentals=0
@@ -207,7 +212,112 @@
 
 
 def rows_spec(columns, tile=TILE):
-    return pl.BlockSpec((tile, columns), lambda i: (i, 0))
+    return pl.BlockSpec((tile, columns), lambda i, *_: (i, 0))
+
+
+def turned(step, core, count):
+    return (step + (count // 2) * core) % count
+
+
+def turned_spec(columns, count):
+    return pl.BlockSpec((TILE, columns), lambda i, core: (turned(i, core[0], count), 0))
+
+
+def halves_specs(columns, count):
+    half = count // 2
+    specs = [
+        pl.BlockSpec((TILE, columns), lambda i, core: (jnp.minimum(i, half), 0)),
+        pl.BlockSpec((TILE, columns), lambda i, core: (jnp.maximum(i - half, 0), 0)),
+    ]
+    return specs, [shaped((half + 1) * TILE, columns, BF16), shaped(half * TILE, columns, BF16)]
+
+
+def add_kernel(left_ref, right_ref, out_ref):
+    out_ref[...] = (left_ref[...].astype(F32) + right_ref[...].astype(F32)).astype(BF16)
+
+
+def add_rows(left, right):
+    rows, columns = right.shape
+    tile = rows // 4 if rows % 64 == 0 else rows
+    return call(
+        add_kernel,
+        (rows // tile,),
+        [rows_spec(columns, tile)] * 2,
+        [rows_spec(columns, tile)],
+        [shaped(rows, columns, BF16)],
+        16,
+        0,
+        name="add_rows",
+    )(left, right)[0]
+
+
+def finish_kernel(core_ref, kept_ref, arrived_ref, mine_ref, other_ref):
+    total = (kept_ref[...].astype(F32) + arrived_ref[...].astype(F32)).astype(BF16)
+
+    @pl.when(pl.program_id(0) == 0)
+    def _():
+        other_ref[...] = total
+
+    @pl.when(pl.program_id(0) == 1)
+    def _():
+        mine_ref[...] = total
+
+
+def finish(core, kept, arrived, axis):
+    rows, columns = kept.shape
+    size = (rows // 2, columns) if axis == 0 else (rows, columns // 2)
+    if size[0] % 16 or (axis == 1 and size[1] % LANES):
+        return split_core(add_low(kept, arrived), core[0], axis)
+
+    def index(i, core):
+        half = jnp.where(i == 0, 1 - core[0], core[0])
+        return (half, 0) if axis == 0 else (0, half)
+
+    return call(
+        finish_kernel,
+        (2,),
+        [pl.BlockSpec(size, index)] * 2,
+        [pl.BlockSpec(size, lambda i, core: (0, 0))] * 2,
+        [shaped(*size, BF16)] * 2,
+        24,
+        0,
+        name="finish",
+        scalars=1,
+    )(core, kept, arrived)
+
+
+def merge_kernel(core_ref, mine_ref, arrived_ref, out_ref):
+    own = pl.program_id(0) == core_ref[0]
+
+    @pl.when(own)
+    def _():
+        out_ref[...] = mine_ref[...].astype(F32).reshape(out_ref.shape)
+
+    @pl.when(~own)
+    def _():
+        out_ref[...] = arrived_ref[...].astype(F32).reshape(out_ref.shape)
+
+
+def merge(core, mine, arrived, axis, part=0, parts=1):
+    rows, columns = mine.shape
+    columns = columns // parts
+    if axis is None:
+        shape, size, index = (2, rows, columns), (1, rows, columns), lambda i, core: (i, 0, 0)
+    elif axis == 0:
+        shape, size, index = (2 * rows, columns), (rows, columns), lambda i, core: (i, 0)
+    else:
+        shape, size, index = (rows, 2 * columns), (rows, columns), lambda i, core: (0, i)
+    return call(
+        merge_kernel,
+        (2,),
+        [pl.BlockSpec((rows, columns), lambda i, core: (0, part))] * 2,
+        [pl.BlockSpec(size, index)],
+        [jax.ShapeDtypeStruct(shape, F32)],
+        24,
+        0,
+        name="merge",
+        scalars=1,
+    )(core[None], mine, arrived)[0]
 
 
 def shaped(rows, columns, dtype):
@@ -362,10 +472,12 @@
     )(query, grad, logs, *before, own, places, low, high, cosine, sine)
 
 
-def collect_kernel(heads, back, quads, dq_ref, own_ref, cos_ref, sin_ref, x_ref, *rest):
+def collect_kernel(heads, back, quads, core_ref, dq_ref, own_ref, cos_ref, sin_ref, x_ref, *rest):
     arrived, wa_refs, wb_refs = rest[:back], rest[back : back + quads], rest[back + quads : back + 2 * quads]
-    out_ref, part_ref, gain_ref, bias_ref = rest[back + 2 * quads :]
+    kept_ref, other_ref, gain_ref, bias_ref, *outs = rest[back + 2 * quads :]
+    x_all, grad_all = outs[-2:]
     columns = heads * HDIM
+    step = pl.program_id(0)
     total = own_ref[...]
     for ref in arrived:
         total = total + ref[...].astype(F32)
@@ -377,9 +489,12 @@
             part = turn(part, cosine, sine)
         heads_out.append(part.astype(BF16))
     grads = jnp.concatenate(heads_out, axis=1)
-    out_ref[...] = grads
-
-    @pl.when(pl.program_id(0) == 0)
+    tile = turned(step, core_ref[0], pl.num_programs(0))
+    rows = pl.ds(pl.multiple_of(tile * TILE, TILE), TILE)
+    x_all[rows, :] = x_ref[...]
+    grad_all[rows, :] = grads
+
+    @pl.when(step == 0)
     def _():
         gain_ref[...] = jnp.zeros_like(gain_ref)
         bias_ref[...] = jnp.zeros_like(bias_ref)
@@ -390,42 +505,56 @@
     for key in range(quads):
         cols = slice(key * block, (key + 1) * block)
         part = dot_last(grads[:, :cut], wa_refs[key][...]) + dot_last(grads[:, cut:], wb_refs[key][...])
-        part_ref[:, cols] = part.astype(BF16)
+        kept_ref[:, cols] = part.astype(BF16)
+        other_ref[:, cols] = part.astype(BF16)
         gain_ref[:, cols] += jnp.sum(part * x_ref[:, cols].astype(F32), axis=0, keepdims=True)
 
-
-def collect(grad_query, own, cosine, sine, x, arrived, wa, wb):
+    @pl.when(step == pl.num_programs(0) - 1)
+    def _():
+        for key in range(quads):
+            weight = dot_first(x_all[:, key * block : (key + 1) * block], grad_all[...]).astype(BF16)
+            for part, up in enumerate((True, False)):
+                half, index = (int(v) for v in place_of(key, quads, up))
+                quarter = quads // 4
+                number = 2 if half else index // quarter
+                first = (index if half else index % quarter) * block
+                outs[part * 3 + number][first : first + block, :] = weight[
+                    :, part * cut : (part + 1) * cut
+                ]
+
+
+def collect(core, grad_query, own, cosine, sine, x, arrived, wa, wb):
     rows, columns = grad_query.shape
     width = x.shape[1]
+    tiles = rows // TILE
     quads, (block, cut) = len(wa), wa[0].shape
-    fixed = lambda i: (0, 0)
-    return call(
+    quarter = width // 4
+    fixed = lambda *_: (0, 0)
+    halves = halves_specs(width, tiles)
+    shapes = [shaped(quarter, cut, BF16), shaped(quarter, cut, BF16), shaped(2 * quarter, cut, BF16)]
+    outs = call(
         functools.partial(collect_kernel, columns // HDIM, len(arrived), quads),
-        (rows // TILE,),
-        [rows_spec(columns), rows_spec(2 * columns)]
-        + [rows_spec(HDIM)] * 2
-        + [rows_spec(width)]
-        + [rows_spec(2 * columns)] * len(arrived)
+        (tiles,),
+        [turned_spec(columns, tiles), turned_spec(2 * columns, tiles)]
+        + [turned_spec(HDIM, tiles)] * 2
+        + [turned_spec(width, tiles)]
+        + [turned_spec(2 * columns, tiles)] * len(arrived)
         + [whole((block, cut))] * (2 * quads),
-        [
-            rows_spec(3 * columns),
-            rows_spec(width),
-            pl.BlockSpec((1, width), fixed),
-            pl.BlockSpec((1, 3 * columns), fixed),
-        ],
-        [
-            shaped(rows, 3 * columns, BF16),
-            shaped(rows, width, BF16),
-            shaped(1, width, F32),
-            shaped(1, 3 * columns, F32),
-        ],
+        halves[0]
+        + [pl.BlockSpec((1, width), fixed)]
+        + [pl.BlockSpec((1, 3 * columns), fixed)]
+        + [pl.BlockSpec(shape.shape, fixed) for shape in shapes] * 2,
+        halves[1] + [shaped(1, width, F32), shaped(1, 3 * columns, F32)] + shapes * 2,
         60,
-        4 * rows * width * cut,
+        8 * rows * width * cut,
+        scratch=[pltpu.VMEM((rows, width), BF16), pltpu.VMEM((rows, 3 * columns), BF16)],
         name="collect",
-    )(grad_query, own, cosine, sine, x, *arrived, *wa, *wb)
-
-
-def expert_kernel(routed, quads, x_ref, wd_ref, cot_ref, scale_ref, *rest):
+        scalars=1,
+    )(core[None], grad_query, own, cosine, sine, x, *arrived, *wa, *wb)
+    return outs[:4], (outs[4:6], outs[6:7]), (outs[7:9], outs[9:])
+
+
+def expert_kernel(routed, quads, core_ref, x_ref, wd_ref, cot_ref, scale_ref, *rest):
     if routed:
         wg_refs, wu_refs, rest = rest[:quads], rest[quads : 2 * quads], rest[2 * quads :]
         part_in, grad_in, dot_in, lane_ref = rest[:4]
@@ -467,50 +596,234 @@
             grad_ref[:, key * block : (key + 1) * block] = grad.astype(BF16)
         inner_ref[...] = inner
         return
-    part_ref, grad_ref, gate_ref, up_ref = rest[2:]
+    part_refs, grad_refs, gate_ref, up_ref = rest[2:4], rest[4:6], rest[6], rest[7]
     grad_gate, grad_up = grad_gate.astype(BF16), grad_up.astype(BF16)
     gate_ref[...] = grad_gate
     up_ref[...] = grad_up
-    part_ref[...] = (part + part_in[...].astype(F32)).astype(BF16)
+    part = (part + part_in[...].astype(F32)).astype(BF16)
+    for ref in part_refs:
+        ref[...] = part
     for key in range(quads):
         cols = slice(key * block, (key + 1) * block)
         grad = dot_last(grad_gate, wg_refs[key][...]) + dot_last(grad_up, wu_refs[key][...])
-        grad = grad.astype(BF16).astype(F32) + grad_in[:, cols].astype(F32)
-        grad_ref[:, cols] = grad.astype(BF16)
+        grad = (grad.astype(BF16).astype(F32) + grad_in[:, cols].astype(F32)).astype(BF16)
+        for ref in grad_refs:
+            ref[:, cols] = grad
     lane = lane_ref[...]
     extra = jnp.zeros((x.shape[0], LANES), F32)
     for slot, value in enumerate((inner, dot_in[...])):
         high = value.astype(BF16).astype(F32)
         extra = extra + jnp.where(lane == 2 * slot, high, 0.0)
         extra = extra + jnp.where(lane == 2 * slot + 1, value - high, 0.0)
-    grad_ref[:, width:] = extra.astype(BF16)
-
-
-def expert(x, pieces, wd, cot, scale, routed=()):
+    for ref in grad_refs:
+        ref[:, width:] = extra.astype(BF16)
+
+
+def expert(core, x, pieces, wd, hidden, cot, scale, routed=()):
     rows, width = x.shape
-    hidden = wd.shape[0]
+    tiles = rows // TILE
     quads = len(pieces) // 2 if routed else len(pieces)
-    ins = [rows_spec(width), whole((hidden, width)), rows_spec(width), rows_spec(1)]
+    spec = lambda columns: turned_spec(columns, tiles)
+    ins = [spec(width), whole((hidden, width)), spec(width), spec(1)]
     ins += [whole(piece.shape) for piece in pieces]
-    outs = [rows_spec(hidden), rows_spec(width), rows_spec(width)]
-    shapes = [shaped(rows, hidden, BF16), shaped(rows, width, BF16), shaped(rows, width, BF16)]
+    outs = [spec(hidden), spec(width)]
+    shapes = [shaped(rows, hidden, BF16), shaped(rows, width, BF16)]
     if routed:
-        ins += [rows_spec(width), rows_spec(width), rows_spec(1), whole((1, LANES))]
-        outs += [rows_spec(width + LANES), rows_spec(hidden), rows_spec(hidden)]
-        shapes += [shaped(rows, width + LANES, BF16)] + [shaped(rows, hidden, BF16)] * 2
+        ins += [spec(width), spec(width), spec(1), whole((1, LANES))]
+        for columns in (width, width + LANES):
+            specs, halves = halves_specs(columns, tiles)
+            outs, shapes = outs + specs, shapes + halves
+        outs += [spec(hidden), spec(hidden)]
+        shapes += [shaped(rows, hidden, BF16)] * 2
     else:
-        outs += [rows_spec(width), rows_spec(1), rows_spec(2 * hidden)]
-        shapes += [shaped(rows, width, BF16), shaped(rows, 1, F32), shaped(rows, 2 * hidden, BF16)]
+        outs += [spec(width), spec(width), spec(1), spec(2 * hidden)]
+        shapes += [shaped(rows, width, BF16)] * 2
+        shapes += [shaped(rows, 1, F32), shaped(rows, 2 * hidden, BF16)]
     return call(
         functools.partial(expert_kernel, bool(routed), quads),
-        (rows // TILE,),
+        (tiles,),
         ins,
         outs,
         shapes,
         60,
         12 * rows * width * hidden,
         name="expert" if routed else "shared",
-    )(x, wd, cot, scale, *pieces, *routed)
+        scalars=1,
+    )(core[None], x, wd, cot, scale, *pieces, *routed)
+
+
+def reversed_bits(value, count):
+    return sum((((value >> k) & 1) << (count - 1 - k) for k in range(count)), 0 * value)
+
+
+def places(step, quads, up):
+    if up:
+        return step & 1, reversed_bits(step >> 1, quads.bit_length() - 2)
+    half = quads // 2
+    return jnp.where(step < half, 0, 1), jnp.where(step < half, step, step - half)
+
+
+def stack_specs(quads, up, rows, columns, merged):
+    quarter = quads // 4
+
+    def spec(half, part):
+        def index(step, *_):
+            if up:
+                return places(step, quads, up)[1] % quarter, 0
+            first = half * 2 * quarter + part * quarter
+            return jnp.clip(step - first, 0, quarter - 1), 0
+
+        return pl.BlockSpec((rows, columns), index)
+
+    def joined(step, *_):
+        if up:
+            return places(step, quads, up)[1], 0
+        return jnp.clip(step - 2 * quarter, 0, 2 * quarter - 1), 0
+
+    specs = [spec(0, 0), spec(0, 1)]
+    shapes = [shaped(quarter * rows, columns, BF16)] * 2
+    if merged:
+        specs.append(pl.BlockSpec((rows, columns), joined))
+        shapes.append(shaped(2 * quarter * rows, columns, BF16))
+    else:
+        specs += [spec(1, 0), spec(1, 1)]
+        shapes += [shaped(quarter * rows, columns, BF16)] * 2
+    return specs, shapes
+
+
+def store_stack(step, quads, up, merged, outs, value):
+    half, index = places(step, quads, up)
+    part = index // (quads // 4)
+    for number, out in enumerate(outs):
+        wanted = (half == number // 2) & ((part == number % 2) | (merged and number == 2))
+
+        @pl.when(wanted)
+        def _():
+            out[...] = value
+
+
+def row_grads_kernel(quads, cuts, x_ref, grad_ref, *outs):
+    step = pl.program_id(0)
+    total = dot_first(x_ref[...], grad_ref[...]).astype(BF16)
+    first = 0
+    for low, high, up, merged in cuts:
+        count = 3 if merged else 4
+        store_stack(step, quads, up, merged, outs[first : first + count], total[:, low:high])
+        first += count
+
+
+def row_grads(rows, grads, quads, cuts):
+    count, width = rows.shape
+    columns = grads.shape[1]
+    block = width // quads
+    specs, shapes = [], []
+    for low, high, up, merged in cuts:
+        more = stack_specs(quads, up, block, high - low, merged)
+        specs, shapes = specs + more[0], shapes + more[1]
+    outs = call(
+        functools.partial(row_grads_kernel, quads, cuts),
+        (quads,),
+        [pl.BlockSpec((count, block), lambda i: (0, i)), whole((count, columns))],
+        specs,
+        shapes,
+        48,
+        2 * count * width * columns,
+        name="row_grads",
+    )(rows, grads)
+    found = []
+    for _, _, _, merged in cuts:
+        size = 3 if merged else 4
+        found.append((outs[:2], outs[2:size]))
+        outs = outs[size:]
+    return found
+
+
+def column_grads_kernel(quads, up, quad_ref, act_ref, grad_ref, *outs):
+    total = dot_first(act_ref[...], grad_ref[...]).astype(BF16)
+    store_stack(pl.program_id(0), quads, up, True, outs, total)
+
+
+def column_grads(acts, grads, quad, quads, up):
+    count, hidden = acts.shape
+    width = grads.shape[1]
+    block = width // quads
+    specs, shapes = stack_specs(quads, up, hidden, block, True)
+    outs = pl.pallas_call(
+        functools.partial(column_grads_kernel, quads, up),
+        grid_spec=pltpu.PrefetchScalarGridSpec(
+            num_scalar_prefetch=1,
+            grid=(quads,),
+            in_specs=[
+                pl.BlockSpec((count, hidden), lambda i, own: (0, 0)),
+                pl.BlockSpec((count, block), lambda i, own: (0, own[0] ^ i)),
+            ],
+            out_specs=specs,
+        ),
+        out_shape=shapes,
+        compiler_params=pltpu.CompilerParams(vmem_limit_bytes=48 * MIB),
+        cost_estimate=pl.CostEstimate(
+            flops=2 * count * hidden * width,
+            bytes_accessed=2 * (count * (hidden + width) + hidden * width),
+            transcendentals=0,
+        ),
+        name="column_grads",
+    )(quad[None], acts, grads)
+    return outs[:2], outs[2:]
+
+
+def down_grads_kernel(quads, quad_ref, act_ref, grad_ref, *rest):
+    outs, total_ref = rest[:-1], rest[-1]
+    step = pl.program_id(0)
+    total_ref[...] = dot_first(act_ref[...], grad_ref[...])
+    size = total_ref.shape[0] // quads
+    quarter = quads // 4
+    for part, up in enumerate((True, False)):
+
+        @pl.when(step == part)
+        def _():
+            for key in range(quads):
+                first = pl.multiple_of((quad_ref[0] ^ key) * size, 8)
+                half, index = (int(v) for v in place_of(key, quads, up))
+                number = 2 if half else index // quarter
+                row = (index if half else index % quarter) * size
+                outs[part * 3 + number][row : row + size, :] = total_ref[
+                    pl.ds(first, size), :
+                ].astype(BF16)
+
+
+def place_of(key, quads, up):
+    count = quads.bit_length() - 1
+    spot = reversed_bits(key, count) if up else key
+    return spot // (quads // 2), spot % (quads // 2)
+
+
+def down_grads(acts, grads, quad, quads):
+    count, hidden = acts.shape
+    cut = grads.shape[1] // 2
+    rows = hidden // 4
+    shapes = [shaped(rows, cut, BF16), shaped(rows, cut, BF16), shaped(2 * rows, cut, BF16)] * 2
+    outs = pl.pallas_call(
+        functools.partial(down_grads_kernel, quads),
+        grid_spec=pltpu.PrefetchScalarGridSpec(
+            num_scalar_prefetch=1,
+            grid=(2,),
+            in_specs=[
+                pl.BlockSpec((count, hidden), lambda i, own: (0, 0)),
+                pl.BlockSpec((count, cut), lambda i, own: (0, i)),
+            ],
+            out_specs=[pl.BlockSpec(shape.shape, lambda i, own: (0, 0)) for shape in shapes],
+            scratch_shapes=[pltpu.VMEM((hidden, cut), F32)],
+        ),
+        out_shape=shapes,
+        compiler_params=pltpu.CompilerParams(vmem_limit_bytes=48 * MIB),
+        cost_estimate=pl.CostEstimate(
+            flops=4 * count * hidden * cut,
+            bytes_accessed=2 * (count * (hidden + 2 * cut) + 2 * hidden * cut),
+            transcendentals=0,
+        ),
+        name="down_grads",
+    )(quad[None], acts, grads)
+    return (outs[:2], outs[2:3]), (outs[3:5], outs[5:])
 
 
 def local(
@@ -579,22 +892,14 @@
         return lax.all_gather(values, "ep", axis=0, tiled=True)
 
     def scattered(values):
-        return lax.psum_scatter(values, "ep", scatter_dimension=0, tiled=True).astype(F32)
-
-    def core_sum(values):
-        keep, other = split_core(values, core, 0)
-        return (keep.astype(F32) + across(other, 1).astype(F32)).astype(BF16)
-
-    def row_grads(rows, grads, keys=range(quads)):
-        return {
-            k: dot_first(rows[:, k * block : (k + 1) * block], grads).astype(BF16) for k in keys
-        }
-
-    def column_grads(acts, grads):
-        return {
-            k: dot_first(acts, part).astype(BF16)
-            for k, part in take_quads(grads, quad, quads, 1).items()
-        }
+        return lax.psum_scatter(values, "ep", scatter_dimension=0, tiled=True)
+
+    def core_sum(kept, other):
+        return add_rows(kept, across(other, 1))
+
+    def finished(kept, arrived, axis):
+        mine, other = finish(core[None], kept, arrived, axis)
+        return mine, across(other, 1)
 
     hidden_in = residual_in.astype(F32)
     grad_out = cotangent.astype(F32)
@@ -626,13 +931,14 @@
     qkv_b_one, qkv_b_two = gather_quads(qkv_b, down_one), gather_quads(qkv_b, down_two)
 
     o_keep, o_other = split_core(output_weight, core, 0)
-    o_block = merge_core(o_keep, across(o_other, 1), core, 1)
     sg_keep, sg_other = split_core(shared_gate_weight, core, 1)
     su_keep, su_other = split_core(shared_up_weight, core, 1)
     gu_keep = jnp.concatenate([sg_keep, su_keep], axis=1)
     gu_other = jnp.concatenate([sg_other, su_other], axis=1)
     gu_block = merge_core(gu_keep, across(gu_other, 1), core, 0)
     sd_keep, sd_other = split_core(shared_down_weight, core, 0)
+    sd_keep = jnp.concatenate([sd_keep, o_keep], axis=0)
+    sd_other = jnp.concatenate([sd_other, o_other], axis=0)
     sd_block = merge_core(sd_keep, across(sd_other, 1), core, 1)
 
     def expert_block(weight):
@@ -645,15 +951,14 @@
     eda_block, edb_block = ed_block[:, :ed_cut], ed_block[:, ed_cut:]
 
     (
-        qkv_a_one, qkv_a_two, qkv_b_one, qkv_b_two, o_block, gu_block, sd_block, eg_block, eu_block,
+        qkv_a_one, qkv_a_two, qkv_b_one, qkv_b_two, gu_block, sd_block, eg_block, eu_block,
         eda_block, edb_block,
     ) = together(
-        qkv_a_one, qkv_a_two, qkv_b_one, qkv_b_two, o_block, gu_block, sd_block, eg_block, eu_block,
+        qkv_a_one, qkv_a_two, qkv_b_one, qkv_b_two, gu_block, sd_block, eg_block, eu_block,
         eda_block, edb_block,
     )
     qkv_a_rest = gather_rest(qkv_a_one, up_two)
     qkv_b_rest = gather_rest(qkv_b_one, down_two)
-    o_one, o_two = gather_quads({0: o_block}, down_one), gather_quads({0: o_block}, down_two)
     sd_one, sd_two = gather_quads({0: sd_block}, down_one), gather_quads({0: sd_block}, down_two)
     chosen = (
         (expert_index[:, :, None] == experts[None, None, :]) & (token_live[:, None, None] > 0)
@@ -672,30 +977,34 @@
     high, key_place = query_place[:, None], key_place[None, :]
     cosine, sine = rope_tables(position)
     (
-        group_one, qkv_a, qkv_b, o_one, o_two, sd_one, sd_two, gu_block, eg_block, eu_block,
-        eda_block, edb_block, cot_packed, bias, cosine, sine, low, high,
+        group_one, qkv_a, qkv_b, sd_one, sd_two, gu_block, eg_block, eu_block, eda_block,
+         edb_block, cot_packed, bias, cosine, sine, low, high,
     ) = together(
-        group_one, qkv_a_one | qkv_a_two | qkv_a_rest, qkv_b_one | qkv_b_two | qkv_b_rest, o_one,
-        o_two, sd_one, sd_two, gu_block, eg_block, eu_block, eda_block, edb_block, cot_packed, bias,
+        group_one, qkv_a_one | qkv_a_two | qkv_a_rest, qkv_b_one | qkv_b_two | qkv_b_rest,
+        sd_one, sd_two, gu_block, eg_block, eu_block, eda_block, edb_block, cot_packed, bias,
         cosine, sine, low, high,
     )
 
     rows_one = merge_core(group_one, across(group_one, 1), core, 0)
     gu_two = gather_quads({0: gu_block}, up_two)
-    o_rest, sd_rest = gather_rest(o_one, down_two), gather_rest(sd_one, down_two)
+    sd_rest = gather_rest(sd_one, down_two)
     cot_group = gathered(cot_packed)
     qkv_a, qkv_b = listed(qkv_a), listed(qkv_b)
     query, key_value = project(rows_one, qkv_a, qkv_b, bias, cosine, sine, heads)
 
-    query, key_value, o_rest, sd_rest = together(query, key_value, o_rest, sd_rest)
+    query, key_value, sd_rest = together(query, key_value, sd_rest)
     before = [shifted(key_value, step) for step in range(back, 0, -1)]
-    o_full = place_quads(o_one | o_two | o_rest, quad, 1)
-    query, before, gu_two, edb_block, o_full = together(query, before, gu_two, edb_block, o_full)
+    down_full = place_quads(sd_one | sd_two | sd_rest, quad, 1)
+    query, before, gu_two, edb_block, down_full = together(
+        query, before, gu_two, edb_block, down_full
+    )
     edb_one, edb_two = gather_quads({0: edb_block}, down_one), gather_quads({0: edb_block}, down_two)
     attended, log_total = attend(query, before, key_value, key_place, low, high)
-    branch = dot(attended, o_full).astype(BF16)
-    branch, cot_group, edb_one, edb_two = together(branch, cot_group, edb_one, edb_two)
-    branch = core_sum(branch)
+    output_rows = down_full[ffs_half:]
+    kept, other = split_core(attended, core, 0)
+    other = dot(other, output_rows).astype(BF16)
+    kept, other, cot_group, edb_one, edb_two = together(kept, other, cot_group, edb_one, edb_two)
+    branch = add_rows(dot(kept, output_rows).astype(BF16), across(other, 1))
     branch, gu_block, eu_block, eda_block, cot_group = together(
         branch, gu_block, eu_block, eda_block, cot_group
     )
@@ -704,20 +1013,18 @@
     gu_one = gather_quads({0: gu_block}, up_one)
     eda_one, eda_two = gather_quads({0: eda_block}, up_one), gather_quads({0: eda_block}, up_two)
     eu_one = gather_quads({0: eu_block}, down_one)
-    sd_full = place_quads(sd_one | sd_two | sd_rest, quad, 1)
     ed_full = jnp.zeros((eda_block.shape[0] * quads, width), BF16)
     ed_full = place_quads(edb_one | edb_two, quad, 0, ed_full, ed_cut)
-    branch_sum, cot_other, gu_one, eda_one, eda_two, eu_one, eg_block, edb_one, sd_full, ed_full = (
+    branch_sum, cot_other, gu_one, eda_one, eda_two, eu_one, eg_block, edb_one, ed_full = (
         together(
-            branch_sum, cot_other, gu_one, eda_one, eda_two, eu_one, eg_block, edb_one, sd_full,
-            ed_full,
+            branch_sum, cot_other, gu_one, eda_one, eda_two, eu_one, eg_block, edb_one, ed_full,
         )
     )
 
     eg_one = gather_quads({0: eg_block}, up_one)
     edb_rest = gather_rest(edb_one, down_two)
     gu_rest, eda_rest = gather_rest(gu_one, up_two), gather_rest(eda_one, up_two)
-    mixed = hidden_in + branch_sum
+    mixed = hidden_in + branch_sum.astype(F32)
     scale_two = norm_scale(mixed)
     unit_two = mixed * scale_two
     normed_two = (unit_two * gain_two).astype(BF16)
@@ -749,66 +1056,69 @@
     gate = jnp.sum(probs_rows * chosen_rows * mine, axis=1, keepdims=True)
 
     shared_active, grad_shared_out, part, grad_part, shared_dot, grad_gu = expert(
-        rows_two, gu_pieces, sd_full, cot_rows, shared_scale_rows
-    )
-    grad_part, part, eu_two, eg_two, eu_rest, eg_rest, eda_rest, edb_rest, ed_full = together(
-        grad_part, part, eu_two, eg_two, eu_rest, eg_rest, eda_rest, edb_rest, ed_full
-    )
+        core, rows_two, gu_pieces, down_full, ffs_half, cot_rows, shared_scale_rows
+    )
+    gu_cut = 2 * ffs_half * 3 // 4 // LANES * LANES
+    (gua_grad, gua_out), (gub_grad, gub_out) = row_grads(
+        rows_two, grad_gu, quads, [(0, gu_cut, True, True), (gu_cut, 2 * ffs_half, False, True)]
+    )
+    sd_grad, sd_out = column_grads(shared_active, grad_shared_out, quad, quads, False)
+    gua_grad, eda_rest, edb_rest, ed_full = together(gua_grad, eda_rest, edb_rest, ed_full)
     ed_full = place_quads(eda_rest, quad, 0, ed_full)
     ed_full = place_quads(edb_rest, quad, 0, ed_full, ed_cut)
-    gu_cut = 2 * ffs_half * 3 // 4 // LANES * LANES
-    gua_grad = row_grads(rows_two, grad_gu[:, :gu_cut])
-    gub_grad = row_grads(rows_two, grad_gu[:, gu_cut:])
-    sd_grad = column_grads(shared_active, grad_shared_out)
-    grad_part, eg_pieces, eu_pieces, ed_full, gua_grad, gub_grad, sd_grad = together(
-        grad_part, eg_one | eg_two | eg_rest, eu_one | eu_two | eu_rest, ed_full, gua_grad,
-        gub_grad, sd_grad,
-    )
-    up_keys = [key for key in gua_grad if key & up_one[0]]
-    down_keys = [key for key in gua_grad if key & down_one[0]]
-    gua_sent = send_quads(gua_grad, up_one[0], up_keys)
-    gub_sent = send_quads(gub_grad, down_one[0], down_keys)
-    sd_sent = send_quads(sd_grad, down_one[0], down_keys)
+    (
+        grad_part, part, eu_two, eg_two, eu_rest, eg_rest, ed_full, gua_grad, gua_out, gub_grad,
+        gub_out, sd_grad, sd_out, gate,
+    ) = together(
+        grad_part, part, eu_two, eg_two, eu_rest, eg_rest, ed_full, gua_grad, gua_out, gub_grad,
+        gub_out, sd_grad, sd_out, gate,
+    )
+    eg_pieces, eu_pieces = eg_one | eg_two | eg_rest, eu_one | eu_two | eu_rest
+
+    def sent(blocks, bit):
+        return [across(part, 2 * bit) for part in blocks]
+
+    gua_sent, gub_sent = sent(gua_out, up_order[0]), sent(gub_out, down_order[0])
+    sd_sent = sent(sd_out, down_order[0])
 
     lanes = jnp.arange(LANES, dtype=jnp.int32)
     lanes = jnp.where(lanes % expert_count == ep * 2 + core, lanes // expert_count, -1)[None, :]
-    active, grad_result, forward_part, packed, grad_gate_pre, grad_up_pre = expert(
+    active, grad_result, *sums, grad_gate_pre, grad_up_pre = expert(
+        core,
         rows_two,
         listed(eg_pieces) + listed(eu_pieces),
         ed_full,
+        ffe,
         cot_rows,
         gate,
         (part, grad_part, shared_dot, lanes),
     )
-    packed, forward_part, gua_sent, gub_sent, sd_sent, gua_grad, gub_grad, sd_grad = together(
-        packed, forward_part, gua_sent, gub_sent, sd_sent, gua_grad, gub_grad, sd_grad
-    )
-    packed = core_sum(packed)
+    sums, gua_sent, gub_sent, sd_sent, gua_grad, gub_grad, sd_grad = together(
+        sums, gua_sent, gub_sent, sd_sent, gua_grad, gub_grad, sd_grad
+    )
+    forward_part, packed = sums[:2], core_sum(*sums[2:])
     (
         packed, gua_grad, gub_grad, sd_grad, active, grad_result, grad_gate_pre, grad_up_pre,
     ) = together(
         packed, gua_grad, gub_grad, sd_grad, active, grad_result, grad_gate_pre, grad_up_pre,
     )
     spread = scattered(packed)
-    gua_grad = reduce_quads(add_quads(gua_grad, gua_sent, up_one[0]), up_one[1:])
-    gub_grad = reduce_quads(add_quads(gub_grad, gub_sent, down_one[0]), down_one[1:])
-    sd_grad = reduce_quads(add_quads(sd_grad, sd_sent, down_one[0]), down_one[1:])
-    ed_grad = take_quads(dot_first(active, grad_result).astype(BF16), quad, quads, 0)
-    eda_grad = {k: v[:, :ed_cut] for k, v in ed_grad.items()}
-    edb_grad = {k: v[:, ed_cut:] for k, v in ed_grad.items()}
-    gua_grad = reduce_quads(gua_grad, up_two)[0]
-    gub_grad = reduce_quads(gub_grad, down_two)[0]
-    sd_grad = reduce_quads(sd_grad, down_two)[0]
-    eda_sent = send_quads(eda_grad, up_one[0], up_keys)
-    edb_sent = send_quads(edb_grad, down_one[0], down_keys)
-    half = len(up_keys) // 2
-    keys = range(quads)
-    eg_grad = row_grads(rows_two, grad_gate_pre, up_keys)
-    eu_grad = row_grads(rows_two, grad_up_pre, down_keys[:half])
-    spread, eg_grad, eu_grad = together(spread, eg_grad, eu_grad)
-
-    grad_normed_two = flip_columns(spread[:, :width], quad)
-    side = spread[:, width : width + 4 * expert_count].reshape(rows_dev, 4, expert_count)
+    (eda_grad, eda_out), (edb_grad, edb_out) = down_grads(active, grad_result, quad, quads)
+    eda_out, edb_out, gua_grad, gub_grad, sd_grad, grad_gate_pre, grad_up_pre = together(
+        eda_out, edb_out, gua_grad, gub_grad, sd_grad, grad_gate_pre, grad_up_pre
+    )
+    eda_sent, edb_sent = sent(eda_out, up_order[0]), sent(edb_out, down_order[0])
+    gua_grad = first_sum(gua_grad, gua_sent)
+    gub_grad = first_sum(gub_grad, gub_sent)
+    sd_grad = first_sum(sd_grad, sd_sent)
+    gua_sent, gub_sent = across(gua_grad[1], 2 * up_order[1]), across(gub_grad[1], 2 * down_order[1])
+    sd_sent = across(sd_grad[1], 2 * down_order[1])
+    ((eg_grad, eg_out),) = row_grads(rows_two, grad_gate_pre, quads, [(0, ffe, True, False)])
+    ((eu_grad, eu_out),) = row_grads(rows_two, grad_up_pre, quads, [(0, ffe, False, False)])
+    spread, eg_grad, eg_out = together(spread, eg_grad, eg_out)
+
+    grad_normed_two = flip_columns(spread[:, :width], quad).astype(F32)
+    side = spread[:, width : width + 4 * expert_count].astype(F32).reshape(rows_dev, 4, expert_count)
     grad_gate_own = side[:, 0] + side[:, 1]
     shared_dot_own = jnp.sum(side[:, 2] + side[:, 3], axis=1, keepdims=True)
     grad_logit = shared_dot_own * shared_scale * (1.0 - shared_scale)
@@ -822,119 +1132,146 @@
     grad_norm_part, ff_gain_grad = norm_backward(grad_normed_two, unit_two, scale_two, gain_two)
     grad_mixed = grad_out + grad_norm_part
     (
-        branch_low, eda_grad, eda_sent, edb_grad, edb_sent, gua_grad, gub_grad, sd_grad,
-        grad_gate_pre, grad_up_pre, eg_grad, eu_grad, forward_part,
+        branch_low, eda_grad, eda_sent, edb_grad, edb_sent, gua_grad, gua_sent, gub_grad, gub_sent,
+        sd_grad, sd_sent, eg_out, eu_grad, eu_out, forward_part,
     ) = together(
-        grad_mixed.astype(BF16), eda_grad, eda_sent, edb_grad, edb_sent, gua_grad, gub_grad, sd_grad,
-        grad_gate_pre, grad_up_pre, eg_grad, eu_grad, forward_part,
+        grad_mixed.astype(BF16), eda_grad, eda_sent, edb_grad, edb_sent, gua_grad, gua_sent, gub_grad,
+        gub_sent, sd_grad, sd_sent, eg_out, eu_grad, eu_out, forward_part,
     )
     group_branch = gathered(branch_low)
-    eg_sent = send_quads(eg_grad, up_one[0], up_keys[:half])
-    eu_sent = send_quads(eu_grad, down_one[0], down_keys[:half])
-    eda_grad = reduce_quads(add_quads(eda_grad, eda_sent, up_one[0]), up_one[1:])
-    edb_grad = reduce_quads(add_quads(edb_grad, edb_sent, down_one[0]), down_one[1:])
-    eda_grad = reduce_quads(eda_grad, up_two)[0]
-    edb_grad = reduce_quads(edb_grad, down_two)[0]
-    eg_grad |= row_grads(rows_two, grad_gate_pre, [k for k in keys if k not in eg_grad])
-    eu_grad |= row_grads(rows_two, grad_up_pre, [k for k in keys if k not in eu_grad])
-    group_branch, forward_part, eg_grad, eg_sent, eu_grad, eu_sent, eda_grad, edb_grad = together(
-        group_branch, forward_part, eg_grad, eg_sent, eu_grad, eu_sent, eda_grad, edb_grad
+    eg_sent = sent(eg_out[:1], up_order[0])
+    eu_sent = sent(eu_out[:1], down_order[0])
+    forward_part = core_sum(*forward_part)
+    eda_grad = first_sum(eda_grad, eda_sent)
+    edb_grad = first_sum(edb_grad, edb_sent)
+    eda_sent, edb_sent = across(eda_grad[1], 2 * up_order[1]), across(edb_grad[1], 2 * down_order[1])
+
+    (
+        group_branch, forward_part, eg_grad, eg_out, eg_sent, eu_grad, eu_out, eu_sent, eda_grad,
+        eda_sent, edb_grad, edb_sent,
+    ) = together(
+        group_branch, forward_part, eg_grad, eg_out, eg_sent, eu_grad, eu_out, eu_sent, eda_grad,
+        eda_sent, edb_grad, edb_sent,
     )
     grad_branch = merge_core(group_branch, across(group_branch, 1), core, 0)
-    eg_sent |= send_quads(eg_grad, up_one[0], up_keys[half:])
-    eu_sent |= send_quads(eu_grad, down_one[0], down_keys[half:])
-
-    layer_sum = scattered(core_sum(forward_part))
-    grad_attended = dot_last(grad_branch, o_full).astype(BF16)
+    eg_sent = eg_sent + sent(eg_out[1:], up_order[0])
+    eu_sent = eu_sent + sent(eu_out[1:], down_order[0])
+
+    layer_sum = scattered(forward_part)
+    grad_attended = dot_last(grad_branch, down_full[ffs_half:]).astype(BF16)
     grad_query, grad_own, *grad_before = attend_back(
         query, grad_attended, log_total, before, key_value, key_place, low, high, cosine, sine
     )
-    def back_to_cores(summed, cut_axis, join_axis):
-        keep, other = split_core(summed, core, cut_axis)
-        return merge_core(keep, across(other, 1), core, join_axis).astype(F32)
-
-    def back_to_experts(summed):
-        keep, other = split_core(summed, core, 0)
-        arrived = across(other, 1)
-        return jnp.stack(
-            [jnp.where(core == 0, keep, arrived), jnp.where(core == 0, arrived, keep)]
+    (
+        grad_query, grad_before, grad_branch, eg_grad, eu_grad, gua_grad, gua_sent, gub_grad,
+        gub_sent, sd_grad, sd_sent,
+    ) = together(
+        grad_query, grad_before, grad_branch, eg_grad, eu_grad, gua_grad, gua_sent, gub_grad,
+        gub_sent, sd_grad, sd_sent,
+    )
+    arrived = [shifted(sent, step - back) for step, sent in enumerate(grad_before)]
+    cut = eg_grad[1].shape[0] // 2
+    eg_grad = [
+        add_low(eg_grad[0], eg_sent[0]),
+        add_low(eg_grad[1][:cut], eg_sent[1][:cut]),
+        add_low(eg_grad[1][cut:], eg_sent[1][cut:]),
+    ]
+    eu_grad = [
+        add_low(eu_grad[0], eu_sent[0]),
+        add_low(eu_grad[1][:cut], eu_sent[1][:cut]),
+        add_low(eu_grad[1][cut:], eu_sent[1][cut:]),
+    ]
+    eg_rest = across(eg_grad[1], 2 * up_order[1])
+    arrived, eg_grad, eu_grad, grad_branch = together(arrived, eg_grad, eu_grad, grad_branch)
+    eu_rest = across(eu_grad[1], 2 * down_order[1])
+    (*partial, att_gain_part, bias_part), (qkv_a_grad, qkv_a_out), (qkv_b_grad, qkv_b_out) = collect(
+        core, grad_query, grad_own, cosine, sine, rows_one, arrived, qkv_a, qkv_b
+    )
+    partial, qkv_a_out, qkv_b_out, eg_grad, eg_rest, eu_grad, eu_rest = together(
+        partial, qkv_a_out, qkv_b_out, eg_grad, eg_rest, eu_grad, eu_rest
+    )
+    eg_last, eu_last = across(eg_grad[2], 2 * up_order[1]), across(eu_grad[2], 2 * down_order[1])
+    qkv_a_sent, qkv_b_sent = sent(qkv_a_out, up_order[0]), sent(qkv_b_out, down_order[0])
+    partial_sum = core_sum(*partial)
+
+    (
+        partial_sum, att_gain_part, bias_part, grad_branch, qkv_a_grad, qkv_b_grad, eda_grad,
+        eda_sent, edb_grad, edb_sent,
+    ) = together(
+        partial_sum, att_gain_part, bias_part, grad_branch, qkv_a_grad, qkv_b_grad, eda_grad,
+        eda_sent, edb_grad, edb_sent,
+    )
+    grad_normed_one = scattered(partial_sum)
+    o_grad, o_out = column_grads(attended, grad_branch, quad, quads, False)
+    att_gain_part = flip_columns(att_gain_part[0], quad) / gain_one
+    late = jnp.concatenate([att_gain_part, ff_gain_grad, router_grad.T.reshape(-1)])
+    late = sum_everywhere(late, [], ep_masks[:1])
+    (
+        late, qkv_a_sent, qkv_b_sent, o_out, eg_last, eu_last, eda_sent, edb_sent, gua_sent,
+        gub_sent, sd_sent,
+    ) = together(
+        late, qkv_a_sent, qkv_b_sent, o_out, eg_last, eu_last, eda_sent, edb_sent, gua_sent,
+        gub_sent, sd_sent,
+    )
+    eg_rest = jnp.concatenate([eg_rest, eg_last], axis=0)
+    eu_rest = jnp.concatenate([eu_rest, eu_last], axis=0)
+    late = sum_everywhere(late, [], ep_masks[1:])
+    bias_part = bias_part.reshape(3, head_width)
+    bias_part = jnp.concatenate(
+        [jnp.where(core == 0, bias_part, 0.0), jnp.where(core == 0, 0.0, bias_part)], axis=1
+    )
+    late = sum_everywhere(jnp.concatenate([late, bias_part.reshape(-1)]), [1], [])
+    qkv_a_grad = first_sum(qkv_a_grad, qkv_a_sent)
+    qkv_b_grad = first_sum(qkv_b_grad, qkv_b_sent)
+    qkv_a_rest = across(qkv_a_grad[1], 2 * up_order[1])
+    qkv_b_rest = across(qkv_b_grad[1], 2 * down_order[1])
+    o_grad = first_sum(o_grad, sent(o_out, down_order[0]))
+    o_rest = across(o_grad[1], 2 * down_order[1])
+    late = sum_everywhere(late, quad_masks, [])
+    eg_grad = merge(core, *finished(*rest_parts(eg_grad[0], eg_rest, up_order), 0), None)
+    eda_mine, eda_arrived = finished(*rest_parts(eda_grad[0], eda_sent, up_order), 0)
+    edb_mine, edb_arrived = finished(*rest_parts(edb_grad[0], edb_sent, down_order), 0)
+    ed_grad = jnp.concatenate(
+        [merge(core, eda_mine, eda_arrived, None), merge(core, edb_mine, edb_arrived, None)], axis=2
+    )
+    gua_mine, gua_arrived = finished(*rest_parts(gua_grad[0], gua_sent, up_order), 0)
+    gub_mine, gub_arrived = finished(*rest_parts(gub_grad[0], gub_sent, down_order), 0)
+    sd_mine, sd_arrived = finished(*rest_parts(sd_grad[0], sd_sent, down_order), 1)
+    gu_mine = jnp.concatenate([gua_mine, gub_mine], axis=1)
+    gu_arrived = jnp.concatenate([gua_arrived, gub_arrived], axis=1)
+    sg_grad, su_grad = [
+        merge_core(
+            gu_mine[:, part * ffs_half : (part + 1) * ffs_half],
+            gu_arrived[:, part * ffs_half : (part + 1) * ffs_half],
+            core,
+            1,
         ).astype(F32)
-
+        for part in range(2)
+    ]
+    sd_grad = merge(core, sd_mine, sd_arrived, 0)
+    layer_out = (mixed + layer_sum.astype(F32)).astype(BF16)
+    qkv_a_mine, qkv_a_arrived = finished(*rest_parts(qkv_a_grad[0], qkv_a_rest, up_order), 0)
+    qkv_b_mine, qkv_b_arrived = finished(*rest_parts(qkv_b_grad[0], qkv_b_rest, down_order), 0)
+    o_mine, o_arrived = finished(*rest_parts(o_grad[0], o_rest, down_order), 1)
     (
-        grad_query, grad_before, grad_branch, eg_grad, eu_grad, gua_grad, gub_grad, sd_grad,
-        eda_grad, edb_grad,
+        grad_normed_one, qkv_a_mine, qkv_a_arrived, qkv_b_mine, qkv_b_arrived, o_mine, o_arrived,
+        late, eu_rest, eg_grad, ed_grad, layer_out, sg_grad, su_grad, sd_grad,
     ) = together(
-        grad_query, grad_before, grad_branch, eg_grad, eu_grad, gua_grad, gub_grad, sd_grad,
-        eda_grad, edb_grad,
-    )
-    arrived = [shifted(sent, step - back) for step, sent in enumerate(grad_before)]
-    eg_grad = reduce_quads(add_quads(eg_grad, eg_sent, up_one[0]), up_one[1:])
-    eu_grad = reduce_quads(add_quads(eu_grad, eu_sent, down_one[0]), down_one[1:])
-    eg_rest = send_quads(eg_grad, up_two[0], [key for key in eg_grad if key & up_two[0]])
-    gu_grad = jnp.concatenate([gua_grad, gub_grad], axis=1)
-    sg_grad = back_to_cores(gu_grad[:, :ffs_half], 0, 1)
-    su_grad = back_to_cores(gu_grad[:, ffs_half:], 0, 1)
-    sd_grad = back_to_cores(sd_grad, 1, 0)
-    o_grad = column_grads(attended, grad_branch)
-    o_sent = send_quads(o_grad, down_order[0], down_keys)
-    arrived, eg_grad, eu_grad, o_grad, sg_grad, su_grad, sd_grad, eda_grad, edb_grad = together(
-        arrived, eg_grad, eu_grad, o_grad, sg_grad, su_grad, sd_grad, eda_grad, edb_grad
-    )
-    eu_keys = [key for key in eu_grad if key & down_two[0]]
-    eu_cut = eu_block.shape[0] // 2
-    eu_rest = send_quads({key: eu_grad[key][:eu_cut] for key in eu_keys}, down_two[0], eu_keys)
-    grad_lin, partial, att_gain_part, bias_part = collect(
-        grad_query, grad_own, cosine, sine, rows_one, arrived, qkv_a, qkv_b
-    )
-    partial, eg_rest, eu_rest, eu_grad, o_grad, o_sent = together(
-        partial, eg_rest, eu_rest, eu_grad, o_grad, o_sent
-    )
-    partial_sum = core_sum(partial)
-
-    (
-        partial_sum, grad_lin, att_gain_part, bias_part, eg_grad, eg_rest, eu_grad, o_grad, o_sent,
-    ) = together(
-        partial_sum, grad_lin, att_gain_part, bias_part, eg_grad, eg_rest, eu_grad, o_grad, o_sent,
-    )
-    grad_normed_one = scattered(partial_sum)
-    eu_last = send_quads({key: eu_grad[key][eu_cut:] for key in eu_keys}, down_two[0], eu_keys)
-    grad_lin_a, grad_lin_b = grad_lin[:, :qkv_cut], grad_lin[:, qkv_cut:]
-    qkv_a_grad = reduce_quads(row_grads(rows_one, grad_lin_a), up_order)[0]
-    qkv_b_grad = reduce_quads(row_grads(rows_one, grad_lin_b), down_order)[0]
-    o_grad = add_quads(o_grad, o_sent, down_order[0])
-    o_grad = reduce_quads(o_grad, down_order[1:])[0]
-    att_gain_part = flip_columns(att_gain_part[0], quad) / gain_one
-    late = jnp.concatenate([bias_part[0], att_gain_part, ff_gain_grad, router_grad.T.reshape(-1)])
-    late = sum_everywhere(late, quad_masks, [])
-    bias_part = late[: 3 * head_width]
-    late = sum_everywhere(late[3 * head_width :], [1], ep_masks)
-    (
-        grad_normed_one, o_grad, qkv_a_grad, qkv_b_grad, bias_part, late, eu_last, eg_grad, eg_rest,
-        eda_grad, edb_grad, layer_sum,
-    ) = together(
-        grad_normed_one, o_grad, qkv_a_grad, qkv_b_grad, bias_part, late, eu_last, eg_grad, eg_rest,
-        eda_grad, edb_grad, layer_sum,
-    )
-    eg_grad = reduce_quads(add_quads(eg_grad, eg_rest, up_two[0]), up_two[1:])[0]
-    eg_grad = back_to_experts(eg_grad)
-    ed_grad = back_to_experts(jnp.concatenate([eda_grad, edb_grad], axis=1))
-    layer_out = (mixed + layer_sum).astype(BF16)
-    bias_mine = merge_core(
-        bias_part.reshape(3, head_width), across(bias_part, 1).reshape(3, head_width), core, 1
-    )
-    eu_rest = {key: jnp.concatenate([eu_rest[key], eu_last[key]], axis=0) for key in eu_rest}
-    eu_grad = reduce_quads(add_quads(eu_grad, eu_rest, down_two[0]), down_two[1:])[0]
-    qkv_grad = jnp.concatenate([qkv_a_grad, qkv_b_grad], axis=1)
+        grad_normed_one, qkv_a_mine, qkv_a_arrived, qkv_b_mine, qkv_b_arrived, o_mine, o_arrived,
+        late, eu_rest, eg_grad, ed_grad, layer_out, sg_grad, su_grad, sd_grad,
+    )
+    eu_grad = merge(core, *finished(*rest_parts(eu_grad[0], eu_rest, down_order), 0), None)
+    qkv_mine = jnp.concatenate([qkv_a_mine, qkv_b_mine], axis=1)
+    qkv_arrived = jnp.concatenate([qkv_a_arrived, qkv_b_arrived], axis=1)
+    q_grad, k_grad, v_grad = [merge(core, qkv_mine, qkv_arrived, 1, part, 3) for part in range(3)]
+    o_grad = merge(core, o_mine, o_arrived, 0)
     att_gain_grad, ff_gain_grad = late[:width], late[width : 2 * width]
-    router_grad = late[2 * width :].reshape(expert_count + 1, width)
+    router_grad = late[2 * width : (expert_count + 3) * width].reshape(expert_count + 1, width)
+    bias_mine = late[(expert_count + 3) * width :].reshape(3, 2 * head_width)
     grad_norm_one, _ = norm_backward(
-        flip_columns(grad_normed_one, quad), unit_one, scale_one, gain_one
+        flip_columns(grad_normed_one, quad).astype(F32), unit_one, scale_one, gain_one
     )
     input_grad = grad_mixed + grad_norm_one
-    q_grad, k_grad, v_grad = [
-        back_to_cores(qkv_grad[:, part * head_width : (part + 1) * head_width], 0, 1)
-        for part in range(3)
-    ]
     return (
         layer_out,
         input_grad,
@@ -945,7 +1282,7 @@
         bias_mine[1],
         v_grad,
         bias_mine[2],
-        back_to_cores(o_grad, 1, 0),
+        o_grad,
         ff_gain_grad,
         router_grad[:expert_count].T,
         router_grad[expert_count],
@@ -953,7 +1290,7 @@
         su_grad,
         sd_grad,
         eg_grad,
-        back_to_experts(eu_grad),
+        eu_grad,
         ed_grad,
     )
 

time: 749 us -> 716 us (0.956)
  Pallas kernels: 117 us -> 198 us
  matrix products: 89.8 us -> 13.1 us
  other arithmetic: 146 us -> 92.2 us
  waiting for transfers between devices: 228 us -> 259 us
  starting transfers between devices: 76.8 us -> 67.5 us
    pallas_call x6 -> x35, Pallas kernels: 117 us -> 198 us  [the longest x32 179 us: run(): pl.pallas_call(kernel, grid_spec=pltpu.PrefetchScalarGridSpec(num_scalar_...]
    dot_general x34 -> x1, matrix products: 80.5 us -> 0.84 us  [dot_first(): lax.dot_general(left, right, (((0,), (0,)), ((), ())), preferred_element_...]
    ppermute x87 -> x75, waiting for transfers between devices: 154 us -> 223 us  [across(): return lax.ppermute(block, 'grp', [(i, i ^ mask) for i in range(count)])]
    convert_element_type x36 -> x15, other arithmetic: 72.4 us -> 33.3 us  [the longest x12 28.5 us: add_low(): return (left.astype(F32) + right.astype(F32)).astype(BF16)]
    reduce_scatter x4, waiting for transfers between devices: 34.2 us -> 0.05 us  [scattered(): return lax.psum_scatter(values, 'ep', scatter_dimension=0, tiled=True)]
    select_n x16 -> x1, other arithmetic: 20.2 us -> 0.02 us  [local(): jnp.where(core == 0, bias_part, 0.0)]
    ppermute x87 -> x75, starting transfers between devices: 69.4 us -> 58.3 us  [across(): return lax.ppermute(block, 'grp', [(i, i ^ mask) for i in range(count)])]
    dynamic_update_slice x18 -> x14, local copies, waits for them, and re-layouts: 28.2 us -> 17.6 us  [place_quads(): whole = lax.dynamic_update_slice(whole, pieces[key], start)]
  transfers between devices with their start and end apart: 99 -> 87, of which waited for: 32 -> 32; matrix products, arithmetic and copies ran while one was open for 33% -> 18% of each run, Pallas kernels for 16% -> 27%
where the time goes in v4:
time: 716 us; the launch traced here: 706 us
  waiting for transfers between devices  259 us (36%)
  Pallas kernels  198 us (28%)
  other arithmetic  92.2 us (13%)
  starting transfers between devices  67.5 us (9%)
  local copies, waits for them, and re-layouts  60.4 us (8%)
  between operations  16.5 us (2%)
  matrix products  13.1 us (2%)
    ppermute x75, waiting for transfers between devices, across(): return lax.ppermute(block, 'grp', [(i, i ^ mask) for i in range(count)])  223 us
    pallas_call x32, Pallas kernels, run(): pl.pallas_call(kernel, grid_spec=pltpu.PrefetchScalarGridSpec(num_scalar_...  179 us
    ppermute x75, starting transfers between devices, across(): return lax.ppermute(block, 'grp', [(i, i ^ mask) for i in range(count)])  58.3 us
    unnamed x267, local copies, waits for them, and re-layouts  30.7 us
    convert_element_type x12, other arithmetic, add_low(): return (left.astype(F32) + right.astype(F32)).astype(BF16)  28.5 us
    ppermute x2, waiting for transfers between devices, shifted(): return lax.ppermute(values, 'grp', route)  26.4 us
    dynamic_update_slice x14, local copies, waits for them, and re-layouts, place_quads(): whole = lax.dynamic_update_slice(whole, pieces[key], start)  17.6 us
  transfers between devices with their start and end apart: 87, of which 32 were waited for; matrix products, arithmetic and copies ran while one was open for 18% of the time, Pallas kernels for 27%

profile of v4, /device:TPU:0, one launch (start us, length us, event | category | flops | bytes accessed | tf_op | source)
XLA Modules:
  0.0 706.3 jit_solution(3595642298898937200)
XLA Ops:
  13.2 2.6 collective-permute-start.1
  29.5 5.9 collective-permute-done.3.rest_6_.rest_7_
  44.1 24.1 %collective-permute-done.10.rest_3_.rest_4_ = bf16[512,384]{1,0:T(8,128)(2,1)} collective-permute-done((bf16[512,384]{1,0:T(8,128)(2,1)S(1)}, bf16[512,384]{1,0:T(8,128)(2,1)}, u32[]{:S(2)}, u32[]{:S(2)}) %collective-permute-start.10) | collective-permute-done | bytes 393248 | tf_op jit(solution)/shard_map/ppermute | solution.py:38
  71.0 3.1 collective-permute-done.14
  74.1 2.6 broadcast_select_fusion.7
  78.0 6.9 project.1
  84.9 9.1 %collective-permute-done.15 = bf16[960,512]{1,0:T(8,128)(2,1)S(1)} collective-permute-done((bf16[960,512]{1,0:T(8,128)(2,1)}, bf16[960,512]{1,0:T(8,128)(2,1)S(1)}, u32[]{:S(2)}, u32[]{:S(2)}) %collective-permute-start.15) | collective-permute-done | bytes 983072 | tf_op jit(solution)/shard_map/ppermute | solution.py:38
  94.1 2.7 collective-permute-start.16
  101.5 2.6 collective-permute-done.17.rest_2_
  104.2 14.7 %collective-permute-done.16.rest_0_ = bf16[1024,512]{1,0:T(8,128)(2,1)S(1)} collective-permute-done((bf16[1024,512]{1,0:T(8,128)(2,1)S(1)}, bf16[1024,512]{1,0:T(8,128)(2,1)S(1)}, u32[]{:S(2)}, u32[]{:S(2)}) %collective-permute-start.16) | collective-permute-done | bytes 1048608 | tf_op jit(solution)/shard_map/ppermute | solution.py:889
  124.8 6.8 attend.1
  133.5 3.3 convolution_convert_fusion.1
  149.1 3.2 broadcast_in_dim.32
  157.6 37.0 %collective-permute-done.23 = bf16[352,1024]{1,0:T(8,128)(2,1)S(1)} collective-permute-done((bf16[352,1024]{1,0:T(8,128)(2,1)S(1)}, bf16[352,1024]{1,0:T(8,128)(2,1)S(1)}, u32[]{:S(2)}, u32[]{:S(2)}) %collective-permute-start.23) | collective-permute-done | bytes 720928 | tf_op jit(solution)/shard_map/ppermute | solution.py:38
  205.8 2.9 broadcast_select_fusion.1
  214.2 34.9 %collective-permute-done.27 = bf16[352,1024]{1,0:T(8,128)(2,1)S(1)} collective-permute-done((bf16[352,1024]{1,0:T(8,128)(2,1)S(1)}, bf16[352,1024]{1,0:T(8,128)(2,1)S(1)}, u32[]{:S(2)}, u32[]{:S(2)}) %collective-permute-start.27) | collective-permute-done | bytes 720928 | tf_op jit(solution)/shard_map/ppermute | solution.py:38
  259.8 2.6 pad_maximum_fusion.2.x_ref
  264.7 27.4 %shared.1 = (bf16[1024,704]{1,0:T(8,128)(2,1)}, bf16[1024,2048]{1,0:T(8,128)(2,1)}, bf16[1024,2048]{1,0:T(8,128)(2,1)}, bf16[1024,2048]{1,0:T(8,128)(2,1)}, f32[...) custom-call(s32[1]{0:T(128)} %bitcast.core_ref, bf16[1024,2048]{1,0:T(8,128)(2,1)} %pad_maximum_fusion.2.x_ref, ...), custom_call_target="tpu_custom_call" | custom-call | flops 17716740096 | bytes 35266564 | tf_op jit(solution)/shard_map/shared/pallas_call | solution.py:190
  292.1 10.2 %row_grads.3 = (bf16[512,1024]{1,0:T(8,128)(2,1)S(1)}, bf16[512,1024]{1,0:T(8,128)(2,1)S(1)}, bf16[1024,1024]{1,0:T(8,128)(2,1)S(1)}, bf16[512,384]{1,0:T(8,128)...) custom-call(bf16[1024,2048]{1,0:T(8,128)(2,1)} %pad_maximum_fusion.2.x_ref, ...), custom_call_target="tpu_custom_call" | custom-call | flops 5905580032 | bytes 12845056 | tf_op jit(solution)/shard_map/row_grads/pallas_call | solution.py:190
  309.2 5.6 column_grads.2
  316.0 2.5 collective-permute-done.33.rest_7_
  323.9 51.8 %expert.1 = (bf16[1024,1408]{1,0:T(8,128)(2,1)}, bf16[1024,2048]{1,0:T(8,128)(2,1)}, bf16[768,2048]{1,0:T(8,128)(2,1)}, bf16[512,2048]{1,0:T(8,128)(2,1)}, bf16[...) custom-call(s32[1]{0:T(128)} %bitcast.core_ref, ...), custom_call_target="tpu_custom_call" | custom-call | flops 35433480192 | bytes 58008068 | tf_op jit(solution)/shard_map/expert/pallas_call | solution.py:190
  375.8 4.5 collective-permute-done.38.right_ref
  387.4 11.2 %down_grads.1 = (bf16[352,1024]{1,0:T(8,128)(2,1)S(1)}, bf16[352,1024]{1,0:T(8,128)(2,1)S(1)}, bf16[704,1024]{1,0:T(8,128)(2,1)}, bf16[352,1024]{1,0:T(8,128)(2,...) custom-call(s32[1]{0:T(128)} %bitcast.13.quad_ref, bf16[1024,1408]{1,0:T(8,128)(2,1)} %get-tuple-element.505.act_ref, ...), custom_call_target="tpu_custom_call" | custom-call | flops 5905580032 | bytes 12845056 | tf_op jit(solution)/shard_map/down_grads/pallas_call | solution.py:805
  398.6 3.9 add_convert_fusion.12
  406.8 3.8 add_convert_fusion.2
  413.5 10.1 %row_grads.5 = (bf16[512,1408]{1,0:T(8,128)(2,1)S(1)}, bf16[512,1408]{1,0:T(8,128)(2,1)S(1)}, bf16[512,1408]{1,0:T(8,128)(2,1)S(1)}, bf16[512,1408]{1,0:T(8,128)(2,1)S(1)}) custom-call(bf16[1024,2048]{1,0:T(8,128)(2,1)} %pad_maximum_fusion.2.x_ref, bf16[1024,1408]{1,0:T(8,128)(2,1)} %get-tuple-element.540.grad_ref), custom_call_target="tpu_custom_call" | custom-call | flops 5905580032 | bytes 12845056 | tf_op jit(solution)/shard_map/row_grads/pallas_call | solution.py:190
  427.0 10.2 %row_grads.4 = (bf16[512,1408]{1,0:T(8,128)(2,1)S(1)}, bf16[512,1408]{1,0:T(8,128)(2,1)S(1)}, bf16[512,1408]{1,0:T(8,128)(2,1)S(1)}, bf16[512,1408]{1,0:T(8,128)(2,1)S(1)}) custom-call(bf16[1024,2048]{1,0:T(8,128)(2,1)} %pad_maximum_fusion.2.x_ref, bf16[1024,1408]{1,0:T(8,128)(2,1)} %get-tuple-element.517.grad_ref), custom_call_target="tpu_custom_call" | custom-call | flops 5905580032 | bytes 12845056 | tf_op jit(solution)/shard_map/row_grads/pallas_call | solution.py:190
  448.8 11.6 %collective-permute-done.39 = bf16[704,1024]{1,0:T(8,128)(2,1)} collective-permute-done((bf16[704,1024]{1,0:T(8,128)(2,1)}, bf16[704,1024]{1,0:T(8,128)(2,1)}, u32[]{:S(2)}, u32[]{:S(2)}) %collective-permute-start.39) | collective-permute-done | bytes 1441824 | tf_op jit(solution)/shard_map/ppermute | solution.py:38
  460.4 6.1 collective-permute-done.40
  468.8 3.5 add_convert_fusion.8
  473.5 3.2 add_convert_fusion.10
  479.5 37.0 %collective-permute-done.48.arrived_ref = bf16[352,1024]{1,0:T(8,128)(2,1)} collective-permute-done((bf16[352,1024]{1,0:T(8,128)(2,1)}, bf16[352,1024]{1,0:T(8,128)(2,1)}, u32[]{:S(2)}, u32[]{:S(2)}) %collective-permute-start.48) | collective-permute-done | bytes 720928 | tf_op jit(solution)/shard_map/ppermute | solution.py:38
  524.1 2.6 pad_maximum_fusion.3.grad_ref
  526.7 2.7 convolution_convert_fusion.2.grad_ref
  529.4 13.7 %attend_back.1 = (bf16[1024,256]{1,0:T(8,128)(2,1)S(1)}, f32[1024,512]{1,0:T(8,128)}, bf16[1024,512]{1,0:T(8,128)(2,1)S(1)}) custom-call(bf16[1024,256]{1,0:T(8,128)(2,1)S(1)} %copy-done.66, bf16[1024,256]{1,0:T(8,128)(2,1)S(1)} %convolution_convert_fusion.2.grad_ref, f32[1024,256]{1,0:T(8,128)S(1)} %copy-done.63, bf16[1024,512]{1,0:T(8,128)(2,1)} %copy-done.50, ...), custom_call_target="tpu_custom_call" | custom-call | flops 3355443200 | bytes 8929280 | tf_op jit(solution)/shard_map/attend_back/pallas_call | solution.py:190
  544.5 8.7 %collective-permute-done.51 = bf16[512,1408]{1,0:T(8,128)(2,1)} collective-permute-done((bf16[512,1408]{1,0:T(8,128)(2,1)}, bf16[512,1408]{1,0:T(8,128)(2,1)}, u32[]{:S(2)}, u32[]{:S(2)}) %collective-permute-start.51) | collective-permute-done | bytes 1441824 | tf_op jit(solution)/shard_map/ppermute | solution.py:38
  553.2 2.8 add_convert_fusion.6
  558.5 2.9 add_convert_fusion.4
  563.1 11.7 %collective-permute-done.50.rest_0_ = bf16[1024,512]{1,0:T(8,128)(2,1)S(1)} collective-permute-done((bf16[1024,512]{1,0:T(8,128)(2,1)S(1)}, bf16[1024,512]{1,0:T(8,128)(2,1)S(1)}, u32[]{:S(2)}, u32[]{:S(2)}) %collective-permute-start.50) | collective-permute-done | bytes 1048608 | tf_op jit(solution)/shard_map/ppermute | solution.py:889
  575.7 15.4 %collect.1 = (bf16[768,2048]{1,0:T(8,128)(2,1)}, bf16[512,2048]{1,0:T(8,128)(2,1)}, f32[1,2048]{1,0:T(1,128)}, f32[1,768]{1,0:T(1,128)}, bf16[512,384]{1,0:T(8,1...) custom-call(s32[1]{0:T(128)} %bitcast.core_ref, ...), custom_call_target="tpu_custom_call" | custom-call | flops 6442450944 | bytes 20458500 | tf_op jit(solution)/shard_map/collect/pallas_call | solution.py:190
  602.5 4.0 add_rows.7
  616.5 13.6 %collective-permute-done.59 = bf16[256,1408]{1,0:T(8,128)(2,1)} collective-permute-done((bf16[256,1408]{1,0:T(8,128)(2,1)}, bf16[256,1408]{1,0:T(8,128)(2,1)}, u32[]{:S(2)}, u32[]{:S(2)}) %collective-permute-start.59) | collective-permute-done | bytes 720928 | tf_op jit(solution)/shard_map/ppermute | solution.py:38
  641.9 8.8 %collective-permute-done.68 = f32[22528]{0:T(1024)S(1)} collective-permute-done((f32[22528]{0:T(1024)S(1)}, f32[22528]{0:T(1024)S(1)}, u32[]{:S(2)}, u32[]{:S(2)}) %collective-permute-start.68) | collective-permute-done | bytes 90144 | tf_op jit(solution)/shard_map/ppermute | solution.py:94
  652.2 2.9 collective-permute-start.70
  660.2 2.6 pad_maximum_fusion.8.arrived_ref
  677.0 5.9 collective-permute-done.66.arrived_ref
  694.3 3.3 fusion.7
  (595 shorter events, 220.7 us)
Async XLA Ops:
  7.2 62.3 %all-gather.5.cloned.1.call-start = ((), (), s32[]{:S(2)}) async-start(), calls=%async_computation.4 | async-start | bytes 2621440 | tf_op jit(solution)/shard_map/all_gather | solution.py:892
  12.3 124.4 %all-gather.7.cloned.1.call-start = ((), (), s32[]{:S(2)}) async-start(), calls=%async_computation.5 | async-start | bytes 2785280 | tf_op jit(solution)/shard_map/all_gather | solution.py:892
  36.7 32.7 %collective-permute-start.12 = (bf16[960,512]{1,0:T(8,128)(2,1)}, bf16[960,512]{1,0:T(8,128)(2,1)}, u32[]{:S(2)}, u32[]{:S(2)}) collective-permute-start(bf16[960,512]{1,0:T(8,128)(2,1)} %pad_maximum_fusion.10), channel_id=1, source_target_pairs={{0,16},{4,20},{8,24},{12,28},{16,0},{20,4},{24,8},{28,12},{1,17},{... | collective-permute-start | bytes 2949128 | tf_op jit(solution)/shard_map/ppermute | solution.py:38
  38.2 31.2 %collective-permute-start.13 = (bf16[960,512]{1,0:T(8,128)(2,1)}, bf16[960,512]{1,0:T(8,128)(2,1)}, u32[]{:S(2)}, u32[]{:S(2)}) collective-permute-start(bf16[960,512]{1,0:T(8,128)(2,1)} %pad_maximum_fusion.10), channel_id=1, source_target_pairs={{0,8},{4,12},{8,0},{12,4},{16,24},{20,28},{24,16},{28,20},{1,9},{5... | collective-permute-start | bytes 2949128 | tf_op jit(solution)/shard_map/ppermute | solution.py:38
  41.7 27.8 %collective-permute-start.11 = (bf16[512,384]{1,0:T(8,128)(2,1)S(1)}, bf16[512,384]{1,0:T(8,128)(2,1)}, u32[]{:S(2)}, u32[]{:S(2)}) collective-permute-start(bf16[512,384]{1,0:T(8,128)(2,1)S(1)} %collective-permute-done.3.rest_6_.rest_7_), channel_id=1, source_target_pairs={{0,8},{4,12},{8,0},{12,4},{16,24},{20,28},{24,16},{28,20},{1,9},{5... | collective-permute-start | bytes 1179656 | tf_op jit(solution)/shard_map/ppermute | solution.py:38
  69.6 126.6 %reduce-scatter.5.cloned.1.call-start = ((), (), s32[]{:S(2)}) async-start(), calls=%async_computation.6 | async-start | bytes 2621440 | tf_op jit(solution)/shard_map/reduce_scatter | solution.py:895
  70.2 33.9 %collective-permute-start.17 = (bf16[512,1408]{1,0:T(8,128)(2,1)}, bf16[512,1408]{1,0:T(8,128)(2,1)S(1)}, u32[]{:S(2)}, u32[]{:S(2)}) collective-permute-start(bf16[512,1408]{1,0:T(8,128)(2,1)} %pad_maximum_fusion.5.rest_0_), channel_id=1, source_target_pairs={{0,16},{4,20},{8,24},{12,28},{16,0},{20,4},{24,8},{28,12},{1,17},{... | collective-permute-start | bytes 4325384 | tf_op jit(solution)/shard_map/ppermute | solution.py:38
  144.8 107.3 %all-gather.9.cloned.1.call-start = ((), (), s32[]{:S(2)}) async-start(), calls=%async_computation.7 | async-start | bytes 2621440 | tf_op jit(solution)/shard_map/all_gather | solution.py:892
  144.9 51.3 %collective-permute-start.21 = (bf16[512,2176]{1,0:T(8,128)(2,1)}, bf16[512,2176]{1,0:T(8,128)(2,1)}, u32[]{:S(2)}, u32[]{:S(2)}) collective-permute-start(bf16[512,2176]{1,0:T(8,128)(2,1)} %all-gather.7.cloned.1.call-done), channel_id=1, source_target_pairs={{0,4},{4,0},{8,12},{12,8},{16,20},{20,16},{24,28},{28,24},{1,5},{5... | collective-permute-start | bytes 6684680 | tf_op jit(solution)/shard_map/ppermute | solution.py:38
  145.1 51.1 %collective-permute-start.22 = (bf16[512,1408]{1,0:T(8,128)(2,1)}, bf16[512,1408]{1,0:T(8,128)(2,1)}, u32[]{:S(2)}, u32[]{:S(2)}) collective-permute-start(bf16[512,1408]{1,0:T(8,128)(2,1)} %pad_maximum_fusion.5.rest_0_), channel_id=1, source_target_pairs={{0,8},{4,12},{8,0},{12,4},{16,24},{20,28},{24,16},{28,20},{1,9},{5... | collective-permute-start | bytes 4325384 | tf_op jit(solution)/shard_map/ppermute | solution.py:38
  146.8 49.3 %collective-permute-start.25 = (bf16[512,1408]{1,0:T(8,128)(2,1)}, bf16[512,1408]{1,0:T(8,128)(2,1)}, u32[]{:S(2)}, u32[]{:S(2)}) collective-permute-start(bf16[512,1408]{1,0:T(8,128)(2,1)} %get-tuple-element.472.rest_4_), channel_id=1, source_target_pairs={{0,16},{4,20},{8,24},{12,28},{16,0},{20,4},{24,8},{28,12},{1,17},{... | collective-permute-start | bytes 4325384 | tf_op jit(solution)/shard_map/ppermute | solution.py:38
  148.1 46.5 %collective-permute-start.23 = (bf16[352,1024]{1,0:T(8,128)(2,1)S(1)}, bf16[352,1024]{1,0:T(8,128)(2,1)S(1)}, u32[]{:S(2)}, u32[]{:S(2)}) collective-permute-start(bf16[352,1024]{1,0:T(8,128)(2,1)S(1)} %copy-done.83), channel_id=1, source_target_pairs={{0,8},{4,12},{8,0},{12,4},{16,24},{20,28},{24,16},{28,20},{1,9},{5... | collective-permute-start | bytes 2162696 | tf_op jit(solution)/shard_map/ppermute | solution.py:38
  148.4 47.7 %collective-permute-start.24 = (bf16[352,1024]{1,0:T(8,128)(2,1)S(1)}, bf16[352,1024]{1,0:T(8,128)(2,1)}, u32[]{:S(2)}, u32[]{:S(2)}) collective-permute-start(bf16[352,1024]{1,0:T(8,128)(2,1)S(1)} %copy-done.83), channel_id=1, source_target_pairs={{0,16},{4,20},{8,24},{12,28},{16,0},{20,4},{24,8},{28,12},{1,17},{... | collective-permute-start | bytes 2162696 | tf_op jit(solution)/shard_map/ppermute | solution.py:38
  200.3 240.3 %reduce-scatter.7.cloned.1.call-start = ((), (), s32[]{:S(2)}) async-start(), calls=%async_computation.8 | async-start | bytes 2785280 | tf_op jit(solution)/shard_map/reduce_scatter | solution.py:895
  200.7 49.4 %collective-permute-start.26 = (bf16[512,1408]{1,0:T(8,128)(2,1)}, bf16[512,1408]{1,0:T(8,128)(2,1)S(1)}, u32[]{:S(2)}, u32[]{:S(2)}) collective-permute-start(bf16[512,1408]{1,0:T(8,128)(2,1)} %get-tuple-element.468.rest_0_), channel_id=1, source_target_pairs={{0,8},{4,12},{8,0},{12,4},{16,24},{20,28},{24,16},{28,20},{1,9},{5... | collective-permute-start | bytes 4325384 | tf_op jit(solution)/shard_map/ppermute | solution.py:38
  201.1 51.0 %collective-permute-start.28 = (bf16[512,1408]{1,0:T(8,128)(2,1)}, bf16[512,1408]{1,0:T(8,128)(2,1)}, u32[]{:S(2)}, u32[]{:S(2)}) collective-permute-start(bf16[512,1408]{1,0:T(8,128)(2,1)} %collective-permute-done.22.rest_1_), channel_id=1, source_target_pairs={{0,16},{4,20},{8,24},{12,28},{16,0},{20,4},{24,8},{28,12},{1,17},{... | collective-permute-start | bytes 4325384 | tf_op jit(solution)/shard_map/ppermute | solution.py:38
  202.4 46.8 %collective-permute-start.27 = (bf16[352,1024]{1,0:T(8,128)(2,1)S(1)}, bf16[352,1024]{1,0:T(8,128)(2,1)S(1)}, u32[]{:S(2)}, u32[]{:S(2)}) collective-permute-start(bf16[352,1024]{1,0:T(8,128)(2,1)S(1)} %copy-done.85), channel_id=1, source_target_pairs={{0,8},{4,12},{8,0},{12,4},{16,24},{20,28},{24,16},{28,20},{1,9},{5... | collective-permute-start | bytes 2162696 | tf_op jit(solution)/shard_map/ppermute | solution.py:38
  204.1 45.4 %collective-permute-start.29 = (bf16[352,1024]{1,0:T(8,128)(2,1)S(1)}, bf16[352,1024]{1,0:T(8,128)(2,1)S(1)}, u32[]{:S(2)}, u32[]{:S(2)}) collective-permute-start(bf16[352,1024]{1,0:T(8,128)(2,1)S(1)} %collective-permute-done.23), channel_id=1, source_target_pairs={{0,16},{4,20},{8,24},{12,28},{16,0},{20,4},{24,8},{28,12},{1,17},{... | collective-permute-start | bytes 2162696 | tf_op jit(solution)/shard_map/ppermute | solution.py:38
  253.2 62.8 %collective-permute-start.31 = (bf16[512,1408]{1,0:T(8,128)(2,1)}, bf16[512,1408]{1,0:T(8,128)(2,1)}, u32[]{:S(2)}, u32[]{:S(2)}) collective-permute-start(bf16[512,1408]{1,0:T(8,128)(2,1)} %get-tuple-element.472.rest_4_), channel_id=1, source_target_pairs={{0,8},{4,12},{8,0},{12,4},{16,24},{20,28},{24,16},{28,20},{1,9},{5... | collective-permute-start | bytes 4325384 | tf_op jit(solution)/shard_map/ppermute | solution.py:38
  254.1 61.9 %collective-permute-start.32 = (bf16[512,1408]{1,0:T(8,128)(2,1)}, bf16[512,1408]{1,0:T(8,128)(2,1)}, u32[]{:S(2)}, u32[]{:S(2)}) collective-permute-start(bf16[512,1408]{1,0:T(8,128)(2,1)} %get-tuple-element.468.rest_0_), channel_id=1, source_target_pairs={{0,16},{4,20},{8,24},{12,28},{16,0},{20,4},{24,8},{28,12},{1,17},{... | collective-permute-start | bytes 4325384 | tf_op jit(solution)/shard_map/ppermute | solution.py:38
  255.4 63.1 %collective-permute-start.33 = (bf16[512,1408]{1,0:T(8,128)(2,1)}, bf16[512,1408]{1,0:T(8,128)(2,1)}, u32[]{:S(2)}, u32[]{:S(2)}) collective-permute-start(bf16[512,1408]{1,0:T(8,128)(2,1)} %collective-permute-done.25.rest_6_), channel_id=1, source_target_pairs={{0,8},{4,12},{8,0},{12,4},{16,24},{20,28},{24,16},{28,20},{1,9},{5... | collective-permute-start | bytes 4325384 | tf_op jit(solution)/shard_map/ppermute | solution.py:38
  256.6 62.4 %collective-permute-start.34 = (bf16[512,1408]{1,0:T(8,128)(2,1)}, bf16[512,1408]{1,0:T(8,128)(2,1)}, u32[]{:S(2)}, u32[]{:S(2)}) collective-permute-start(bf16[512,1408]{1,0:T(8,128)(2,1)} %copy-done.129), channel_id=1, source_target_pairs={{0,16},{4,20},{8,24},{12,28},{16,0},{20,4},{24,8},{28,12},{1,17},{... | collective-permute-start | bytes 4325384 | tf_op jit(solution)/shard_map/ppermute | solution.py:38
  320.7 55.0 %collective-permute-start.35 = (bf16[1024,1024]{1,0:T(8,128)(2,1)}, bf16[1024,1024]{1,0:T(8,128)(2,1)}, u32[]{:S(2)}, u32[]{:S(2)}) collective-permute-start(bf16[1024,1024]{1,0:T(8,128)(2,1)} %copy-done.43), channel_id=1, source_target_pairs={{0,8},{4,12},{8,0},{12,4},{16,24},{20,28},{24,16},{28,20},{1,9},{5... | collective-permute-start | bytes 6291464 | tf_op jit(solution)/shard_map/ppermute | solution.py:38
  321.9 53.8 %collective-permute-start.37 = (bf16[1408,512]{1,0:T(8,128)(2,1)}, bf16[1408,512]{1,0:T(8,128)(2,1)}, u32[]{:S(2)}, u32[]{:S(2)}) collective-permute-start(bf16[1408,512]{1,0:T(8,128)(2,1)} %copy-done.48), channel_id=1, source_target_pairs={{0,16},{4,20},{8,24},{12,28},{16,0},{20,4},{24,8},{28,12},{1,17},{... | collective-permute-start | bytes 4325384 | tf_op jit(solution)/shard_map/ppermute | solution.py:38
  323.2 52.5 %collective-permute-start.36 = (bf16[1024,384]{1,0:T(8,128)(2,1)}, bf16[1024,384]{1,0:T(8,128)(2,1)}, u32[]{:S(2)}, u32[]{:S(2)}) collective-permute-start(bf16[1024,384]{1,0:T(8,128)(2,1)} %copy-done.52), channel_id=1, source_target_pairs={{0,16},{4,20},{8,24},{12,28},{16,0},{20,4},{24,8},{28,12},{1,17},{... | collective-permute-start | bytes 2359304 | tf_op jit(solution)/shard_map/ppermute | solution.py:38
  384.4 132.6 %all-gather.11.cloned.1.call-start = ((), (), s32[]{:S(2)}) async-start(), calls=%async_computation.9 | async-start | bytes 2621440 | tf_op jit(solution)/shard_map/all_gather | solution.py:892
  402.5 46.3 %collective-permute-start.43 = (bf16[704,512]{1,0:T(8,128)(2,1)}, bf16[704,512]{1,0:T(8,128)(2,1)}, u32[]{:S(2)}, u32[]{:S(2)}) collective-permute-start(bf16[704,512]{1,0:T(8,128)(2,1)} %get-tuple-element.721), channel_id=1, source_target_pairs={{0,8},{4,12},{8,0},{12,4},{16,24},{20,28},{24,16},{28,20},{1,9},{5... | collective-permute-start | bytes 2162696 | tf_op jit(solution)/shard_map/ppermute | solution.py:38
  405.6 43.2 %collective-permute-start.42 = (bf16[512,384]{1,0:T(8,128)(2,1)}, bf16[512,384]{1,0:T(8,128)(2,1)S(1)}, u32[]{:S(2)}, u32[]{:S(2)}) collective-permute-start(bf16[512,384]{1,0:T(8,128)(2,1)} %get-tuple-element.733), channel_id=1, source_target_pairs={{0,8},{4,12},{8,0},{12,4},{16,24},{20,28},{24,16},{28,20},{1,9},{5... | collective-permute-start | bytes 1179656 | tf_op jit(solution)/shard_map/ppermute | solution.py:38
  410.6 38.1 %collective-permute-start.41 = (bf16[512,1024]{1,0:T(8,128)(2,1)}, bf16[512,1024]{1,0:T(8,128)(2,1)}, u32[]{:S(2)}, u32[]{:S(2)}) collective-permute-start(bf16[512,1024]{1,0:T(8,128)(2,1)} %get-tuple-element.711), channel_id=1, source_target_pairs={{0,16},{4,20},{8,24},{12,28},{16,0},{20,4},{24,8},{28,12},{1,17},{... | collective-permute-start | bytes 3145736 | tf_op jit(solution)/shard_map/ppermute | solution.py:38
  411.9 48.5 %collective-permute-start.39 = (bf16[704,1024]{1,0:T(8,128)(2,1)}, bf16[704,1024]{1,0:T(8,128)(2,1)}, u32[]{:S(2)}, u32[]{:S(2)}) collective-permute-start(bf16[704,1024]{1,0:T(8,128)(2,1)} %get-tuple-element.525), channel_id=1, source_target_pairs={{0,8},{4,12},{8,0},{12,4},{16,24},{20,28},{24,16},{28,20},{1,9},{5... | collective-permute-start | bytes 4325384 | tf_op jit(solution)/shard_map/ppermute | solution.py:38
  412.7 53.8 %collective-permute-start.40 = (bf16[704,1024]{1,0:T(8,128)(2,1)}, bf16[704,1024]{1,0:T(8,128)(2,1)}, u32[]{:S(2)}, u32[]{:S(2)}) collective-permute-start(bf16[704,1024]{1,0:T(8,128)(2,1)} %get-tuple-element.528), channel_id=1, source_target_pairs={{0,16},{4,20},{8,24},{12,28},{16,0},{20,4},{24,8},{28,12},{1,17},{... | collective-permute-start | bytes 4325384 | tf_op jit(solution)/shard_map/ppermute | solution.py:38
  466.5 131.8 %reduce-scatter.11.cloned.1.call-start = ((), (), s32[]{:S(2)}) async-start(), calls=%async_computation.11 | async-start | bytes 2621440 | tf_op jit(solution)/shard_map/reduce_scatter | solution.py:895
  466.7 50.3 %collective-permute-start.45 = (bf16[512,1408]{1,0:T(8,128)(2,1)}, bf16[512,1408]{1,0:T(8,128)(2,1)}, u32[]{:S(2)}, u32[]{:S(2)}) collective-permute-start(bf16[512,1408]{1,0:T(8,128)(2,1)} %copy-done.47), channel_id=1, source_target_pairs={{0,8},{4,12},{8,0},{12,4},{16,24},{20,28},{24,16},{28,20},{1,9},{5... | collective-permute-start | bytes 4325384 | tf_op jit(solution)/shard_map/ppermute | solution.py:38
  467.6 49.4 %collective-permute-start.46 = (bf16[512,1408]{1,0:T(8,128)(2,1)}, bf16[512,1408]{1,0:T(8,128)(2,1)}, u32[]{:S(2)}, u32[]{:S(2)}) collective-permute-start(bf16[512,1408]{1,0:T(8,128)(2,1)} %copy-done.46), channel_id=1, source_target_pairs={{0,16},{4,20},{8,24},{12,28},{16,0},{20,4},{24,8},{28,12},{1,17},{... | collective-permute-start | bytes 4325384 | tf_op jit(solution)/shard_map/ppermute | solution.py:38
  472.3 44.1 %collective-permute-start.48 = (bf16[352,1024]{1,0:T(8,128)(2,1)}, bf16[352,1024]{1,0:T(8,128)(2,1)}, u32[]{:S(2)}, u32[]{:S(2)}) collective-permute-start(bf16[352,1024]{1,0:T(8,128)(2,1)} %get-tuple-element.717), channel_id=1, source_target_pairs={{0,8},{4,12},{8,0},{12,4},{16,24},{20,28},{24,16},{28,20},{1,9},{5... | collective-permute-start | bytes 2162696 | tf_op jit(solution)/shard_map/ppermute | solution.py:38
  476.8 40.2 %collective-permute-start.47 = (bf16[352,1024]{1,0:T(8,128)(2,1)}, bf16[352,1024]{1,0:T(8,128)(2,1)}, u32[]{:S(2)}, u32[]{:S(2)}) collective-permute-start(bf16[352,1024]{1,0:T(8,128)(2,1)} %get-tuple-element.719), channel_id=1, source_target_pairs={{0,16},{4,20},{8,24},{12,28},{16,0},{20,4},{24,8},{28,12},{1,17},{... | collective-permute-start | bytes 2162696 | tf_op jit(solution)/shard_map/ppermute | solution.py:38
  517.1 41.4 %collective-permute-start.52 = (bf16[512,1408]{1,0:T(8,128)(2,1)}, bf16[512,1408]{1,0:T(8,128)(2,1)}, u32[]{:S(2)}, u32[]{:S(2)}) collective-permute-start(bf16[512,1408]{1,0:T(8,128)(2,1)} %copy-done.44), channel_id=1, source_target_pairs={{0,16},{4,20},{8,24},{12,28},{16,0},{20,4},{24,8},{28,12},{1,17},{... | collective-permute-start | bytes 4325384 | tf_op jit(solution)/shard_map/ppermute | solution.py:38
  518.4 34.7 %collective-permute-start.51 = (bf16[512,1408]{1,0:T(8,128)(2,1)}, bf16[512,1408]{1,0:T(8,128)(2,1)}, u32[]{:S(2)}, u32[]{:S(2)}) collective-permute-start(bf16[512,1408]{1,0:T(8,128)(2,1)} %copy-done.45), channel_id=1, source_target_pairs={{0,8},{4,12},{8,0},{12,4},{16,24},{20,28},{24,16},{28,20},{1,9},{5... | collective-permute-start | bytes 4325384 | tf_op jit(solution)/shard_map/ppermute | solution.py:38
  519.7 166.5 %reduce-scatter.9.cloned.1.call-start = ((), (), s32[]{:S(2)}) async-start(), calls=%async_computation.10 | async-start | bytes 2621440 | tf_op jit(solution)/shard_map/reduce_scatter | solution.py:895
  543.1 31.7 %collective-permute-start.50 = (bf16[1024,512]{1,0:T(8,128)(2,1)S(1)}, bf16[1024,512]{1,0:T(8,128)(2,1)S(1)}, u32[]{:S(2)}, u32[]{:S(2)}) collective-permute-start(bf16[1024,512]{1,0:T(8,128)(2,1)S(1)} %get-tuple-element.580), channel_id=1, source_target_pairs={{8,0},{12,4},{24,16},{28,20},{9,1},{13,5},{25,17},{29,21},{10,2},{... | collective-permute-start | bytes 3145736 | tf_op jit(solution)/shard_map/ppermute | solution.py:889
  555.9 35.2 %collective-permute-start.53 = (bf16[256,1408]{1,0:T(8,128)(2,1)}, bf16[256,1408]{1,0:T(8,128)(2,1)}, u32[]{:S(2)}, u32[]{:S(2)}) collective-permute-start(bf16[256,1408]{1,0:T(8,128)(2,1)} %get-tuple-element.704), channel_id=1, source_target_pairs={{0,16},{4,20},{8,24},{12,28},{16,0},{20,4},{24,8},{28,12},{1,17},{... | collective-permute-start | bytes 2162696 | tf_op jit(solution)/shard_map/ppermute | solution.py:38
  594.2 35.9 %collective-permute-start.57 = (bf16[1024,384]{1,0:T(8,128)(2,1)}, bf16[1024,384]{1,0:T(8,128)(2,1)}, u32[]{:S(2)}, u32[]{:S(2)}) collective-permute-start(bf16[1024,384]{1,0:T(8,128)(2,1)} %get-tuple-element.616), channel_id=1, source_target_pairs={{0,8},{4,12},{8,0},{12,4},{16,24},{20,28},{24,16},{28,20},{1,9},{5... | collective-permute-start | bytes 2359304 | tf_op jit(solution)/shard_map/ppermute | solution.py:38
  594.6 35.5 %collective-permute-start.58 = (bf16[1024,384]{1,0:T(8,128)(2,1)}, bf16[1024,384]{1,0:T(8,128)(2,1)}, u32[]{:S(2)}, u32[]{:S(2)}) collective-permute-start(bf16[1024,384]{1,0:T(8,128)(2,1)} %get-tuple-element.617), channel_id=1, source_target_pairs={{0,16},{4,20},{8,24},{12,28},{16,0},{20,4},{24,8},{28,12},{1,17},{... | collective-permute-start | bytes 2359304 | tf_op jit(solution)/shard_map/ppermute | solution.py:38
  595.3 34.8 %collective-permute-start.59 = (bf16[256,1408]{1,0:T(8,128)(2,1)}, bf16[256,1408]{1,0:T(8,128)(2,1)}, u32[]{:S(2)}, u32[]{:S(2)}) collective-permute-start(bf16[256,1408]{1,0:T(8,128)(2,1)} %get-tuple-element.620), channel_id=1, source_target_pairs={{0,16},{4,20},{8,24},{12,28},{16,0},{20,4},{24,8},{28,12},{1,17},{... | collective-permute-start | bytes 2162696 | tf_op jit(solution)/shard_map/ppermute | solution.py:38
  596.6 33.5 %collective-permute-start.60 = (bf16[256,1408]{1,0:T(8,128)(2,1)}, bf16[256,1408]{1,0:T(8,128)(2,1)}, u32[]{:S(2)}, u32[]{:S(2)}) collective-permute-start(bf16[256,1408]{1,0:T(8,128)(2,1)} %get-tuple-element.621), channel_id=1, source_target_pairs={{0,8},{4,12},{8,0},{12,4},{16,24},{20,28},{24,16},{28,20},{1,9},{5... | collective-permute-start | bytes 2162696 | tf_op jit(solution)/shard_map/ppermute | solution.py:38
  632.7 33.2 %collective-permute-start.77 = (bf16[704,256]{1,0:T(8,128)(2,1)S(1)}, bf16[704,256]{1,0:T(8,128)(2,1)S(1)}, u32[]{:S(2)}, u32[]{:S(2)}) collective-permute-start(bf16[704,256]{1,0:T(8,128)(2,1)S(1)} %get-tuple-element.670), channel_id=1, source_target_pairs={{0,4},{4,0},{8,12},{12,8},{16,20},{20,16},{24,28},{28,24},{1,5},{5... | collective-permute-start | bytes 1081352 | tf_op jit(solution)/shard_map/ppermute | solution.py:38
  637.3 28.4 %collective-permute-start.74 = (bf16[176,1024]{1,0:T(8,128)(2,1)S(1)}, bf16[176,1024]{1,0:T(8,128)(2,1)S(1)}, u32[]{:S(2)}, u32[]{:S(2)}) collective-permute-start(bf16[176,1024]{1,0:T(8,128)(2,1)S(1)} %get-tuple-element.657), channel_id=1, source_target_pairs={{0,4},{4,0},{8,12},{12,8},{16,20},{20,16},{24,28},{28,24},{1,5},{5... | collective-permute-start | bytes 1081352 | tf_op jit(solution)/shard_map/ppermute | solution.py:38
  639.8 34.1 %collective-permute-start.65 = (bf16[512,512]{1,0:T(8,128)(2,1)S(1)}, bf16[512,512]{1,0:T(8,128)(2,1)S(1)}, u32[]{:S(2)}, u32[]{:S(2)}) collective-permute-start(bf16[512,512]{1,0:T(8,128)(2,1)S(1)} %copy-done.54), channel_id=1, source_target_pairs={{0,16},{4,20},{8,24},{12,28},{16,0},{20,4},{24,8},{28,12},{1,17},{... | collective-permute-start | bytes 1572872 | tf_op jit(solution)/shard_map/ppermute | solution.py:38
  (172 other events, 1468.2 us)
Sparse Core Ops, SparseCore 0:
  12.4 48.3 all-gather.4
  69.7 47.8 all-gather.6
  144.9 45.0 reduce-scatter.4
  200.4 46.0 all-gather.8
  384.5 46.3 reduce-scatter.6
  466.7 46.2 all-gather.10
  519.8 43.4 reduce-scatter.10
  608.9 44.1 reduce-scatter.8

commit v5 on v4

--- a/solution.py
+++ b/solution.py
@@ -249,6 +249,42 @@
         0,
         name="add_rows",
     )(left, right)[0]
+
+
+def join_kernel(core_ref, own_ref, other_ref, out_ref):
+    own = pl.program_id(0) // (pl.num_programs(0) // 2) == core_ref[0]
+
+    @pl.when(own)
+    def _():
+        out_ref[...] = own_ref[...]
+
+    @pl.when(~own)
+    def _():
+        out_ref[...] = other_ref[...]
+
+
+def join_rows(core, own, other):
+    rows, columns = own.shape
+    tile = rows // 4
+
+    def spec(mine):
+        def index(i, core):
+            place = i - 4 * jnp.where(mine, core[0], 1 - core[0])
+            return jnp.clip(place, 0, 3), 0
+
+        return pl.BlockSpec((tile, columns), index)
+
+    return call(
+        join_kernel,
+        (8,),
+        [spec(True), spec(False)],
+        [pl.BlockSpec((tile, columns), lambda i, core: (i, 0))],
+        [shaped(2 * rows, columns, BF16)],
+        24,
+        0,
+        name="join_rows",
+        scalars=1,
+    )(core[None], own, other)[0]
 
 
 def finish_kernel(core_ref, kept_ref, arrived_ref, mine_ref, other_ref):
@@ -985,14 +1021,13 @@
         cosine, sine, low, high,
     )
 
-    rows_one = merge_core(group_one, across(group_one, 1), core, 0)
+    rows_one = join_rows(core, group_one, across(group_one, 1))
     gu_two = gather_quads({0: gu_block}, up_two)
     sd_rest = gather_rest(sd_one, down_two)
     cot_group = gathered(cot_packed)
     qkv_a, qkv_b = listed(qkv_a), listed(qkv_b)
     query, key_value = project(rows_one, qkv_a, qkv_b, bias, cosine, sine, heads)
 
-    query, key_value, sd_rest = together(query, key_value, sd_rest)
     before = [shifted(key_value, step) for step in range(back, 0, -1)]
     down_full = place_quads(sd_one | sd_two | sd_rest, quad, 1)
     query, before, gu_two, edb_block, down_full = together(
@@ -1029,7 +1064,7 @@
     unit_two = mixed * scale_two
     normed_two = (unit_two * gain_two).astype(BF16)
     group_two = gathered(flip_columns(normed_two, quad))
-    cot_rows = merge_core(cot_group, cot_other, core, 0)
+    cot_rows = join_rows(core, cot_group, cot_other)
     ed_full = place_quads(eda_one | eda_two, quad, 0, ed_full)
     (
         group_two, eg_one, edb_rest, gu_rest, eda_rest, eu_block, eg_block, eu_one, cot_rows,
@@ -1040,7 +1075,7 @@
     )
     eu_two, eg_two = gather_quads({0: eu_block}, down_two), gather_quads({0: eg_block}, up_two)
     eu_rest, eg_rest = gather_rest(eu_one, down_two), gather_rest(eg_one, up_two)
-    rows_two = merge_core(group_two, across(group_two, 1), core, 0)
+    rows_two = join_rows(core, group_two, across(group_two, 1))
     gu_pieces = listed(gu_one | gu_two | gu_rest)
 
     def router(rows, weight):
@@ -1097,22 +1132,22 @@
         sums, gua_sent, gub_sent, sd_sent, gua_grad, gub_grad, sd_grad
     )
     forward_part, packed = sums[:2], core_sum(*sums[2:])
+    gua_grad = first_sum(gua_grad, gua_sent)
+    gub_grad = first_sum(gub_grad, gub_sent)
+    sd_grad = first_sum(sd_grad, sd_sent)
     (
         packed, gua_grad, gub_grad, sd_grad, active, grad_result, grad_gate_pre, grad_up_pre,
     ) = together(
         packed, gua_grad, gub_grad, sd_grad, active, grad_result, grad_gate_pre, grad_up_pre,
     )
     spread = scattered(packed)
-    (eda_grad, eda_out), (edb_grad, edb_out) = down_grads(active, grad_result, quad, quads)
-    eda_out, edb_out, gua_grad, gub_grad, sd_grad, grad_gate_pre, grad_up_pre = together(
-        eda_out, edb_out, gua_grad, gub_grad, sd_grad, grad_gate_pre, grad_up_pre
-    )
-    eda_sent, edb_sent = sent(eda_out, up_order[0]), sent(edb_out, down_order[0])
-    gua_grad = first_sum(gua_grad, gua_sent)
-    gub_grad = first_sum(gub_grad, gub_sent)
-    sd_grad = first_sum(sd_grad, sd_sent)
     gua_sent, gub_sent = across(gua_grad[1], 2 * up_order[1]), across(gub_grad[1], 2 * down_order[1])
     sd_sent = across(sd_grad[1], 2 * down_order[1])
+    (eda_grad, eda_out), (edb_grad, edb_out) = down_grads(active, grad_result, quad, quads)
+    eda_out, edb_out, grad_gate_pre, grad_up_pre, gua_sent, gub_sent, sd_sent = together(
+        eda_out, edb_out, grad_gate_pre, grad_up_pre, gua_sent, gub_sent, sd_sent
+    )
+    eda_sent, edb_sent = sent(eda_out, up_order[0]), sent(edb_out, down_order[0])
     ((eg_grad, eg_out),) = row_grads(rows_two, grad_gate_pre, quads, [(0, ffe, True, False)])
     ((eu_grad, eu_out),) = row_grads(rows_two, grad_up_pre, quads, [(0, ffe, False, False)])
     spread, eg_grad, eg_out = together(spread, eg_grad, eg_out)
@@ -1142,18 +1177,36 @@
     eg_sent = sent(eg_out[:1], up_order[0])
     eu_sent = sent(eu_out[:1], down_order[0])
     forward_part = core_sum(*forward_part)
+    forward_part, gua_grad, gua_sent, gub_grad, gub_sent, sd_grad, sd_sent = together(
+        forward_part, gua_grad, gua_sent, gub_grad, gub_sent, sd_grad, sd_sent
+    )
     eda_grad = first_sum(eda_grad, eda_sent)
     edb_grad = first_sum(edb_grad, edb_sent)
     eda_sent, edb_sent = across(eda_grad[1], 2 * up_order[1]), across(edb_grad[1], 2 * down_order[1])
 
+    gua_mine, gua_arrived = finished(*rest_parts(gua_grad[0], gua_sent, up_order), 0)
+    gub_mine, gub_arrived = finished(*rest_parts(gub_grad[0], gub_sent, down_order), 0)
+    sd_mine, sd_arrived = finished(*rest_parts(sd_grad[0], sd_sent, down_order), 1)
+    gu_mine = jnp.concatenate([gua_mine, gub_mine], axis=1)
+    gu_arrived = jnp.concatenate([gua_arrived, gub_arrived], axis=1)
+    sg_grad, su_grad = [
+        merge_core(
+            gu_mine[:, part * ffs_half : (part + 1) * ffs_half],
+            gu_arrived[:, part * ffs_half : (part + 1) * ffs_half],
+            core,
+            1,
+        ).astype(F32)
+        for part in range(2)
+    ]
+    sd_grad = merge(core, sd_mine, sd_arrived, 0)
     (
-        group_branch, forward_part, eg_grad, eg_out, eg_sent, eu_grad, eu_out, eu_sent, eda_grad,
+        group_branch, forward_part, sg_grad, su_grad, sd_grad, eg_grad, eg_out, eg_sent, eu_grad, eu_out, eu_sent, eda_grad,
         eda_sent, edb_grad, edb_sent,
     ) = together(
-        group_branch, forward_part, eg_grad, eg_out, eg_sent, eu_grad, eu_out, eu_sent, eda_grad,
+        group_branch, forward_part, sg_grad, su_grad, sd_grad, eg_grad, eg_out, eg_sent, eu_grad, eu_out, eu_sent, eda_grad,
         eda_sent, edb_grad, edb_sent,
     )
-    grad_branch = merge_core(group_branch, across(group_branch, 1), core, 0)
+    grad_branch = join_rows(core, group_branch, across(group_branch, 1))
     eg_sent = eg_sent + sent(eg_out[1:], up_order[0])
     eu_sent = eu_sent + sent(eu_out[1:], down_order[0])
 
@@ -1163,11 +1216,9 @@
         query, grad_attended, log_total, before, key_value, key_place, low, high, cosine, sine
     )
     (
-        grad_query, grad_before, grad_branch, eg_grad, eu_grad, gua_grad, gua_sent, gub_grad,
-        gub_sent, sd_grad, sd_sent,
+        grad_query, grad_before, grad_branch, eg_grad, eu_grad,
     ) = together(
-        grad_query, grad_before, grad_branch, eg_grad, eu_grad, gua_grad, gua_sent, gub_grad,
-        gub_sent, sd_grad, sd_sent,
+        grad_query, grad_before, grad_branch, eg_grad, eu_grad,
     )
     arrived = [shifted(sent, step - back) for step, sent in enumerate(grad_before)]
     cut = eg_grad[1].shape[0] // 2
@@ -1205,17 +1256,15 @@
     o_grad, o_out = column_grads(attended, grad_branch, quad, quads, False)
     att_gain_part = flip_columns(att_gain_part[0], quad) / gain_one
     late = jnp.concatenate([att_gain_part, ff_gain_grad, router_grad.T.reshape(-1)])
-    late = sum_everywhere(late, [], ep_masks[:1])
+    late = sum_everywhere(late, [], ep_masks)
+    o_sent = sent(o_out, down_order[0])
     (
-        late, qkv_a_sent, qkv_b_sent, o_out, eg_last, eu_last, eda_sent, edb_sent, gua_sent,
-        gub_sent, sd_sent,
+        late, qkv_a_sent, qkv_b_sent, eg_last, eu_last, eda_sent, edb_sent,
     ) = together(
-        late, qkv_a_sent, qkv_b_sent, o_out, eg_last, eu_last, eda_sent, edb_sent, gua_sent,
-        gub_sent, sd_sent,
+        late, qkv_a_sent, qkv_b_sent, eg_last, eu_last, eda_sent, edb_sent,
     )
     eg_rest = jnp.concatenate([eg_rest, eg_last], axis=0)
     eu_rest = jnp.concatenate([eu_rest, eu_last], axis=0)
-    late = sum_everywhere(late, [], ep_masks[1:])
     bias_part = bias_part.reshape(3, head_width)
     bias_part = jnp.concatenate(
         [jnp.where(core == 0, bias_part, 0.0), jnp.where(core == 0, 0.0, bias_part)], axis=1
@@ -1225,42 +1274,27 @@
     qkv_b_grad = first_sum(qkv_b_grad, qkv_b_sent)
     qkv_a_rest = across(qkv_a_grad[1], 2 * up_order[1])
     qkv_b_rest = across(qkv_b_grad[1], 2 * down_order[1])
-    o_grad = first_sum(o_grad, sent(o_out, down_order[0]))
+    o_grad = first_sum(o_grad, o_sent)
     o_rest = across(o_grad[1], 2 * down_order[1])
     late = sum_everywhere(late, quad_masks, [])
     eg_grad = merge(core, *finished(*rest_parts(eg_grad[0], eg_rest, up_order), 0), None)
+    eu_grad = merge(core, *finished(*rest_parts(eu_grad[0], eu_rest, down_order), 0), None)
     eda_mine, eda_arrived = finished(*rest_parts(eda_grad[0], eda_sent, up_order), 0)
     edb_mine, edb_arrived = finished(*rest_parts(edb_grad[0], edb_sent, down_order), 0)
     ed_grad = jnp.concatenate(
         [merge(core, eda_mine, eda_arrived, None), merge(core, edb_mine, edb_arrived, None)], axis=2
     )
-    gua_mine, gua_arrived = finished(*rest_parts(gua_grad[0], gua_sent, up_order), 0)
-    gub_mine, gub_arrived = finished(*rest_parts(gub_grad[0], gub_sent, down_order), 0)
-    sd_mine, sd_arrived = finished(*rest_parts(sd_grad[0], sd_sent, down_order), 1)
-    gu_mine = jnp.concatenate([gua_mine, gub_mine], axis=1)
-    gu_arrived = jnp.concatenate([gua_arrived, gub_arrived], axis=1)
-    sg_grad, su_grad = [
-        merge_core(
-            gu_mine[:, part * ffs_half : (part + 1) * ffs_half],
-            gu_arrived[:, part * ffs_half : (part + 1) * ffs_half],
-            core,
-            1,
-        ).astype(F32)
-        for part in range(2)
-    ]
-    sd_grad = merge(core, sd_mine, sd_arrived, 0)
     layer_out = (mixed + layer_sum.astype(F32)).astype(BF16)
     qkv_a_mine, qkv_a_arrived = finished(*rest_parts(qkv_a_grad[0], qkv_a_rest, up_order), 0)
     qkv_b_mine, qkv_b_arrived = finished(*rest_parts(qkv_b_grad[0], qkv_b_rest, down_order), 0)
     o_mine, o_arrived = finished(*rest_parts(o_grad[0], o_rest, down_order), 1)
     (
         grad_normed_one, qkv_a_mine, qkv_a_arrived, qkv_b_mine, qkv_b_arrived, o_mine, o_arrived,
-        late, eu_rest, eg_grad, ed_grad, layer_out, sg_grad, su_grad, sd_grad,
+        late, eu_grad, eg_grad, ed_grad, layer_out,
     ) = together(
         grad_normed_one, qkv_a_mine, qkv_a_arrived, qkv_b_mine, qkv_b_arrived, o_mine, o_arrived,
-        late, eu_rest, eg_grad, ed_grad, layer_out, sg_grad, su_grad, sd_grad,
-    )
-    eu_grad = merge(core, *finished(*rest_parts(eu_grad[0], eu_rest, down_order), 0), None)
+        late, eu_grad, eg_grad, ed_grad, layer_out,
+    )
     qkv_mine = jnp.concatenate([qkv_a_mine, qkv_b_mine], axis=1)
     qkv_arrived = jnp.concatenate([qkv_a_arrived, qkv_b_arrived], axis=1)
     q_grad, k_grad, v_grad = [merge(core, qkv_mine, qkv_arrived, 1, part, 3) for part in range(3)]

time: 716 us -> 685 us (0.957)
  waiting for transfers between devices: 259 us -> 226 us
  other arithmetic: 92.2 us -> 69.3 us
  local copies, waits for them, and re-layouts: 60.4 us -> 80.2 us
    ppermute x75, waiting for transfers between devices: 223 us -> 193 us  [across(): return lax.ppermute(block, 'grp', [(i, i ^ mask) for i in range(count)])]
    unnamed x267 -> x300, local copies, waits for them, and re-layouts: 30.7 us -> 45 us
    select_n x9 -> x5, other arithmetic: 12 us -> 1.48 us  [merge_core(): first = jnp.where(core == 0, kept, arrived)]
    concatenate x9 -> x5, other arithmetic: 13.6 us -> 5.31 us  [merge_core(): return jnp.concatenate([first, second], axis=axis)]
    pallas_call x32 -> x36, Pallas kernels: 179 us -> 186 us  [run(): pl.pallas_call(kernel, grid_spec=pltpu.PrefetchScalarGridSpec(num_scalar_...]
  transfers between devices with their start and end apart: 87 -> 87, of which waited for: 32 -> 30; matrix products, arithmetic and copies ran while one was open for 18% -> 16% of each run, Pallas kernels for 27% -> 29%
where the time goes in v5:
time: 685 us; the launch traced here: 676 us
  waiting for transfers between devices  226 us (33%)
  Pallas kernels  205 us (30%)
  local copies, waits for them, and re-layouts  80.2 us (12%)
  other arithmetic  69.3 us (10%)
  starting transfers between devices  66.6 us (10%)
  between operations  16.5 us (2%)
  matrix products  11.8 us (2%)
    ppermute x75, waiting for transfers between devices, across(): return lax.ppermute(block, 'grp', [(i, i ^ mask) for i in range(count)])  193 us
    pallas_call x36, Pallas kernels, run(): pl.pallas_call(kernel, grid_spec=pltpu.PrefetchScalarGridSpec(num_scalar_...  186 us
    ppermute x75, starting transfers between devices, across(): return lax.ppermute(block, 'grp', [(i, i ^ mask) for i in range(count)])  57.7 us
    unnamed x300, local copies, waits for them, and re-layouts  45 us
    convert_element_type x12, other arithmetic, add_low(): return (left.astype(F32) + right.astype(F32)).astype(BF16)  26.9 us
    ppermute x2, waiting for transfers between devices, shifted(): return lax.ppermute(values, 'grp', route)  24.5 us
    dynamic_update_slice x14, local copies, waits for them, and re-layouts, place_quads(): whole = lax.dynamic_update_slice(whole, pieces[key], start)  24.3 us
  transfers between devices with their start and end apart: 87, of which 30 were waited for; matrix products, arithmetic and copies ran while one was open for 16% of the time, Pallas kernels for 29%

profile of v5, /device:TPU:0, one launch (start us, length us, event | category | flops | bytes accessed | tf_op | source)
XLA Modules:
  0.0 675.6 jit_solution(9714847346949804073)
XLA Ops:
  13.3 2.6 collective-permute-start.1
  28.8 6.7 collective-permute-done.3.rest_6_.rest_7_
  43.0 24.4 %collective-permute-done.10.rest_3_.rest_4_ = bf16[512,384]{1,0:T(8,128)(2,1)S(1)} collective-permute-done((bf16[512,384]{1,0:T(8,128)(2,1)S(1)}, bf16[512,384]{1,0:T(8,128)(2,1)S(1)}, u32[]{:S(2)}, u32[]{:S(2)}) %collective-permute-start.10) | collective-permute-done | bytes 393248 | tf_op jit(solution)/shard_map/ppermute | solution.py:38
  71.1 2.7 collective-permute-done.14.other_ref
  77.3 5.2 project.1
  82.5 2.8 collective-permute-start.15
  89.9 4.7 collective-permute-done.17
  94.8 8.9 %collective-permute-done.16.rest_2_ = bf16[512,1408]{1,0:T(8,128)(2,1)S(1)} collective-permute-done((bf16[512,1408]{1,0:T(8,128)(2,1)}, bf16[512,1408]{1,0:T(8,128)(2,1)S(1)}, u32[]{:S(2)}, u32[]{:S(2)}) %collective-permute-start.16) | collective-permute-done | bytes 1441824 | tf_op jit(solution)/shard_map/ppermute | solution.py:38
  103.8 11.4 %collective-permute-done.15.rest_0_ = bf16[1024,512]{1,0:T(8,128)(2,1)S(1)} collective-permute-done((bf16[1024,512]{1,0:T(8,128)(2,1)S(1)}, bf16[1024,512]{1,0:T(8,128)(2,1)S(1)}, u32[]{:S(2)}, u32[]{:S(2)}) %collective-permute-start.15) | collective-permute-done | bytes 1048608 | tf_op jit(solution)/shard_map/ppermute | solution.py:925
  117.2 2.5 collective-permute-start.19
  121.4 6.7 attend.1
  131.1 2.8 collective-permute-done.18
  146.0 3.2 broadcast_in_dim.32
  155.5 36.1 %collective-permute-done.23 = bf16[352,1024]{1,0:T(8,128)(2,1)} collective-permute-done((bf16[352,1024]{1,0:T(8,128)(2,1)}, bf16[352,1024]{1,0:T(8,128)(2,1)}, u32[]{:S(2)}, u32[]{:S(2)}) %collective-permute-start.23) | collective-permute-done | bytes 720928 | tf_op jit(solution)/shard_map/ppermute | solution.py:38
  201.7 3.7 join_rows.5.cot_ref
  212.6 33.5 %collective-permute-done.27 = bf16[352,1024]{1,0:T(8,128)(2,1)} collective-permute-done((bf16[352,1024]{1,0:T(8,128)(2,1)}, bf16[352,1024]{1,0:T(8,128)(2,1)}, u32[]{:S(2)}, u32[]{:S(2)}) %collective-permute-start.27) | collective-permute-done | bytes 720928 | tf_op jit(solution)/shard_map/ppermute | solution.py:38
  256.4 27.3 %shared.1 = (bf16[1024,704]{1,0:T(8,128)(2,1)}, bf16[1024,2048]{1,0:T(8,128)(2,1)}, bf16[1024,2048]{1,0:T(8,128)(2,1)}, bf16[1024,2048]{1,0:T(8,128)(2,1)}, f32[...) custom-call(s32[1]{0:T(128)} %bitcast.core_ref, bf16[1024,2048]{1,0:T(8,128)(2,1)} %copy-done.4, bf16[960,2048]{1,0:T(8,128)(2,1)} %copy-done.101, ...), custom_call_target="tpu_custom_call" | custom-call | flops 17716740096 | bytes 35266564 | tf_op jit(solution)/shard_map/shared/pallas_call | solution.py:190
  283.8 10.2 %row_grads.3 = (bf16[512,1024]{1,0:T(8,128)(2,1)S(1)}, bf16[512,1024]{1,0:T(8,128)(2,1)S(1)}, bf16[1024,1024]{1,0:T(8,128)(2,1)S(1)}, bf16[512,384]{1,0:T(8,128)...) custom-call(bf16[1024,2048]{1,0:T(8,128)(2,1)} %copy-done.4, ...), custom_call_target="tpu_custom_call" | custom-call | flops 5905580032 | bytes 12845056 | tf_op jit(solution)/shard_map/row_grads/pallas_call | solution.py:190
  294.9 2.6 constant_dynamic-update-slice_fusion.8
  305.8 5.6 column_grads.2
  317.2 51.8 %expert.1 = (bf16[1024,1408]{1,0:T(8,128)(2,1)}, bf16[1024,2048]{1,0:T(8,128)(2,1)}, bf16[768,2048]{1,0:T(8,128)(2,1)}, bf16[512,2048]{1,0:T(8,128)(2,1)}, bf16[...) custom-call(s32[1]{0:T(128)} %bitcast.core_ref, ...), custom_call_target="tpu_custom_call" | custom-call | flops 35433480192 | bytes 58008068 | tf_op jit(solution)/shard_map/expert/pallas_call | solution.py:190
  371.2 2.8 add_convert_fusion.12
  374.0 3.7 add_convert_fusion.2
  383.7 11.5 %down_grads.1 = (bf16[352,1024]{1,0:T(8,128)(2,1)S(1)}, bf16[352,1024]{1,0:T(8,128)(2,1)S(1)}, bf16[704,1024]{1,0:T(8,128)(2,1)}, bf16[352,1024]{1,0:T(8,128)(2,...) custom-call(s32[1]{0:T(128)} %bitcast.13.quad_ref, bf16[1024,1408]{1,0:T(8,128)(2,1)} %get-tuple-element.494.act_ref, ...), custom_call_target="tpu_custom_call" | custom-call | flops 5905580032 | bytes 12845056 | tf_op jit(solution)/shard_map/down_grads/pallas_call | solution.py:841
  397.9 10.3 %collective-permute-done.40.arrived_ref = bf16[512,384]{1,0:T(8,128)(2,1)S(1)} collective-permute-done((bf16[512,384]{1,0:T(8,128)(2,1)}, bf16[512,384]{1,0:T(8,128)(2,1)S(1)}, u32[]{:S(2)}, u32[]{:S(2)}) %collective-permute-start.40) | collective-permute-done | bytes 393248 | tf_op jit(solution)/shard_map/ppermute | solution.py:38
  412.2 10.1 %row_grads.5 = (bf16[512,1408]{1,0:T(8,128)(2,1)S(1)}, bf16[512,1408]{1,0:T(8,128)(2,1)S(1)}, bf16[512,1408]{1,0:T(8,128)(2,1)S(1)}, bf16[512,1408]{1,0:T(8,128)(2,1)S(1)}) custom-call(bf16[1024,2048]{1,0:T(8,128)(2,1)} %copy-done.4, bf16[1024,1408]{1,0:T(8,128)(2,1)} %get-tuple-element.523.grad_ref), custom_call_target="tpu_custom_call" | custom-call | flops 5905580032 | bytes 12845056 | tf_op jit(solution)/shard_map/row_grads/pallas_call | solution.py:190
  426.9 10.1 %row_grads.4 = (bf16[512,1408]{1,0:T(8,128)(2,1)S(1)}, bf16[512,1408]{1,0:T(8,128)(2,1)S(1)}, bf16[512,1408]{1,0:T(8,128)(2,1)S(1)}, bf16[512,1408]{1,0:T(8,128)(2,1)S(1)}) custom-call(bf16[1024,2048]{1,0:T(8,128)(2,1)} %copy-done.4, bf16[1024,1408]{1,0:T(8,128)(2,1)} %get-tuple-element.503.grad_ref), custom_call_target="tpu_custom_call" | custom-call | flops 5905580032 | bytes 12845056 | tf_op jit(solution)/shard_map/row_grads/pallas_call | solution.py:190
  454.0 2.6 collective-permute-done.44.right_ref
  458.6 4.0 add_rows.6
  465.7 2.9 add_convert_fusion.8
  469.1 2.8 add_convert_fusion.10
  477.9 24.1 %collective-permute-done.51.arrived_ref = bf16[352,1024]{1,0:T(8,128)(2,1)S(1)} collective-permute-done((bf16[352,1024]{1,0:T(8,128)(2,1)S(1)}, bf16[352,1024]{1,0:T(8,128)(2,1)S(1)}, u32[]{:S(2)}, u32[]{:S(2)}) %collective-permute-start.51) | collective-permute-done | bytes 720928 | tf_op jit(solution)/shard_map/ppermute | solution.py:38
  508.4 3.8 join_rows.7.grad_ref
  512.2 3.6 convolution_convert_fusion.2.grad_ref
  516.0 13.8 %attend_back.1 = (bf16[1024,256]{1,0:T(8,128)(2,1)S(1)}, f32[1024,512]{1,0:T(8,128)}, bf16[1024,512]{1,0:T(8,128)(2,1)S(1)}) custom-call(bf16[1024,256]{1,0:T(8,128)(2,1)S(1)} %copy-done.92, bf16[1024,256]{1,0:T(8,128)(2,1)S(1)} %convolution_convert_fusion.2.grad_ref, f32[1024,256]{1,0:T(8,128)S(1)} %copy-done.89, bf16[1024,512]{1,0:T(8,128)(2,1)} %copy-done.73, ...), custom_call_target="tpu_custom_call" | custom-call | flops 3355443200 | bytes 8929280 | tf_op jit(solution)/shard_map/attend_back/pallas_call | solution.py:190
  531.2 7.5 %collective-permute-done.54 = bf16[512,1408]{1,0:T(8,128)(2,1)} collective-permute-done((bf16[512,1408]{1,0:T(8,128)(2,1)}, bf16[512,1408]{1,0:T(8,128)(2,1)}, u32[]{:S(2)}, u32[]{:S(2)}) %collective-permute-start.54) | collective-permute-done | bytes 1441824 | tf_op jit(solution)/shard_map/ppermute | solution.py:38
  538.6 2.9 add_convert_fusion.6
  547.5 13.1 %collective-permute-done.53.rest_0_ = bf16[1024,512]{1,0:T(8,128)(2,1)S(1)} collective-permute-done((bf16[1024,512]{1,0:T(8,128)(2,1)S(1)}, bf16[1024,512]{1,0:T(8,128)(2,1)S(1)}, u32[]{:S(2)}, u32[]{:S(2)}) %collective-permute-start.53) | collective-permute-done | bytes 1048608 | tf_op jit(solution)/shard_map/ppermute | solution.py:925
  561.5 15.4 %collect.1 = (bf16[768,2048]{1,0:T(8,128)(2,1)}, bf16[512,2048]{1,0:T(8,128)(2,1)}, f32[1,2048]{1,0:T(1,128)}, f32[1,768]{1,0:T(1,128)}, bf16[512,384]{1,0:T(8,1...) custom-call(s32[1]{0:T(128)} %bitcast.core_ref, ...), custom_call_target="tpu_custom_call" | custom-call | flops 6442450944 | bytes 20458500 | tf_op jit(solution)/shard_map/collect/pallas_call | solution.py:190
  586.4 4.0 add_rows.7
  593.3 3.3 collective-permute-done.59
  597.5 2.7 collective-permute-start.60
  604.7 5.2 collective-permute-done.60
  611.2 5.7 collective-permute-done.63
  634.5 3.3 collective-permute-done.74
  642.4 2.5 add_convert_fusion.14
  645.9 4.2 collective-permute-done.67.arrived_ref
  651.1 3.4 collective-permute-done.70.arrived_ref
  (624 shorter events, 224.6 us)
Async XLA Ops:
  7.2 62.1 %all-gather.5.cloned.1.call-start = ((), (), s32[]{:S(2)}) async-start(), calls=%async_computation.4 | async-start | bytes 2621440 | tf_op jit(solution)/shard_map/all_gather | solution.py:928
  12.3 118.8 %all-gather.7.cloned.1.call-start = ((), (), s32[]{:S(2)}) async-start(), calls=%async_computation.5 | async-start | bytes 2785280 | tf_op jit(solution)/shard_map/all_gather | solution.py:928
  35.6 33.8 %collective-permute-start.12 = (bf16[960,512]{1,0:T(8,128)(2,1)}, bf16[960,512]{1,0:T(8,128)(2,1)}, u32[]{:S(2)}, u32[]{:S(2)}) collective-permute-start(bf16[960,512]{1,0:T(8,128)(2,1)} %pad_maximum_fusion.6), channel_id=1, source_target_pairs={{0,16},{4,20},{8,24},{12,28},{16,0},{20,4},{24,8},{28,12},{1,17},{... | collective-permute-start | bytes 2949128 | tf_op jit(solution)/shard_map/ppermute | solution.py:38
  37.1 32.2 %collective-permute-start.13 = (bf16[960,512]{1,0:T(8,128)(2,1)}, bf16[960,512]{1,0:T(8,128)(2,1)}, u32[]{:S(2)}, u32[]{:S(2)}) collective-permute-start(bf16[960,512]{1,0:T(8,128)(2,1)} %pad_maximum_fusion.6), channel_id=1, source_target_pairs={{0,8},{4,12},{8,0},{12,4},{16,24},{20,28},{24,16},{28,20},{1,9},{5... | collective-permute-start | bytes 2949128 | tf_op jit(solution)/shard_map/ppermute | solution.py:38
  40.0 27.3 %collective-permute-start.10 = (bf16[512,384]{1,0:T(8,128)(2,1)S(1)}, bf16[512,384]{1,0:T(8,128)(2,1)S(1)}, u32[]{:S(2)}, u32[]{:S(2)}) collective-permute-start(bf16[512,384]{1,0:T(8,128)(2,1)S(1)} %collective-permute-done.1.rest_1_.rest_2_), channel_id=1, source_target_pairs={{0,16},{4,20},{8,24},{12,28},{16,0},{20,4},{24,8},{28,12},{1,17},{... | collective-permute-start | bytes 1179656 | tf_op jit(solution)/shard_map/ppermute | solution.py:38
  40.8 27.8 %collective-permute-start.11 = (bf16[512,384]{1,0:T(8,128)(2,1)S(1)}, bf16[512,384]{1,0:T(8,128)(2,1)S(1)}, u32[]{:S(2)}, u32[]{:S(2)}) collective-permute-start(bf16[512,384]{1,0:T(8,128)(2,1)S(1)} %collective-permute-done.3.rest_6_.rest_7_), channel_id=1, source_target_pairs={{0,8},{4,12},{8,0},{12,4},{16,24},{20,28},{24,16},{28,20},{1,9},{5... | collective-permute-start | bytes 1179656 | tf_op jit(solution)/shard_map/ppermute | solution.py:38
  69.4 123.6 %reduce-scatter.5.cloned.1.call-start = ((), (), s32[]{:S(2)}) async-start(), calls=%async_computation.6 | async-start | bytes 2621440 | tf_op jit(solution)/shard_map/reduce_scatter | solution.py:931
  69.5 34.3 %collective-permute-start.16 = (bf16[512,1408]{1,0:T(8,128)(2,1)}, bf16[512,1408]{1,0:T(8,128)(2,1)S(1)}, u32[]{:S(2)}, u32[]{:S(2)}) collective-permute-start(bf16[512,1408]{1,0:T(8,128)(2,1)} %pad_maximum_fusion.1.rest_0_), channel_id=1, source_target_pairs={{0,16},{4,20},{8,24},{12,28},{16,0},{20,4},{24,8},{28,12},{1,17},{... | collective-permute-start | bytes 4325384 | tf_op jit(solution)/shard_map/ppermute | solution.py:38
  82.5 32.6 %collective-permute-start.15 = (bf16[1024,512]{1,0:T(8,128)(2,1)S(1)}, bf16[1024,512]{1,0:T(8,128)(2,1)S(1)}, u32[]{:S(2)}, u32[]{:S(2)}) collective-permute-start(bf16[1024,512]{1,0:T(8,128)(2,1)S(1)} %get-tuple-element.378.rest_1_), channel_id=1, source_target_pairs={{0,8},{4,12},{16,24},{20,28},{1,9},{5,13},{17,25},{21,29},{2,10},{... | collective-permute-start | bytes 3145736 | tf_op jit(solution)/shard_map/ppermute | solution.py:925
  141.7 104.8 %all-gather.9.cloned.1.call-start = ((), (), s32[]{:S(2)}) async-start(), calls=%async_computation.7 | async-start | bytes 2621440 | tf_op jit(solution)/shard_map/all_gather | solution.py:928
  141.8 51.3 %collective-permute-start.21 = (bf16[512,2176]{1,0:T(8,128)(2,1)S(1)}, bf16[512,2176]{1,0:T(8,128)(2,1)}, u32[]{:S(2)}, u32[]{:S(2)}) collective-permute-start(bf16[512,2176]{1,0:T(8,128)(2,1)S(1)} %copy-done.10), channel_id=1, source_target_pairs={{0,4},{4,0},{8,12},{12,8},{16,20},{20,16},{24,28},{28,24},{1,5},{5... | collective-permute-start | bytes 6684680 | tf_op jit(solution)/shard_map/ppermute | solution.py:38
  142.0 51.1 %collective-permute-start.22 = (bf16[512,1408]{1,0:T(8,128)(2,1)}, bf16[512,1408]{1,0:T(8,128)(2,1)}, u32[]{:S(2)}, u32[]{:S(2)}) collective-permute-start(bf16[512,1408]{1,0:T(8,128)(2,1)} %pad_maximum_fusion.1.rest_0_), channel_id=1, source_target_pairs={{0,8},{4,12},{8,0},{12,4},{16,24},{20,28},{24,16},{28,20},{1,9},{5... | collective-permute-start | bytes 4325384 | tf_op jit(solution)/shard_map/ppermute | solution.py:38
  143.7 49.3 %collective-permute-start.25 = (bf16[512,1408]{1,0:T(8,128)(2,1)}, bf16[512,1408]{1,0:T(8,128)(2,1)}, u32[]{:S(2)}, u32[]{:S(2)}) collective-permute-start(bf16[512,1408]{1,0:T(8,128)(2,1)} %get-tuple-element.458.rest_4_), channel_id=1, source_target_pairs={{0,16},{4,20},{8,24},{12,28},{16,0},{20,4},{24,8},{28,12},{1,17},{... | collective-permute-start | bytes 4325384 | tf_op jit(solution)/shard_map/ppermute | solution.py:38
  144.7 46.9 %collective-permute-start.23 = (bf16[352,1024]{1,0:T(8,128)(2,1)}, bf16[352,1024]{1,0:T(8,128)(2,1)}, u32[]{:S(2)}, u32[]{:S(2)}) collective-permute-start(bf16[352,1024]{1,0:T(8,128)(2,1)} %get-tuple-element.414), channel_id=1, source_target_pairs={{0,8},{4,12},{8,0},{12,4},{16,24},{20,28},{24,16},{28,20},{1,9},{5... | collective-permute-start | bytes 2162696 | tf_op jit(solution)/shard_map/ppermute | solution.py:38
  145.0 48.0 %collective-permute-start.24 = (bf16[352,1024]{1,0:T(8,128)(2,1)}, bf16[352,1024]{1,0:T(8,128)(2,1)}, u32[]{:S(2)}, u32[]{:S(2)}) collective-permute-start(bf16[352,1024]{1,0:T(8,128)(2,1)} %get-tuple-element.414), channel_id=1, source_target_pairs={{0,16},{4,20},{8,24},{12,28},{16,0},{20,4},{24,8},{28,12},{1,17},{... | collective-permute-start | bytes 2162696 | tf_op jit(solution)/shard_map/ppermute | solution.py:38
  197.4 244.1 %reduce-scatter.7.cloned.1.call-start = ((), (), s32[]{:S(2)}) async-start(), calls=%async_computation.8 | async-start | bytes 2785280 | tf_op jit(solution)/shard_map/reduce_scatter | solution.py:931
  197.6 48.9 %collective-permute-start.26 = (bf16[512,1408]{1,0:T(8,128)(2,1)}, bf16[512,1408]{1,0:T(8,128)(2,1)}, u32[]{:S(2)}, u32[]{:S(2)}) collective-permute-start(bf16[512,1408]{1,0:T(8,128)(2,1)} %get-tuple-element.454.rest_0_), channel_id=1, source_target_pairs={{0,8},{4,12},{8,0},{12,4},{16,24},{20,28},{24,16},{28,20},{1,9},{5... | collective-permute-start | bytes 4325384 | tf_op jit(solution)/shard_map/ppermute | solution.py:38
  198.0 48.5 %collective-permute-start.28 = (bf16[512,1408]{1,0:T(8,128)(2,1)}, bf16[512,1408]{1,0:T(8,128)(2,1)}, u32[]{:S(2)}, u32[]{:S(2)}) collective-permute-start(bf16[512,1408]{1,0:T(8,128)(2,1)} %collective-permute-done.22.rest_1_), channel_id=1, source_target_pairs={{0,16},{4,20},{8,24},{12,28},{16,0},{20,4},{24,8},{28,12},{1,17},{... | collective-permute-start | bytes 4325384 | tf_op jit(solution)/shard_map/ppermute | solution.py:38
  199.0 47.2 %collective-permute-start.27 = (bf16[352,1024]{1,0:T(8,128)(2,1)}, bf16[352,1024]{1,0:T(8,128)(2,1)}, u32[]{:S(2)}, u32[]{:S(2)}) collective-permute-start(bf16[352,1024]{1,0:T(8,128)(2,1)} %collective-permute-done.18), channel_id=1, source_target_pairs={{0,8},{4,12},{8,0},{12,4},{16,24},{20,28},{24,16},{28,20},{1,9},{5... | collective-permute-start | bytes 2162696 | tf_op jit(solution)/shard_map/ppermute | solution.py:38
  200.7 45.8 %collective-permute-start.29 = (bf16[352,1024]{1,0:T(8,128)(2,1)}, bf16[352,1024]{1,0:T(8,128)(2,1)}, u32[]{:S(2)}, u32[]{:S(2)}) collective-permute-start(bf16[352,1024]{1,0:T(8,128)(2,1)} %collective-permute-done.23), channel_id=1, source_target_pairs={{0,16},{4,20},{8,24},{12,28},{16,0},{20,4},{24,8},{28,12},{1,17},{... | collective-permute-start | bytes 2162696 | tf_op jit(solution)/shard_map/ppermute | solution.py:38
  247.2 65.3 %collective-permute-start.31 = (bf16[512,1408]{1,0:T(8,128)(2,1)}, bf16[512,1408]{1,0:T(8,128)(2,1)}, u32[]{:S(2)}, u32[]{:S(2)}) collective-permute-start(bf16[512,1408]{1,0:T(8,128)(2,1)} %get-tuple-element.458.rest_4_), channel_id=1, source_target_pairs={{0,8},{4,12},{8,0},{12,4},{16,24},{20,28},{24,16},{28,20},{1,9},{5... | collective-permute-start | bytes 4325384 | tf_op jit(solution)/shard_map/ppermute | solution.py:38
  248.7 63.8 %collective-permute-start.32 = (bf16[512,1408]{1,0:T(8,128)(2,1)}, bf16[512,1408]{1,0:T(8,128)(2,1)}, u32[]{:S(2)}, u32[]{:S(2)}) collective-permute-start(bf16[512,1408]{1,0:T(8,128)(2,1)} %get-tuple-element.454.rest_0_), channel_id=1, source_target_pairs={{0,16},{4,20},{8,24},{12,28},{16,0},{20,4},{24,8},{28,12},{1,17},{... | collective-permute-start | bytes 4325384 | tf_op jit(solution)/shard_map/ppermute | solution.py:38
  249.7 62.8 %collective-permute-start.33 = (bf16[512,1408]{1,0:T(8,128)(2,1)}, bf16[512,1408]{1,0:T(8,128)(2,1)}, u32[]{:S(2)}, u32[]{:S(2)}) collective-permute-start(bf16[512,1408]{1,0:T(8,128)(2,1)} %collective-permute-done.25.rest_6_), channel_id=1, source_target_pairs={{0,8},{4,12},{8,0},{12,4},{16,24},{20,28},{24,16},{28,20},{1,9},{5... | collective-permute-start | bytes 4325384 | tf_op jit(solution)/shard_map/ppermute | solution.py:38
  250.3 63.3 %collective-permute-start.34 = (bf16[512,1408]{1,0:T(8,128)(2,1)}, bf16[512,1408]{1,0:T(8,128)(2,1)}, u32[]{:S(2)}, u32[]{:S(2)}) collective-permute-start(bf16[512,1408]{1,0:T(8,128)(2,1)} %collective-permute-done.26.rest_1_), channel_id=1, source_target_pairs={{0,16},{4,20},{8,24},{12,28},{16,0},{20,4},{24,8},{28,12},{1,17},{... | collective-permute-start | bytes 4325384 | tf_op jit(solution)/shard_map/ppermute | solution.py:38
  314.6 54.5 %collective-permute-start.35 = (bf16[1024,1024]{1,0:T(8,128)(2,1)}, bf16[1024,1024]{1,0:T(8,128)(2,1)}, u32[]{:S(2)}, u32[]{:S(2)}) collective-permute-start(bf16[1024,1024]{1,0:T(8,128)(2,1)} %copy-done.65), channel_id=1, source_target_pairs={{0,8},{4,12},{8,0},{12,4},{16,24},{20,28},{24,16},{28,20},{1,9},{5... | collective-permute-start | bytes 6291464 | tf_op jit(solution)/shard_map/ppermute | solution.py:38
  315.2 53.8 %collective-permute-start.37 = (bf16[1408,512]{1,0:T(8,128)(2,1)}, bf16[1408,512]{1,0:T(8,128)(2,1)}, u32[]{:S(2)}, u32[]{:S(2)}) collective-permute-start(bf16[1408,512]{1,0:T(8,128)(2,1)} %copy-done.70), channel_id=1, source_target_pairs={{0,16},{4,20},{8,24},{12,28},{16,0},{20,4},{24,8},{28,12},{1,17},{... | collective-permute-start | bytes 4325384 | tf_op jit(solution)/shard_map/ppermute | solution.py:38
  316.2 52.8 %collective-permute-start.36 = (bf16[1024,384]{1,0:T(8,128)(2,1)}, bf16[1024,384]{1,0:T(8,128)(2,1)}, u32[]{:S(2)}, u32[]{:S(2)}) collective-permute-start(bf16[1024,384]{1,0:T(8,128)(2,1)} %copy-done.75), channel_id=1, source_target_pairs={{0,16},{4,20},{8,24},{12,28},{16,0},{20,4},{24,8},{28,12},{1,17},{... | collective-permute-start | bytes 2359304 | tf_op jit(solution)/shard_map/ppermute | solution.py:38
  379.7 124.0 %all-gather.11.cloned.1.call-start = ((), (), s32[]{:S(2)}) async-start(), calls=%async_computation.9 | async-start | bytes 2621440 | tf_op jit(solution)/shard_map/all_gather | solution.py:928
  379.8 30.0 %collective-permute-start.39 = (bf16[512,1024]{1,0:T(8,128)(2,1)}, bf16[512,1024]{1,0:T(8,128)(2,1)S(1)}, u32[]{:S(2)}, u32[]{:S(2)}) collective-permute-start(bf16[512,1024]{1,0:T(8,128)(2,1)} %get-tuple-element.500), channel_id=1, source_target_pairs={{0,16},{4,20},{8,24},{12,28},{16,0},{20,4},{24,8},{28,12},{1,17},{... | collective-permute-start | bytes 3145736 | tf_op jit(solution)/shard_map/ppermute | solution.py:38
  381.1 27.8 %collective-permute-start.41 = (bf16[704,512]{1,0:T(8,128)(2,1)}, bf16[704,512]{1,0:T(8,128)(2,1)S(1)}, u32[]{:S(2)}, u32[]{:S(2)}) collective-permute-start(bf16[704,512]{1,0:T(8,128)(2,1)} %get-tuple-element.502), channel_id=1, source_target_pairs={{0,8},{4,12},{8,0},{12,4},{16,24},{20,28},{24,16},{28,20},{1,9},{5... | collective-permute-start | bytes 2162696 | tf_op jit(solution)/shard_map/ppermute | solution.py:38
  409.8 42.4 %collective-permute-start.42 = (bf16[704,1024]{1,0:T(8,128)(2,1)}, bf16[704,1024]{1,0:T(8,128)(2,1)}, u32[]{:S(2)}, u32[]{:S(2)}) collective-permute-start(bf16[704,1024]{1,0:T(8,128)(2,1)} %get-tuple-element.511), channel_id=1, source_target_pairs={{0,8},{4,12},{8,0},{12,4},{16,24},{20,28},{24,16},{28,20},{1,9},{5... | collective-permute-start | bytes 4325384 | tf_op jit(solution)/shard_map/ppermute | solution.py:38
  411.2 41.0 %collective-permute-start.43 = (bf16[704,1024]{1,0:T(8,128)(2,1)}, bf16[704,1024]{1,0:T(8,128)(2,1)}, u32[]{:S(2)}, u32[]{:S(2)}) collective-permute-start(bf16[704,1024]{1,0:T(8,128)(2,1)} %get-tuple-element.514), channel_id=1, source_target_pairs={{0,16},{4,20},{8,24},{12,28},{16,0},{20,4},{24,8},{28,12},{1,17},{... | collective-permute-start | bytes 4325384 | tf_op jit(solution)/shard_map/ppermute | solution.py:38
  452.2 190.2 %reduce-scatter.11.cloned.1.call-start = ((), (), s32[]{:S(2)}) async-start(), calls=%async_computation.11 | async-start | bytes 2621440 | tf_op jit(solution)/shard_map/reduce_scatter | solution.py:931
  452.3 51.5 %collective-permute-start.48 = (bf16[512,1408]{1,0:T(8,128)(2,1)}, bf16[512,1408]{1,0:T(8,128)(2,1)}, u32[]{:S(2)}, u32[]{:S(2)}) collective-permute-start(bf16[512,1408]{1,0:T(8,128)(2,1)} %copy-done.69), channel_id=1, source_target_pairs={{0,8},{4,12},{8,0},{12,4},{16,24},{20,28},{24,16},{28,20},{1,9},{5... | collective-permute-start | bytes 4325384 | tf_op jit(solution)/shard_map/ppermute | solution.py:38
  453.0 50.8 %collective-permute-start.49 = (bf16[512,1408]{1,0:T(8,128)(2,1)}, bf16[512,1408]{1,0:T(8,128)(2,1)}, u32[]{:S(2)}, u32[]{:S(2)}) collective-permute-start(bf16[512,1408]{1,0:T(8,128)(2,1)} %copy-done.68), channel_id=1, source_target_pairs={{0,16},{4,20},{8,24},{12,28},{16,0},{20,4},{24,8},{28,12},{1,17},{... | collective-permute-start | bytes 4325384 | tf_op jit(solution)/shard_map/ppermute | solution.py:38
  472.0 30.0 %collective-permute-start.51 = (bf16[352,1024]{1,0:T(8,128)(2,1)S(1)}, bf16[352,1024]{1,0:T(8,128)(2,1)S(1)}, u32[]{:S(2)}, u32[]{:S(2)}) collective-permute-start(bf16[352,1024]{1,0:T(8,128)(2,1)S(1)} %get-tuple-element.687), channel_id=1, source_target_pairs={{0,8},{4,12},{8,0},{12,4},{16,24},{20,28},{24,16},{28,20},{1,9},{5... | collective-permute-start | bytes 2162696 | tf_op jit(solution)/shard_map/ppermute | solution.py:38
  473.7 29.1 %collective-permute-start.50 = (bf16[352,1024]{1,0:T(8,128)(2,1)S(1)}, bf16[352,1024]{1,0:T(8,128)(2,1)S(1)}, u32[]{:S(2)}, u32[]{:S(2)}) collective-permute-start(bf16[352,1024]{1,0:T(8,128)(2,1)S(1)} %get-tuple-element.689), channel_id=1, source_target_pairs={{0,16},{4,20},{8,24},{12,28},{16,0},{20,4},{24,8},{28,12},{1,17},{... | collective-permute-start | bytes 2162696 | tf_op jit(solution)/shard_map/ppermute | solution.py:38
  503.9 34.8 %collective-permute-start.54 = (bf16[512,1408]{1,0:T(8,128)(2,1)}, bf16[512,1408]{1,0:T(8,128)(2,1)}, u32[]{:S(2)}, u32[]{:S(2)}) collective-permute-start(bf16[512,1408]{1,0:T(8,128)(2,1)} %copy-done.67), channel_id=1, source_target_pairs={{0,8},{4,12},{8,0},{12,4},{16,24},{20,28},{24,16},{28,20},{1,9},{5... | collective-permute-start | bytes 4325384 | tf_op jit(solution)/shard_map/ppermute | solution.py:38
  504.8 156.2 %reduce-scatter.9.cloned.1.call-start = ((), (), s32[]{:S(2)}) async-start(), calls=%async_computation.10 | async-start | bytes 2621440 | tf_op jit(solution)/shard_map/reduce_scatter | solution.py:931
  504.9 39.4 %collective-permute-start.55 = (bf16[512,1408]{1,0:T(8,128)(2,1)}, bf16[512,1408]{1,0:T(8,128)(2,1)S(1)}, u32[]{:S(2)}, u32[]{:S(2)}) collective-permute-start(bf16[512,1408]{1,0:T(8,128)(2,1)} %copy-done.66), channel_id=1, source_target_pairs={{0,16},{4,20},{8,24},{12,28},{16,0},{20,4},{24,8},{28,12},{1,17},{... | collective-permute-start | bytes 4325384 | tf_op jit(solution)/shard_map/ppermute | solution.py:38
  529.8 30.8 %collective-permute-start.53 = (bf16[1024,512]{1,0:T(8,128)(2,1)S(1)}, bf16[1024,512]{1,0:T(8,128)(2,1)S(1)}, u32[]{:S(2)}, u32[]{:S(2)}) collective-permute-start(bf16[1024,512]{1,0:T(8,128)(2,1)S(1)} %get-tuple-element.576), channel_id=1, source_target_pairs={{8,0},{12,4},{24,16},{28,20},{9,1},{13,5},{25,17},{29,21},{10,2},{... | collective-permute-start | bytes 3145736 | tf_op jit(solution)/shard_map/ppermute | solution.py:925
  541.5 35.4 %collective-permute-start.56 = (bf16[256,1408]{1,0:T(8,128)(2,1)}, bf16[256,1408]{1,0:T(8,128)(2,1)}, u32[]{:S(2)}, u32[]{:S(2)}) collective-permute-start(bf16[256,1408]{1,0:T(8,128)(2,1)} %get-tuple-element.676), channel_id=1, source_target_pairs={{0,16},{4,20},{8,24},{12,28},{16,0},{20,4},{24,8},{28,12},{1,17},{... | collective-permute-start | bytes 2162696 | tf_op jit(solution)/shard_map/ppermute | solution.py:38
  580.3 36.5 %collective-permute-start.61 = (bf16[1024,384]{1,0:T(8,128)(2,1)}, bf16[1024,384]{1,0:T(8,128)(2,1)}, u32[]{:S(2)}, u32[]{:S(2)}) collective-permute-start(bf16[1024,384]{1,0:T(8,128)(2,1)} %get-tuple-element.612), channel_id=1, source_target_pairs={{0,8},{4,12},{8,0},{12,4},{16,24},{20,28},{24,16},{28,20},{1,9},{5... | collective-permute-start | bytes 2359304 | tf_op jit(solution)/shard_map/ppermute | solution.py:38
  580.7 36.1 %collective-permute-start.62 = (bf16[1024,384]{1,0:T(8,128)(2,1)}, bf16[1024,384]{1,0:T(8,128)(2,1)}, u32[]{:S(2)}, u32[]{:S(2)}) collective-permute-start(bf16[1024,384]{1,0:T(8,128)(2,1)} %get-tuple-element.613), channel_id=1, source_target_pairs={{0,16},{4,20},{8,24},{12,28},{16,0},{20,4},{24,8},{28,12},{1,17},{... | collective-permute-start | bytes 2359304 | tf_op jit(solution)/shard_map/ppermute | solution.py:38
  581.7 35.1 %collective-permute-start.63 = (bf16[256,1408]{1,0:T(8,128)(2,1)}, bf16[256,1408]{1,0:T(8,128)(2,1)}, u32[]{:S(2)}, u32[]{:S(2)}) collective-permute-start(bf16[256,1408]{1,0:T(8,128)(2,1)} %get-tuple-element.614), channel_id=1, source_target_pairs={{0,16},{4,20},{8,24},{12,28},{16,0},{20,4},{24,8},{28,12},{1,17},{... | collective-permute-start | bytes 2162696 | tf_op jit(solution)/shard_map/ppermute | solution.py:38
  582.7 34.1 %collective-permute-start.64 = (bf16[256,1408]{1,0:T(8,128)(2,1)}, bf16[256,1408]{1,0:T(8,128)(2,1)}, u32[]{:S(2)}, u32[]{:S(2)}) collective-permute-start(bf16[256,1408]{1,0:T(8,128)(2,1)} %get-tuple-element.615), channel_id=1, source_target_pairs={{0,8},{4,12},{8,0},{12,4},{16,24},{20,28},{24,16},{28,20},{1,9},{5... | collective-permute-start | bytes 2162696 | tf_op jit(solution)/shard_map/ppermute | solution.py:38
  622.0 35.6 %collective-permute-start.76 = (bf16[256,1408]{1,0:T(8,128)(2,1)}, bf16[256,1408]{1,0:T(8,128)(2,1)S(1)}, u32[]{:S(2)}, u32[]{:S(2)}) collective-permute-start(bf16[256,1408]{1,0:T(8,128)(2,1)} %get-tuple-element.644), channel_id=1, source_target_pairs={{0,4},{4,0},{8,12},{12,8},{16,20},{20,16},{24,28},{28,24},{1,5},{5... | collective-permute-start | bytes 2162696 | tf_op jit(solution)/shard_map/ppermute | solution.py:38
  632.5 26.7 %collective-permute-start.75 = (bf16[256,1408]{1,0:T(8,128)(2,1)}, bf16[256,1408]{1,0:T(8,128)(2,1)S(1)}, u32[]{:S(2)}, u32[]{:S(2)}) collective-permute-start(bf16[256,1408]{1,0:T(8,128)(2,1)} %get-tuple-element.639), channel_id=1, source_target_pairs={{0,4},{4,0},{8,12},{12,8},{16,20},{20,16},{24,28},{28,24},{1,5},{5... | collective-permute-start | bytes 2162696 | tf_op jit(solution)/shard_map/ppermute | solution.py:38
  (188 other events, 1242.1 us)
Sparse Core Ops, SparseCore 0:
  12.4 48.3 all-gather.4
  69.6 48.2 all-gather.6
  141.8 44.7 reduce-scatter.4
  197.5 45.6 all-gather.8
  379.9 46.6 reduce-scatter.6
  452.3 45.9 all-gather.10
  504.9 44.2 reduce-scatter.10
  590.5 45.5 reduce-scatter.8

commit v6 on v5

--- a/solution.py
+++ b/solution.py
@@ -458,12 +458,18 @@
     )(query, *before, own, places, low, high)
 
 
-def attend_back_kernel(back, pair_rows, heads, q_ref, grad_ref, log_ref, *rest):
+def attend_back_kernel(
+    back, pair_rows, heads, core_ref, q_ref, mine_ref, other_ref, weight_ref, log_ref, *rest
+):
     before = rest[:back]
     own_ref, place_ref, low_ref, high_ref, cos_ref, sin_ref = rest[back : back + 6]
     dq_ref, own_out = rest[back + 6 : back + 8]
     before_out = rest[back + 8 : 2 * back + 8]
-    total_ref = rest[-1]
+    total_ref, grad_ref = rest[-2:]
+    half = pair_rows // 2
+    for ref, place in ((mine_ref, core_ref[0]), (other_ref, 1 - core_ref[0])):
+        rows = pl.ds(pl.multiple_of(place * half, half), half)
+        grad_ref[rows, :] = dot_last(ref[...], weight_ref[...]).astype(BF16)
     total_ref[...] = jnp.zeros_like(total_ref)
     for head in range(heads):
         cols = slice(head * HDIM, (head + 1) * HDIM)
@@ -491,21 +497,30 @@
         before_out[step][...] = total_ref[step * pair_rows : (step + 1) * pair_rows, :].astype(BF16)
 
 
-def attend_back(query, grad, logs, before, own, places, low, high, cosine, sine):
+def attend_back(
+    core, query, mine, other, weight, logs, before, own, places, low, high, cosine, sine
+):
     rows, columns = query.shape
     back = len(before)
+    vmem = pl.BlockSpec(memory_space=pltpu.VMEM)
     return call(
         functools.partial(attend_back_kernel, back, rows, columns // HDIM),
         (),
-        [pl.BlockSpec(memory_space=pltpu.VMEM)] * (9 + back),
-        [pl.BlockSpec(memory_space=pltpu.VMEM)] * (2 + back),
+        [vmem] * (11 + back),
+        [vmem] * (2 + back),
         [shaped(rows, columns, BF16), shaped(rows, 2 * columns, F32)]
         + [shaped(rows, 2 * columns, BF16)] * back,
-        48,
+        56,
         10 * rows * columns * (WINDOW + TILE),
-        scratch=[pltpu.VMEM(((back + 1) * rows, 2 * columns), F32)],
+        scratch=[
+            pltpu.VMEM(((back + 1) * rows, 2 * columns), F32),
+            pltpu.VMEM((rows, columns), BF16),
+        ],
         name="attend_back",
-    )(query, grad, logs, *before, own, places, low, high, cosine, sine)
+        scalars=1,
+    )(
+        core[None], query, mine, other, weight, logs, *before, own, places, low, high, cosine, sine
+    )
 
 
 def collect_kernel(heads, back, quads, core_ref, dq_ref, own_ref, cos_ref, sin_ref, x_ref, *rest):
@@ -937,6 +952,9 @@
         mine, other = finish(core[None], kept, arrived, axis)
         return mine, across(other, 1)
 
+    def merged(halves):
+        return merge(core, halves[0], across(halves[1], 1), None)
+
     hidden_in = residual_in.astype(F32)
     grad_out = cotangent.astype(F32)
     gain_one = attention_gain.astype(F32)
@@ -1030,12 +1048,12 @@
 
     before = [shifted(key_value, step) for step in range(back, 0, -1)]
     down_full = place_quads(sd_one | sd_two | sd_rest, quad, 1)
-    query, before, gu_two, edb_block, down_full = together(
-        query, before, gu_two, edb_block, down_full
+    output_rows = down_full[ffs_half:]
+    query, before, gu_two, edb_block, down_full, output_rows = together(
+        query, before, gu_two, edb_block, down_full, output_rows
     )
     edb_one, edb_two = gather_quads({0: edb_block}, down_one), gather_quads({0: edb_block}, down_two)
     attended, log_total = attend(query, before, key_value, key_place, low, high)
-    output_rows = down_full[ffs_half:]
     kept, other = split_core(attended, core, 0)
     other = dot(other, output_rows).astype(BF16)
     kept, other, cot_group, edb_one, edb_two = together(kept, other, cot_group, edb_one, edb_two)
@@ -1144,11 +1162,12 @@
     gua_sent, gub_sent = across(gua_grad[1], 2 * up_order[1]), across(gub_grad[1], 2 * down_order[1])
     sd_sent = across(sd_grad[1], 2 * down_order[1])
     (eda_grad, eda_out), (edb_grad, edb_out) = down_grads(active, grad_result, quad, quads)
-    eda_out, edb_out, grad_gate_pre, grad_up_pre, gua_sent, gub_sent, sd_sent = together(
-        eda_out, edb_out, grad_gate_pre, grad_up_pre, gua_sent, gub_sent, sd_sent
-    )
+    eda_out, edb_out, grad_gate_pre = together(eda_out, edb_out, grad_gate_pre)
     eda_sent, edb_sent = sent(eda_out, up_order[0]), sent(edb_out, down_order[0])
     ((eg_grad, eg_out),) = row_grads(rows_two, grad_gate_pre, quads, [(0, ffe, True, False)])
+    eg_grad, eg_out, grad_up_pre, gua_sent, gub_sent, sd_sent = together(
+        eg_grad, eg_out, grad_up_pre, gua_sent, gub_sent, sd_sent
+    )
     ((eu_grad, eu_out),) = row_grads(rows_two, grad_up_pre, quads, [(0, ffe, False, False)])
     spread, eg_grad, eg_out = together(spread, eg_grad, eg_out)
 
@@ -1206,19 +1225,17 @@
         group_branch, forward_part, sg_grad, su_grad, sd_grad, eg_grad, eg_out, eg_sent, eu_grad, eu_out, eu_sent, eda_grad,
         eda_sent, edb_grad, edb_sent,
     )
-    grad_branch = join_rows(core, group_branch, across(group_branch, 1))
+    other_branch = across(group_branch, 1)
     eg_sent = eg_sent + sent(eg_out[1:], up_order[0])
     eu_sent = eu_sent + sent(eu_out[1:], down_order[0])
 
     layer_sum = scattered(forward_part)
-    grad_attended = dot_last(grad_branch, down_full[ffs_half:]).astype(BF16)
     grad_query, grad_own, *grad_before = attend_back(
-        query, grad_attended, log_total, before, key_value, key_place, low, high, cosine, sine
-    )
-    (
-        grad_query, grad_before, grad_branch, eg_grad, eu_grad,
-    ) = together(
-        grad_query, grad_before, grad_branch, eg_grad, eu_grad,
+        core, query, group_branch, other_branch, output_rows, log_total, before, key_value, key_place,
+        low, high, cosine, sine,
+    )
+    grad_query, grad_before, group_branch, other_branch, eg_grad, eu_grad = together(
+        grad_query, grad_before, group_branch, other_branch, eg_grad, eu_grad
     )
     arrived = [shifted(sent, step - back) for step, sent in enumerate(grad_before)]
     cut = eg_grad[1].shape[0] // 2
@@ -1233,7 +1250,9 @@
         add_low(eu_grad[1][cut:], eu_sent[1][cut:]),
     ]
     eg_rest = across(eg_grad[1], 2 * up_order[1])
-    arrived, eg_grad, eu_grad, grad_branch = together(arrived, eg_grad, eu_grad, grad_branch)
+    arrived, eg_grad, eu_grad, group_branch, other_branch = together(
+        arrived, eg_grad, eu_grad, group_branch, other_branch
+    )
     eu_rest = across(eu_grad[1], 2 * down_order[1])
     (*partial, att_gain_part, bias_part), (qkv_a_grad, qkv_a_out), (qkv_b_grad, qkv_b_out) = collect(
         core, grad_query, grad_own, cosine, sine, rows_one, arrived, qkv_a, qkv_b
@@ -1246,13 +1265,14 @@
     partial_sum = core_sum(*partial)
 
     (
-        partial_sum, att_gain_part, bias_part, grad_branch, qkv_a_grad, qkv_b_grad, eda_grad,
+        partial_sum, att_gain_part, bias_part, group_branch, other_branch, qkv_a_grad, qkv_b_grad, eda_grad,
         eda_sent, edb_grad, edb_sent,
     ) = together(
-        partial_sum, att_gain_part, bias_part, grad_branch, qkv_a_grad, qkv_b_grad, eda_grad,
+        partial_sum, att_gain_part, bias_part, group_branch, other_branch, qkv_a_grad, qkv_b_grad, eda_grad,
         eda_sent, edb_grad, edb_sent,
     )
     grad_normed_one = scattered(partial_sum)
+    grad_branch = join_rows(core, group_branch, other_branch)
     o_grad, o_out = column_grads(attended, grad_branch, quad, quads, False)
     att_gain_part = flip_columns(att_gain_part[0], quad) / gain_one
     late = jnp.concatenate([att_gain_part, ff_gain_grad, router_grad.T.reshape(-1)])
@@ -1263,8 +1283,6 @@
     ) = together(
         late, qkv_a_sent, qkv_b_sent, eg_last, eu_last, eda_sent, edb_sent,
     )
-    eg_rest = jnp.concatenate([eg_rest, eg_last], axis=0)
-    eu_rest = jnp.concatenate([eu_rest, eu_last], axis=0)
     bias_part = bias_part.reshape(3, head_width)
     bias_part = jnp.concatenate(
         [jnp.where(core == 0, bias_part, 0.0), jnp.where(core == 0, 0.0, bias_part)], axis=1
@@ -1272,18 +1290,28 @@
     late = sum_everywhere(jnp.concatenate([late, bias_part.reshape(-1)]), [1], [])
     qkv_a_grad = first_sum(qkv_a_grad, qkv_a_sent)
     qkv_b_grad = first_sum(qkv_b_grad, qkv_b_sent)
+    o_grad = first_sum(o_grad, o_sent)
+    qkv_a_grad, qkv_b_grad, o_grad, eg_last, eu_last, eda_sent, edb_sent = together(
+        qkv_a_grad, qkv_b_grad, o_grad, eg_last, eu_last, eda_sent, edb_sent
+    )
+    eg_rest = jnp.concatenate([eg_rest, eg_last], axis=0)
+    eu_rest = jnp.concatenate([eu_rest, eu_last], axis=0)
     qkv_a_rest = across(qkv_a_grad[1], 2 * up_order[1])
     qkv_b_rest = across(qkv_b_grad[1], 2 * down_order[1])
-    o_grad = first_sum(o_grad, o_sent)
     o_rest = across(o_grad[1], 2 * down_order[1])
     late = sum_everywhere(late, quad_masks, [])
-    eg_grad = merge(core, *finished(*rest_parts(eg_grad[0], eg_rest, up_order), 0), None)
-    eu_grad = merge(core, *finished(*rest_parts(eu_grad[0], eu_rest, down_order), 0), None)
-    eda_mine, eda_arrived = finished(*rest_parts(eda_grad[0], eda_sent, up_order), 0)
-    edb_mine, edb_arrived = finished(*rest_parts(edb_grad[0], edb_sent, down_order), 0)
-    ed_grad = jnp.concatenate(
-        [merge(core, eda_mine, eda_arrived, None), merge(core, edb_mine, edb_arrived, None)], axis=2
-    )
+    last = [
+        finish(core[None], *rest_parts(kept, arrived, order), 0)
+        for kept, arrived, order in (
+            (eg_grad[0], eg_rest, up_order),
+            (eu_grad[0], eu_rest, down_order),
+            (eda_grad[0], eda_sent, up_order),
+            (edb_grad[0], edb_sent, down_order),
+        )
+    ]
+    last, qkv_a_rest, qkv_b_rest, o_rest = together(last, qkv_a_rest, qkv_b_rest, o_rest)
+    eg_grad, eu_grad, eda_grad, edb_grad = [merged(halves) for halves in last]
+    ed_grad = jnp.concatenate([eda_grad, edb_grad], axis=2)
     layer_out = (mixed + layer_sum.astype(F32)).astype(BF16)
     qkv_a_mine, qkv_a_arrived = finished(*rest_parts(qkv_a_grad[0], qkv_a_rest, up_order), 0)
     qkv_b_mine, qkv_b_arrived = finished(*rest_parts(qkv_b_grad[0], qkv_b_rest, down_order), 0)

time: 685 us -> 676 us (0.987)
  waiting for transfers between devices: 226 us -> 209 us
  local copies, waits for them, and re-layouts: 80.2 us -> 87.1 us
    ppermute x75, waiting for transfers between devices: 193 us -> 177 us  [across(): return lax.ppermute(block, 'grp', [(i, i ^ mask) for i in range(count)])]
  transfers between devices with their start and end apart: 87 -> 87, of which waited for: 30 -> 28; matrix products, arithmetic and copies ran while one was open for 16% -> 15% of each run, Pallas kernels for 29% -> 30%
where the time goes in v6:
time: 676 us; the launch traced here: 667 us
  waiting for transfers between devices  209 us (31%)
  Pallas kernels  209 us (31%)
  local copies, waits for them, and re-layouts  87.1 us (13%)
  other arithmetic  69.5 us (10%)
  starting transfers between devices  68.3 us (10%)
  between operations  16.4 us (2%)
  matrix products  7.13 us (1%)
    pallas_call x36, Pallas kernels, run(): pl.pallas_call(kernel, grid_spec=pltpu.PrefetchScalarGridSpec(num_scalar_...  190 us
    ppermute x75, waiting for transfers between devices, across(): return lax.ppermute(block, 'grp', [(i, i ^ mask) for i in range(count)])  177 us
    ppermute x75, starting transfers between devices, across(): return lax.ppermute(block, 'grp', [(i, i ^ mask) for i in range(count)])  58.6 us
    unnamed x300, local copies, waits for them, and re-layouts  51.8 us
    convert_element_type x12, other arithmetic, add_low(): return (left.astype(F32) + right.astype(F32)).astype(BF16)  26.2 us
    ppermute x2, waiting for transfers between devices, shifted(): return lax.ppermute(values, 'grp', route)  24.9 us
    dynamic_update_slice x14, local copies, waits for them, and re-layouts, place_quads(): whole = lax.dynamic_update_slice(whole, pieces[key], start)  24.2 us
  transfers between devices with their start and end apart: 87, of which 28 were waited for; matrix products, arithmetic and copies ran while one was open for 15% of the time, Pallas kernels for 30%

profile of v6, /device:TPU:0, one launch (start us, length us, event | category | flops | bytes accessed | tf_op | source)
XLA Modules:
  0.0 666.8 jit_solution(16908923851648947547)
XLA Ops:
  13.5 2.7 collective-permute-start.1
  30.3 5.4 collective-permute-done.3.rest_6_.rest_7_
  44.3 23.9 %collective-permute-done.10.rest_3_.rest_4_ = bf16[512,384]{1,0:T(8,128)(2,1)S(1)} collective-permute-done((bf16[512,384]{1,0:T(8,128)(2,1)S(1)}, bf16[512,384]{1,0:T(8,128)(2,1)S(1)}, u32[]{:S(2)}, u32[]{:S(2)}) %collective-permute-start.10) | collective-permute-done | bytes 393248 | tf_op jit(solution)/shard_map/ppermute | solution.py:38
  78.0 5.2 project.1
  83.3 3.5 collective-permute-start.15
  91.4 4.1 collective-permute-done.17
  96.7 7.9 %collective-permute-done.16.rest_2_ = bf16[512,1408]{1,0:T(8,128)(2,1)S(1)} collective-permute-done((bf16[512,1408]{1,0:T(8,128)(2,1)}, bf16[512,1408]{1,0:T(8,128)(2,1)S(1)}, u32[]{:S(2)}, u32[]{:S(2)}) %collective-permute-start.16) | collective-permute-done | bytes 1441824 | tf_op jit(solution)/shard_map/ppermute | solution.py:38
  104.6 12.1 %collective-permute-done.15.rest_0_ = bf16[1024,512]{1,0:T(8,128)(2,1)S(1)} collective-permute-done((bf16[1024,512]{1,0:T(8,128)(2,1)S(1)}, bf16[1024,512]{1,0:T(8,128)(2,1)S(1)}, u32[]{:S(2)}, u32[]{:S(2)}) %collective-permute-start.15) | collective-permute-done | bytes 1048608 | tf_op jit(solution)/shard_map/ppermute | solution.py:940
  118.7 2.5 collective-permute-start.19
  122.9 6.7 %attend.1 = (bf16[1024,256]{1,0:T(8,128)(2,1)S(1)}, f32[1024,256]{1,0:T(8,128)S(1)}) custom-call(bf16[1024,256]{1,0:T(8,128)(2,1)S(1)} %copy-done.91, bf16[1024,512]{1,0:T(8,128)(2,1)S(1)} %copy-done.75, bf16[1024,512]{1,0:T(8,128)(2,1)S(1)} %copy-done.73, s32[1,2048]{1,0:T(1,128)S(1)} %iota_add_fusion.rest_2_, s32[1024,1]{1,0:T(8,128)S(1)} %copy.89.rest_3_, ...), custom_call_target="tpu_custom_call" | custom-call | flops 1342177280 | bytes 4210688 | tf_op jit(solution)/shard_map/attend/pallas_call | solution.py:190
  132.7 2.7 collective-permute-done.18
  137.7 3.6 collective-permute-done.20.right_ref
  147.8 3.2 broadcast_in_dim.32
  153.0 2.1 constant_dynamic-update-slice_fusion.20
  157.2 36.1 %collective-permute-done.23 = bf16[352,1024]{1,0:T(8,128)(2,1)} collective-permute-done((bf16[352,1024]{1,0:T(8,128)(2,1)}, bf16[352,1024]{1,0:T(8,128)(2,1)}, u32[]{:S(2)}, u32[]{:S(2)}) %collective-permute-start.23) | collective-permute-done | bytes 720928 | tf_op jit(solution)/shard_map/ppermute | solution.py:38
  203.4 3.7 join_rows.5.cot_ref
  207.1 2.1 copy-done
  215.4 32.4 %collective-permute-done.27 = bf16[352,1024]{1,0:T(8,128)(2,1)S(1)} collective-permute-done((bf16[352,1024]{1,0:T(8,128)(2,1)}, bf16[352,1024]{1,0:T(8,128)(2,1)S(1)}, u32[]{:S(2)}, u32[]{:S(2)}) %collective-permute-start.27) | collective-permute-done | bytes 720928 | tf_op jit(solution)/shard_map/ppermute | solution.py:38
  258.1 27.3 %shared.1 = (bf16[1024,704]{1,0:T(8,128)(2,1)}, bf16[1024,2048]{1,0:T(8,128)(2,1)}, bf16[1024,2048]{1,0:T(8,128)(2,1)}, bf16[1024,2048]{1,0:T(8,128)(2,1)}, f32[...) custom-call(s32[1]{0:T(128)} %bitcast.core_ref, bf16[1024,2048]{1,0:T(8,128)(2,1)} %copy-done.2, bf16[960,2048]{1,0:T(8,128)(2,1)} %copy-done.104, ...), custom_call_target="tpu_custom_call" | custom-call | flops 17716740096 | bytes 35266564 | tf_op jit(solution)/shard_map/shared/pallas_call | solution.py:190
  285.4 10.2 %row_grads.3 = (bf16[512,1024]{1,0:T(8,128)(2,1)S(1)}, bf16[512,1024]{1,0:T(8,128)(2,1)S(1)}, bf16[1024,1024]{1,0:T(8,128)(2,1)S(1)}, bf16[512,384]{1,0:T(8,128)...) custom-call(bf16[1024,2048]{1,0:T(8,128)(2,1)} %copy-done.2, ...), custom_call_target="tpu_custom_call" | custom-call | flops 5905580032 | bytes 12845056 | tf_op jit(solution)/shard_map/row_grads/pallas_call | solution.py:190
  296.5 2.6 constant_dynamic-update-slice_fusion.8
  299.1 2.1 constant_dynamic-update-slice_fusion.7
  306.2 5.6 column_grads.2
  318.9 51.8 %expert.1 = (bf16[1024,1408]{1,0:T(8,128)(2,1)}, bf16[1024,2048]{1,0:T(8,128)(2,1)}, bf16[768,2048]{1,0:T(8,128)(2,1)}, bf16[512,2048]{1,0:T(8,128)(2,1)}, bf16[...) custom-call(s32[1]{0:T(128)} %bitcast.core_ref, ...), custom_call_target="tpu_custom_call" | custom-call | flops 35433480192 | bytes 58008068 | tf_op jit(solution)/shard_map/expert/pallas_call | solution.py:190
  372.9 2.8 add_convert_fusion.12
  375.7 3.7 add_convert_fusion.2
  379.3 2.1 add_rows.5
  385.7 11.7 %down_grads.1 = (bf16[352,1024]{1,0:T(8,128)(2,1)S(1)}, bf16[352,1024]{1,0:T(8,128)(2,1)S(1)}, bf16[704,1024]{1,0:T(8,128)(2,1)}, bf16[352,1024]{1,0:T(8,128)(2,...) custom-call(s32[1]{0:T(128)} %bitcast.13.quad_ref, bf16[1024,1408]{1,0:T(8,128)(2,1)} %get-tuple-element.524.act_ref, ...), custom_call_target="tpu_custom_call" | custom-call | flops 5905580032 | bytes 12845056 | tf_op jit(solution)/shard_map/down_grads/pallas_call | solution.py:856
  402.9 10.1 %row_grads.4 = (bf16[512,1408]{1,0:T(8,128)(2,1)S(1)}, bf16[512,1408]{1,0:T(8,128)(2,1)S(1)}, bf16[512,1408]{1,0:T(8,128)(2,1)S(1)}, bf16[512,1408]{1,0:T(8,128)(2,1)S(1)}) custom-call(bf16[1024,2048]{1,0:T(8,128)(2,1)} %copy-done.2, bf16[1024,1408]{1,0:T(8,128)(2,1)} %get-tuple-element.529.grad_ref), custom_call_target="tpu_custom_call" | custom-call | flops 5905580032 | bytes 12845056 | tf_op jit(solution)/shard_map/row_grads/pallas_call | solution.py:190
  418.9 10.1 %row_grads.5 = (bf16[512,1408]{1,0:T(8,128)(2,1)S(1)}, bf16[512,1408]{1,0:T(8,128)(2,1)S(1)}, bf16[512,1408]{1,0:T(8,128)(2,1)S(1)}, bf16[512,1408]{1,0:T(8,128)(2,1)S(1)}) custom-call(bf16[1024,2048]{1,0:T(8,128)(2,1)} %copy-done.2, bf16[1024,1408]{1,0:T(8,128)(2,1)} %get-tuple-element.557.grad_ref), custom_call_target="tpu_custom_call" | custom-call | flops 5905580032 | bytes 12845056 | tf_op jit(solution)/shard_map/row_grads/pallas_call | solution.py:190
  444.8 2.4 collective-permute-done.44.right_ref
  449.1 4.0 add_rows.6
  456.2 2.9 add_convert_fusion.8
  459.7 2.8 add_convert_fusion.10
  468.8 23.8 %collective-permute-done.51.arrived_ref = bf16[352,1024]{1,0:T(8,128)(2,1)S(1)} collective-permute-done((bf16[352,1024]{1,0:T(8,128)(2,1)S(1)}, bf16[352,1024]{1,0:T(8,128)(2,1)S(1)}, u32[]{:S(2)}, u32[]{:S(2)}) %collective-permute-start.51) | collective-permute-done | bytes 720928 | tf_op jit(solution)/shard_map/ppermute | solution.py:38
  500.0 18.4 %attend_back.1 = (bf16[1024,256]{1,0:T(8,128)(2,1)}, f32[1024,512]{1,0:T(8,128)}, bf16[1024,512]{1,0:T(8,128)(2,1)}) custom-call(s32[1]{0:T(128)} %bitcast.core_ref, bf16[1024,256]{1,0:T(8,128)(2,1)} %copy-done.90, bf16[512,2048]{1,0:T(8,128)(2,1)} %all-gather.11.cloned.1.call-done.mine_ref.own_ref, bf16[512,2048]{1,0:T(8,128)(2,1)} %copy-done.11, ...), custom_call_target="tpu_custom_call" | custom-call | flops 3355443200 | bytes 13647876 | tf_op jit(solution)/shard_map/attend_back/pallas_call | solution.py:190
  519.8 9.3 %collective-permute-done.54 = bf16[512,1408]{1,0:T(8,128)(2,1)} collective-permute-done((bf16[512,1408]{1,0:T(8,128)(2,1)}, bf16[512,1408]{1,0:T(8,128)(2,1)}, u32[]{:S(2)}, u32[]{:S(2)}) %collective-permute-start.54) | collective-permute-done | bytes 1441824 | tf_op jit(solution)/shard_map/ppermute | solution.py:38
  529.1 2.8 add_convert_fusion.6
  538.2 12.9 %collective-permute-done.53.rest_0_ = bf16[1024,512]{1,0:T(8,128)(2,1)S(1)} collective-permute-done((bf16[1024,512]{1,0:T(8,128)(2,1)}, bf16[1024,512]{1,0:T(8,128)(2,1)S(1)}, u32[]{:S(2)}, u32[]{:S(2)}) %collective-permute-start.53) | collective-permute-done | bytes 1048608 | tf_op jit(solution)/shard_map/ppermute | solution.py:940
  552.0 15.4 %collect.1 = (bf16[768,2048]{1,0:T(8,128)(2,1)}, bf16[512,2048]{1,0:T(8,128)(2,1)}, f32[1,2048]{1,0:T(1,128)}, f32[1,768]{1,0:T(1,128)}, bf16[512,384]{1,0:T(8,1...) custom-call(s32[1]{0:T(128)} %bitcast.core_ref, ...), custom_call_target="tpu_custom_call" | custom-call | flops 6442450944 | bytes 20458500 | tf_op jit(solution)/shard_map/collect/pallas_call | solution.py:190
  576.9 4.0 add_rows.7
  588.6 2.6 collective-permute-start.60
  591.2 2.4 column_grads.3
  593.6 7.2 %collective-permute-done.60 = f32[22528]{0:T(1024)S(1)} collective-permute-done((f32[22528]{0:T(1024)S(1)}, f32[22528]{0:T(1024)S(1)}, u32[]{:S(2)}, u32[]{:S(2)}) %collective-permute-start.60) | collective-permute-done | bytes 90144 | tf_op jit(solution)/shard_map/ppermute | solution.py:94
  601.9 5.5 collective-permute-done.63
  615.9 2.3 collective-permute-done.65
  633.0 2.9 collective-permute-done.68.arrived_ref
  639.1 2.5 add_convert_fusion.14
  (625 shorter events, 226.7 us)
Async XLA Ops:
  7.2 62.9 %all-gather.5.cloned.1.call-start = ((), (), s32[]{:S(2)}) async-start(), calls=%async_computation.4 | async-start | bytes 2621440 | tf_op jit(solution)/shard_map/all_gather | solution.py:943
  12.3 120.4 %all-gather.7.cloned.1.call-start = ((), (), s32[]{:S(2)}) async-start(), calls=%async_computation.5 | async-start | bytes 2785280 | tf_op jit(solution)/shard_map/all_gather | solution.py:943
  36.9 33.3 %collective-permute-start.12 = (bf16[960,512]{1,0:T(8,128)(2,1)}, bf16[960,512]{1,0:T(8,128)(2,1)}, u32[]{:S(2)}, u32[]{:S(2)}) collective-permute-start(bf16[960,512]{1,0:T(8,128)(2,1)} %pad_maximum_fusion.6), channel_id=1, source_target_pairs={{0,16},{4,20},{8,24},{12,28},{16,0},{20,4},{24,8},{28,12},{1,17},{... | collective-permute-start | bytes 2949128 | tf_op jit(solution)/shard_map/ppermute | solution.py:38
  38.4 31.7 %collective-permute-start.13 = (bf16[960,512]{1,0:T(8,128)(2,1)}, bf16[960,512]{1,0:T(8,128)(2,1)}, u32[]{:S(2)}, u32[]{:S(2)}) collective-permute-start(bf16[960,512]{1,0:T(8,128)(2,1)} %pad_maximum_fusion.6), channel_id=1, source_target_pairs={{0,8},{4,12},{8,0},{12,4},{16,24},{20,28},{24,16},{28,20},{1,9},{5... | collective-permute-start | bytes 2949128 | tf_op jit(solution)/shard_map/ppermute | solution.py:38
  41.3 26.8 %collective-permute-start.10 = (bf16[512,384]{1,0:T(8,128)(2,1)S(1)}, bf16[512,384]{1,0:T(8,128)(2,1)S(1)}, u32[]{:S(2)}, u32[]{:S(2)}) collective-permute-start(bf16[512,384]{1,0:T(8,128)(2,1)S(1)} %collective-permute-done.1.rest_1_.rest_2_), channel_id=1, source_target_pairs={{0,16},{4,20},{8,24},{12,28},{16,0},{20,4},{24,8},{28,12},{1,17},{... | collective-permute-start | bytes 1179656 | tf_op jit(solution)/shard_map/ppermute | solution.py:38
  42.6 26.8 %collective-permute-start.11 = (bf16[512,384]{1,0:T(8,128)(2,1)S(1)}, bf16[512,384]{1,0:T(8,128)(2,1)S(1)}, u32[]{:S(2)}, u32[]{:S(2)}) collective-permute-start(bf16[512,384]{1,0:T(8,128)(2,1)S(1)} %collective-permute-done.3.rest_6_.rest_7_), channel_id=1, source_target_pairs={{0,8},{4,12},{8,0},{12,4},{16,24},{20,28},{24,16},{28,20},{1,9},{5... | collective-permute-start | bytes 1179656 | tf_op jit(solution)/shard_map/ppermute | solution.py:38
  70.3 124.5 %reduce-scatter.5.cloned.1.call-start = ((), (), s32[]{:S(2)}) async-start(), calls=%async_computation.6 | async-start | bytes 2621440 | tf_op jit(solution)/shard_map/reduce_scatter | solution.py:946
  70.3 34.3 %collective-permute-start.16 = (bf16[512,1408]{1,0:T(8,128)(2,1)}, bf16[512,1408]{1,0:T(8,128)(2,1)S(1)}, u32[]{:S(2)}, u32[]{:S(2)}) collective-permute-start(bf16[512,1408]{1,0:T(8,128)(2,1)} %pad_maximum_fusion.1.rest_0_), channel_id=1, source_target_pairs={{0,16},{4,20},{8,24},{12,28},{16,0},{20,4},{24,8},{28,12},{1,17},{... | collective-permute-start | bytes 4325384 | tf_op jit(solution)/shard_map/ppermute | solution.py:38
  71.4 24.1 %collective-permute-start.17 = (bf16[960,512]{1,0:T(8,128)(2,1)}, bf16[960,512]{1,0:T(8,128)(2,1)S(1)}, u32[]{:S(2)}, u32[]{:S(2)}) collective-permute-start(bf16[960,512]{1,0:T(8,128)(2,1)} %collective-permute-done.12), channel_id=1, source_target_pairs={{0,8},{4,12},{8,0},{12,4},{16,24},{20,28},{24,16},{28,20},{1,9},{5... | collective-permute-start | bytes 2949128 | tf_op jit(solution)/shard_map/ppermute | solution.py:38
  83.3 33.3 %collective-permute-start.15 = (bf16[1024,512]{1,0:T(8,128)(2,1)S(1)}, bf16[1024,512]{1,0:T(8,128)(2,1)S(1)}, u32[]{:S(2)}, u32[]{:S(2)}) collective-permute-start(bf16[1024,512]{1,0:T(8,128)(2,1)S(1)} %get-tuple-element.407.rest_1_), channel_id=1, source_target_pairs={{0,8},{4,12},{16,24},{20,28},{1,9},{5,13},{17,25},{21,29},{2,10},{... | collective-permute-start | bytes 3145736 | tf_op jit(solution)/shard_map/ppermute | solution.py:940
  143.4 104.8 %all-gather.9.cloned.1.call-start = ((), (), s32[]{:S(2)}) async-start(), calls=%async_computation.7 | async-start | bytes 2621440 | tf_op jit(solution)/shard_map/all_gather | solution.py:943
  143.5 51.3 %collective-permute-start.21 = (bf16[512,2176]{1,0:T(8,128)(2,1)S(1)}, bf16[512,2176]{1,0:T(8,128)(2,1)}, u32[]{:S(2)}, u32[]{:S(2)}) collective-permute-start(bf16[512,2176]{1,0:T(8,128)(2,1)S(1)} %copy-done.8), channel_id=1, source_target_pairs={{0,4},{4,0},{8,12},{12,8},{16,20},{20,16},{24,28},{28,24},{1,5},{5... | collective-permute-start | bytes 6684680 | tf_op jit(solution)/shard_map/ppermute | solution.py:38
  143.7 51.1 %collective-permute-start.22 = (bf16[512,1408]{1,0:T(8,128)(2,1)}, bf16[512,1408]{1,0:T(8,128)(2,1)}, u32[]{:S(2)}, u32[]{:S(2)}) collective-permute-start(bf16[512,1408]{1,0:T(8,128)(2,1)} %pad_maximum_fusion.1.rest_0_), channel_id=1, source_target_pairs={{0,8},{4,12},{8,0},{12,4},{16,24},{20,28},{24,16},{28,20},{1,9},{5... | collective-permute-start | bytes 4325384 | tf_op jit(solution)/shard_map/ppermute | solution.py:38
  145.4 49.3 %collective-permute-start.25 = (bf16[512,1408]{1,0:T(8,128)(2,1)}, bf16[512,1408]{1,0:T(8,128)(2,1)}, u32[]{:S(2)}, u32[]{:S(2)}) collective-permute-start(bf16[512,1408]{1,0:T(8,128)(2,1)} %get-tuple-element.488.rest_4_), channel_id=1, source_target_pairs={{0,16},{4,20},{8,24},{12,28},{16,0},{20,4},{24,8},{28,12},{1,17},{... | collective-permute-start | bytes 4325384 | tf_op jit(solution)/shard_map/ppermute | solution.py:38
  146.4 46.9 %collective-permute-start.23 = (bf16[352,1024]{1,0:T(8,128)(2,1)}, bf16[352,1024]{1,0:T(8,128)(2,1)}, u32[]{:S(2)}, u32[]{:S(2)}) collective-permute-start(bf16[352,1024]{1,0:T(8,128)(2,1)} %get-tuple-element.443), channel_id=1, source_target_pairs={{0,8},{4,12},{8,0},{12,4},{16,24},{20,28},{24,16},{28,20},{1,9},{5... | collective-permute-start | bytes 2162696 | tf_op jit(solution)/shard_map/ppermute | solution.py:38
  146.7 48.0 %collective-permute-start.24 = (bf16[352,1024]{1,0:T(8,128)(2,1)}, bf16[352,1024]{1,0:T(8,128)(2,1)}, u32[]{:S(2)}, u32[]{:S(2)}) collective-permute-start(bf16[352,1024]{1,0:T(8,128)(2,1)} %get-tuple-element.443), channel_id=1, source_target_pairs={{0,16},{4,20},{8,24},{12,28},{16,0},{20,4},{24,8},{28,12},{1,17},{... | collective-permute-start | bytes 2162696 | tf_op jit(solution)/shard_map/ppermute | solution.py:38
  199.1 234.5 %reduce-scatter.7.cloned.1.call-start = ((), (), s32[]{:S(2)}) async-start(), calls=%async_computation.8 | async-start | bytes 2785280 | tf_op jit(solution)/shard_map/reduce_scatter | solution.py:946
  199.3 48.9 %collective-permute-start.26 = (bf16[512,1408]{1,0:T(8,128)(2,1)}, bf16[512,1408]{1,0:T(8,128)(2,1)}, u32[]{:S(2)}, u32[]{:S(2)}) collective-permute-start(bf16[512,1408]{1,0:T(8,128)(2,1)} %get-tuple-element.484.rest_0_), channel_id=1, source_target_pairs={{0,8},{4,12},{8,0},{12,4},{16,24},{20,28},{24,16},{28,20},{1,9},{5... | collective-permute-start | bytes 4325384 | tf_op jit(solution)/shard_map/ppermute | solution.py:38
  199.7 48.5 %collective-permute-start.28 = (bf16[512,1408]{1,0:T(8,128)(2,1)}, bf16[512,1408]{1,0:T(8,128)(2,1)}, u32[]{:S(2)}, u32[]{:S(2)}) collective-permute-start(bf16[512,1408]{1,0:T(8,128)(2,1)} %collective-permute-done.22.rest_1_), channel_id=1, source_target_pairs={{0,16},{4,20},{8,24},{12,28},{16,0},{20,4},{24,8},{28,12},{1,17},{... | collective-permute-start | bytes 4325384 | tf_op jit(solution)/shard_map/ppermute | solution.py:38
  200.7 47.1 %collective-permute-start.27 = (bf16[352,1024]{1,0:T(8,128)(2,1)}, bf16[352,1024]{1,0:T(8,128)(2,1)S(1)}, u32[]{:S(2)}, u32[]{:S(2)}) collective-permute-start(bf16[352,1024]{1,0:T(8,128)(2,1)} %collective-permute-done.18), channel_id=1, source_target_pairs={{0,8},{4,12},{8,0},{12,4},{16,24},{20,28},{24,16},{28,20},{1,9},{5... | collective-permute-start | bytes 2162696 | tf_op jit(solution)/shard_map/ppermute | solution.py:38
  202.4 45.8 %collective-permute-start.29 = (bf16[352,1024]{1,0:T(8,128)(2,1)}, bf16[352,1024]{1,0:T(8,128)(2,1)}, u32[]{:S(2)}, u32[]{:S(2)}) collective-permute-start(bf16[352,1024]{1,0:T(8,128)(2,1)} %collective-permute-done.23), channel_id=1, source_target_pairs={{0,16},{4,20},{8,24},{12,28},{16,0},{20,4},{24,8},{28,12},{1,17},{... | collective-permute-start | bytes 2162696 | tf_op jit(solution)/shard_map/ppermute | solution.py:38
  248.9 64.0 %collective-permute-start.31 = (bf16[512,1408]{1,0:T(8,128)(2,1)}, bf16[512,1408]{1,0:T(8,128)(2,1)}, u32[]{:S(2)}, u32[]{:S(2)}) collective-permute-start(bf16[512,1408]{1,0:T(8,128)(2,1)} %get-tuple-element.488.rest_4_), channel_id=1, source_target_pairs={{0,8},{4,12},{8,0},{12,4},{16,24},{20,28},{24,16},{28,20},{1,9},{5... | collective-permute-start | bytes 4325384 | tf_op jit(solution)/shard_map/ppermute | solution.py:38
  250.4 62.6 %collective-permute-start.32 = (bf16[512,1408]{1,0:T(8,128)(2,1)}, bf16[512,1408]{1,0:T(8,128)(2,1)}, u32[]{:S(2)}, u32[]{:S(2)}) collective-permute-start(bf16[512,1408]{1,0:T(8,128)(2,1)} %get-tuple-element.484.rest_0_), channel_id=1, source_target_pairs={{0,16},{4,20},{8,24},{12,28},{16,0},{20,4},{24,8},{28,12},{1,17},{... | collective-permute-start | bytes 4325384 | tf_op jit(solution)/shard_map/ppermute | solution.py:38
  251.4 62.8 %collective-permute-start.33 = (bf16[512,1408]{1,0:T(8,128)(2,1)}, bf16[512,1408]{1,0:T(8,128)(2,1)}, u32[]{:S(2)}, u32[]{:S(2)}) collective-permute-start(bf16[512,1408]{1,0:T(8,128)(2,1)} %collective-permute-done.25.rest_6_), channel_id=1, source_target_pairs={{0,8},{4,12},{8,0},{12,4},{16,24},{20,28},{24,16},{28,20},{1,9},{5... | collective-permute-start | bytes 4325384 | tf_op jit(solution)/shard_map/ppermute | solution.py:38
  252.0 63.3 %collective-permute-start.34 = (bf16[512,1408]{1,0:T(8,128)(2,1)}, bf16[512,1408]{1,0:T(8,128)(2,1)}, u32[]{:S(2)}, u32[]{:S(2)}) collective-permute-start(bf16[512,1408]{1,0:T(8,128)(2,1)} %collective-permute-done.26.rest_1_), channel_id=1, source_target_pairs={{0,16},{4,20},{8,24},{12,28},{16,0},{20,4},{24,8},{28,12},{1,17},{... | collective-permute-start | bytes 4325384 | tf_op jit(solution)/shard_map/ppermute | solution.py:38
  316.3 54.5 %collective-permute-start.35 = (bf16[1024,1024]{1,0:T(8,128)(2,1)}, bf16[1024,1024]{1,0:T(8,128)(2,1)}, u32[]{:S(2)}, u32[]{:S(2)}) collective-permute-start(bf16[1024,1024]{1,0:T(8,128)(2,1)} %copy-done.66), channel_id=1, source_target_pairs={{0,8},{4,12},{8,0},{12,4},{16,24},{20,28},{24,16},{28,20},{1,9},{5... | collective-permute-start | bytes 6291464 | tf_op jit(solution)/shard_map/ppermute | solution.py:38
  316.9 53.8 %collective-permute-start.37 = (bf16[1408,512]{1,0:T(8,128)(2,1)}, bf16[1408,512]{1,0:T(8,128)(2,1)}, u32[]{:S(2)}, u32[]{:S(2)}) collective-permute-start(bf16[1408,512]{1,0:T(8,128)(2,1)} %copy-done.71), channel_id=1, source_target_pairs={{0,16},{4,20},{8,24},{12,28},{16,0},{20,4},{24,8},{28,12},{1,17},{... | collective-permute-start | bytes 4325384 | tf_op jit(solution)/shard_map/ppermute | solution.py:38
  317.9 52.8 %collective-permute-start.36 = (bf16[1024,384]{1,0:T(8,128)(2,1)}, bf16[1024,384]{1,0:T(8,128)(2,1)}, u32[]{:S(2)}, u32[]{:S(2)}) collective-permute-start(bf16[1024,384]{1,0:T(8,128)(2,1)} %copy-done.76), channel_id=1, source_target_pairs={{0,16},{4,20},{8,24},{12,28},{16,0},{20,4},{24,8},{28,12},{1,17},{... | collective-permute-start | bytes 2359304 | tf_op jit(solution)/shard_map/ppermute | solution.py:38
  381.5 112.8 %all-gather.11.cloned.1.call-start = ((), (), s32[]{:S(2)}) async-start(), calls=%async_computation.9 | async-start | bytes 2621440 | tf_op jit(solution)/shard_map/all_gather | solution.py:943
  383.3 34.6 %collective-permute-start.39 = (bf16[512,1024]{1,0:T(8,128)(2,1)}, bf16[512,1024]{1,0:T(8,128)(2,1)S(1)}, u32[]{:S(2)}, u32[]{:S(2)}) collective-permute-start(bf16[512,1024]{1,0:T(8,128)(2,1)} %get-tuple-element.535), channel_id=1, source_target_pairs={{0,16},{4,20},{8,24},{12,28},{16,0},{20,4},{24,8},{28,12},{1,17},{... | collective-permute-start | bytes 3145736 | tf_op jit(solution)/shard_map/ppermute | solution.py:38
  384.3 32.8 %collective-permute-start.41 = (bf16[704,512]{1,0:T(8,128)(2,1)}, bf16[704,512]{1,0:T(8,128)(2,1)S(1)}, u32[]{:S(2)}, u32[]{:S(2)}) collective-permute-start(bf16[704,512]{1,0:T(8,128)(2,1)} %get-tuple-element.537), channel_id=1, source_target_pairs={{0,8},{4,12},{8,0},{12,4},{16,24},{20,28},{24,16},{28,20},{1,9},{5... | collective-permute-start | bytes 2162696 | tf_op jit(solution)/shard_map/ppermute | solution.py:38
  400.4 42.3 %collective-permute-start.42 = (bf16[704,1024]{1,0:T(8,128)(2,1)}, bf16[704,1024]{1,0:T(8,128)(2,1)}, u32[]{:S(2)}, u32[]{:S(2)}) collective-permute-start(bf16[704,1024]{1,0:T(8,128)(2,1)} %get-tuple-element.545), channel_id=1, source_target_pairs={{0,8},{4,12},{8,0},{12,4},{16,24},{20,28},{24,16},{28,20},{1,9},{5... | collective-permute-start | bytes 4325384 | tf_op jit(solution)/shard_map/ppermute | solution.py:38
  402.1 40.7 %collective-permute-start.43 = (bf16[704,1024]{1,0:T(8,128)(2,1)}, bf16[704,1024]{1,0:T(8,128)(2,1)}, u32[]{:S(2)}, u32[]{:S(2)}) collective-permute-start(bf16[704,1024]{1,0:T(8,128)(2,1)} %get-tuple-element.548), channel_id=1, source_target_pairs={{0,16},{4,20},{8,24},{12,28},{16,0},{20,4},{24,8},{28,12},{1,17},{... | collective-permute-start | bytes 4325384 | tf_op jit(solution)/shard_map/ppermute | solution.py:38
  442.8 196.3 %reduce-scatter.11.cloned.1.call-start = ((), (), s32[]{:S(2)}) async-start(), calls=%async_computation.11 | async-start | bytes 2621440 | tf_op jit(solution)/shard_map/reduce_scatter | solution.py:946
  442.8 51.5 %collective-permute-start.48 = (bf16[512,1408]{1,0:T(8,128)(2,1)}, bf16[512,1408]{1,0:T(8,128)(2,1)}, u32[]{:S(2)}, u32[]{:S(2)}) collective-permute-start(bf16[512,1408]{1,0:T(8,128)(2,1)} %copy-done.69), channel_id=1, source_target_pairs={{0,8},{4,12},{8,0},{12,4},{16,24},{20,28},{24,16},{28,20},{1,9},{5... | collective-permute-start | bytes 4325384 | tf_op jit(solution)/shard_map/ppermute | solution.py:38
  443.8 50.5 %collective-permute-start.49 = (bf16[512,1408]{1,0:T(8,128)(2,1)}, bf16[512,1408]{1,0:T(8,128)(2,1)}, u32[]{:S(2)}, u32[]{:S(2)}) collective-permute-start(bf16[512,1408]{1,0:T(8,128)(2,1)} %copy-done.70), channel_id=1, source_target_pairs={{0,16},{4,20},{8,24},{12,28},{16,0},{20,4},{24,8},{28,12},{1,17},{... | collective-permute-start | bytes 4325384 | tf_op jit(solution)/shard_map/ppermute | solution.py:38
  462.6 30.0 %collective-permute-start.51 = (bf16[352,1024]{1,0:T(8,128)(2,1)S(1)}, bf16[352,1024]{1,0:T(8,128)(2,1)S(1)}, u32[]{:S(2)}, u32[]{:S(2)}) collective-permute-start(bf16[352,1024]{1,0:T(8,128)(2,1)S(1)} %get-tuple-element.745), channel_id=1, source_target_pairs={{0,8},{4,12},{8,0},{12,4},{16,24},{20,28},{24,16},{28,20},{1,9},{5... | collective-permute-start | bytes 2162696 | tf_op jit(solution)/shard_map/ppermute | solution.py:38
  464.6 28.9 %collective-permute-start.50 = (bf16[352,1024]{1,0:T(8,128)(2,1)S(1)}, bf16[352,1024]{1,0:T(8,128)(2,1)S(1)}, u32[]{:S(2)}, u32[]{:S(2)}) collective-permute-start(bf16[352,1024]{1,0:T(8,128)(2,1)S(1)} %get-tuple-element.747), channel_id=1, source_target_pairs={{0,16},{4,20},{8,24},{12,28},{16,0},{20,4},{24,8},{28,12},{1,17},{... | collective-permute-start | bytes 2162696 | tf_op jit(solution)/shard_map/ppermute | solution.py:38
  494.4 34.8 %collective-permute-start.54 = (bf16[512,1408]{1,0:T(8,128)(2,1)}, bf16[512,1408]{1,0:T(8,128)(2,1)}, u32[]{:S(2)}, u32[]{:S(2)}) collective-permute-start(bf16[512,1408]{1,0:T(8,128)(2,1)} %copy-done.67), channel_id=1, source_target_pairs={{0,8},{4,12},{8,0},{12,4},{16,24},{20,28},{24,16},{28,20},{1,9},{5... | collective-permute-start | bytes 4325384 | tf_op jit(solution)/shard_map/ppermute | solution.py:38
  495.4 156.9 %reduce-scatter.9.cloned.1.call-start = ((), (), s32[]{:S(2)}) async-start(), calls=%async_computation.10 | async-start | bytes 2621440 | tf_op jit(solution)/shard_map/reduce_scatter | solution.py:946
  495.6 39.4 %collective-permute-start.55 = (bf16[512,1408]{1,0:T(8,128)(2,1)}, bf16[512,1408]{1,0:T(8,128)(2,1)S(1)}, u32[]{:S(2)}, u32[]{:S(2)}) collective-permute-start(bf16[512,1408]{1,0:T(8,128)(2,1)} %copy-done.68), channel_id=1, source_target_pairs={{0,16},{4,20},{8,24},{12,28},{16,0},{20,4},{24,8},{28,12},{1,17},{... | collective-permute-start | bytes 4325384 | tf_op jit(solution)/shard_map/ppermute | solution.py:38
  518.4 32.6 %collective-permute-start.53 = (bf16[1024,512]{1,0:T(8,128)(2,1)}, bf16[1024,512]{1,0:T(8,128)(2,1)S(1)}, u32[]{:S(2)}, u32[]{:S(2)}) collective-permute-start(bf16[1024,512]{1,0:T(8,128)(2,1)} %get-tuple-element.610), channel_id=1, source_target_pairs={{8,0},{12,4},{24,16},{28,20},{9,1},{13,5},{25,17},{29,21},{10,2},{... | collective-permute-start | bytes 3145736 | tf_op jit(solution)/shard_map/ppermute | solution.py:940
  532.0 35.5 %collective-permute-start.56 = (bf16[256,1408]{1,0:T(8,128)(2,1)}, bf16[256,1408]{1,0:T(8,128)(2,1)}, u32[]{:S(2)}, u32[]{:S(2)}) collective-permute-start(bf16[256,1408]{1,0:T(8,128)(2,1)} %get-tuple-element.734), channel_id=1, source_target_pairs={{0,16},{4,20},{8,24},{12,28},{16,0},{20,4},{24,8},{28,12},{1,17},{... | collective-permute-start | bytes 2162696 | tf_op jit(solution)/shard_map/ppermute | solution.py:38
  570.8 36.5 %collective-permute-start.61 = (bf16[1024,384]{1,0:T(8,128)(2,1)}, bf16[1024,384]{1,0:T(8,128)(2,1)}, u32[]{:S(2)}, u32[]{:S(2)}) collective-permute-start(bf16[1024,384]{1,0:T(8,128)(2,1)} %get-tuple-element.648), channel_id=1, source_target_pairs={{0,8},{4,12},{8,0},{12,4},{16,24},{20,28},{24,16},{28,20},{1,9},{5... | collective-permute-start | bytes 2359304 | tf_op jit(solution)/shard_map/ppermute | solution.py:38
  571.2 36.1 %collective-permute-start.62 = (bf16[1024,384]{1,0:T(8,128)(2,1)}, bf16[1024,384]{1,0:T(8,128)(2,1)}, u32[]{:S(2)}, u32[]{:S(2)}) collective-permute-start(bf16[1024,384]{1,0:T(8,128)(2,1)} %get-tuple-element.649), channel_id=1, source_target_pairs={{0,16},{4,20},{8,24},{12,28},{16,0},{20,4},{24,8},{28,12},{1,17},{... | collective-permute-start | bytes 2359304 | tf_op jit(solution)/shard_map/ppermute | solution.py:38
  572.4 34.9 %collective-permute-start.63 = (bf16[256,1408]{1,0:T(8,128)(2,1)}, bf16[256,1408]{1,0:T(8,128)(2,1)}, u32[]{:S(2)}, u32[]{:S(2)}) collective-permute-start(bf16[256,1408]{1,0:T(8,128)(2,1)} %get-tuple-element.650), channel_id=1, source_target_pairs={{0,16},{4,20},{8,24},{12,28},{16,0},{20,4},{24,8},{28,12},{1,17},{... | collective-permute-start | bytes 2162696 | tf_op jit(solution)/shard_map/ppermute | solution.py:38
  573.2 34.1 %collective-permute-start.64 = (bf16[256,1408]{1,0:T(8,128)(2,1)}, bf16[256,1408]{1,0:T(8,128)(2,1)}, u32[]{:S(2)}, u32[]{:S(2)}) collective-permute-start(bf16[256,1408]{1,0:T(8,128)(2,1)} %get-tuple-element.651), channel_id=1, source_target_pairs={{0,8},{4,12},{8,0},{12,4},{16,24},{20,28},{24,16},{28,20},{1,9},{5... | collective-permute-start | bytes 2162696 | tf_op jit(solution)/shard_map/ppermute | solution.py:38
  614.7 26.9 %collective-permute-start.74 = (f32[24064]{0:T(1024)}, f32[24064]{0:T(1024)}, u32[]{:S(2)}, u32[]{:S(2)}) collective-permute-start(f32[24064]{0:T(1024)} %add.307), channel_id=1, source_target_pairs={{0,16},{4,20},{8,24},{12,28},{16,0},{20,4},{24,8},{28,12},{1,17},{... | collective-permute-start | bytes 288776 | tf_op jit(solution)/shard_map/ppermute | solution.py:38
  (189 other events, 1166.9 us)
Sparse Core Ops, SparseCore 0:
  12.4 48.3 all-gather.4
  70.4 48.9 all-gather.6
  143.5 44.6 reduce-scatter.4
  199.2 45.6 all-gather.8
  381.6 46.6 reduce-scatter.6
  442.9 46.2 all-gather.10
  495.5 44.1 reduce-scatter.10
  581.0 45.5 reduce-scatter.8

commit v7 on v6

--- a/solution.py
+++ b/solution.py
@@ -1150,24 +1150,32 @@
         sums, gua_sent, gub_sent, sd_sent, gua_grad, gub_grad, sd_grad
     )
     forward_part, packed = sums[:2], core_sum(*sums[2:])
-    gua_grad = first_sum(gua_grad, gua_sent)
-    gub_grad = first_sum(gub_grad, gub_sent)
-    sd_grad = first_sum(sd_grad, sd_sent)
+    lead = [
+        add_low(parts[1], arrived[0][parts[0].shape[0] :])
+        for parts, arrived in ((gua_grad, gua_sent), (gub_grad, gub_sent), (sd_grad, sd_sent))
+    ]
     (
-        packed, gua_grad, gub_grad, sd_grad, active, grad_result, grad_gate_pre, grad_up_pre,
+        packed, lead, gua_grad, gua_sent, gub_grad, gub_sent, sd_grad, sd_sent, active, grad_result,
+        grad_gate_pre, grad_up_pre,
     ) = together(
-        packed, gua_grad, gub_grad, sd_grad, active, grad_result, grad_gate_pre, grad_up_pre,
-    )
+        packed, lead, gua_grad, gua_sent, gub_grad, gub_sent, sd_grad, sd_sent, active, grad_result,
+        grad_gate_pre, grad_up_pre,
+    )
+    first_parts = [gua_grad[0], gua_sent[0], gub_grad[0], gub_sent[0], sd_grad[0], sd_sent[0]]
     spread = scattered(packed)
-    gua_sent, gub_sent = across(gua_grad[1], 2 * up_order[1]), across(gub_grad[1], 2 * down_order[1])
-    sd_sent = across(sd_grad[1], 2 * down_order[1])
+    gua_sent, gub_sent = across(lead[0], 2 * up_order[1]), across(lead[1], 2 * down_order[1])
+    sd_sent = across(lead[2], 2 * down_order[1])
     (eda_grad, eda_out), (edb_grad, edb_out) = down_grads(active, grad_result, quad, quads)
     eda_out, edb_out, grad_gate_pre = together(eda_out, edb_out, grad_gate_pre)
     eda_sent, edb_sent = sent(eda_out, up_order[0]), sent(edb_out, down_order[0])
     ((eg_grad, eg_out),) = row_grads(rows_two, grad_gate_pre, quads, [(0, ffe, True, False)])
-    eg_grad, eg_out, grad_up_pre, gua_sent, gub_sent, sd_sent = together(
-        eg_grad, eg_out, grad_up_pre, gua_sent, gub_sent, sd_sent
-    )
+    eg_grad, eg_out, grad_up_pre, gua_sent, gub_sent, sd_sent, first_parts = together(
+        eg_grad, eg_out, grad_up_pre, gua_sent, gub_sent, sd_sent, first_parts
+    )
+    gua_grad, gub_grad, sd_grad = [
+        [add_low(kept, arrived[: kept.shape[0]])]
+        for kept, arrived in zip(first_parts[::2], first_parts[1::2])
+    ]
     ((eu_grad, eu_out),) = row_grads(rows_two, grad_up_pre, quads, [(0, ffe, False, False)])
     spread, eg_grad, eg_out = together(spread, eg_grad, eg_out)
 
@@ -1288,12 +1296,20 @@
         [jnp.where(core == 0, bias_part, 0.0), jnp.where(core == 0, 0.0, bias_part)], axis=1
     )
     late = sum_everywhere(jnp.concatenate([late, bias_part.reshape(-1)]), [1], [])
-    qkv_a_grad = first_sum(qkv_a_grad, qkv_a_sent)
-    qkv_b_grad = first_sum(qkv_b_grad, qkv_b_sent)
-    o_grad = first_sum(o_grad, o_sent)
-    qkv_a_grad, qkv_b_grad, o_grad, eg_last, eu_last, eda_sent, edb_sent = together(
-        qkv_a_grad, qkv_b_grad, o_grad, eg_last, eu_last, eda_sent, edb_sent
-    )
+    lead = [
+        add_low(parts[1], arrived[0][parts[0].shape[0] :])
+        for parts, arrived in ((qkv_a_grad, qkv_a_sent), (qkv_b_grad, qkv_b_sent), (o_grad, o_sent))
+    ]
+    lead, qkv_a_grad, qkv_b_grad, o_grad, qkv_a_sent, qkv_b_sent, o_sent, eg_last, eu_last = together(
+        lead, qkv_a_grad, qkv_b_grad, o_grad, qkv_a_sent, qkv_b_sent, o_sent, eg_last, eu_last
+    )
+    eda_sent, edb_sent, _ = together(eda_sent, edb_sent, lead)
+    qkv_a_grad, qkv_b_grad, o_grad = [
+        [add_low(parts[0], arrived[0][: parts[0].shape[0]]), ahead]
+        for parts, arrived, ahead in zip(
+            (qkv_a_grad, qkv_b_grad, o_grad), (qkv_a_sent, qkv_b_sent, o_sent), lead
+        )
+    ]
     eg_rest = jnp.concatenate([eg_rest, eg_last], axis=0)
     eu_rest = jnp.concatenate([eu_rest, eu_last], axis=0)
     qkv_a_rest = across(qkv_a_grad[1], 2 * up_order[1])

time: 676 us -> 671 us (level)
    convert_element_type x12 -> x18, other arithmetic: 26.2 us -> 31.6 us  [add_low(): return (left.astype(F32) + right.astype(F32)).astype(BF16)]
    unnamed x300 -> x276, local copies, waits for them, and re-layouts: 51.8 us -> 48.4 us
where the time goes in v7:
time: 671 us; the launch traced here: 661 us
  waiting for transfers between devices  211 us (31%)
  Pallas kernels  205 us (31%)
  local copies, waits for them, and re-layouts  83.3 us (12%)
  other arithmetic  71.4 us (11%)
  starting transfers between devices  66.9 us (10%)
  between operations  16.4 us (2%)
  matrix products  6.89 us (1%)
    pallas_call x36, Pallas kernels, run(): pl.pallas_call(kernel, grid_spec=pltpu.PrefetchScalarGridSpec(num_scalar_...  185 us
    ppermute x75, waiting for transfers between devices, across(): return lax.ppermute(block, 'grp', [(i, i ^ mask) for i in range(count)])  182 us
    ppermute x75, starting transfers between devices, across(): return lax.ppermute(block, 'grp', [(i, i ^ mask) for i in range(count)])  57.2 us
    unnamed x276, local copies, waits for them, and re-layouts  48.4 us
    convert_element_type x18, other arithmetic, add_low(): return (left.astype(F32) + right.astype(F32)).astype(BF16)  31.6 us
    dynamic_update_slice x14, local copies, waits for them, and re-layouts, place_quads(): whole = lax.dynamic_update_slice(whole, pieces[key], start)  24.1 us
    ppermute x2, waiting for transfers between devices, shifted(): return lax.ppermute(values, 'grp', route)  23.4 us
  transfers between devices with their start and end apart: 87, of which 28 were waited for; matrix products, arithmetic and copies ran while one was open for 15% of the time, Pallas kernels for 30%

profile of v7, /device:TPU:0, one launch (start us, length us, event | category | flops | bytes accessed | tf_op | source)
XLA Modules:
  0.0 661.4 jit_solution(12763440362099234807)
XLA Ops:
  13.3 2.6 collective-permute-start.1
  30.1 5.5 collective-permute-done.3.rest_6_.rest_7_
  44.8 23.1 %collective-permute-done.10.rest_3_.rest_4_ = bf16[512,384]{1,0:T(8,128)(2,1)S(1)} collective-permute-done((bf16[512,384]{1,0:T(8,128)(2,1)S(1)}, bf16[512,384]{1,0:T(8,128)(2,1)S(1)}, u32[]{:S(2)}, u32[]{:S(2)}) %collective-permute-start.10) | collective-permute-done | bytes 393248 | tf_op jit(solution)/shard_map/ppermute | solution.py:38
  72.3 2.1 collective-permute-done.14.other_ref
  78.0 5.2 project.1
  83.2 3.4 collective-permute-start.15
  91.1 4.2 collective-permute-done.17
  96.7 7.7 %collective-permute-done.16.rest_2_ = bf16[512,1408]{1,0:T(8,128)(2,1)S(1)} collective-permute-done((bf16[512,1408]{1,0:T(8,128)(2,1)}, bf16[512,1408]{1,0:T(8,128)(2,1)S(1)}, u32[]{:S(2)}, u32[]{:S(2)}) %collective-permute-start.16) | collective-permute-done | bytes 1441824 | tf_op jit(solution)/shard_map/ppermute | solution.py:38
  104.4 12.0 %collective-permute-done.15.rest_0_ = bf16[1024,512]{1,0:T(8,128)(2,1)S(1)} collective-permute-done((bf16[1024,512]{1,0:T(8,128)(2,1)S(1)}, bf16[1024,512]{1,0:T(8,128)(2,1)S(1)}, u32[]{:S(2)}, u32[]{:S(2)}) %collective-permute-start.15) | collective-permute-done | bytes 1048608 | tf_op jit(solution)/shard_map/ppermute | solution.py:940
  118.4 2.5 collective-permute-start.19
  122.6 6.8 %attend.1 = (bf16[1024,256]{1,0:T(8,128)(2,1)S(1)}, f32[1024,256]{1,0:T(8,128)S(1)}) custom-call(bf16[1024,256]{1,0:T(8,128)(2,1)S(1)} %get-tuple-element.425.q_ref, bf16[1024,512]{1,0:T(8,128)(2,1)S(1)} %copy-done.63, bf16[1024,512]{1,0:T(8,128)(2,1)S(1)} %get-tuple-element.419.rest_1_, s32[1,2048]{1,0:T(1,128)S(1)} %iota_add_fusion.rest_2_, ...), custom_call_target="tpu_custom_call" | custom-call | flops 1342177280 | bytes 4210688 | tf_op jit(solution)/shard_map/attend/pallas_call | solution.py:190
  132.5 2.6 collective-permute-done.18
  137.5 3.6 collective-permute-done.20.right_ref
  147.5 3.2 broadcast_in_dim.32
  152.7 2.1 constant_dynamic-update-slice_fusion.20
  156.9 36.1 %collective-permute-done.23 = bf16[352,1024]{1,0:T(8,128)(2,1)} collective-permute-done((bf16[352,1024]{1,0:T(8,128)(2,1)}, bf16[352,1024]{1,0:T(8,128)(2,1)}, u32[]{:S(2)}, u32[]{:S(2)}) %collective-permute-start.23) | collective-permute-done | bytes 720928 | tf_op jit(solution)/shard_map/ppermute | solution.py:38
  203.1 3.7 join_rows.5.cot_ref
  206.8 2.2 copy-done
  215.2 32.3 %collective-permute-done.27 = bf16[352,1024]{1,0:T(8,128)(2,1)S(1)} collective-permute-done((bf16[352,1024]{1,0:T(8,128)(2,1)}, bf16[352,1024]{1,0:T(8,128)(2,1)S(1)}, u32[]{:S(2)}, u32[]{:S(2)}) %collective-permute-start.27) | collective-permute-done | bytes 720928 | tf_op jit(solution)/shard_map/ppermute | solution.py:38
  257.8 27.4 %shared.1 = (bf16[1024,704]{1,0:T(8,128)(2,1)}, bf16[1024,2048]{1,0:T(8,128)(2,1)}, bf16[1024,2048]{1,0:T(8,128)(2,1)}, bf16[1024,2048]{1,0:T(8,128)(2,1)}, f32[...) custom-call(s32[1]{0:T(128)} %bitcast.core_ref, bf16[1024,2048]{1,0:T(8,128)(2,1)} %copy-done.2, bf16[960,2048]{1,0:T(8,128)(2,1)} %copy-done.91, ...), custom_call_target="tpu_custom_call" | custom-call | flops 17716740096 | bytes 35266564 | tf_op jit(solution)/shard_map/shared/pallas_call | solution.py:190
  285.2 10.2 %row_grads.3 = (bf16[512,1024]{1,0:T(8,128)(2,1)S(1)}, bf16[512,1024]{1,0:T(8,128)(2,1)S(1)}, bf16[1024,1024]{1,0:T(8,128)(2,1)S(1)}, bf16[512,384]{1,0:T(8,128)...) custom-call(bf16[1024,2048]{1,0:T(8,128)(2,1)} %copy-done.2, ...), custom_call_target="tpu_custom_call" | custom-call | flops 5905580032 | bytes 12845056 | tf_op jit(solution)/shard_map/row_grads/pallas_call | solution.py:190
  296.7 2.6 constant_dynamic-update-slice_fusion.8
  306.4 5.6 column_grads.2
  318.7 51.8 %expert.1 = (bf16[1024,1408]{1,0:T(8,128)(2,1)}, bf16[1024,2048]{1,0:T(8,128)(2,1)}, bf16[768,2048]{1,0:T(8,128)(2,1)}, bf16[512,2048]{1,0:T(8,128)(2,1)}, bf16[...) custom-call(s32[1]{0:T(128)} %bitcast.core_ref, ...), custom_call_target="tpu_custom_call" | custom-call | flops 35433480192 | bytes 58008068 | tf_op jit(solution)/shard_map/expert/pallas_call | solution.py:190
  372.4 2.3 add_convert_fusion.13
  382.7 11.7 %down_grads.1 = (bf16[352,1024]{1,0:T(8,128)(2,1)S(1)}, bf16[352,1024]{1,0:T(8,128)(2,1)S(1)}, bf16[704,1024]{1,0:T(8,128)(2,1)}, bf16[352,1024]{1,0:T(8,128)(2,...) custom-call(s32[1]{0:T(128)} %bitcast.13.quad_ref, bf16[1024,1408]{1,0:T(8,128)(2,1)} %get-tuple-element.536.act_ref, ...), custom_call_target="tpu_custom_call" | custom-call | flops 5905580032 | bytes 12845056 | tf_op jit(solution)/shard_map/down_grads/pallas_call | solution.py:856
  400.7 10.1 %row_grads.4 = (bf16[512,1408]{1,0:T(8,128)(2,1)S(1)}, bf16[512,1408]{1,0:T(8,128)(2,1)S(1)}, bf16[512,1408]{1,0:T(8,128)(2,1)S(1)}, bf16[512,1408]{1,0:T(8,128)(2,1)S(1)}) custom-call(bf16[1024,2048]{1,0:T(8,128)(2,1)} %copy-done.2, bf16[1024,1408]{1,0:T(8,128)(2,1)} %get-tuple-element.541.grad_ref), custom_call_target="tpu_custom_call" | custom-call | flops 5905580032 | bytes 12845056 | tf_op jit(solution)/shard_map/row_grads/pallas_call | solution.py:190
  420.3 10.1 %row_grads.5 = (bf16[512,1408]{1,0:T(8,128)(2,1)S(1)}, bf16[512,1408]{1,0:T(8,128)(2,1)S(1)}, bf16[512,1408]{1,0:T(8,128)(2,1)S(1)}, bf16[512,1408]{1,0:T(8,128)(2,1)S(1)}) custom-call(bf16[1024,2048]{1,0:T(8,128)(2,1)} %copy-done.2, bf16[1024,1408]{1,0:T(8,128)(2,1)} %get-tuple-element.578.grad_ref), custom_call_target="tpu_custom_call" | custom-call | flops 5905580032 | bytes 12845056 | tf_op jit(solution)/shard_map/row_grads/pallas_call | solution.py:190
  443.0 2.8 collective-permute-done.44.right_ref
  447.7 4.1 add_rows.6
  453.8 3.0 add_convert_fusion.8
  457.4 2.9 add_convert_fusion.10
  466.1 25.0 %collective-permute-done.51.arrived_ref = bf16[352,1024]{1,0:T(8,128)(2,1)S(1)} collective-permute-done((bf16[352,1024]{1,0:T(8,128)(2,1)S(1)}, bf16[352,1024]{1,0:T(8,128)(2,1)S(1)}, u32[]{:S(2)}, u32[]{:S(2)}) %collective-permute-start.51) | collective-permute-done | bytes 720928 | tf_op jit(solution)/shard_map/ppermute | solution.py:38
  498.6 18.3 %attend_back.1 = (bf16[1024,256]{1,0:T(8,128)(2,1)}, f32[1024,512]{1,0:T(8,128)}, bf16[1024,512]{1,0:T(8,128)(2,1)}) custom-call(s32[1]{0:T(128)} %bitcast.core_ref, bf16[1024,256]{1,0:T(8,128)(2,1)} %copy-done.78, bf16[512,2048]{1,0:T(8,128)(2,1)} %all-gather.11.cloned.1.call-done.mine_ref.own_ref, bf16[512,2048]{1,0:T(8,128)(2,1)} %copy-done.11, ...), custom_call_target="tpu_custom_call" | custom-call | flops 3355443200 | bytes 13647876 | tf_op jit(solution)/shard_map/attend_back/pallas_call | solution.py:190
  518.3 9.4 %collective-permute-done.54 = bf16[512,1408]{1,0:T(8,128)(2,1)} collective-permute-done((bf16[512,1408]{1,0:T(8,128)(2,1)}, bf16[512,1408]{1,0:T(8,128)(2,1)}, u32[]{:S(2)}, u32[]{:S(2)}) %collective-permute-start.54) | collective-permute-done | bytes 1441824 | tf_op jit(solution)/shard_map/ppermute | solution.py:38
  527.7 2.8 add_convert_fusion.6
  533.6 2.9 add_convert_fusion.4
  538.2 11.4 %collective-permute-done.53.rest_0_ = bf16[1024,512]{1,0:T(8,128)(2,1)S(1)} collective-permute-done((bf16[1024,512]{1,0:T(8,128)(2,1)}, bf16[1024,512]{1,0:T(8,128)(2,1)S(1)}, u32[]{:S(2)}, u32[]{:S(2)}) %collective-permute-start.53) | collective-permute-done | bytes 1048608 | tf_op jit(solution)/shard_map/ppermute | solution.py:940
  550.6 15.4 %collect.1 = (bf16[768,2048]{1,0:T(8,128)(2,1)}, bf16[512,2048]{1,0:T(8,128)(2,1)}, f32[1,2048]{1,0:T(1,128)}, f32[1,768]{1,0:T(1,128)}, bf16[512,384]{1,0:T(8,1...) custom-call(s32[1]{0:T(128)} %bitcast.core_ref, ...), custom_call_target="tpu_custom_call" | custom-call | flops 6442450944 | bytes 20458500 | tf_op jit(solution)/shard_map/collect/pallas_call | solution.py:190
  575.5 4.0 add_rows.7
  586.4 2.6 collective-permute-start.60
  589.0 3.1 column_grads.3
  593.5 5.7 collective-permute-done.60
  599.2 6.7 %collective-permute-done.63 = bf16[256,1408]{1,0:T(8,128)(2,1)} collective-permute-done((bf16[256,1408]{1,0:T(8,128)(2,1)}, bf16[256,1408]{1,0:T(8,128)(2,1)}, u32[]{:S(2)}, u32[]{:S(2)}) %collective-permute-start.63) | collective-permute-done | bytes 720928 | tf_op jit(solution)/shard_map/ppermute | solution.py:38
  606.1 2.4 add_convert_fusion.14
  611.6 2.2 collective-permute-done.73
  616.4 2.2 collective-permute-done.74
  630.9 5.7 collective-permute-done.68.arrived_ref
  (607 shorter events, 219.7 us)
Async XLA Ops:
  7.2 62.8 %all-gather.5.cloned.1.call-start = ((), (), s32[]{:S(2)}) async-start(), calls=%async_computation.4 | async-start | bytes 2621440 | tf_op jit(solution)/shard_map/all_gather | solution.py:943
  12.3 120.2 %all-gather.7.cloned.1.call-start = ((), (), s32[]{:S(2)}) async-start(), calls=%async_computation.5 | async-start | bytes 2785280 | tf_op jit(solution)/shard_map/all_gather | solution.py:943
  36.7 33.3 %collective-permute-start.12 = (bf16[960,512]{1,0:T(8,128)(2,1)}, bf16[960,512]{1,0:T(8,128)(2,1)}, u32[]{:S(2)}, u32[]{:S(2)}) collective-permute-start(bf16[960,512]{1,0:T(8,128)(2,1)} %pad_maximum_fusion.6), channel_id=1, source_target_pairs={{0,16},{4,20},{8,24},{12,28},{16,0},{20,4},{24,8},{28,12},{1,17},{... | collective-permute-start | bytes 2949128 | tf_op jit(solution)/shard_map/ppermute | solution.py:38
  38.3 31.7 %collective-permute-start.13 = (bf16[960,512]{1,0:T(8,128)(2,1)}, bf16[960,512]{1,0:T(8,128)(2,1)}, u32[]{:S(2)}, u32[]{:S(2)}) collective-permute-start(bf16[960,512]{1,0:T(8,128)(2,1)} %pad_maximum_fusion.6), channel_id=1, source_target_pairs={{0,8},{4,12},{8,0},{12,4},{16,24},{20,28},{24,16},{28,20},{1,9},{5... | collective-permute-start | bytes 2949128 | tf_op jit(solution)/shard_map/ppermute | solution.py:38
  41.9 26.0 %collective-permute-start.10 = (bf16[512,384]{1,0:T(8,128)(2,1)S(1)}, bf16[512,384]{1,0:T(8,128)(2,1)S(1)}, u32[]{:S(2)}, u32[]{:S(2)}) collective-permute-start(bf16[512,384]{1,0:T(8,128)(2,1)S(1)} %collective-permute-done.1.rest_1_.rest_2_), channel_id=1, source_target_pairs={{0,16},{4,20},{8,24},{12,28},{16,0},{20,4},{24,8},{28,12},{1,17},{... | collective-permute-start | bytes 1179656 | tf_op jit(solution)/shard_map/ppermute | solution.py:38
  43.1 26.1 %collective-permute-start.11 = (bf16[512,384]{1,0:T(8,128)(2,1)S(1)}, bf16[512,384]{1,0:T(8,128)(2,1)S(1)}, u32[]{:S(2)}, u32[]{:S(2)}) collective-permute-start(bf16[512,384]{1,0:T(8,128)(2,1)S(1)} %collective-permute-done.3.rest_6_.rest_7_), channel_id=1, source_target_pairs={{0,8},{4,12},{8,0},{12,4},{16,24},{20,28},{24,16},{28,20},{1,9},{5... | collective-permute-start | bytes 1179656 | tf_op jit(solution)/shard_map/ppermute | solution.py:38
  70.1 124.4 %reduce-scatter.5.cloned.1.call-start = ((), (), s32[]{:S(2)}) async-start(), calls=%async_computation.6 | async-start | bytes 2621440 | tf_op jit(solution)/shard_map/reduce_scatter | solution.py:946
  70.2 34.3 %collective-permute-start.16 = (bf16[512,1408]{1,0:T(8,128)(2,1)}, bf16[512,1408]{1,0:T(8,128)(2,1)S(1)}, u32[]{:S(2)}, u32[]{:S(2)}) collective-permute-start(bf16[512,1408]{1,0:T(8,128)(2,1)} %pad_maximum_fusion.1.rest_0_), channel_id=1, source_target_pairs={{0,16},{4,20},{8,24},{12,28},{16,0},{20,4},{24,8},{28,12},{1,17},{... | collective-permute-start | bytes 4325384 | tf_op jit(solution)/shard_map/ppermute | solution.py:38
  71.2 24.1 %collective-permute-start.17 = (bf16[960,512]{1,0:T(8,128)(2,1)}, bf16[960,512]{1,0:T(8,128)(2,1)S(1)}, u32[]{:S(2)}, u32[]{:S(2)}) collective-permute-start(bf16[960,512]{1,0:T(8,128)(2,1)} %collective-permute-done.12), channel_id=1, source_target_pairs={{0,8},{4,12},{8,0},{12,4},{16,24},{20,28},{24,16},{28,20},{1,9},{5... | collective-permute-start | bytes 2949128 | tf_op jit(solution)/shard_map/ppermute | solution.py:38
  83.2 33.1 %collective-permute-start.15 = (bf16[1024,512]{1,0:T(8,128)(2,1)S(1)}, bf16[1024,512]{1,0:T(8,128)(2,1)S(1)}, u32[]{:S(2)}, u32[]{:S(2)}) collective-permute-start(bf16[1024,512]{1,0:T(8,128)(2,1)S(1)} %get-tuple-element.419.rest_1_), channel_id=1, source_target_pairs={{0,8},{4,12},{16,24},{20,28},{1,9},{5,13},{17,25},{21,29},{2,10},{... | collective-permute-start | bytes 3145736 | tf_op jit(solution)/shard_map/ppermute | solution.py:940
  143.1 104.8 %all-gather.9.cloned.1.call-start = ((), (), s32[]{:S(2)}) async-start(), calls=%async_computation.7 | async-start | bytes 2621440 | tf_op jit(solution)/shard_map/all_gather | solution.py:943
  143.2 51.3 %collective-permute-start.21 = (bf16[512,2176]{1,0:T(8,128)(2,1)S(1)}, bf16[512,2176]{1,0:T(8,128)(2,1)}, u32[]{:S(2)}, u32[]{:S(2)}) collective-permute-start(bf16[512,2176]{1,0:T(8,128)(2,1)S(1)} %copy-done.8), channel_id=1, source_target_pairs={{0,4},{4,0},{8,12},{12,8},{16,20},{20,16},{24,28},{28,24},{1,5},{5... | collective-permute-start | bytes 6684680 | tf_op jit(solution)/shard_map/ppermute | solution.py:38
  143.4 51.1 %collective-permute-start.22 = (bf16[512,1408]{1,0:T(8,128)(2,1)}, bf16[512,1408]{1,0:T(8,128)(2,1)}, u32[]{:S(2)}, u32[]{:S(2)}) collective-permute-start(bf16[512,1408]{1,0:T(8,128)(2,1)} %pad_maximum_fusion.1.rest_0_), channel_id=1, source_target_pairs={{0,8},{4,12},{8,0},{12,4},{16,24},{20,28},{24,16},{28,20},{1,9},{5... | collective-permute-start | bytes 4325384 | tf_op jit(solution)/shard_map/ppermute | solution.py:38
  145.1 49.3 %collective-permute-start.25 = (bf16[512,1408]{1,0:T(8,128)(2,1)}, bf16[512,1408]{1,0:T(8,128)(2,1)}, u32[]{:S(2)}, u32[]{:S(2)}) collective-permute-start(bf16[512,1408]{1,0:T(8,128)(2,1)} %get-tuple-element.500.rest_4_), channel_id=1, source_target_pairs={{0,16},{4,20},{8,24},{12,28},{16,0},{20,4},{24,8},{28,12},{1,17},{... | collective-permute-start | bytes 4325384 | tf_op jit(solution)/shard_map/ppermute | solution.py:38
  146.1 46.9 %collective-permute-start.23 = (bf16[352,1024]{1,0:T(8,128)(2,1)}, bf16[352,1024]{1,0:T(8,128)(2,1)}, u32[]{:S(2)}, u32[]{:S(2)}) collective-permute-start(bf16[352,1024]{1,0:T(8,128)(2,1)} %get-tuple-element.455), channel_id=1, source_target_pairs={{0,8},{4,12},{8,0},{12,4},{16,24},{20,28},{24,16},{28,20},{1,9},{5... | collective-permute-start | bytes 2162696 | tf_op jit(solution)/shard_map/ppermute | solution.py:38
  146.4 48.0 %collective-permute-start.24 = (bf16[352,1024]{1,0:T(8,128)(2,1)}, bf16[352,1024]{1,0:T(8,128)(2,1)}, u32[]{:S(2)}, u32[]{:S(2)}) collective-permute-start(bf16[352,1024]{1,0:T(8,128)(2,1)} %get-tuple-element.455), channel_id=1, source_target_pairs={{0,16},{4,20},{8,24},{12,28},{16,0},{20,4},{24,8},{28,12},{1,17},{... | collective-permute-start | bytes 2162696 | tf_op jit(solution)/shard_map/ppermute | solution.py:38
  198.8 236.2 %reduce-scatter.7.cloned.1.call-start = ((), (), s32[]{:S(2)}) async-start(), calls=%async_computation.8 | async-start | bytes 2785280 | tf_op jit(solution)/shard_map/reduce_scatter | solution.py:946
  199.0 48.9 %collective-permute-start.26 = (bf16[512,1408]{1,0:T(8,128)(2,1)}, bf16[512,1408]{1,0:T(8,128)(2,1)}, u32[]{:S(2)}, u32[]{:S(2)}) collective-permute-start(bf16[512,1408]{1,0:T(8,128)(2,1)} %get-tuple-element.496.rest_0_), channel_id=1, source_target_pairs={{0,8},{4,12},{8,0},{12,4},{16,24},{20,28},{24,16},{28,20},{1,9},{5... | collective-permute-start | bytes 4325384 | tf_op jit(solution)/shard_map/ppermute | solution.py:38
  199.4 48.5 %collective-permute-start.28 = (bf16[512,1408]{1,0:T(8,128)(2,1)}, bf16[512,1408]{1,0:T(8,128)(2,1)}, u32[]{:S(2)}, u32[]{:S(2)}) collective-permute-start(bf16[512,1408]{1,0:T(8,128)(2,1)} %collective-permute-done.22.rest_1_), channel_id=1, source_target_pairs={{0,16},{4,20},{8,24},{12,28},{16,0},{20,4},{24,8},{28,12},{1,17},{... | collective-permute-start | bytes 4325384 | tf_op jit(solution)/shard_map/ppermute | solution.py:38
  200.4 47.1 %collective-permute-start.27 = (bf16[352,1024]{1,0:T(8,128)(2,1)}, bf16[352,1024]{1,0:T(8,128)(2,1)S(1)}, u32[]{:S(2)}, u32[]{:S(2)}) collective-permute-start(bf16[352,1024]{1,0:T(8,128)(2,1)} %collective-permute-done.18), channel_id=1, source_target_pairs={{0,8},{4,12},{8,0},{12,4},{16,24},{20,28},{24,16},{28,20},{1,9},{5... | collective-permute-start | bytes 2162696 | tf_op jit(solution)/shard_map/ppermute | solution.py:38
  202.1 45.8 %collective-permute-start.29 = (bf16[352,1024]{1,0:T(8,128)(2,1)}, bf16[352,1024]{1,0:T(8,128)(2,1)}, u32[]{:S(2)}, u32[]{:S(2)}) collective-permute-start(bf16[352,1024]{1,0:T(8,128)(2,1)} %collective-permute-done.23), channel_id=1, source_target_pairs={{0,16},{4,20},{8,24},{12,28},{16,0},{20,4},{24,8},{28,12},{1,17},{... | collective-permute-start | bytes 2162696 | tf_op jit(solution)/shard_map/ppermute | solution.py:38
  248.6 64.5 %collective-permute-start.31 = (bf16[512,1408]{1,0:T(8,128)(2,1)}, bf16[512,1408]{1,0:T(8,128)(2,1)}, u32[]{:S(2)}, u32[]{:S(2)}) collective-permute-start(bf16[512,1408]{1,0:T(8,128)(2,1)} %get-tuple-element.500.rest_4_), channel_id=1, source_target_pairs={{0,8},{4,12},{8,0},{12,4},{16,24},{20,28},{24,16},{28,20},{1,9},{5... | collective-permute-start | bytes 4325384 | tf_op jit(solution)/shard_map/ppermute | solution.py:38
  250.1 63.0 %collective-permute-start.32 = (bf16[512,1408]{1,0:T(8,128)(2,1)}, bf16[512,1408]{1,0:T(8,128)(2,1)}, u32[]{:S(2)}, u32[]{:S(2)}) collective-permute-start(bf16[512,1408]{1,0:T(8,128)(2,1)} %get-tuple-element.496.rest_0_), channel_id=1, source_target_pairs={{0,16},{4,20},{8,24},{12,28},{16,0},{20,4},{24,8},{28,12},{1,17},{... | collective-permute-start | bytes 4325384 | tf_op jit(solution)/shard_map/ppermute | solution.py:38
  251.1 62.8 %collective-permute-start.33 = (bf16[512,1408]{1,0:T(8,128)(2,1)}, bf16[512,1408]{1,0:T(8,128)(2,1)}, u32[]{:S(2)}, u32[]{:S(2)}) collective-permute-start(bf16[512,1408]{1,0:T(8,128)(2,1)} %collective-permute-done.25.rest_6_), channel_id=1, source_target_pairs={{0,8},{4,12},{8,0},{12,4},{16,24},{20,28},{24,16},{28,20},{1,9},{5... | collective-permute-start | bytes 4325384 | tf_op jit(solution)/shard_map/ppermute | solution.py:38
  251.7 63.3 %collective-permute-start.34 = (bf16[512,1408]{1,0:T(8,128)(2,1)}, bf16[512,1408]{1,0:T(8,128)(2,1)}, u32[]{:S(2)}, u32[]{:S(2)}) collective-permute-start(bf16[512,1408]{1,0:T(8,128)(2,1)} %collective-permute-done.26.rest_1_), channel_id=1, source_target_pairs={{0,16},{4,20},{8,24},{12,28},{16,0},{20,4},{24,8},{28,12},{1,17},{... | collective-permute-start | bytes 4325384 | tf_op jit(solution)/shard_map/ppermute | solution.py:38
  316.0 54.5 %collective-permute-start.35 = (bf16[1024,1024]{1,0:T(8,128)(2,1)}, bf16[1024,1024]{1,0:T(8,128)(2,1)}, u32[]{:S(2)}, u32[]{:S(2)}) collective-permute-start(bf16[1024,1024]{1,0:T(8,128)(2,1)} %copy-done.55), channel_id=1, source_target_pairs={{0,8},{4,12},{8,0},{12,4},{16,24},{20,28},{24,16},{28,20},{1,9},{5... | collective-permute-start | bytes 6291464 | tf_op jit(solution)/shard_map/ppermute | solution.py:38
  316.6 53.8 %collective-permute-start.37 = (bf16[1408,512]{1,0:T(8,128)(2,1)}, bf16[1408,512]{1,0:T(8,128)(2,1)}, u32[]{:S(2)}, u32[]{:S(2)}) collective-permute-start(bf16[1408,512]{1,0:T(8,128)(2,1)} %copy-done.60), channel_id=1, source_target_pairs={{0,16},{4,20},{8,24},{12,28},{16,0},{20,4},{24,8},{28,12},{1,17},{... | collective-permute-start | bytes 4325384 | tf_op jit(solution)/shard_map/ppermute | solution.py:38
  317.6 52.8 %collective-permute-start.36 = (bf16[1024,384]{1,0:T(8,128)(2,1)}, bf16[1024,384]{1,0:T(8,128)(2,1)}, u32[]{:S(2)}, u32[]{:S(2)}) collective-permute-start(bf16[1024,384]{1,0:T(8,128)(2,1)} %copy-done.64), channel_id=1, source_target_pairs={{0,16},{4,20},{8,24},{12,28},{16,0},{20,4},{24,8},{28,12},{1,17},{... | collective-permute-start | bytes 2359304 | tf_op jit(solution)/shard_map/ppermute | solution.py:38
  378.5 114.4 %all-gather.11.cloned.1.call-start = ((), (), s32[]{:S(2)}) async-start(), calls=%async_computation.9 | async-start | bytes 2621440 | tf_op jit(solution)/shard_map/all_gather | solution.py:943
  380.3 34.9 %collective-permute-start.39 = (bf16[512,1024]{1,0:T(8,128)(2,1)S(1)}, bf16[512,1024]{1,0:T(8,128)(2,1)S(1)}, u32[]{:S(2)}, u32[]{:S(2)}) collective-permute-start(bf16[512,1024]{1,0:T(8,128)(2,1)S(1)} %add_convert_fusion.3), channel_id=1, source_target_pairs={{0,16},{4,20},{8,24},{12,28},{16,0},{20,4},{24,8},{28,12},{1,17},{... | collective-permute-start | bytes 3145736 | tf_op jit(solution)/shard_map/ppermute | solution.py:38
  381.3 32.6 %collective-permute-start.41 = (bf16[704,512]{1,0:T(8,128)(2,1)}, bf16[704,512]{1,0:T(8,128)(2,1)S(1)}, u32[]{:S(2)}, u32[]{:S(2)}) collective-permute-start(bf16[704,512]{1,0:T(8,128)(2,1)} %add_convert_fusion.13), channel_id=1, source_target_pairs={{0,8},{4,12},{8,0},{12,4},{16,24},{20,28},{24,16},{28,20},{1,9},{5... | collective-permute-start | bytes 2162696 | tf_op jit(solution)/shard_map/ppermute | solution.py:38
  398.3 43.0 %collective-permute-start.42 = (bf16[704,1024]{1,0:T(8,128)(2,1)}, bf16[704,1024]{1,0:T(8,128)(2,1)}, u32[]{:S(2)}, u32[]{:S(2)}) collective-permute-start(bf16[704,1024]{1,0:T(8,128)(2,1)} %get-tuple-element.563), channel_id=1, source_target_pairs={{0,8},{4,12},{8,0},{12,4},{16,24},{20,28},{24,16},{28,20},{1,9},{5... | collective-permute-start | bytes 4325384 | tf_op jit(solution)/shard_map/ppermute | solution.py:38
  400.0 41.3 %collective-permute-start.43 = (bf16[704,1024]{1,0:T(8,128)(2,1)}, bf16[704,1024]{1,0:T(8,128)(2,1)}, u32[]{:S(2)}, u32[]{:S(2)}) collective-permute-start(bf16[704,1024]{1,0:T(8,128)(2,1)} %get-tuple-element.566), channel_id=1, source_target_pairs={{0,16},{4,20},{8,24},{12,28},{16,0},{20,4},{24,8},{28,12},{1,17},{... | collective-permute-start | bytes 4325384 | tf_op jit(solution)/shard_map/ppermute | solution.py:38
  441.3 164.7 %reduce-scatter.11.cloned.1.call-start = ((), (), s32[]{:S(2)}) async-start(), calls=%async_computation.11 | async-start | bytes 2621440 | tf_op jit(solution)/shard_map/reduce_scatter | solution.py:946
  441.4 51.5 %collective-permute-start.48 = (bf16[512,1408]{1,0:T(8,128)(2,1)}, bf16[512,1408]{1,0:T(8,128)(2,1)}, u32[]{:S(2)}, u32[]{:S(2)}) collective-permute-start(bf16[512,1408]{1,0:T(8,128)(2,1)} %copy-done.58), channel_id=1, source_target_pairs={{0,8},{4,12},{8,0},{12,4},{16,24},{20,28},{24,16},{28,20},{1,9},{5... | collective-permute-start | bytes 4325384 | tf_op jit(solution)/shard_map/ppermute | solution.py:38
  442.0 50.8 %collective-permute-start.49 = (bf16[512,1408]{1,0:T(8,128)(2,1)}, bf16[512,1408]{1,0:T(8,128)(2,1)}, u32[]{:S(2)}, u32[]{:S(2)}) collective-permute-start(bf16[512,1408]{1,0:T(8,128)(2,1)} %copy-done.59), channel_id=1, source_target_pairs={{0,16},{4,20},{8,24},{12,28},{16,0},{20,4},{24,8},{28,12},{1,17},{... | collective-permute-start | bytes 4325384 | tf_op jit(solution)/shard_map/ppermute | solution.py:38
  460.3 30.8 %collective-permute-start.51 = (bf16[352,1024]{1,0:T(8,128)(2,1)S(1)}, bf16[352,1024]{1,0:T(8,128)(2,1)S(1)}, u32[]{:S(2)}, u32[]{:S(2)}) collective-permute-start(bf16[352,1024]{1,0:T(8,128)(2,1)S(1)} %get-tuple-element.767), channel_id=1, source_target_pairs={{0,8},{4,12},{8,0},{12,4},{16,24},{20,28},{24,16},{28,20},{1,9},{5... | collective-permute-start | bytes 2162696 | tf_op jit(solution)/shard_map/ppermute | solution.py:38
  462.0 30.0 %collective-permute-start.50 = (bf16[352,1024]{1,0:T(8,128)(2,1)S(1)}, bf16[352,1024]{1,0:T(8,128)(2,1)S(1)}, u32[]{:S(2)}, u32[]{:S(2)}) collective-permute-start(bf16[352,1024]{1,0:T(8,128)(2,1)S(1)} %get-tuple-element.769), channel_id=1, source_target_pairs={{0,16},{4,20},{8,24},{12,28},{16,0},{20,4},{24,8},{28,12},{1,17},{... | collective-permute-start | bytes 2162696 | tf_op jit(solution)/shard_map/ppermute | solution.py:38
  492.9 34.8 %collective-permute-start.54 = (bf16[512,1408]{1,0:T(8,128)(2,1)}, bf16[512,1408]{1,0:T(8,128)(2,1)}, u32[]{:S(2)}, u32[]{:S(2)}) collective-permute-start(bf16[512,1408]{1,0:T(8,128)(2,1)} %copy-done.56), channel_id=1, source_target_pairs={{0,8},{4,12},{8,0},{12,4},{16,24},{20,28},{24,16},{28,20},{1,9},{5... | collective-permute-start | bytes 4325384 | tf_op jit(solution)/shard_map/ppermute | solution.py:38
  493.9 152.9 %reduce-scatter.9.cloned.1.call-start = ((), (), s32[]{:S(2)}) async-start(), calls=%async_computation.10 | async-start | bytes 2621440 | tf_op jit(solution)/shard_map/reduce_scatter | solution.py:946
  494.1 39.5 %collective-permute-start.55 = (bf16[512,1408]{1,0:T(8,128)(2,1)}, bf16[512,1408]{1,0:T(8,128)(2,1)}, u32[]{:S(2)}, u32[]{:S(2)}) collective-permute-start(bf16[512,1408]{1,0:T(8,128)(2,1)} %copy-done.57), channel_id=1, source_target_pairs={{0,16},{4,20},{8,24},{12,28},{16,0},{20,4},{24,8},{28,12},{1,17},{... | collective-permute-start | bytes 4325384 | tf_op jit(solution)/shard_map/ppermute | solution.py:38
  516.9 32.7 %collective-permute-start.53 = (bf16[1024,512]{1,0:T(8,128)(2,1)}, bf16[1024,512]{1,0:T(8,128)(2,1)S(1)}, u32[]{:S(2)}, u32[]{:S(2)}) collective-permute-start(bf16[1024,512]{1,0:T(8,128)(2,1)} %get-tuple-element.631), channel_id=1, source_target_pairs={{8,0},{12,4},{24,16},{28,20},{9,1},{13,5},{25,17},{29,21},{10,2},{... | collective-permute-start | bytes 3145736 | tf_op jit(solution)/shard_map/ppermute | solution.py:940
  530.5 35.5 %collective-permute-start.56 = (bf16[256,1408]{1,0:T(8,128)(2,1)}, bf16[256,1408]{1,0:T(8,128)(2,1)}, u32[]{:S(2)}, u32[]{:S(2)}) collective-permute-start(bf16[256,1408]{1,0:T(8,128)(2,1)} %get-tuple-element.758), channel_id=1, source_target_pairs={{0,16},{4,20},{8,24},{12,28},{16,0},{20,4},{24,8},{28,12},{1,17},{... | collective-permute-start | bytes 2162696 | tf_op jit(solution)/shard_map/ppermute | solution.py:38
  569.5 36.5 %collective-permute-start.61 = (bf16[1024,384]{1,0:T(8,128)(2,1)}, bf16[1024,384]{1,0:T(8,128)(2,1)}, u32[]{:S(2)}, u32[]{:S(2)}) collective-permute-start(bf16[1024,384]{1,0:T(8,128)(2,1)} %get-tuple-element.669), channel_id=1, source_target_pairs={{0,8},{4,12},{8,0},{12,4},{16,24},{20,28},{24,16},{28,20},{1,9},{5... | collective-permute-start | bytes 2359304 | tf_op jit(solution)/shard_map/ppermute | solution.py:38
  569.8 36.1 %collective-permute-start.62 = (bf16[1024,384]{1,0:T(8,128)(2,1)}, bf16[1024,384]{1,0:T(8,128)(2,1)}, u32[]{:S(2)}, u32[]{:S(2)}) collective-permute-start(bf16[1024,384]{1,0:T(8,128)(2,1)} %get-tuple-element.670), channel_id=1, source_target_pairs={{0,16},{4,20},{8,24},{12,28},{16,0},{20,4},{24,8},{28,12},{1,17},{... | collective-permute-start | bytes 2359304 | tf_op jit(solution)/shard_map/ppermute | solution.py:38
  571.1 34.8 %collective-permute-start.63 = (bf16[256,1408]{1,0:T(8,128)(2,1)}, bf16[256,1408]{1,0:T(8,128)(2,1)}, u32[]{:S(2)}, u32[]{:S(2)}) collective-permute-start(bf16[256,1408]{1,0:T(8,128)(2,1)} %get-tuple-element.671), channel_id=1, source_target_pairs={{0,16},{4,20},{8,24},{12,28},{16,0},{20,4},{24,8},{28,12},{1,17},{... | collective-permute-start | bytes 2162696 | tf_op jit(solution)/shard_map/ppermute | solution.py:38
  571.8 34.1 %collective-permute-start.64 = (bf16[256,1408]{1,0:T(8,128)(2,1)}, bf16[256,1408]{1,0:T(8,128)(2,1)}, u32[]{:S(2)}, u32[]{:S(2)}) collective-permute-start(bf16[256,1408]{1,0:T(8,128)(2,1)} %get-tuple-element.672), channel_id=1, source_target_pairs={{0,8},{4,12},{8,0},{12,4},{16,24},{20,28},{24,16},{28,20},{1,9},{5... | collective-permute-start | bytes 2162696 | tf_op jit(solution)/shard_map/ppermute | solution.py:38
  599.2 19.4 %collective-permute-start.65 = (bf16[512,512]{1,0:T(8,128)(2,1)}, bf16[512,512]{1,0:T(8,128)(2,1)}, u32[]{:S(2)}, u32[]{:S(2)}) collective-permute-start(bf16[512,512]{1,0:T(8,128)(2,1)} %get-tuple-element.681), channel_id=1, source_target_pairs={{0,16},{4,20},{8,24},{12,28},{16,0},{20,4},{24,8},{28,12},{1,17},{... | collective-permute-start | bytes 1572872 | tf_op jit(solution)/shard_map/ppermute | solution.py:38
  (177 other events, 1203.6 us)
Sparse Core Ops, SparseCore 0:
  12.4 48.3 all-gather.4
  70.2 48.7 all-gather.6
  143.2 44.7 reduce-scatter.4
  198.9 45.6 all-gather.8
  378.6 46.6 reduce-scatter.6
  441.5 45.9 all-gather.10
  494.0 44.3 reduce-scatter.10
  581.9 43.6 reduce-scatter.8
